TPU v7x, 32 devices: a whole 2x2x4 slice. The times are simulated.
32 devices in a mesh: sample: 2 (over x), space: 16 (over z, y, core).
Axes of the slice: x: 2, y: 2, z: 4, core: 2. Of those that a mesh axis runs over, the one named last changes fastest.
Arguments:
- volumes: bfloat16 [2, 64, 16, 64, 128], P('sample', 'space'), may hold values from -6 to 6
- fine_kernel: bfloat16 [27, 128, 128], replicated, may hold values from -0.109375 to 0.109375
- coarse_kernel: bfloat16 [27, 128, 256], replicated, may hold values from -0.109375 to 0.109375
- cotangent: bfloat16 [2, 32, 8, 32, 256], P('sample', 'space'), may hold values from -6 to 6
Outputs:
- coarse_out: bfloat16 [2, 32, 8, 32, 256], P('sample', 'space')
- fine_grad: float32 [128, 3456], P('space')
- coarse_grad: float32 [256, 3456], P('space')
All inputs are finite; a program needn't handle non-finite values.
Results may differ from a plain program's by a relative error of at most 0.014.
Values may be sent and summed in bfloat16 or wider, within the bound.
No kernel may reach another device: no remote copies, remote signals or barrier semaphores. Data moves between devices by JAX's collectives and lax.ppermute only.
A program may use at most 128 MiB of HBM per device.

v0:
```python
import jax
import jax.numpy as jnp
from jax import lax
from jax.sharding import PartitionSpec as P


def padded_2(x, sides, width):
    for axis, dim in sides:
        count, length = (lax.axis_size(axis), x.shape[dim])
        up = [(i, (i + 1) % count) for i in range(count - 1)]
        down = [(j, i) for i, j in up]
        last = lax.slice_in_dim(x, length - width, length, axis=dim)
        initial = lax.slice_in_dim(x, 0, width, axis=dim)
        before = lax.ppermute(last, axis, up)
        after = lax.ppermute(initial, axis, down)
        x = jnp.concatenate([before, x, after], axis=dim)
    return x


def silu_slope(value):
    sig = jax.nn.sigmoid(value)
    return sig * (1.0 + value * (1.0 - sig))


def shifted(padded, tap, shape):
    first, second, third = (tap // 9, tap // 3 % 3, tap % 3)
    piece = padded[first : first + shape[0], second : second + shape[1], third : third + shape[2]]
    return piece.reshape(-1, padded.shape[-1])


def pad_sides(walled):
    return jnp.pad(walled, ((0, 0), (0, 0), (1, 1), (1, 1), (0, 0)))


def forward_taps(padded, kernel, shape):
    total = jnp.zeros((shape[0] * shape[1] * shape[2], kernel.shape[2]), jnp.float32)
    for tap in range(27):
        total = total + jnp.dot(
            shifted(padded, tap, shape), kernel[tap], preferred_element_type=jnp.float32
        )
    return total


def backward_taps(padded, kernel, shape):
    total = jnp.zeros((shape[0] * shape[1] * shape[2], kernel.shape[1]), jnp.float32)
    for tap in range(27):
        total = total + lax.dot_general(
            shifted(padded, 26 - tap, shape),
            kernel[tap],
            (((1,), (1,)), ((), ())),
            preferred_element_type=jnp.float32,
        )
    return total


def kernel_term(deltas, paddeds, shape):
    pieces = []
    for tap in range(27):
        total = None
        for delta_rows, padded in zip(deltas, paddeds):
            term = lax.dot_general(
                delta_rows,
                shifted(padded, tap, shape),
                (((0,), (0,)), ((), ())),
                preferred_element_type=jnp.float32,
            )
            total = term
        pieces.append(total)
    return jnp.concatenate(pieces, axis=1)


def shards(volumes, fine_kernel, coarse_kernel, cotangent):
    count_here, planes, fy, fz, chan = volumes.shape
    wide = coarse_kernel.shape[2]
    fine_shape = (planes, fy, fz)
    coarse_shape = (planes // 2, fy // 2, fz // 2)
    fine_pad = pad_sides(padded_2(volumes, (("space", 1),), 1))
    index = 0
    fine_pre = forward_taps(fine_pad[index], fine_kernel, fine_shape)
    fine_act = jax.nn.silu(fine_pre).astype(jnp.bfloat16)
    blocks = fine_act.astype(jnp.float32).reshape(planes // 2, 2, fy // 2, 2, fz // 2, 2, chan)
    pooled_list = [jnp.mean(blocks, axis=(1, 3, 5)).astype(jnp.bfloat16)]
    fine_pres = [fine_pre]
    pooled = jnp.stack(pooled_list)
    coarse_pad = pad_sides(padded_2(pooled, (("space", 1),), 1))
    index = 0
    coarse_pre = forward_taps(coarse_pad[index], coarse_kernel, coarse_shape)
    outputs = [jax.nn.silu(coarse_pre).astype(jnp.bfloat16).reshape(coarse_shape + (wide,))]
    grad_rows = cotangent[index].reshape(-1, wide).astype(jnp.float32)
    coarse_deltas = [(grad_rows * silu_slope(coarse_pre)).astype(jnp.bfloat16)]
    delta_field = jnp.stack([item.reshape(coarse_shape + (wide,)) for item in coarse_deltas])
    delta_pad = pad_sides(padded_2(delta_field, (("space", 1),), 1))
    index = 0
    pooled_grad = backward_taps(delta_pad[index], coarse_kernel, coarse_shape).astype(jnp.bfloat16)
    spread = pooled_grad.astype(jnp.float32).reshape(coarse_shape + (chan,)) / 8.0
    spread = jnp.repeat(jnp.repeat(jnp.repeat(spread, 2, axis=0), 2, axis=1), 2, axis=2)
    fine_deltas = [(spread.reshape(-1, chan) * silu_slope(fine_pres[index])).astype(jnp.bfloat16)]
    fine_pads = [fine_pad[0]]
    coarse_pads = [coarse_pad[0]]
    fine_full = kernel_term(fine_deltas, fine_pads, fine_shape)
    coarse_full = kernel_term(coarse_deltas, coarse_pads, coarse_shape)
    fine_part, coarse_part = (
        lax.psum_scatter(fine_full, "space", scatter_dimension=0, tiled=True),
        lax.psum_scatter(coarse_full, "space", scatter_dimension=0, tiled=True),
    )
    fine_grad, coarse_grad = (
        lax.psum(fine_part.astype(jnp.bfloat16), "sample").astype(jnp.float32),
        lax.psum(coarse_part.astype(jnp.bfloat16), "sample").astype(jnp.float32),
    )
    return (jnp.stack(outputs), fine_grad, coarse_grad)


def solution(mesh):
    placed = (
        P("sample", "space", None, None, None),
        P(),
        P(),
        P("sample", "space", None, None, None),
    )
    return jax.shard_map(
        shards,
        mesh=mesh,
        in_specs=placed,
        out_specs=(P("sample", "space", None, None, None), P("space", None), P("space", None)),
        check_vma=False,
    )
```

profile of v0, /device:TPU:0, one launch (start us, length us, event | category | flops | bytes accessed | tf_op | source)
XLA Modules:
  0.0 288.2 jit_solution(18135642409389463954)
XLA Ops:
  7.2 1.1 fusion.193
  8.3 1.3 collective-permute-start.1
  9.6 3.0 %collective-permute-start = (bf16[1,1,16,64,128]{4,3,2,1,0:T(8,128)(2,1)S(1)}, bf16[1,1,16,64,128]{4,3,2,1,0:T(8,128)(2,1)S(1)}, u32[]{:S(2)}, u32[]{:S(2)}) collective-permute-start(bf16[1,1,16,64,128]{4,3,2,1,0:T(8,128)(2,1)S(1)} %get-tuple-element.36), channel_id=1, source_target_pairs={{0,1},{1,2},{2,3},{3,4},{4,5},{5,6},{6,7},{7,8},{8,9},{9,10},{10,1... | collective-permute-start | bytes 786440 | tf_op jit(solution)/shard_map/ppermute | solution.py:14
  12.6 1.1 collective-permute-done
  13.8 2.7 fusion.3
  16.5 3.5 %fusion.192 = (bf16[4,16,64,128]{3,2,1,0:T(8,128)(2,1)}, bf16[4,16,64,128]{3,2,1,0:T(8,128)(2,1)}, bf16[4,16,64,128]{3,2,1,0:T(8,128)(2,1)}, bf16[4,16,64,128]{3...) fusion(bf16[6,18,66,128]{3,2,1,0:T(8,128)(2,1)S(1)} %fusion.3), kind=kLoop, calls=%fused_computation.351 | loop fusion | bytes 16777216 | tf_op jit(solution)/shard_map/slice | solution.py:27
  20.0 7.7 %fusion.191 = (bf16[4,16,64,128]{3,2,1,0:T(8,128)(2,1)}, bf16[4,16,64,128]{3,2,1,0:T(8,128)(2,1)S(1)}, bf16[4,16,64,128]{3,2,1,0:T(8,128)(2,1)S(1)}, bf16[4,16,6...) fusion(bf16[6,18,66,128]{3,2,1,0:T(8,128)(2,1)S(1)} %fusion.3), kind=kLoop, calls=%fused_computation.350 | loop fusion | bytes 39845888 | tf_op jit(solution)/shard_map/slice | solution.py:27
  27.8 1.3 fusion.162
  29.8 0.9 copy-done.51
  31.2 1.2 copy-done.40
  53.0 2.1 multiply_convert_fusion.1
  55.0 1.3 convert_reduce_fusion
  56.4 1.3 collective-permute-start.3
  57.7 9.2 %collective-permute-start.2 = (bf16[1,1,8,32,128]{4,3,2,1,0:T(8,128)(2,1)S(1)}, bf16[1,1,8,32,128]{4,3,2,1,0:T(8,128)(2,1)S(1)}, u32[]{:S(2)}, u32[]{:S(2)}) collective-permute-start(bf16[1,1,8,32,128]{4,3,2,1,0:T(8,128)(2,1)S(1)} %get-tuple-element.96), channel_id=1, source_target_pairs={{0,1},{1,2},{2,3},{3,4},{4,5},{5,6},{6,7},{7,8},{8,9},{9,10},{10,1... | collective-permute-start | bytes 196616 | tf_op jit(solution)/shard_map/ppermute | solution.py:14
  69.0 1.0 copy-done.46
  76.0 1.1 fusion.20
  77.1 0.9 convolution_dynamic-update-slice_fusion.26
  78.7 1.3 collective-permute-start.5
  79.9 5.7 %collective-permute-start.4 = (bf16[1,1,8,32,256]{4,3,2,1,0:T(8,128)(2,1)S(1)}, bf16[1,1,8,32,256]{4,3,2,1,0:T(8,128)(2,1)}, u32[]{:S(2)}, u32[]{:S(2)}) collective-permute-start(bf16[1,1,8,32,256]{4,3,2,1,0:T(8,128)(2,1)S(1)} %get-tuple-element.94), channel_id=1, source_target_pairs={{0,1},{1,2},{2,3},{3,4},{4,5},{5,6},{6,7},{7,8},{8,9},{9,10},{10,1... | collective-permute-start | bytes 393224 | tf_op jit(solution)/shard_map/ppermute | solution.py:14
  85.7 0.9 convolution_dynamic-update-slice_fusion.25
  87.5 0.9 convolution_dynamic-update-slice_fusion.23
  89.3 0.9 convolution_dynamic-update-slice_fusion.21
  91.0 0.9 convolution_dynamic-update-slice_fusion.19
  92.0 0.9 convolution_dynamic-update-slice_fusion.18
  92.9 0.9 convolution_dynamic-update-slice_fusion.17
  93.8 0.9 convolution_dynamic-update-slice_fusion.16
  97.3 0.9 convolution_dynamic-update-slice_fusion.12
  102.7 0.9 convolution_dynamic-update-slice_fusion.6
  108.0 0.9 convolution_dynamic-update-slice_fusion
  108.9 5.2 %copy.13 = f32[256,3456]{1,0:T(8,128)} copy(f32[256,3456]{0,1:T(8,128)} %convolution_dynamic-update-slice_fusion) | data formatting | bytes 7077888
  114.4 1.3 fusion.13
  126.7 1.1 convolution_dynamic-update-slice_fusion.53
  128.0 1.1 convolution_dynamic-update-slice_fusion.52
  129.1 1.1 convolution_dynamic-update-slice_fusion.51
  130.2 1.1 convolution_dynamic-update-slice_fusion.50
  131.4 1.1 convolution_dynamic-update-slice_fusion.49
  132.5 1.1 convolution_dynamic-update-slice_fusion.48
  133.6 1.1 convolution_dynamic-update-slice_fusion.47
  134.7 1.1 convolution_dynamic-update-slice_fusion.46
  135.9 1.1 convolution_dynamic-update-slice_fusion.45
  137.0 1.1 convolution_dynamic-update-slice_fusion.44
  138.1 1.1 convolution_dynamic-update-slice_fusion.43
  139.3 1.1 convolution_dynamic-update-slice_fusion.42
  140.4 1.1 convolution_dynamic-update-slice_fusion.41
  141.5 1.1 convolution_dynamic-update-slice_fusion.40
  142.7 1.4 convolution_dynamic-update-slice_fusion.39
  144.0 1.2 convolution_dynamic-update-slice_fusion.38
  145.2 1.1 convolution_dynamic-update-slice_fusion.37
  146.3 1.1 convolution_dynamic-update-slice_fusion.36
  147.5 1.1 convolution_dynamic-update-slice_fusion.35
  148.6 1.1 convolution_dynamic-update-slice_fusion.34
  149.7 1.1 convolution_dynamic-update-slice_fusion.33
  150.9 1.1 convolution_dynamic-update-slice_fusion.32
  152.0 1.1 convolution_dynamic-update-slice_fusion.31
  153.1 1.1 convolution_dynamic-update-slice_fusion.30
  154.3 1.1 convolution_dynamic-update-slice_fusion.29
  155.4 1.1 convolution_dynamic-update-slice_fusion.28
  156.5 1.1 convolution_dynamic-update-slice_fusion.27
  157.6 75.8 %all-reduce.8 = bf16[128,3456]{0,1:T(8,128)(2,1)S(1)} all-reduce(f32[128,3456]{0,1:T(8,128)} %convolution_dynamic-update-slice_fusion.27), channel_id=2, replica_groups=mesh['sample'=2,'space'=16] {'space'}, use_global_device_ids=true, to_apply=%region_1.2.clone | all-reduce | flops 442368 | bytes 2654208
  233.5 2.2 copy.14
  236.1 31.1 %psum.14 = bf16[8,3456]{0,1:T(8,128)(2,1)S(1)} all-reduce(bf16[8,3456]{0,1:T(8,128)(2,1)S(1)} %dynamic-slice_convert_fusion), channel_id=1, replica_groups=mesh['sample'=2,'space'=16] {'sample'}, use_global_device_ids=true, to_apply=%region_2.3 | all-reduce | flops 27648 | bytes 110592 | tf_op jit(solution)/shard_map/psum | solution.py:107
  267.2 0.9 copy.9
  268.1 10.9 %all-reduce.7.cloned.1.call-done = bf16[16,3456]{0,1:T(8,128)(2,1)} async-done(((bf16[16,3456]{0,1:T(8,128)(2,1)}), bf16[16,3456]{0,1:T(8,128)(2,1)}) %all-reduce.7.cloned.1.call-update) | async-done | bytes 110608 | tf_op jit(solution)/shard_map/psum | solution.py:108
  279.0 2.1 copy.10
  (223 shorter events, 55.2 us)
Async XLA Ops:
  7.2 226.3 %reduce-scatter.5.cloned.1.call-start = ((), (), s32[]{:S(2)}) async-start(), calls=%async_computation.2 | async-start | bytes 3760128
  8.3 4.4 %collective-permute-start.1 = (bf16[1,1,16,64,128]{4,3,2,1,0:T(8,128)(2,1)S(1)}, bf16[1,1,16,64,128]{4,3,2,1,0:T(8,128)(2,1)S(1)}, u32[]{:S(2)}, u32[]{:S(2)}) collective-permute-start(bf16[1,1,16,64,128]{4,3,2,1,0:T(8,128)(2,1)S(1)} %get-tuple-element.37), channel_id=1, source_target_pairs={{1,0},{2,1},{3,2},{4,3},{5,4},{6,5},{7,6},{8,7},{9,8},{10,9},{11,1... | collective-permute-start | bytes 786440 | tf_op jit(solution)/shard_map/ppermute | solution.py:15
  9.6 4.2 %collective-permute-start = (bf16[1,1,16,64,128]{4,3,2,1,0:T(8,128)(2,1)S(1)}, bf16[1,1,16,64,128]{4,3,2,1,0:T(8,128)(2,1)S(1)}, u32[]{:S(2)}, u32[]{:S(2)}) collective-permute-start(bf16[1,1,16,64,128]{4,3,2,1,0:T(8,128)(2,1)S(1)} %get-tuple-element.36), channel_id=1, source_target_pairs={{0,1},{1,2},{2,3},{3,4},{4,5},{5,6},{6,7},{7,8},{8,9},{9,10},{10,1... | collective-permute-start | bytes 786440 | tf_op jit(solution)/shard_map/ppermute | solution.py:14
  20.0 7.8 %copy-start.44 = (bf16[4,16,64,128]{3,2,1,0:T(8,128)(2,1)}, bf16[4,16,64,128]{3,2,1,0:T(8,128)(2,1)S(1)}, u32[]{:S(2)}) copy-start(bf16[4,16,64,128]{3,2,1,0:T(8,128)(2,1)S(1)} %get-tuple-element.35) | copy-start | bytes 3145732
  27.7 19.8 %copy-start.14 = (bf16[4,16,64,128]{3,2,1,0:T(8,128)(2,1)}, bf16[4,16,64,128]{3,2,1,0:T(8,128)(2,1)S(1)}, u32[]{:S(2)}) copy-start(bf16[4,16,64,128]{3,2,1,0:T(8,128)(2,1)S(1)} %get-tuple-element.20) | copy-start | bytes 3145732
  27.7 20.2 %copy-start.12 = (bf16[4,16,64,128]{3,2,1,0:T(8,128)(2,1)}, bf16[4,16,64,128]{3,2,1,0:T(8,128)(2,1)S(1)}, u32[]{:S(2)}) copy-start(bf16[4,16,64,128]{3,2,1,0:T(8,128)(2,1)S(1)} %get-tuple-element.19) | copy-start | bytes 3145732
  27.7 20.6 %copy-start.10 = (bf16[4,16,64,128]{3,2,1,0:T(8,128)(2,1)}, bf16[4,16,64,128]{3,2,1,0:T(8,128)(2,1)S(1)}, u32[]{:S(2)}) copy-start(bf16[4,16,64,128]{3,2,1,0:T(8,128)(2,1)S(1)} %get-tuple-element.18) | copy-start | bytes 3145732
  27.7 21.0 %copy-start.8 = (bf16[4,16,64,128]{3,2,1,0:T(8,128)(2,1)}, bf16[4,16,64,128]{3,2,1,0:T(8,128)(2,1)S(1)}, u32[]{:S(2)}) copy-start(bf16[4,16,64,128]{3,2,1,0:T(8,128)(2,1)S(1)} %get-tuple-element.17) | copy-start | bytes 3145732
  27.7 21.4 %copy-start.6 = (bf16[4,16,64,128]{3,2,1,0:T(8,128)(2,1)}, bf16[4,16,64,128]{3,2,1,0:T(8,128)(2,1)S(1)}, u32[]{:S(2)}) copy-start(bf16[4,16,64,128]{3,2,1,0:T(8,128)(2,1)S(1)} %get-tuple-element.16) | copy-start | bytes 3145732
  27.7 21.9 %copy-start.4 = (bf16[4,16,64,128]{3,2,1,0:T(8,128)(2,1)}, bf16[4,16,64,128]{3,2,1,0:T(8,128)(2,1)S(1)}, u32[]{:S(2)}) copy-start(bf16[4,16,64,128]{3,2,1,0:T(8,128)(2,1)S(1)} %get-tuple-element.15) | copy-start | bytes 3145732
  27.7 22.3 %copy-start.2 = (bf16[4,16,64,128]{3,2,1,0:T(8,128)(2,1)}, bf16[4,16,64,128]{3,2,1,0:T(8,128)(2,1)S(1)}, u32[]{:S(2)}) copy-start(bf16[4,16,64,128]{3,2,1,0:T(8,128)(2,1)S(1)} %get-tuple-element.14) | copy-start | bytes 3145732
  27.8 22.7 %copy-start = (bf16[4,16,64,128]{3,2,1,0:T(8,128)(2,1)}, bf16[4,16,64,128]{3,2,1,0:T(8,128)(2,1)S(1)}, u32[]{:S(2)}) copy-start(bf16[4,16,64,128]{3,2,1,0:T(8,128)(2,1)S(1)} %get-tuple-element.13) | copy-start | bytes 3145732
  27.8 2.1 copy-start.42
  27.8 3.0 %copy-start.51 = (bf16[27,128,128]{2,1,0:T(8,128)(2,1)S(1)}, bf16[27,128,128]{2,1,0:T(8,128)(2,1)}, u32[]{:S(2)}) copy-start(bf16[27,128,128]{2,1,0:T(8,128)(2,1)} %param.5) | copy-start | bytes 2654212
  30.7 1.6 copy-start.40
  32.3 1.2 copy-start.38
  33.6 1.2 copy-start.36
  34.8 1.2 copy-start.34
  36.0 1.2 copy-start.32
  37.2 1.2 copy-start.30
  38.5 1.2 copy-start.28
  39.7 1.2 copy-start.26
  40.9 1.2 copy-start.24
  42.1 1.2 copy-start.22
  43.4 1.2 copy-start.20
  44.6 1.2 copy-start.18
  45.8 1.2 copy-start.16
  51.7 1.2 copy-start.48
  53.0 14.0 %copy-start.53 = (u32[32]{0:T(128)S(1)}, u32[32]{0:T(128)}, u32[]{:S(2)}) copy-start(u32[32]{0:T(128)} %constant.26) | copy-start | bytes 388
  56.4 11.8 %collective-permute-start.3 = (bf16[1,1,8,32,128]{4,3,2,1,0:T(8,128)(2,1)S(1)}, bf16[1,1,8,32,128]{4,3,2,1,0:T(8,128)(2,1)S(1)}, u32[]{:S(2)}, u32[]{:S(2)}) collective-permute-start(bf16[1,1,8,32,128]{4,3,2,1,0:T(8,128)(2,1)S(1)} %get-tuple-element.97), channel_id=1, source_target_pairs={{1,0},{2,1},{3,2},{4,3},{5,4},{6,5},{7,6},{8,7},{9,8},{10,9},{11,1... | collective-permute-start | bytes 196616 | tf_op jit(solution)/shard_map/ppermute | solution.py:15
  57.7 10.5 %collective-permute-start.2 = (bf16[1,1,8,32,128]{4,3,2,1,0:T(8,128)(2,1)S(1)}, bf16[1,1,8,32,128]{4,3,2,1,0:T(8,128)(2,1)S(1)}, u32[]{:S(2)}, u32[]{:S(2)}) collective-permute-start(bf16[1,1,8,32,128]{4,3,2,1,0:T(8,128)(2,1)S(1)} %get-tuple-element.96), channel_id=1, source_target_pairs={{0,1},{1,2},{2,3},{3,4},{4,5},{5,6},{6,7},{7,8},{8,9},{9,10},{10,1... | collective-permute-start | bytes 196616 | tf_op jit(solution)/shard_map/ppermute | solution.py:14
  68.5 1.5 copy-start.46
  75.0 1.0 copy-start.52
  78.7 35.7 %collective-permute-start.5 = (bf16[1,1,8,32,256]{4,3,2,1,0:T(8,128)(2,1)}, bf16[1,1,8,32,256]{4,3,2,1,0:T(8,128)(2,1)}, u32[]{:S(2)}, u32[]{:S(2)}) collective-permute-start(bf16[1,1,8,32,256]{4,3,2,1,0:T(8,128)(2,1)} %get-tuple-element.95), channel_id=1, source_target_pairs={{1,0},{2,1},{3,2},{4,3},{5,4},{6,5},{7,6},{8,7},{9,8},{10,9},{11,1... | collective-permute-start | bytes 393224 | tf_op jit(solution)/shard_map/ppermute | solution.py:15
  79.9 34.4 %collective-permute-start.4 = (bf16[1,1,8,32,256]{4,3,2,1,0:T(8,128)(2,1)S(1)}, bf16[1,1,8,32,256]{4,3,2,1,0:T(8,128)(2,1)}, u32[]{:S(2)}, u32[]{:S(2)}) collective-permute-start(bf16[1,1,8,32,256]{4,3,2,1,0:T(8,128)(2,1)S(1)} %get-tuple-element.94), channel_id=1, source_target_pairs={{0,1},{1,2},{2,3},{3,4},{4,5},{5,6},{6,7},{7,8},{8,9},{9,10},{10,1... | collective-permute-start | bytes 393224 | tf_op jit(solution)/shard_map/ppermute | solution.py:14
  114.1 164.9 %all-reduce.7.cloned.1.call-start = ((), (), s32[]{:S(2)}) async-start(), calls=%async_computation.1 | async-start | bytes 1769472 | tf_op jit(solution)/shard_map/psum | solution.py:108
  116.0 1.5 copy-start.47
  123.8 1.7 copy-start.50
  125.5 1.3 copy-start.45
  126.7 1.3 copy-start.43
  126.7 2.4 copy-start.41
  128.0 2.3 copy-start.39
  129.1 2.2 copy-start.37
  130.2 2.3 copy-start.35
  131.4 2.3 copy-start.33
  132.5 2.2 copy-start.31
  133.6 2.3 copy-start.29
  134.7 2.3 copy-start.27
  135.9 2.3 copy-start.25
  137.0 2.3 copy-start.23
  138.1 2.2 copy-start.21
  139.3 2.3 copy-start.19
  140.4 2.3 copy-start.17
  141.5 2.5 copy-start.15
  142.6 2.5 copy-start.13
  144.0 2.3 copy-start.11
  145.2 2.3 copy-start.9
  146.3 2.3 copy-start.7
  147.5 2.3 copy-start.5
  148.6 2.3 copy-start.3
  149.7 2.3 copy-start.1
  154.3 2.3 copy-start.49
Sparse Core Ops, SparseCore 0:
  114.2 72.4 reduce-scatter.4
  235.9 43.0 all-reduce.6
where the time goes:
time: 293 us; the launch traced here: 288 us
  blocking collectives  107 us (37%)
  matrix products  81.2 us (28%)
  local copies, waits for them, and re-layouts  43.7 us (15%)
  starting transfers between devices  22.2 us (8%)
  between operations  15.9 us (5%)
  waiting for transfers between devices  12 us (4%)
  other arithmetic  6.28 us (2%)
    unnamed x1, blocking collectives  75.8 us
    dot_general x54, matrix products, kernel_term(): lax.dot_general(delta_rows, shifted(padded, tap, shape), (((0,), (0,)), (...  54.7 us
    psum x1, blocking collectives, shards(): lax.psum(fine_part.astype(jnp.bfloat16), 'sample').astype(jnp.float32)  31.1 us
    unnamed x113, local copies, waits for them, and re-layouts  28 us
    dot_general x54, matrix products, forward_taps(): jnp.dot(shifted(padded, tap, shape), kernel[tap], preferred_element_type=...  20.3 us
    ppermute x3, starting transfers between devices, padded_2(): before = lax.ppermute(last, axis, up)  18 us
    slice x6, local copies, waits for them, and re-layouts, shifted(): padded[first:first + shape[0], second:second + shape[1], third:third + sh...  12.7 us
    psum x1, waiting for transfers between devices, shards(): lax.psum(coarse_part.astype(jnp.bfloat16), 'sample').astype(jnp.float32)  10.9 us
  transfers between devices with their start and end apart: 8, of which 2 were waited for; matrix products, arithmetic and copies ran while one was open for 25% of the time, Pallas kernels for 0%

commit v1 on v0

v1 whole, which is shorter than its diff:
```python
import functools

import jax
import jax.numpy as jnp
from jax import lax
from jax.experimental import pallas as pl
from jax.experimental.pallas import tpu as pltpu
from jax.sharding import PartitionSpec as P

F32 = jnp.float32
BF16 = jnp.bfloat16
VMEM = pl.BlockSpec(memory_space=pltpu.VMEM)
SMEM = pl.BlockSpec(memory_space=pltpu.SMEM)


def size_of(shapes):
    total = 0
    for item in shapes:
        count = jnp.dtype(item.dtype).itemsize
        for extent in item.shape:
            count *= extent
        total += count
    return total


def kernel_call(body, operands, outs, scratch, flops, limit, scalars=0):
    cost = pl.CostEstimate(
        flops=flops, bytes_accessed=size_of(operands) + size_of(outs), transcendentals=0
    )
    specs = [SMEM] * scalars + [VMEM] * (len(operands) - scalars)
    return pl.pallas_call(
        body,
        out_shape=outs,
        in_specs=specs,
        out_specs=[VMEM] * len(outs),
        scratch_shapes=scratch,
        cost_estimate=cost,
        compiler_params=pltpu.CompilerParams(vmem_limit_bytes=limit * 2**20),
    )(*operands)


def neighbours(first, last, axis):
    count = lax.axis_size(axis)
    up = [(i, i + 1) for i in range(count - 1)]
    down = [(i + 1, i) for i in range(count - 1)]
    return lax.ppermute(last, axis, up), lax.ppermute(first, axis, down)


def silu_slope(value, sig):
    return sig * (1.0 + value * (1.0 - sig))


def three_shifts(value):
    depth = value.shape[1]
    at = lax.broadcasted_iota(jnp.int32, value.shape, 1)
    lower = jnp.where(at == 0, 0.0, pltpu.roll(value, 1, 1))
    upper = jnp.where(at == depth - 1, 0.0, pltpu.roll(value, depth - 1, 1))
    return lower, value, upper


def tap_dot(left, right):
    return lax.dot_general(left, right, (((0,), (0,)), ((), ())), preferred_element_type=F32)


def fine_forward(before, own, after, kernel, wide6, pooled, slope, weights, sums):
    planes, fy, fz, chan = own.shape
    half = fy // 2
    for s in range(2):
        for r in range(2):
            for q in range(2):
                b = 2 * s + r - q
                for a in range(3):
                    place = (a, s, pl.ds(r * 3 * chan, 3 * chan), pl.ds(q * chan, chan))
                    if 0 <= b <= 2:
                        weights[place] = kernel[3 * a + b]
                    else:
                        weights[place] = jnp.zeros((3 * chan, chan), BF16)

    def spread(source, plane, target):
        zero = jnp.zeros((fz, 3 * chan), BF16)
        wide6[target, 0, :, 0 : 3 * chan] = zero
        wide6[target, half, :, 3 * chan : 6 * chan] = zero

        @pl.loop(0, half)
        def _(j):
            for odd in range(2):
                row = source[plane, pl.ds(2 * j + odd, 1)].astype(F32)
                for c, piece in enumerate(three_shifts(row)):
                    lane = (1 - odd) * 3 * chan + c * chan
                    wide6[target, pl.ds(j + odd, 1), :, lane : lane + chan] = piece.astype(BF16)

    spread(before, 0, 0)
    spread(after, 0, planes + 1)

    @pl.loop(0, planes)
    def _(p):
        spread(own, p, p + 1)

    @pl.loop(0, planes // 2)
    def _(pair):
        for u in range(2):
            p = 2 * pair + u
            pre = None
            for a in range(3):
                for s in range(2):
                    rows = wide6[p + a, s : s + half].reshape(half * fz, 6 * chan)
                    term = jnp.dot(rows, weights[a, s], preferred_element_type=F32)
                    pre = term if pre is None else pre + term
            sig = jax.nn.sigmoid(pre)
            act = (pre * sig).astype(BF16).astype(F32)
            slope[p] = silu_slope(pre, sig).astype(BF16).reshape(half, fz, 2 * chan)
            act = (act[:, :chan] + act[:, chan:]).reshape(half, fz, chan)
            if u == 0:
                sums[...] = act
            else:
                sums[...] += act
        both = sums[:, pl.ds(0, fz // 2, stride=2), :] + sums[:, pl.ds(1, fz // 2, stride=2), :]
        pooled[pair] = (both * 0.125).astype(BF16)


def fill_wide3(target, plane, value):
    rows, depth, chan = value.shape
    zero = jnp.zeros((depth, 3 * chan), BF16)
    target[plane, 0] = zero
    target[plane, rows + 1] = zero
    for c, piece in enumerate(three_shifts(value.astype(F32))):
        target[plane, 1 : rows + 1, :, c * chan : (c + 1) * chan] = piece.astype(BF16)


def coarse_forward(before, own, after, kernel, cotangent, wide3, out, delta):
    planes, cy, cz, chan = own.shape
    wide = kernel.shape[-1]
    fill_wide3(wide3, 0, before[0])
    for p in range(planes):
        fill_wide3(wide3, p + 1, own[p])
    fill_wide3(wide3, planes + 1, after[0])
    for p in range(planes):
        pre = None
        for a in range(3):
            for b in range(3):
                rows = wide3[p + a, b : b + cy].reshape(cy * cz, 3 * chan)
                term = jnp.dot(rows, kernel[3 * a + b], preferred_element_type=F32)
                pre = term if pre is None else pre + term
        sig = jax.nn.sigmoid(pre)
        out[p] = (pre * sig).astype(BF16).reshape(cy, cz, wide)
        grad = cotangent[p].reshape(cy * cz, wide).astype(F32) * silu_slope(pre, sig)
        delta[p] = grad.astype(BF16).reshape(cy, cz, wide)


def put_term(term, lane, place, keep, send, order):
    if send is None:
        keep[:, lane : lane + term.shape[1]] = term.astype(BF16)
        return
    here = place[0] == 0
    rows = term.shape[0] // (2 * len(order))
    for at, owner in enumerate(order):
        low = term[owner * rows : (owner + 1) * rows]
        high = term[(owner + 1) * rows : (owner + 2) * rows]
        keep[at, :, lane : lane + term.shape[1]] = jnp.where(here, low, high).astype(BF16)
        send[at, :, lane : lane + term.shape[1]] = jnp.where(here, high, low).astype(BF16)


def coarse_terms(place, wide3, delta, keep, send=None, *, order):
    planes, cy, cz, wide = delta.shape
    span = wide3.shape[-1]
    rows = delta[...].reshape(planes * cy * cz, wide)
    for a in range(3):
        for b in range(3):
            piece = wide3[a : a + planes, b : b + cy].reshape(planes * cy * cz, span)
            put_term(tap_dot(rows, piece), (3 * a + b) * span, place, keep, send, order)


def fine_backward(before, own, after, kernel, slope, delta, wide3, spread):
    planes, cy, cz, wide = own.shape
    chan = kernel.shape[1]
    fill_wide3(wide3, 0, before[0])
    for p in range(planes):
        fill_wide3(wide3, p + 1, own[p])
    fill_wide3(wide3, planes + 1, after[0])
    for p in range(planes):
        grad = None
        for a in range(3):
            for b in range(3):
                for c in range(3):
                    rows = wide3[p + a, b : b + cy, :, c * wide : (c + 1) * wide]
                    term = lax.dot_general(
                        rows.reshape(cy * cz, wide),
                        kernel[26 - (9 * a + 3 * b + c)],
                        (((1,), (1,)), ((), ())),
                        preferred_element_type=F32,
                    )
                    grad = term if grad is None else grad + term
        grad = grad.astype(BF16).astype(F32).reshape(cy, cz, chan) * 0.125
        spread[:, pl.ds(0, cz, stride=2), :] = grad
        spread[:, pl.ds(1, cz, stride=2), :] = grad
        near = spread[...]
        both = jnp.concatenate([near, near], axis=-1)
        for u in range(2):
            delta[2 * p + u] = (both * slope[2 * p + u].astype(F32)).astype(BF16)


def fine_terms(place, wide6, delta, keep, send=None, *, order):
    planes, half, fz, double = delta.shape
    chan = double // 2
    for a in range(3):
        for b in range(3):
            total = None
            for p in range(planes):
                for q in range(2):
                    pair, parity = ((q + b) // 2, (q + b) % 2)
                    rows = delta[p, :, :, q * chan : (q + 1) * chan].reshape(half * fz, chan)
                    piece = wide6[
                        p + a, pair : pair + half, :, parity * 3 * chan : (parity + 1) * 3 * chan
                    ].reshape(half * fz, 3 * chan)
                    term = tap_dot(rows, piece)
                    total = term if total is None else total + term
            put_term(total, (3 * a + b) * 3 * chan, place, keep, send, order)


def swap(value, axis, bit):
    count = lax.axis_size(axis)
    return lax.ppermute(value, axis, [(i, i ^ bit) for i in range(count)])


def exchange_order(count):
    bits = count.bit_length() - 1
    order = []
    for at in range(count // 2):
        owner = 0
        for k in range(bits - 1):
            owner |= ((at >> (bits - 2 - k)) & 1) << (k + 1)
        order.append(owner)
    return order


def sum_terms(body, wide6, delta, rows, columns, flops, limit):
    count = lax.axis_size("space")
    me = lax.axis_index("space")
    bits = count.bit_length() - 1
    owned = rows // count
    place = jnp.reshape(me % 2, (1,)).astype(jnp.int32)
    order = exchange_order(count)
    direct = owned % 8 == 0
    if direct:
        shape = jax.ShapeDtypeStruct((count // 2, owned, columns), BF16)
        outs = [shape, shape]
    else:
        outs = [jax.ShapeDtypeStruct((rows, columns), BF16)]
    result = kernel_call(
        functools.partial(body, order=order),
        [place, wide6, delta],
        outs,
        [],
        flops,
        limit,
        scalars=1,
    )
    if direct:
        keep, send = result
    else:
        parts = result[0].reshape((2,) * bits + (owned, columns))
        parts = parts.transpose(tuple(reversed(range(bits))) + (bits, bits + 1))
        keep = lax.dynamic_index_in_dim(parts, me % 2, 0, keepdims=False)
        send = lax.dynamic_index_in_dim(parts, 1 - me % 2, 0, keepdims=False)
    total = keep.astype(F32) + swap(send, "space", 1).astype(F32)
    for k in range(1, bits):
        total = total.reshape(2, -1, owned, columns)
        mine = (me >> k) & 1
        send = lax.dynamic_index_in_dim(total, 1 - mine, 0, keepdims=False).astype(BF16)
        keep = lax.dynamic_index_in_dim(total, mine, 0, keepdims=False)
        total = keep + swap(send, "space", 1 << k).astype(F32)
    total = total.reshape(owned, columns)
    samples = lax.axis_size("sample")
    base = total.astype(BF16)
    if samples != 2:
        return lax.psum(base, "sample").astype(F32)
    return base.astype(F32) + swap(base, "sample", 1).astype(F32)


def shards(volumes, fine_kernel, coarse_kernel, cotangent):
    planes, fy, fz, chan = volumes.shape[1:]
    wide = coarse_kernel.shape[2]
    cp, cy, cz = (planes // 2, fy // 2, fz // 2)
    half = fy // 2
    shape = jax.ShapeDtypeStruct
    x = volumes[0]
    cells, few = (planes * fy * fz, cp * cy * cz)
    fine_flops, coarse_flops = (54 * cells * chan * chan, 54 * few * chan * wide)

    before, after = neighbours(x[:1], x[-1:], "space")
    wide6, pooled, slope = kernel_call(
        fine_forward,
        [before, x, after, fine_kernel.reshape(9, 3 * chan, chan)],
        [
            shape((planes + 2, half + 1, fz, 6 * chan), BF16),
            shape((cp, cy, cz, chan), BF16),
            shape((planes, half, fz, 2 * chan), BF16),
        ],
        [pltpu.VMEM((3, 2, 6 * chan, 2 * chan), BF16), pltpu.VMEM((half, fz, chan), F32)],
        fine_flops,
        24,
    )
    before, after = neighbours(pooled[:1], pooled[-1:], "space")
    wide3, out, coarse_delta = kernel_call(
        coarse_forward,
        [before, pooled, after, coarse_kernel.reshape(9, 3 * chan, wide), cotangent[0]],
        [
            shape((cp + 2, cy + 2, cz, 3 * chan), BF16),
            shape((cp, cy, cz, wide), BF16),
            shape((cp, cy, cz, wide), BF16),
        ],
        [],
        coarse_flops,
        16,
    )
    before, after = neighbours(coarse_delta[:1], coarse_delta[-1:], "space")
    coarse_grad = sum_terms(
        coarse_terms, wide3, coarse_delta, wide, 27 * chan, coarse_flops, 16
    )
    (fine_delta,) = kernel_call(
        fine_backward,
        [before, coarse_delta, after, coarse_kernel, slope],
        [shape((planes, half, fz, 2 * chan), BF16)],
        [pltpu.VMEM((cp + 2, cy + 2, cz, 3 * wide), BF16), pltpu.VMEM((cy, fz, chan), F32)],
        coarse_flops,
        16,
    )
    fine_grad = sum_terms(fine_terms, wide6, fine_delta, chan, 27 * chan, fine_flops, 24)
    return (out[None], fine_grad, coarse_grad)


def solution(mesh):
    placed = (
        P("sample", "space", None, None, None),
        P(),
        P(),
        P("sample", "space", None, None, None),
    )
    return jax.shard_map(
        shards,
        mesh=mesh,
        in_specs=placed,
        out_specs=(P("sample", "space", None, None, None), P("space", None), P("space", None)),
        check_vma=False,
    )
```

time: 293 us -> 101 us (0.34); the launches traced: 288 us -> 101 us
  blocking collectives: 107 us -> 0 us
  matrix products: 81.2 us -> 0 us
  local copies, waits for them, and re-layouts: 43.7 us -> 10.1 us
  waiting for transfers between devices: 12 us -> 34 us
  Pallas kernels: 0 us -> 18.2 us
  between operations: 15.9 us -> 0.85 us
  starting transfers between devices: 22.2 us -> 35.7 us
  other arithmetic: 6.28 us -> 1.86 us
    dot_general x135 -> x0, matrix products: 81.2 us -> none  [the longest x54 54.7 us: kernel_term(): lax.dot_general(delta_rows, shifted(padded, tap, shape), (((0,), (0,)), (...]
    unnamed x1 -> x0, blocking collectives: 75.8 us -> none
    ppermute x6 -> x16, waiting for transfers between devices: 1.13 us -> 34 us  [the longest x10 26.1 us: swap(): return lax.ppermute(value, axis, [(i, i ^ bit) for i in range(count)])]
    psum x1 -> x0, blocking collectives: 31.1 us -> none  [shards(): lax.psum(fine_part.astype(jnp.bfloat16), 'sample').astype(jnp.float32)]
    unnamed x113 -> x16, local copies, waits for them, and re-layouts: 28 us -> 8.22 us
    pallas_call x0 -> x5, Pallas kernels: none -> 18.2 us  [kernel_call(): pl.pallas_call(body, out_shape=outs, in_specs=specs, out_specs=[VMEM] * l...]
    ppermute x6 -> x16, starting transfers between devices: 21.9 us -> 35.7 us  [the longest x6 18.2 us: neighbours(): return (lax.ppermute(last, axis, up), lax.ppermute(first, axis, down))]
    slice x9 -> x3, local copies, waits for them, and re-layouts: 14.5 us -> 1.75 us  [the longest x1 1.07 us: shards(): before, after = neighbours(x[:1], x[-1:], 'space')]
  transfers between devices with their start and end apart: 8 -> 16, of which waited for: 2 -> 10; matrix products, arithmetic and copies ran while one was open for 25% -> 1% of each run, Pallas kernels for 0% -> 1%
where the time goes in v1:
time: 101 us
  starting transfers between devices  35.7 us (35%)
  waiting for transfers between devices  34 us (34%)
  Pallas kernels  18.2 us (18%)
  local copies, waits for them, and re-layouts  10.1 us (10%)
  other arithmetic  1.86 us (2%)
    ppermute x10, waiting for transfers between devices, swap(): return lax.ppermute(value, axis, [(i, i ^ bit) for i in range(count)])  26.1 us
    pallas_call x5, Pallas kernels, kernel_call(): pl.pallas_call(body, out_shape=outs, in_specs=specs, out_specs=[VMEM] * l...  18.2 us
    ppermute x6, starting transfers between devices, neighbours(): return (lax.ppermute(last, axis, up), lax.ppermute(first, axis, down))  18.2 us
    ppermute x10, starting transfers between devices, swap(): return lax.ppermute(value, axis, [(i, i ^ bit) for i in range(count)])  17.5 us
    unnamed x16, local copies, waits for them, and re-layouts  8.22 us
    ppermute x6, waiting for transfers between devices, neighbours(): return (lax.ppermute(last, axis, up), lax.ppermute(first, axis, down))  7.82 us
  transfers between devices with their start and end apart: 16, of which 10 were waited for; matrix products, arithmetic and copies ran while one was open for 1% of the time, Pallas kernels for 1%

profile of v1, /device:TPU:0, one launch (start us, length us, event | category | flops | bytes accessed | tf_op | source)
XLA Modules:
  0.0 100.7 jit_solution(6320152305897205337)
XLA Ops:
  0.6 1.1 %slice_bitcast_fusion = (bf16[1,16,64,128]{3,2,1,0:T(8,128)(2,1)S(1)}, bf16[1,16,64,128]{3,2,1,0:T(8,128)(2,1)S(1)}) fusion(bf16[1,4,16,64,128]{4,3,2,1,0:T(8,128)(2,1)} %param.4), kind=kLoop, calls=%fused_computation.9 | loop fusion | bytes 1048576 | tf_op jit(solution)/shard_map/slice | solution.py:290
  1.7 2.4 %collective-permute-start = (bf16[1,16,64,128]{3,2,1,0:T(8,128)(2,1)S(1)}, bf16[1,16,64,128]{3,2,1,0:T(8,128)(2,1)S(1)}, u32[]{:S(2)}, u32[]{:S(2)}) collective-permute-start(bf16[1,16,64,128]{3,2,1,0:T(8,128)(2,1)S(1)} %get-tuple-element.24), channel_id=1, source_target_pairs={{0,1},{1,2},{2,3},{3,4},{4,5},{5,6},{6,7},{7,8},{8,9},{9,10},{10,1... | collective-permute-start | bytes 786440 | tf_op jit(solution)/shard_map/ppermute | solution.py:46
  4.1 1.3 %collective-permute-start.1 = (bf16[1,16,64,128]{3,2,1,0:T(8,128)(2,1)S(1)}, bf16[1,16,64,128]{3,2,1,0:T(8,128)(2,1)S(1)}, u32[]{:S(2)}, u32[]{:S(2)}) collective-permute-start(bf16[1,16,64,128]{3,2,1,0:T(8,128)(2,1)S(1)} %get-tuple-element.23), channel_id=1, source_target_pairs={{1,0},{2,1},{3,2},{4,3},{5,4},{6,5},{7,6},{8,7},{9,8},{10,9},{11,1... | collective-permute-start | bytes 786440 | tf_op jit(solution)/shard_map/ppermute | solution.py:46
  5.4 0.0 collective-permute-done.before
  5.4 4.2 %collective-permute-done.1.after = bf16[1,16,64,128]{3,2,1,0:T(8,128)(2,1)S(1)} collective-permute-done((bf16[1,16,64,128]{3,2,1,0:T(8,128)(2,1)S(1)}, bf16[1,16,64,128]{3,2,1,0:T(8,128)(2,1)S(1)}, u32[]{:S(2)}, u32[]{:S(2)}) %collective-permute-start.1) | collective-permute-done | bytes 262176 | tf_op jit(solution)/shard_map/ppermute | solution.py:46
  9.6 0.0 copy-start.1
  9.6 1.2 %copy-done.1 = bf16[1,4,16,64,128]{4,3,2,1,0:T(8,128)(2,1)S(1)} copy-done((bf16[1,4,16,64,128]{4,3,2,1,0:T(8,128)(2,1)S(1)}, bf16[1,4,16,64,128]{4,3,2,1,0:T(8,128)(2,1)}, u32[]{:S(2)}) %copy-start.1) | copy-done | bytes 1048600
  10.9 0.0 copy-start.2
  10.9 1.2 %copy-done.2 = bf16[27,128,128]{2,1,0:T(8,128)(2,1)S(1)} copy-done((bf16[27,128,128]{2,1,0:T(8,128)(2,1)S(1)}, bf16[27,128,128]{2,1,0:T(8,128)(2,1)}, u32[]{:S(2)}) %copy-start.2) | copy-done | bytes 884760
  12.0 0.0 copy-start
  12.0 0.0 copy-start.3
  12.0 7.3 %shard_map.67 = (bf16[6,9,64,768]{3,2,1,0:T(8,128)(2,1)S(1)}, bf16[2,8,32,128]{3,2,1,0:T(8,128)(2,1)S(1)}, bf16[4,8,64,256]{3,2,1,0:T(8,128)(2,1)S(1)}) custom-call(bf16[1,16,64,128]{3,2,1,0:T(8,128)(2,1)S(1)} %collective-permute-done.before, bf16[4,16,64,128]{3,2,1,0:T(8,128)(2,1)S(1)} %bitcast.35, ...), custom_call_target="tpu_custom_call" | custom-call | flops 3623878656 | bytes 8945664 | tf_op jit(solution)/shard_map/pallas_call | solution.py:31
  19.3 0.0 copy-start.6
  19.3 2.4 %copy-done.6 = bf16[6,9,64,768]{3,2,1,0:T(8,128)(2,1)} copy-done((bf16[6,9,64,768]{3,2,1,0:T(8,128)(2,1)}, bf16[6,9,64,768]{3,2,1,0:T(8,128)(2,1)S(1)}, u32[]{:S(2)}) %copy-start.6) | copy-done | bytes 5308440
  21.7 6.7 %collective-permute-start.2 = (bf16[1,8,32,128]{3,2,1,0:T(8,128)(2,1)S(1)}, bf16[1,8,32,128]{3,2,1,0:T(8,128)(2,1)S(1)}, u32[]{:S(2)}, u32[]{:S(2)}) collective-permute-start(bf16[1,8,32,128]{3,2,1,0:T(8,128)(2,1)S(1)} %get-tuple-element.28), channel_id=1, source_target_pairs={{0,1},{1,2},{2,3},{3,4},{4,5},{5,6},{6,7},{7,8},{8,9},{9,10},{10,1... | collective-permute-start | bytes 196616 | tf_op jit(solution)/shard_map/ppermute | solution.py:46
  28.4 1.3 %collective-permute-start.3 = (bf16[1,8,32,128]{3,2,1,0:T(8,128)(2,1)S(1)}, bf16[1,8,32,128]{3,2,1,0:T(8,128)(2,1)S(1)}, u32[]{:S(2)}, u32[]{:S(2)}) collective-permute-start(bf16[1,8,32,128]{3,2,1,0:T(8,128)(2,1)S(1)} %get-tuple-element.27), channel_id=1, source_target_pairs={{1,0},{2,1},{3,2},{4,3},{5,4},{6,5},{7,6},{8,7},{9,8},{10,9},{11,1... | collective-permute-start | bytes 196616 | tf_op jit(solution)/shard_map/ppermute | solution.py:46
  29.7 0.0 collective-permute-done.2.before
  29.7 1.8 %collective-permute-done.3.after = bf16[1,8,32,128]{3,2,1,0:T(8,128)(2,1)S(1)} collective-permute-done((bf16[1,8,32,128]{3,2,1,0:T(8,128)(2,1)S(1)}, bf16[1,8,32,128]{3,2,1,0:T(8,128)(2,1)S(1)}, u32[]{:S(2)}, u32[]{:S(2)}) %collective-permute-start.3) | collective-permute-done | bytes 65568 | tf_op jit(solution)/shard_map/ppermute | solution.py:46
  31.5 0.0 copy-done
  31.5 0.0 copy-done.3
  31.5 2.3 %shard_map.68 = (bf16[4,10,32,384]{3,2,1,0:T(8,128)(2,1)S(1)}, bf16[2,8,32,256]{3,2,1,0:T(8,128)(2,1)}, bf16[2,8,32,256]{3,2,1,0:T(8,128)(2,1)S(1)}) custom-call(bf16[1,8,32,128]{3,2,1,0:T(8,128)(2,1)S(1)} %collective-permute-done.2.before, bf16[2,8,32,128]{3,2,1,0:T(8,128)(2,1)S(1)} %get-tuple-element.13.own, ...), custom_call_target="tpu_custom_call" | custom-call | flops 905969664 | bytes 3801088 | tf_op jit(solution)/shard_map/pallas_call | solution.py:31
  33.8 0.0 copy-start.4
  33.8 1.0 copy-done.4
  34.7 0.7 fusion.6
  35.4 5.1 %collective-permute-start.4 = (bf16[1,8,32,256]{3,2,1,0:T(8,128)(2,1)}, bf16[1,8,32,256]{3,2,1,0:T(8,128)(2,1)S(1)}, u32[]{:S(2)}, u32[]{:S(2)}) collective-permute-start(bf16[1,8,32,256]{3,2,1,0:T(8,128)(2,1)} %get-tuple-element.26), channel_id=1, source_target_pairs={{0,1},{1,2},{2,3},{3,4},{4,5},{5,6},{6,7},{7,8},{8,9},{9,10},{10,1... | collective-permute-start | bytes 393224 | tf_op jit(solution)/shard_map/ppermute | solution.py:46
  40.5 1.5 %collective-permute-start.5 = (bf16[1,8,32,256]{3,2,1,0:T(8,128)(2,1)S(1)}, bf16[1,8,32,256]{3,2,1,0:T(8,128)(2,1)S(1)}, u32[]{:S(2)}, u32[]{:S(2)}) collective-permute-start(bf16[1,8,32,256]{3,2,1,0:T(8,128)(2,1)S(1)} %get-tuple-element.25), channel_id=1, source_target_pairs={{1,0},{2,1},{3,2},{4,3},{5,4},{6,5},{7,6},{8,7},{9,8},{10,9},{11,1... | collective-permute-start | bytes 393224 | tf_op jit(solution)/shard_map/ppermute | solution.py:46
  42.0 0.0 collective-permute-done.4.before
  42.1 1.7 %collective-permute-done.5.after = bf16[1,8,32,256]{3,2,1,0:T(8,128)(2,1)S(1)} collective-permute-done((bf16[1,8,32,256]{3,2,1,0:T(8,128)(2,1)S(1)}, bf16[1,8,32,256]{3,2,1,0:T(8,128)(2,1)S(1)}, u32[]{:S(2)}, u32[]{:S(2)}) %collective-permute-start.5) | collective-permute-done | bytes 131104 | tf_op jit(solution)/shard_map/ppermute | solution.py:46
  43.8 2.2 %shard_map.69.delta = bf16[4,8,64,256]{3,2,1,0:T(8,128)(2,1)S(1)} custom-call(bf16[1,8,32,256]{3,2,1,0:T(8,128)(2,1)S(1)} %collective-permute-done.4.before, bf16[2,8,32,256]{3,2,1,0:T(8,128)(2,1)S(1)} %get-tuple-element.16.own.delta, bf16[1,8,32,256]{3,2,1,0:T(8,128)(2,1)S(1)} %collective-permute-done.5.after, bf16[27,128,256]{2,1,0:T(8,128)(2,1)S(1)} %copy-done, ...), custom_call_target="tpu_custom_call" | custom-call | flops 905969664 | bytes 4390912 | tf_op jit(solution)/shard_map/pallas_call | solution.py:31
  46.0 0.0 copy-start.7
  46.0 2.5 %copy-done.7 = bf16[6,9,64,768]{3,2,1,0:T(8,128)(2,1)S(1)} copy-done((bf16[6,9,64,768]{3,2,1,0:T(8,128)(2,1)S(1)}, bf16[6,9,64,768]{3,2,1,0:T(8,128)(2,1)}, u32[]{:S(2)}) %copy-start.7) | copy-done | bytes 5308440
  48.5 5.1 %shard_map.70 = (bf16[8,8,3456]{2,1,0:T(8,128)(2,1)S(1)}, bf16[8,8,3456]{2,1,0:T(8,128)(2,1)S(1)}) custom-call(s32[1]{0:T(128)} %bitcast.7.place, bf16[6,9,64,768]{3,2,1,0:T(8,128)(2,1)S(1)} %copy-done.7, bf16[4,8,64,256]{3,2,1,0:T(8,128)(2,1)S(1)} %shard_map.69.delta), custom_call_target="tpu_custom_call" | custom-call | flops 3623878656 | bytes 7241732 | tf_op jit(solution)/shard_map/pallas_call | solution.py:31
  53.6 0.0 copy-start.5
  53.6 4.0 %collective-permute-start.6 = (bf16[8,8,3456]{2,1,0:T(8,128)(2,1)S(1)}, bf16[8,8,3456]{2,1,0:T(8,128)(2,1)S(1)}, u32[]{:S(2)}, u32[]{:S(2)}) collective-permute-start(bf16[8,8,3456]{2,1,0:T(8,128)(2,1)S(1)} %get-tuple-element.19), channel_id=1, source_target_pairs={{0,1},{1,0},{2,3},{3,2},{4,5},{5,4},{6,7},{7,6},{8,9},{9,8},{10,11... | collective-permute-start | bytes 1327112 | tf_op jit(solution)/shard_map/ppermute | solution.py:222
  57.6 1.4 %collective-permute-done.6 = bf16[8,8,3456]{2,1,0:T(8,128)(2,1)S(1)} collective-permute-done((bf16[8,8,3456]{2,1,0:T(8,128)(2,1)S(1)}, bf16[8,8,3456]{2,1,0:T(8,128)(2,1)S(1)}, u32[]{:S(2)}, u32[]{:S(2)}) %collective-permute-start.6) | collective-permute-done | bytes 442400 | tf_op jit(solution)/shard_map/ppermute | solution.py:222
  59.0 0.1 convert_add_fusion.1
  59.2 2.6 %collective-permute-start.7 = (bf16[4,8,3456]{2,1,0:T(8,128)(2,1)S(1)}, bf16[4,8,3456]{2,1,0:T(8,128)(2,1)S(1)}, u32[]{:S(2)}, u32[]{:S(2)}) collective-permute-start(bf16[4,8,3456]{2,1,0:T(8,128)(2,1)S(1)} %fusion.1), channel_id=1, source_target_pairs={{0,2},{1,3},{2,0},{3,1},{4,6},{5,7},{6,4},{7,5},{8,10},{9,11},{10,... | collective-permute-start | bytes 663560 | tf_op jit(solution)/shard_map/ppermute | solution.py:222
  61.8 0.0 copy-done.5
  61.8 1.4 %shard_map.71 = (bf16[8,16,3456]{2,1,0:T(8,128)(2,1)S(1)}, bf16[8,16,3456]{2,1,0:T(8,128)(2,1)S(1)}) custom-call(s32[1]{0:T(128)} %bitcast.7.place, bf16[4,10,32,384]{3,2,1,0:T(8,128)(2,1)S(1)} %copy-done.5, bf16[2,8,32,256]{3,2,1,0:T(8,128)(2,1)S(1)} %get-tuple-element.16.own.delta), custom_call_target="tpu_custom_call" | custom-call | flops 905969664 | bytes 3014660 | tf_op jit(solution)/shard_map/pallas_call | solution.py:31
  63.2 0.1 collective-permute-start.11
  63.4 4.4 %collective-permute-done.7 = bf16[4,8,3456]{2,1,0:T(8,128)(2,1)S(1)} collective-permute-done((bf16[4,8,3456]{2,1,0:T(8,128)(2,1)S(1)}, bf16[4,8,3456]{2,1,0:T(8,128)(2,1)S(1)}, u32[]{:S(2)}, u32[]{:S(2)}) %collective-permute-start.7) | collective-permute-done | bytes 221216 | tf_op jit(solution)/shard_map/ppermute | solution.py:222
  67.8 1.6 %collective-permute-start.8 = (bf16[2,8,3456]{2,1,0:T(8,128)(2,1)S(1)}, bf16[2,8,3456]{2,1,0:T(8,128)(2,1)S(1)}, u32[]{:S(2)}, u32[]{:S(2)}) collective-permute-start(bf16[2,8,3456]{2,1,0:T(8,128)(2,1)S(1)} %fusion.3), channel_id=1, source_target_pairs={{0,4},{1,5},{2,6},{3,7},{4,0},{5,1},{6,2},{7,3},{8,12},{9,13},{10,... | collective-permute-start | bytes 331784 | tf_op jit(solution)/shard_map/ppermute | solution.py:222
  69.5 0.0 collective-permute-done.11
  69.5 0.2 convert_add_fusion
  69.6 0.1 fusion
  69.7 1.8 %collective-permute-start.12 = (bf16[4,16,3456]{2,1,0:T(8,128)(2,1)S(1)}, bf16[4,16,3456]{2,1,0:T(8,128)(2,1)S(1)}, u32[]{:S(2)}, u32[]{:S(2)}) collective-permute-start(bf16[4,16,3456]{2,1,0:T(8,128)(2,1)S(1)} %fusion), channel_id=1, source_target_pairs={{0,2},{1,3},{2,0},{3,1},{4,6},{5,7},{6,4},{7,5},{8,10},{9,11},{10,... | collective-permute-start | bytes 1327112 | tf_op jit(solution)/shard_map/ppermute | solution.py:222
  71.5 1.1 %collective-permute-done.8 = bf16[2,8,3456]{2,1,0:T(8,128)(2,1)S(1)} collective-permute-done((bf16[2,8,3456]{2,1,0:T(8,128)(2,1)S(1)}, bf16[2,8,3456]{2,1,0:T(8,128)(2,1)S(1)}, u32[]{:S(2)}, u32[]{:S(2)}) %collective-permute-start.8) | collective-permute-done | bytes 110624 | tf_op jit(solution)/shard_map/ppermute | solution.py:222
  72.7 8.7 %collective-permute-done.12 = bf16[4,16,3456]{2,1,0:T(8,128)(2,1)S(1)} collective-permute-done((bf16[4,16,3456]{2,1,0:T(8,128)(2,1)S(1)}, bf16[4,16,3456]{2,1,0:T(8,128)(2,1)S(1)}, u32[]{:S(2)}, u32[]{:S(2)}) %collective-permute-start.12) | collective-permute-done | bytes 442400 | tf_op jit(solution)/shard_map/ppermute | solution.py:222
  81.4 0.1 bitcast_add_fusion
  81.5 0.5 collective-permute-start.13
  82.0 2.6 %collective-permute-start.9 = (bf16[1,8,3456]{2,1,0:T(8,128)(2,1)S(1)}, bf16[1,8,3456]{2,1,0:T(8,128)(2,1)S(1)}, u32[]{:S(2)}, u32[]{:S(2)}) collective-permute-start(bf16[1,8,3456]{2,1,0:T(8,128)(2,1)S(1)} %dynamic-slice_convert_fusion.5), channel_id=1, source_target_pairs={{0,8},{1,9},{2,10},{3,11},{4,12},{5,13},{6,14},{7,15},{8,0},{9,1},... | collective-permute-start | bytes 165896 | tf_op jit(solution)/shard_map/ppermute | solution.py:222
  84.7 4.0 %collective-permute-done.13 = bf16[2,16,3456]{2,1,0:T(8,128)(2,1)S(1)} collective-permute-done((bf16[2,16,3456]{2,1,0:T(8,128)(2,1)S(1)}, bf16[2,16,3456]{2,1,0:T(8,128)(2,1)S(1)}, u32[]{:S(2)}, u32[]{:S(2)}) %collective-permute-start.13) | collective-permute-done | bytes 221216 | tf_op jit(solution)/shard_map/ppermute | solution.py:222
  88.7 0.9 collective-permute-start.14
  89.7 0.0 collective-permute-done.9
  89.7 1.6 %collective-permute-start.10 = (bf16[8,3456]{1,0:T(8,128)(2,1)S(1)}, bf16[8,3456]{1,0:T(8,128)(2,1)S(1)}, u32[]{:S(2)}, u32[]{:S(2)}) collective-permute-start(bf16[8,3456]{1,0:T(8,128)(2,1)S(1)} %fusion.5), channel_id=1, source_target_pairs={{0,16},{16,0},{1,17},{17,1},{2,18},{18,2},{3,19},{19,3},{4,20},{20... | collective-permute-start | bytes 165896 | tf_op jit(solution)/shard_map/ppermute | solution.py:222
  91.3 3.9 %collective-permute-done.14 = bf16[1,16,3456]{2,1,0:T(8,128)(2,1)S(1)} collective-permute-done((bf16[1,16,3456]{2,1,0:T(8,128)(2,1)S(1)}, bf16[1,16,3456]{2,1,0:T(8,128)(2,1)S(1)}, u32[]{:S(2)}, u32[]{:S(2)}) %collective-permute-start.14) | collective-permute-done | bytes 110624 | tf_op jit(solution)/shard_map/ppermute | solution.py:222
  95.2 1.6 %collective-permute-start.15 = (bf16[16,3456]{1,0:T(8,128)(2,1)S(1)}, bf16[16,3456]{1,0:T(8,128)(2,1)S(1)}, u32[]{:S(2)}, u32[]{:S(2)}) collective-permute-start(bf16[16,3456]{1,0:T(8,128)(2,1)S(1)} %fusion.4), channel_id=1, source_target_pairs={{0,16},{16,0},{1,17},{17,1},{2,18},{18,2},{3,19},{19,3},{4,20},{20... | collective-permute-start | bytes 331784 | tf_op jit(solution)/shard_map/ppermute | solution.py:222
  96.8 0.0 collective-permute-done.10
  96.8 0.7 convert_add_fusion.3
  97.5 2.6 %collective-permute-done.15 = bf16[16,3456]{1,0:T(8,128)(2,1)S(1)} collective-permute-done((bf16[16,3456]{1,0:T(8,128)(2,1)S(1)}, bf16[16,3456]{1,0:T(8,128)(2,1)S(1)}, u32[]{:S(2)}, u32[]{:S(2)}) %collective-permute-start.15) | collective-permute-done | bytes 110624 | tf_op jit(solution)/shard_map/ppermute | solution.py:222
  100.0 0.7 convert_add_fusion.2
  (11 shorter events, 0.3 us)
Async XLA Ops:
  1.7 3.7 %collective-permute-start = (bf16[1,16,64,128]{3,2,1,0:T(8,128)(2,1)S(1)}, bf16[1,16,64,128]{3,2,1,0:T(8,128)(2,1)S(1)}, u32[]{:S(2)}, u32[]{:S(2)}) collective-permute-start(bf16[1,16,64,128]{3,2,1,0:T(8,128)(2,1)S(1)} %get-tuple-element.24), channel_id=1, source_target_pairs={{0,1},{1,2},{2,3},{3,4},{4,5},{5,6},{6,7},{7,8},{8,9},{9,10},{10,1... | collective-permute-start | bytes 786440 | tf_op jit(solution)/shard_map/ppermute | solution.py:46
  4.1 5.5 %collective-permute-start.1 = (bf16[1,16,64,128]{3,2,1,0:T(8,128)(2,1)S(1)}, bf16[1,16,64,128]{3,2,1,0:T(8,128)(2,1)S(1)}, u32[]{:S(2)}, u32[]{:S(2)}) collective-permute-start(bf16[1,16,64,128]{3,2,1,0:T(8,128)(2,1)S(1)} %get-tuple-element.23), channel_id=1, source_target_pairs={{1,0},{2,1},{3,2},{4,3},{5,4},{6,5},{7,6},{8,7},{9,8},{10,9},{11,1... | collective-permute-start | bytes 786440 | tf_op jit(solution)/shard_map/ppermute | solution.py:46
  9.6 1.2 %copy-start.1 = (bf16[1,4,16,64,128]{4,3,2,1,0:T(8,128)(2,1)S(1)}, bf16[1,4,16,64,128]{4,3,2,1,0:T(8,128)(2,1)}, u32[]{:S(2)}) copy-start(bf16[1,4,16,64,128]{4,3,2,1,0:T(8,128)(2,1)} %param.4) | copy-start | bytes 3145732
  10.9 1.2 %copy-start.2 = (bf16[27,128,128]{2,1,0:T(8,128)(2,1)S(1)}, bf16[27,128,128]{2,1,0:T(8,128)(2,1)}, u32[]{:S(2)}) copy-start(bf16[27,128,128]{2,1,0:T(8,128)(2,1)} %param.5) | copy-start | bytes 2654212
  12.0 19.5 %copy-start = (bf16[27,128,256]{2,1,0:T(8,128)(2,1)S(1)}, bf16[27,128,256]{2,1,0:T(8,128)(2,1)}, u32[]{:S(2)}) copy-start(bf16[27,128,256]{2,1,0:T(8,128)(2,1)} %kernel.1) | copy-start | bytes 5308420
  12.0 19.5 %copy-start.3 = (bf16[1,2,8,32,256]{4,3,2,1,0:T(8,128)(2,1)S(1)}, bf16[1,2,8,32,256]{4,3,2,1,0:T(8,128)(2,1)}, u32[]{:S(2)}) copy-start(bf16[1,2,8,32,256]{4,3,2,1,0:T(8,128)(2,1)} %param.7) | copy-start | bytes 786436
  19.3 2.4 %copy-start.6 = (bf16[6,9,64,768]{3,2,1,0:T(8,128)(2,1)}, bf16[6,9,64,768]{3,2,1,0:T(8,128)(2,1)S(1)}, u32[]{:S(2)}) copy-start(bf16[6,9,64,768]{3,2,1,0:T(8,128)(2,1)S(1)} %get-tuple-element.15.wide6) | copy-start | bytes 15925252
  21.7 8.0 %collective-permute-start.2 = (bf16[1,8,32,128]{3,2,1,0:T(8,128)(2,1)S(1)}, bf16[1,8,32,128]{3,2,1,0:T(8,128)(2,1)S(1)}, u32[]{:S(2)}, u32[]{:S(2)}) collective-permute-start(bf16[1,8,32,128]{3,2,1,0:T(8,128)(2,1)S(1)} %get-tuple-element.28), channel_id=1, source_target_pairs={{0,1},{1,2},{2,3},{3,4},{4,5},{5,6},{6,7},{7,8},{8,9},{9,10},{10,1... | collective-permute-start | bytes 196616 | tf_op jit(solution)/shard_map/ppermute | solution.py:46
  28.4 3.1 %collective-permute-start.3 = (bf16[1,8,32,128]{3,2,1,0:T(8,128)(2,1)S(1)}, bf16[1,8,32,128]{3,2,1,0:T(8,128)(2,1)S(1)}, u32[]{:S(2)}, u32[]{:S(2)}) collective-permute-start(bf16[1,8,32,128]{3,2,1,0:T(8,128)(2,1)S(1)} %get-tuple-element.27), channel_id=1, source_target_pairs={{1,0},{2,1},{3,2},{4,3},{5,4},{6,5},{7,6},{8,7},{9,8},{10,9},{11,1... | collective-permute-start | bytes 196616 | tf_op jit(solution)/shard_map/ppermute | solution.py:46
  33.8 1.0 copy-start.4
  35.4 6.6 %collective-permute-start.4 = (bf16[1,8,32,256]{3,2,1,0:T(8,128)(2,1)}, bf16[1,8,32,256]{3,2,1,0:T(8,128)(2,1)S(1)}, u32[]{:S(2)}, u32[]{:S(2)}) collective-permute-start(bf16[1,8,32,256]{3,2,1,0:T(8,128)(2,1)} %get-tuple-element.26), channel_id=1, source_target_pairs={{0,1},{1,2},{2,3},{3,4},{4,5},{5,6},{6,7},{7,8},{8,9},{9,10},{10,1... | collective-permute-start | bytes 393224 | tf_op jit(solution)/shard_map/ppermute | solution.py:46
  40.5 3.2 %collective-permute-start.5 = (bf16[1,8,32,256]{3,2,1,0:T(8,128)(2,1)S(1)}, bf16[1,8,32,256]{3,2,1,0:T(8,128)(2,1)S(1)}, u32[]{:S(2)}, u32[]{:S(2)}) collective-permute-start(bf16[1,8,32,256]{3,2,1,0:T(8,128)(2,1)S(1)} %get-tuple-element.25), channel_id=1, source_target_pairs={{1,0},{2,1},{3,2},{4,3},{5,4},{6,5},{7,6},{8,7},{9,8},{10,9},{11,1... | collective-permute-start | bytes 393224 | tf_op jit(solution)/shard_map/ppermute | solution.py:46
  46.0 2.5 %copy-start.7 = (bf16[6,9,64,768]{3,2,1,0:T(8,128)(2,1)S(1)}, bf16[6,9,64,768]{3,2,1,0:T(8,128)(2,1)}, u32[]{:S(2)}) copy-start(bf16[6,9,64,768]{3,2,1,0:T(8,128)(2,1)} %copy-done.6) | copy-start | bytes 15925252
  53.6 8.2 %copy-start.5 = (bf16[4,10,32,384]{3,2,1,0:T(8,128)(2,1)S(1)}, bf16[4,10,32,384]{3,2,1,0:T(8,128)(2,1)}, u32[]{:S(2)}) copy-start(bf16[4,10,32,384]{3,2,1,0:T(8,128)(2,1)} %copy-done.4) | copy-start | bytes 2949124
  53.6 5.4 %collective-permute-start.6 = (bf16[8,8,3456]{2,1,0:T(8,128)(2,1)S(1)}, bf16[8,8,3456]{2,1,0:T(8,128)(2,1)S(1)}, u32[]{:S(2)}, u32[]{:S(2)}) collective-permute-start(bf16[8,8,3456]{2,1,0:T(8,128)(2,1)S(1)} %get-tuple-element.19), channel_id=1, source_target_pairs={{0,1},{1,0},{2,3},{3,2},{4,5},{5,4},{6,7},{7,6},{8,9},{9,8},{10,11... | collective-permute-start | bytes 1327112 | tf_op jit(solution)/shard_map/ppermute | solution.py:222
  59.2 8.6 %collective-permute-start.7 = (bf16[4,8,3456]{2,1,0:T(8,128)(2,1)S(1)}, bf16[4,8,3456]{2,1,0:T(8,128)(2,1)S(1)}, u32[]{:S(2)}, u32[]{:S(2)}) collective-permute-start(bf16[4,8,3456]{2,1,0:T(8,128)(2,1)S(1)} %fusion.1), channel_id=1, source_target_pairs={{0,2},{1,3},{2,0},{3,1},{4,6},{5,7},{6,4},{7,5},{8,10},{9,11},{10,... | collective-permute-start | bytes 663560 | tf_op jit(solution)/shard_map/ppermute | solution.py:222
  63.2 6.2 %collective-permute-start.11 = (bf16[8,16,3456]{2,1,0:T(8,128)(2,1)S(1)}, bf16[8,16,3456]{2,1,0:T(8,128)(2,1)S(1)}, u32[]{:S(2)}, u32[]{:S(2)}) collective-permute-start(bf16[8,16,3456]{2,1,0:T(8,128)(2,1)S(1)} %get-tuple-element.22), channel_id=1, source_target_pairs={{0,1},{1,0},{2,3},{3,2},{4,5},{5,4},{6,7},{7,6},{8,9},{9,8},{10,11... | collective-permute-start | bytes 2654216 | tf_op jit(solution)/shard_map/ppermute | solution.py:222
  67.8 4.8 %collective-permute-start.8 = (bf16[2,8,3456]{2,1,0:T(8,128)(2,1)S(1)}, bf16[2,8,3456]{2,1,0:T(8,128)(2,1)S(1)}, u32[]{:S(2)}, u32[]{:S(2)}) collective-permute-start(bf16[2,8,3456]{2,1,0:T(8,128)(2,1)S(1)} %fusion.3), channel_id=1, source_target_pairs={{0,4},{1,5},{2,6},{3,7},{4,0},{5,1},{6,2},{7,3},{8,12},{9,13},{10,... | collective-permute-start | bytes 331784 | tf_op jit(solution)/shard_map/ppermute | solution.py:222
  69.7 11.7 %collective-permute-start.12 = (bf16[4,16,3456]{2,1,0:T(8,128)(2,1)S(1)}, bf16[4,16,3456]{2,1,0:T(8,128)(2,1)S(1)}, u32[]{:S(2)}, u32[]{:S(2)}) collective-permute-start(bf16[4,16,3456]{2,1,0:T(8,128)(2,1)S(1)} %fusion), channel_id=1, source_target_pairs={{0,2},{1,3},{2,0},{3,1},{4,6},{5,7},{6,4},{7,5},{8,10},{9,11},{10,... | collective-permute-start | bytes 1327112 | tf_op jit(solution)/shard_map/ppermute | solution.py:222
  81.5 7.2 %collective-permute-start.13 = (bf16[2,16,3456]{2,1,0:T(8,128)(2,1)S(1)}, bf16[2,16,3456]{2,1,0:T(8,128)(2,1)S(1)}, u32[]{:S(2)}, u32[]{:S(2)}) collective-permute-start(bf16[2,16,3456]{2,1,0:T(8,128)(2,1)S(1)} %fusion.2), channel_id=1, source_target_pairs={{0,4},{1,5},{2,6},{3,7},{4,0},{5,1},{6,2},{7,3},{8,12},{9,13},{10,... | collective-permute-start | bytes 663560 | tf_op jit(solution)/shard_map/ppermute | solution.py:222
  82.0 7.7 %collective-permute-start.9 = (bf16[1,8,3456]{2,1,0:T(8,128)(2,1)S(1)}, bf16[1,8,3456]{2,1,0:T(8,128)(2,1)S(1)}, u32[]{:S(2)}, u32[]{:S(2)}) collective-permute-start(bf16[1,8,3456]{2,1,0:T(8,128)(2,1)S(1)} %dynamic-slice_convert_fusion.5), channel_id=1, source_target_pairs={{0,8},{1,9},{2,10},{3,11},{4,12},{5,13},{6,14},{7,15},{8,0},{9,1},... | collective-permute-start | bytes 165896 | tf_op jit(solution)/shard_map/ppermute | solution.py:222
  88.7 6.4 %collective-permute-start.14 = (bf16[1,16,3456]{2,1,0:T(8,128)(2,1)S(1)}, bf16[1,16,3456]{2,1,0:T(8,128)(2,1)S(1)}, u32[]{:S(2)}, u32[]{:S(2)}) collective-permute-start(bf16[1,16,3456]{2,1,0:T(8,128)(2,1)S(1)} %dynamic-slice_convert_fusion.3), channel_id=1, source_target_pairs={{0,8},{1,9},{2,10},{3,11},{4,12},{5,13},{6,14},{7,15},{8,0},{9,1},... | collective-permute-start | bytes 331784 | tf_op jit(solution)/shard_map/ppermute | solution.py:222
  89.7 7.1 %collective-permute-start.10 = (bf16[8,3456]{1,0:T(8,128)(2,1)S(1)}, bf16[8,3456]{1,0:T(8,128)(2,1)S(1)}, u32[]{:S(2)}, u32[]{:S(2)}) collective-permute-start(bf16[8,3456]{1,0:T(8,128)(2,1)S(1)} %fusion.5), channel_id=1, source_target_pairs={{0,16},{16,0},{1,17},{17,1},{2,18},{18,2},{3,19},{19,3},{4,20},{20... | collective-permute-start | bytes 165896 | tf_op jit(solution)/shard_map/ppermute | solution.py:222
  95.2 4.8 %collective-permute-start.15 = (bf16[16,3456]{1,0:T(8,128)(2,1)S(1)}, bf16[16,3456]{1,0:T(8,128)(2,1)S(1)}, u32[]{:S(2)}, u32[]{:S(2)}) collective-permute-start(bf16[16,3456]{1,0:T(8,128)(2,1)S(1)} %fusion.4), channel_id=1, source_target_pairs={{0,16},{16,0},{1,17},{17,1},{2,18},{18,2},{3,19},{19,3},{4,20},{20... | collective-permute-start | bytes 331784 | tf_op jit(solution)/shard_map/ppermute | solution.py:222

commit v2 on v0

v2 whole, which is shorter than its diff:
```python
import functools

import jax
import jax.numpy as jnp
from jax import lax
from jax.experimental import pallas as pl
from jax.experimental.pallas import tpu as pltpu
from jax.sharding import PartitionSpec as P

F32 = jnp.float32
BF16 = jnp.bfloat16
VMEM = pl.BlockSpec(memory_space=pltpu.VMEM)
SMEM = pl.BlockSpec(memory_space=pltpu.SMEM)


def size_of(shapes):
    total = 0
    for item in shapes:
        count = jnp.dtype(item.dtype).itemsize
        for extent in item.shape:
            count *= extent
        total += count
    return total


def kernel_call(body, operands, outs, scratch, flops, limit, scalars=0, after=()):
    cost = pl.CostEstimate(
        flops=flops, bytes_accessed=size_of(operands) + size_of(outs), transcendentals=0
    )
    used, extra = (len(operands), len(after))
    specs = [SMEM] * scalars + [VMEM] * (used - scalars)
    specs += [pl.BlockSpec(memory_space=pl.ANY)] * extra

    def inner(*refs):
        body(*refs[:used], *refs[used + extra :])

    return pl.pallas_call(
        inner,
        out_shape=outs,
        in_specs=specs,
        out_specs=[VMEM] * len(outs),
        scratch_shapes=scratch,
        cost_estimate=cost,
        compiler_params=pltpu.CompilerParams(vmem_limit_bytes=limit * 2**20),
    )(*operands, *after)


def exchange(to_pair, to_next):
    count = lax.axis_size("space")
    pair = [(i, i ^ 1) for i in range(count) if i ^ 1 < count]
    odd = [i for i in range(1, count - 1, 2)]
    across = [(i, i + 1) for i in odd] + [(i + 1, i) for i in odd]
    return lax.ppermute(to_pair, "space", pair), lax.ppermute(to_next, "space", across)


def silu_slope(value, sig):
    return sig * (1.0 + value * (1.0 - sig))


def three_shifts(value):
    depth = value.shape[1]
    at = lax.broadcasted_iota(jnp.int32, value.shape, 1)
    lower = jnp.where(at == 0, 0.0, pltpu.roll(value, 1, 1))
    upper = jnp.where(at == depth - 1, 0.0, pltpu.roll(value, depth - 1, 1))
    return lower, value, upper


def facing(place, edge, from_pair, from_next):
    return jnp.where(place[0] != edge, from_pair.astype(F32), from_next.astype(F32))


def send_planes(place, first, last, to_pair, to_next):
    even = place[0] == 0
    first, last = (first.astype(F32), last.astype(F32))
    to_pair[0] = jnp.where(even, last, first).astype(BF16)
    to_next[0] = jnp.where(even, first, last).astype(BF16)


def dot(left, right):
    return jnp.dot(left, right, preferred_element_type=F32)


def tap_dot(left, right):
    return lax.dot_general(left, right, (((0,), (0,)), ((), ())), preferred_element_type=F32)


def plus(total, term):
    return term if total is None else total + term


def fill_wide6(target, plane, row_of):
    half = target.shape[1] - 1
    depth, lanes = target.shape[2:]
    three = lanes // 2
    zero = jnp.zeros((depth, three), BF16)
    target[plane, 0, :, 0:three] = zero
    target[plane, half, :, three:lanes] = zero
    for y in range(2 * half):
        pair, parity = ((y + 1) // 2, (y + 1) % 2)
        for c, piece in enumerate(three_shifts(row_of(y))):
            lane = parity * three + c * (three // 3)
            target[plane, pair : pair + 1, :, lane : lane + three // 3] = piece.astype(BF16)


def fill_wide3(target, plane, value):
    rows, depth, chan = value.shape
    zero = jnp.zeros((depth, 3 * chan), BF16)
    target[plane, 0] = zero
    target[plane, rows + 1] = zero
    for c, piece in enumerate(three_shifts(value)):
        target[plane, 1 : rows + 1, :, c * chan : (c + 1) * chan] = piece.astype(BF16)


def fine_conv(wide6, plane, weights, a):
    half = wide6.shape[1] - 1
    total = None
    for s in range(2):
        rows = wide6[plane, s : s + half].reshape(half * wide6.shape[2], wide6.shape[3])
        total = plus(total, dot(rows, weights[a, s]))
    return total


def fine_finish(pre, half, depth):
    chan = pre.shape[1] // 2
    sig = jax.nn.sigmoid(pre)
    act = (pre * sig).astype(BF16).astype(F32)
    slope = silu_slope(pre, sig).astype(BF16).reshape(half, depth, 2 * chan)
    return (act[:, :chan] + act[:, chan:]).reshape(half, depth, chan), slope


def fine_inner(own, kernel, wide6, weights, edge, act, slope):
    planes, fy, fz, chan = own.shape
    half = fy // 2
    for s in range(2):
        for r in range(2):
            for q in range(2):
                b = 2 * s + r - q
                for a in range(3):
                    place = (a, s, pl.ds(r * 3 * chan, 3 * chan), pl.ds(q * chan, chan))
                    if 0 <= b <= 2:
                        weights[place] = kernel[3 * a + b]
                    else:
                        weights[place] = jnp.zeros((3 * chan, chan), BF16)
    done = 0
    for p in range(planes):
        while done < min(p + 2, planes):
            fill_wide6(wide6, done, lambda y: own[done, y : y + 1].astype(F32))
            done += 1
        pre = None
        for a in range(3):
            if 0 <= p + a - 1 < planes:
                pre = plus(pre, fine_conv(wide6, p + a - 1, weights, a))
        if p == 0:
            edge[0] = pre
        elif p == planes - 1:
            edge[1] = pre
        else:
            act[p - 1], slope[p - 1] = fine_finish(pre, half, fz)


def fine_outer(
    place, from_pair, from_next, weights, edge, act, halo6, pooled, slope, to_pair, to_next, sums
):
    half, fz = act.shape[1:3]
    coarse = pooled.shape[0]
    ends = []
    for e in range(2):
        fill_wide6(
            halo6,
            e,
            lambda y: facing(place, e, from_pair[0, y : y + 1], from_next[0, y : y + 1]),
        )
        total, slope[e] = fine_finish(edge[e] + fine_conv(halo6, e, weights, 2 * e), half, fz)
        if coarse == 1:
            ends.append(total)
            continue
        sums[e] = total + act[0 if e == 0 else 2 * coarse - 3]
    if coarse == 1:
        sums[0] = ends[0] + ends[1]
    for pair in range(1, coarse - 1):
        sums[1 + pair] = act[2 * pair - 1] + act[2 * pair]
    for pair in range(coarse):
        at = 0 if pair == 0 else (1 if pair == coarse - 1 else 1 + pair)
        even = sums[at, :, pl.ds(0, fz // 2, stride=2), :]
        odd = sums[at, :, pl.ds(1, fz // 2, stride=2), :]
        pooled[pair] = ((even + odd) * 0.125).astype(BF16)
    send_planes(place, pooled[0], pooled[coarse - 1], to_pair, to_next)


def coarse_inner(own, kernel, wide3, pre):
    planes, cy, cz, chan = own.shape
    for p in range(planes):
        fill_wide3(wide3, p, own[p].astype(F32))
    for p in range(planes):
        total = None
        for a in range(3):
            if 0 <= p + a - 1 < planes:
                for b in range(3):
                    rows = wide3[p + a - 1, b : b + cy].reshape(cy * cz, 3 * chan)
                    total = plus(total, dot(rows, kernel[3 * a + b]))
        pre[p] = total


def coarse_outer(
    place, from_pair, from_next, kernel, pre, cotangent, halo3, out, delta, to_pair, to_next
):
    planes, cy, cz, wide = cotangent.shape
    for e in range(2):
        fill_wide3(halo3, e, facing(place, e, from_pair[0], from_next[0]))
    for p in range(planes):
        total = pre[p]
        for e in range(2):
            if p == e * (planes - 1):
                for b in range(3):
                    rows = halo3[e, b : b + cy].reshape(cy * cz, halo3.shape[-1])
                    total = total + dot(rows, kernel[6 * e + b])
        sig = jax.nn.sigmoid(total)
        out[p] = (total * sig).astype(BF16).reshape(cy, cz, wide)
        grad = cotangent[p].reshape(cy * cz, wide).astype(F32) * silu_slope(total, sig)
        delta[p] = grad.astype(BF16).reshape(cy, cz, wide)
    send_planes(place, delta[0], delta[planes - 1], to_pair, to_next)


def source(own, halo, plane):
    if plane < 0:
        return halo, 0
    if plane >= own.shape[0]:
        return halo, 1
    return own, plane


def put_term(term, lane, place, orders, keep, send):
    columns = pl.ds(lane, term.shape[1])
    if send is None:
        keep[:, columns] = term.astype(BF16)
        return
    here = place[0] == 0
    rows = term.shape[0] // (2 * len(orders))
    for at, owner in enumerate(orders):
        low = term[owner * rows : (owner + 1) * rows]
        high = term[(owner + 1) * rows : (owner + 2) * rows]
        keep[at, :, columns] = jnp.where(here, low, high).astype(BF16)
        send[at, :, columns] = jnp.where(here, high, low).astype(BF16)


def coarse_terms(place, wide3, halo3, delta, keep, send=None, *, orders, split):
    planes, cy, cz, wide = delta.shape
    span = wide3.shape[-1]
    for tap in range(9):
        a, b = (tap // 3, tap % 3)
        total = None
        for p in range(planes):
            ref, at = source(wide3, halo3, p + a - 1)
            piece = ref[at, b : b + cy].reshape(cy * cz, span)
            total = plus(total, tap_dot(delta[p].reshape(cy * cz, wide), piece))
        put_term(total, tap * span, place, orders[tap >= split], keep, send)


def backward_taps(wide3, plane, kernel, a, grad):
    cy, cz = (wide3.shape[1] - 2, wide3.shape[2])
    wide = kernel.shape[2]
    for b in range(3):
        for c in range(3):
            rows = wide3[plane, b : b + cy, :, c * wide : (c + 1) * wide]
            term = lax.dot_general(
                rows.reshape(cy * cz, wide),
                kernel[26 - (9 * a + 3 * b + c)],
                (((1,), (1,)), ((), ())),
                preferred_element_type=F32,
            )
            grad = plus(grad, term)
    return grad


def coarse_backward(delta, kernel, partial, wide3):
    planes = delta.shape[0]
    for p in range(planes):
        fill_wide3(wide3, p, delta[p].astype(F32))
    for p in range(planes):
        grad = None
        for a in range(3):
            if 0 <= p + a - 1 < planes:
                grad = backward_taps(wide3, p + a - 1, kernel, a, grad)
        partial[p] = grad


def fine_deltas(
    place, from_pair, from_next, kernel, partial, slope, slope_edge, delta, halo3, spread
):
    planes, rows, chan = partial.shape
    cy, fz = spread.shape[:2]
    cz = fz // 2
    for e in range(2):
        fill_wide3(halo3, e, facing(place, e, from_pair[0], from_next[0]))
    for p in range(planes):
        grad = partial[p]
        for e in range(2):
            if p == e * (planes - 1):
                grad = backward_taps(halo3, e, kernel, 2 * e, grad)
        grad = grad.astype(BF16).astype(F32).reshape(cy, cz, chan) * 0.125
        spread[:, pl.ds(0, cz, stride=2), :] = grad
        spread[:, pl.ds(1, cz, stride=2), :] = grad
        near = spread[...]
        both = jnp.concatenate([near, near], axis=-1)
        for at in range(2 * p, 2 * p + 2):
            ref, index = source(slope, slope_edge, at - 1)
            delta[at] = (both * ref[index].astype(F32)).astype(BF16)


def fine_part(place, wide6, halo6, delta, keep, send, order, taps):
    planes, half, fz, double = delta.shape
    chan = double // 2
    three = 3 * chan
    for tap in taps:
        a, b = (tap // 3, tap % 3)
        total = None
        for p in range(planes):
            ref, at = source(wide6, halo6, p + a - 1)
            for q in range(2):
                pair, parity = ((q + b) // 2, (q + b) % 2)
                rows = delta[p, :, :, q * chan : (q + 1) * chan].reshape(half * fz, chan)
                piece = ref[at, pair : pair + half, :, parity * three : (parity + 1) * three]
                total = plus(total, tap_dot(rows, piece.reshape(half * fz, three)))
        put_term(total, (tap - taps[0]) * three, place, order, keep, send)


def fine_first(
    place, from_pair, from_next, kernel, partial, slope, slope_edge, wide6, halo6, *rest, order, taps
):
    if len(rest) == 5:
        delta, keep, send, halo3, spread = rest
    else:
        delta, keep, halo3, spread = rest
        send = None
    fine_deltas(
        place, from_pair, from_next, kernel, partial, slope, slope_edge, delta, halo3, spread
    )
    fine_part(place, wide6, halo6, delta, keep, send, order, taps)


def fine_second(place, wide6, halo6, delta, keep, send=None, *, order, taps):
    fine_part(place, wide6, halo6, delta, keep, send, order, taps)


def swap(value, bit):
    count = lax.axis_size("space")
    return lax.ppermute(value, "space", [(i, i ^ bit) for i in range(count)])


def swap_sample(value, bit=0):
    count = lax.axis_size("space")
    return lax.ppermute(
        value,
        ("sample", "space"),
        [(s * count + i, (1 - s) * count + (i ^ bit)) for s in range(2) for i in range(count)],
    )


def middle_bits(count):
    bits = [1 << k for k in range(1, count.bit_length() - 2)]
    return bits, bits[1:] + bits[:1]


def order_of(middle, count):
    bits = middle + [count // 2]
    return [
        sum(bit for k, bit in enumerate(bits) if at >> (len(bits) - 1 - k) & 1)
        for at in range(count // 2)
    ]


def term_shapes(rows, columns, count):
    owned = rows // count
    if owned % 8:
        return [jax.ShapeDtypeStruct((rows, columns), BF16)]
    return [jax.ShapeDtypeStruct((count // 2, owned, columns), BF16)] * 2


def pick(parts, bit):
    mine = lax.axis_index("space") // bit % 2
    keep = lax.dynamic_index_in_dim(parts, mine, 0, keepdims=False)
    return keep, lax.dynamic_index_in_dim(parts, 1 - mine, 0, keepdims=False)


def sided(terms, middle, count, columns):
    if len(terms) == 2:
        return [item[:, :, columns] for item in terms]
    whole = terms[0][:, columns]
    bits = count.bit_length() - 1
    parts = whole.reshape((2,) * bits + (whole.shape[0] // count, -1))
    sequence = [1] + middle + [count // 2]
    axes = [bits - bit.bit_length() for bit in sequence]
    return pick(parts.transpose(tuple(axes) + (bits, bits + 1)), 1)


def halved(total, middle):
    for bit in middle:
        owned, columns = total.shape[-2:]
        keep, send = pick(total.reshape(2, -1, owned, columns), bit)
        total = keep + swap(send.astype(BF16), bit).astype(F32)
    return total.reshape((2,) + total.shape[-2:])


def last_halved(total):
    bit = lax.axis_size("space") // 2
    keep, send = pick(total, bit)
    base = (keep + swap(send.astype(BF16), bit).astype(F32)).astype(BF16)
    if lax.axis_size("sample") != 2:
        return lax.psum(base, "sample").astype(F32)
    return base.astype(F32) + swap_sample(base).astype(F32)


def last_direct(total):
    if lax.axis_size("sample") != 2:
        return last_halved(total)
    bit = lax.axis_size("space") // 2
    keep, send = pick(total.astype(BF16), bit)
    near, cross, other = (swap(send, bit), swap_sample(send, bit), swap_sample(keep))
    return (keep.astype(F32) + other.astype(F32)) + (near.astype(F32) + cross.astype(F32))


def shards(volumes, fine_kernel, coarse_kernel, cotangent):
    planes, fy, fz, chan = volumes.shape[1:]
    wide = coarse_kernel.shape[2]
    cp, cy, cz = (planes // 2, fy // 2, fz // 2)
    half = fy // 2
    count = lax.axis_size("space")
    me = lax.axis_index("space")
    parity = me % 2
    place = jnp.reshape(parity, (1,)).astype(jnp.int32)
    x = volumes[0]
    cells, few = (planes * fy * fz, cp * cy * cz)
    fine_flops, coarse_flops = (54 * cells * chan * chan, 54 * few * chan * wide)

    def shape(*extents, kind=BF16):
        return jax.ShapeDtypeStruct(extents, kind)

    to_pair = lax.dynamic_slice_in_dim(x, (1 - parity) * (planes - 1), 1, axis=0)
    to_next = lax.dynamic_slice_in_dim(x, parity * (planes - 1), 1, axis=0)
    from_pair, from_next = exchange(to_pair, to_next)
    mid = max(planes - 2, 1)
    wide6, weights, edge, act, slope = kernel_call(
        fine_inner,
        [x, fine_kernel.reshape(9, 3 * chan, chan)],
        [
            shape(planes, half + 1, fz, 6 * chan),
            shape(3, 2, 6 * chan, 2 * chan),
            shape(2, half * fz, 2 * chan, kind=F32),
            shape(mid, half, fz, chan, kind=F32),
            shape(mid, half, fz, 2 * chan),
        ],
        [],
        fine_flops,
        16,
    )
    halo6, pooled, slope_edge, to_pair, to_next = kernel_call(
        fine_outer,
        [place, from_pair, from_next, weights, edge, act],
        [
            shape(2, half + 1, fz, 6 * chan),
            shape(cp, cy, cz, chan),
            shape(2, half, fz, 2 * chan),
            shape(1, cy, cz, chan),
            shape(1, cy, cz, chan),
        ],
        [pltpu.VMEM((max(cp, 2), half, fz, chan), F32)],
        fine_flops // 6,
        16,
        scalars=1,
    )
    from_pair, from_next = exchange(to_pair, to_next)
    taps = coarse_kernel.reshape(9, 3 * chan, wide)
    wide3, pre = kernel_call(
        coarse_inner,
        [pooled, taps],
        [shape(cp, cy + 2, cz, 3 * chan), shape(cp, cy * cz, wide, kind=F32)],
        [],
        coarse_flops,
        16,
    )
    halo3, out, coarse_delta, to_pair, to_next = kernel_call(
        coarse_outer,
        [place, from_pair, from_next, taps, pre, cotangent[0]],
        [
            shape(2, cy + 2, cz, 3 * chan),
            shape(cp, cy, cz, wide),
            shape(cp, cy, cz, wide),
            shape(1, cy, cz, wide),
            shape(1, cy, cz, wide),
        ],
        [],
        coarse_flops // 3,
        16,
        scalars=1,
    )
    from_pair, from_next = exchange(to_pair, to_next)
    first, second = middle_bits(count)
    orders = (order_of(first, count), order_of(second, count))
    split = 5
    border = split * 3 * chan
    low, high = (slice(0, border), slice(border, 27 * chan))
    terms = kernel_call(
        functools.partial(coarse_terms, orders=orders, split=split),
        [place, wide3, halo3, coarse_delta],
        term_shapes(wide, 27 * chan, count),
        [],
        coarse_flops,
        16,
        scalars=1,
    )
    halves = [sided(terms, first, count, low), sided(terms, second, count, high)]
    if len(terms) == 2:
        got = swap(terms[1], 1)
        gots = [got[:, :, low], got[:, :, high]]
    else:
        gots = [swap(send, 1) for keep, send in halves]
    sums = []
    for (keep, _), got, middle in zip(halves, gots, (first, second)):
        sums.append(halved(keep.astype(F32) + got.astype(F32), middle))
    coarse_grad = last_halved(jnp.concatenate(sums, axis=-1))

    (partial,) = kernel_call(
        coarse_backward,
        [coarse_delta, coarse_kernel],
        [shape(cp, cy * cz, chan, kind=F32)],
        [pltpu.VMEM((cp, cy + 2, cz, 3 * wide), BF16)],
        coarse_flops,
        16,
        after=[terms[-1]],
    )
    fine_delta, *one = kernel_call(
        functools.partial(fine_first, order=orders[0], taps=range(split)),
        [place, from_pair, from_next, coarse_kernel, partial, slope, slope_edge, wide6, halo6],
        [shape(planes, half, fz, 2 * chan)] + term_shapes(chan, border, count),
        [pltpu.VMEM((2, cy + 2, cz, 3 * wide), BF16), pltpu.VMEM((cy, fz, chan), F32)],
        fine_flops * 2 // 3,
        16,
        scalars=1,
    )
    two = kernel_call(
        functools.partial(fine_second, order=orders[1], taps=range(split, 9)),
        [place, wide6, halo6, fine_delta],
        term_shapes(chan, 27 * chan - border, count),
        [],
        fine_flops // 2,
        16,
        scalars=1,
    )
    sums = []
    for terms, middle in ((one, first), (two, second)):
        keep, send = sided(terms, middle, count, slice(None))
        sums.append(halved(keep.astype(F32) + swap(send, 1).astype(F32), middle))
    fine_grad = last_direct(jnp.concatenate(sums, axis=-1))
    return (out[None], fine_grad, coarse_grad)


def solution(mesh):
    placed = (
        P("sample", "space", None, None, None),
        P(),
        P(),
        P("sample", "space", None, None, None),
    )
    return jax.shard_map(
        shards,
        mesh=mesh,
        in_specs=placed,
        out_specs=(P("sample", "space", None, None, None), P("space", None), P("space", None)),
        check_vma=False,
    )
```

time: 293 us -> 79.4 us (0.27); the launches traced: 288 us -> 79.2 us
  blocking collectives: 107 us -> 0 us
  matrix products: 81.2 us -> 0 us
  local copies, waits for them, and re-layouts: 43.7 us -> 3.66 us
  Pallas kernels: 0 us -> 17.7 us
  between operations: 15.9 us -> 0.97 us
  starting transfers between devices: 22.2 us -> 37 us
  waiting for transfers between devices: 12 us -> 18 us
  other arithmetic: 6.28 us -> 1.93 us
    dot_general x135 -> x0, matrix products: 81.2 us -> none  [the longest x54 54.7 us: kernel_term(): lax.dot_general(delta_rows, shifted(padded, tap, shape), (((0,), (0,)), (...]
    unnamed x1 -> x0, blocking collectives: 75.8 us -> none
    psum x1 -> x0, blocking collectives: 31.1 us -> none  [shards(): lax.psum(fine_part.astype(jnp.bfloat16), 'sample').astype(jnp.float32)]
    unnamed x113 -> x8, local copies, waits for them, and re-layouts: 28 us -> 2.4 us
    pallas_call x0 -> x8, Pallas kernels: none -> 17.7 us  [kernel_call(): pl.pallas_call(inner, out_shape=outs, in_specs=specs, out_specs=[VMEM] *...]
    ppermute x6 -> x22, waiting for transfers between devices: 1.13 us -> 18 us  [the longest x13 17.1 us: swap(): return lax.ppermute(value, 'space', [(i, i ^ bit) for i in range(count)])]
    ppermute x6 -> x22, starting transfers between devices: 21.9 us -> 37 us  [the longest x13 21.9 us: swap(): return lax.ppermute(value, 'space', [(i, i ^ bit) for i in range(count)])]
    slice x9 -> x0, local copies, waits for them, and re-layouts: 14.5 us -> none  [the longest x6 12.7 us: shifted(): padded[first:first + shape[0], second:second + shape[1], third:third + sh...]
  transfers between devices with their start and end apart: 8 -> 22, of which waited for: 2 -> 12; matrix products, arithmetic and copies ran while one was open for 25% -> 2% of each run, Pallas kernels for 0% -> 11%
where the time goes in v2:
time: 79.4 us; the launch traced here: 79.2 us
  starting transfers between devices  37 us (47%)
  waiting for transfers between devices  18 us (23%)
  Pallas kernels  17.7 us (22%)
  local copies, waits for them, and re-layouts  3.66 us (5%)
  other arithmetic  1.93 us (2%)
  between operations  0.97 us (1%)
    ppermute x13, starting transfers between devices, swap(): return lax.ppermute(value, 'space', [(i, i ^ bit) for i in range(count)])  21.9 us
    pallas_call x8, Pallas kernels, kernel_call(): pl.pallas_call(inner, out_shape=outs, in_specs=specs, out_specs=[VMEM] *...  17.7 us
    ppermute x13, waiting for transfers between devices, swap(): return lax.ppermute(value, 'space', [(i, i ^ bit) for i in range(count)])  17.1 us
    ppermute x3, starting transfers between devices, exchange(): lax.ppermute(to_pair, 'space', pair)  8.36 us
    ppermute x3, starting transfers between devices, swap_sample(): lax.ppermute(value, ('sample', 'space'), [(s * count + i, (1 - s) * count...  4.6 us
    unnamed x8, local copies, waits for them, and re-layouts  2.4 us
    ppermute x3, starting transfers between devices, exchange(): lax.ppermute(to_next, 'space', across)  2.16 us
  transfers between devices with their start and end apart: 22, of which 12 were waited for; matrix products, arithmetic and copies ran while one was open for 2% of the time, Pallas kernels for 11%

profile of v2, /device:TPU:0, one launch (start us, length us, event | category | flops | bytes accessed | tf_op | source)
XLA Modules:
  0.0 79.2 jit_solution(6034871818714542641)
XLA Ops:
  0.7 1.1 %dynamic-slice_bitcast_fusion = (bf16[1,16,64,128]{3,2,1,0:T(8,128)(2,1)S(1)}, bf16[1,16,64,128]{3,2,1,0:T(8,128)(2,1)S(1)}) fusion(bf16[1,4,16,64,128]{4,3,2,1,0:T(8,128)(2,1)} %param.4, s32[]{:T(128)S(6)} %select_n.100, s32[]{:T(128)S(6)} %select_n.99), kind=kLoop, calls=%fused_computation.12 | loop fusion | bytes 1048584 | tf_op jit(solution)/shard_map/dynamic_slice | solution.py:439
  1.7 0.5 collective-permute-start
  2.2 0.7 collective-permute-start.1
  2.9 0.0 copy-start.2
  2.9 1.2 %copy-done.2 = bf16[1,4,16,64,128]{4,3,2,1,0:T(8,128)(2,1)S(1)} copy-done((bf16[1,4,16,64,128]{4,3,2,1,0:T(8,128)(2,1)S(1)}, bf16[1,4,16,64,128]{4,3,2,1,0:T(8,128)(2,1)}, u32[]{:S(2)}) %copy-start.2) | copy-done | bytes 1048600
  4.1 1.2 %copy-done.3 = bf16[27,128,128]{2,1,0:T(8,128)(2,1)S(1)} copy-done((bf16[27,128,128]{2,1,0:T(8,128)(2,1)S(1)}, bf16[27,128,128]{2,1,0:T(8,128)(2,1)}, u32[]{:S(2)}) %copy-start.3) | copy-done | bytes 884760
  5.3 4.6 %shard_map.67 = (bf16[4,9,64,768]{3,2,1,0:T(8,128)(2,1)S(1)}, bf16[3,2,768,256]{3,2,1,0:T(8,128)(2,1)S(1)}, f32[2,512,256]{2,1,0:T(8,128)S(1)}, f32[2,8,64,128]{3,2,1,0:T(8,128)S(1)}, bf16[2,8,64,256]{3,2,1,0:T(8,128)(2,1)S(1)}) custom-call(bf16[4,16,64,128]{3,2,1,0:T(8,128)(2,1)S(1)} %bitcast.69, bf16[9,384,128]{2,1,0:T(8,128)(2,1)S(1)} %bitcast.70), custom_call_target="tpu_custom_call" | custom-call | flops 3623878656 | bytes 9928704 | tf_op jit(solution)/shard_map/pallas_call | solution.py:37
  9.9 0.0 copy-start
  9.9 0.0 collective-permute-done.refs_1_
  9.9 0.0 collective-permute-done.1.refs_2_
  9.9 1.5 %shard_map.68 = (bf16[2,9,64,768]{3,2,1,0:T(8,128)(2,1)S(1)}, bf16[2,8,32,128]{3,2,1,0:T(8,128)(2,1)S(1)}, bf16[2,8,64,256]{3,2,1,0:T(8,128)(2,1)S(1)}, bf16[1,8...) custom-call(s32[1]{0:T(128)} %bitcast.refs_0_, bf16[1,16,64,128]{3,2,1,0:T(8,128)(2,1)S(1)} %collective-permute-done.refs_1_, ...), custom_call_target="tpu_custom_call" | custom-call | flops 603979776 | bytes 7012356 | tf_op jit(solution)/shard_map/pallas_call | solution.py:37
  11.4 0.0 copy-start.1
  11.4 4.0 %collective-permute-start.2 = (bf16[1,8,32,128]{3,2,1,0:T(8,128)(2,1)S(1)}, bf16[1,8,32,128]{3,2,1,0:T(8,128)(2,1)S(1)}, u32[]{:S(2)}, u32[]{:S(2)}) collective-permute-start(bf16[1,8,32,128]{3,2,1,0:T(8,128)(2,1)S(1)} %get-tuple-element.30), channel_id=1, source_target_pairs={{0,1},{1,0},{2,3},{3,2},{4,5},{5,4},{6,7},{7,6},{8,9},{9,8},{10,11... | collective-permute-start | bytes 196616 | tf_op jit(solution)/shard_map/ppermute | solution.py:53
  15.4 0.7 collective-permute-start.3
  16.0 0.0 copy-done
  16.0 1.0 %shard_map.69 = (bf16[2,10,32,384]{3,2,1,0:T(8,128)(2,1)S(1)}, f32[2,256,256]{2,1,0:T(8,128)S(1)}) custom-call(bf16[2,8,32,128]{3,2,1,0:T(8,128)(2,1)S(1)} %get-tuple-element.32.refs_0_, bf16[9,384,256]{2,1,0:T(8,128)(2,1)S(1)} %bitcast.66), custom_call_target="tpu_custom_call" | custom-call | flops 905969664 | bytes 2916352 | tf_op jit(solution)/shard_map/pallas_call | solution.py:37
  17.0 0.0 collective-permute-done.2.refs_1_
  17.0 0.0 collective-permute-done.3.refs_2_
  17.1 1.5 %shard_map.70 = (bf16[2,10,32,384]{3,2,1,0:T(8,128)(2,1)S(1)}, bf16[2,8,32,256]{3,2,1,0:T(8,128)(2,1)}, bf16[2,8,32,256]{3,2,1,0:T(8,128)(2,1)S(1)}, bf16[1,8,32...) custom-call(s32[1]{0:T(128)} %bitcast.refs_0_, bf16[1,8,32,128]{3,2,1,0:T(8,128)(2,1)S(1)} %collective-permute-done.2.refs_1_, ...), custom_call_target="tpu_custom_call" | custom-call | flops 301989888 | bytes 3964932 | tf_op jit(solution)/shard_map/pallas_call | solution.py:37
  18.5 3.9 %collective-permute-start.4 = (bf16[1,8,32,256]{3,2,1,0:T(8,128)(2,1)S(1)}, bf16[1,8,32,256]{3,2,1,0:T(8,128)(2,1)S(1)}, u32[]{:S(2)}, u32[]{:S(2)}) collective-permute-start(bf16[1,8,32,256]{3,2,1,0:T(8,128)(2,1)S(1)} %get-tuple-element.35), channel_id=1, source_target_pairs={{0,1},{1,0},{2,3},{3,2},{4,5},{5,4},{6,7},{7,6},{8,9},{9,8},{10,11... | collective-permute-start | bytes 393224 | tf_op jit(solution)/shard_map/ppermute | solution.py:53
  22.4 0.8 %collective-permute-start.5 = (bf16[1,8,32,256]{3,2,1,0:T(8,128)(2,1)S(1)}, bf16[1,8,32,256]{3,2,1,0:T(8,128)(2,1)S(1)}, u32[]{:S(2)}, u32[]{:S(2)}) collective-permute-start(bf16[1,8,32,256]{3,2,1,0:T(8,128)(2,1)S(1)} %get-tuple-element.36), channel_id=1, source_target_pairs={{1,2},{3,4},{5,6},{7,8},{9,10},{11,12},{13,14},{2,1},{4,3},{6,5},{... | collective-permute-start | bytes 393224 | tf_op jit(solution)/shard_map/ppermute | solution.py:53
  23.3 1.4 %shard_map.71 = (bf16[8,16,3456]{2,1,0:T(8,128)(2,1)S(1)}, bf16[8,16,3456]{2,1,0:T(8,128)(2,1)S(1)}) custom-call(s32[1]{0:T(128)} %bitcast.refs_0_, bf16[2,10,32,384]{3,2,1,0:T(8,128)(2,1)S(1)} %get-tuple-element.38.refs_1_, bf16[2,10,32,384]{3,2,1,0:T(8,128)(2,1)S(1)} %get-tuple-element.39.refs_2_, bf16[2,8,32,256]{3,2,1,0:T(8,128)(2,1)S(1)} %get-tuple-element.37.refs_3_.refs_0_), custom_call_target="tpu_custom_call" | custom-call | flops 905969664 | bytes 3014660 | tf_op jit(solution)/shard_map/pallas_call | solution.py:37
  24.7 1.4 %shard_map.72.refs_4_ = f32[2,256,128]{2,1,0:T(8,128)S(1)} custom-call(bf16[2,8,32,256]{3,2,1,0:T(8,128)(2,1)S(1)} %get-tuple-element.37.refs_3_.refs_0_, bf16[27,128,256]{2,1,0:T(8,128)(2,1)S(1)} %copy-done, bf16[8,16,3456]{2,1,0:T(8,128)(2,1)S(1)} %get-tuple-element.40.refs_2_), custom_call_target="tpu_custom_call" | custom-call | flops 905969664 | bytes 2293760 | tf_op jit(solution)/shard_map/pallas_call | solution.py:37
  26.1 0.0 collective-permute-done.4.refs_1_
  26.1 0.0 collective-permute-done.5.refs_2_
  26.1 3.9 %shard_map.73 = (bf16[4,8,64,256]{3,2,1,0:T(8,128)(2,1)S(1)}, bf16[8,8,1920]{2,1,0:T(8,128)(2,1)S(1)}, bf16[8,8,1920]{2,1,0:T(8,128)(2,1)S(1)}) custom-call(s32[1]{0:T(128)} %bitcast.refs_0_, bf16[1,8,32,256]{3,2,1,0:T(8,128)(2,1)S(1)} %collective-permute-done.4.refs_1_, bf16[1,8,32,256]{3,2,1,0:T(8,128)(2,1)S(1)} %collective-permute-done.5.refs_2_, ...), custom_call_target="tpu_custom_call" | custom-call | flops 2415919104 | bytes 10190852 | tf_op jit(solution)/shard_map/pallas_call | solution.py:37
  30.1 2.4 %shard_map.74 = (bf16[8,8,1536]{2,1,0:T(8,128)(2,1)S(1)}, bf16[8,8,1536]{2,1,0:T(8,128)(2,1)S(1)}) custom-call(s32[1]{0:T(128)} %bitcast.refs_0_, bf16[4,9,64,768]{3,2,1,0:T(8,128)(2,1)S(1)} %get-tuple-element.43.refs_7_.refs_1_, bf16[2,9,64,768]{3,2,1,0:T(8,128)(2,1)S(1)} %get-tuple-element.44.refs_8_.refs_2_, ...), custom_call_target="tpu_custom_call" | custom-call | flops 1811939328 | bytes 6750212 | tf_op jit(solution)/shard_map/pallas_call | solution.py:37
  32.5 4.5 %collective-permute-start.9 = (bf16[8,8,1536]{2,1,0:T(8,128)(2,1)S(1)}, bf16[8,8,1536]{2,1,0:T(8,128)(2,1)S(1)}, u32[]{:S(2)}, u32[]{:S(2)}) collective-permute-start(bf16[8,8,1536]{2,1,0:T(8,128)(2,1)S(1)} %get-tuple-element.49), channel_id=1, source_target_pairs={{0,1},{1,0},{2,3},{3,2},{4,5},{5,4},{6,7},{7,6},{8,9},{9,8},{10,11... | collective-permute-start | bytes 589832 | tf_op jit(solution)/shard_map/ppermute | solution.py:347
  37.0 0.2 collective-permute-start.15
  37.2 0.3 collective-permute-start.6
  37.5 0.6 collective-permute-done.9
  38.2 3.0 %collective-permute-start.10 = (bf16[4,8,1536]{2,1,0:T(8,128)(2,1)S(1)}, bf16[4,8,1536]{2,1,0:T(8,128)(2,1)S(1)}, u32[]{:S(2)}, u32[]{:S(2)}) collective-permute-start(bf16[4,8,1536]{2,1,0:T(8,128)(2,1)S(1)} %fusion.12), channel_id=1, source_target_pairs={{0,4},{1,5},{2,6},{3,7},{4,0},{5,1},{6,2},{7,3},{8,12},{9,13},{10,... | collective-permute-start | bytes 294920 | tf_op jit(solution)/shard_map/ppermute | solution.py:347
  41.1 0.0 collective-permute-done.6
  41.1 0.1 convert_add_fusion.2
  41.2 1.4 %collective-permute-start.7 = (bf16[4,8,1920]{2,1,0:T(8,128)(2,1)S(1)}, bf16[4,8,1920]{2,1,0:T(8,128)(2,1)S(1)}, u32[]{:S(2)}, u32[]{:S(2)}) collective-permute-start(bf16[4,8,1920]{2,1,0:T(8,128)(2,1)S(1)} %fusion.8), channel_id=1, source_target_pairs={{0,2},{1,3},{2,0},{3,1},{4,6},{5,7},{6,4},{7,5},{8,10},{9,11},{10,... | collective-permute-start | bytes 368648 | tf_op jit(solution)/shard_map/ppermute | solution.py:347
  42.7 1.8 %collective-permute-done.10 = bf16[4,8,1536]{2,1,0:T(8,128)(2,1)S(1)} collective-permute-done((bf16[4,8,1536]{2,1,0:T(8,128)(2,1)S(1)}, bf16[4,8,1536]{2,1,0:T(8,128)(2,1)S(1)}, u32[]{:S(2)}, u32[]{:S(2)}) %collective-permute-start.10) | collective-permute-done | bytes 98336 | tf_op jit(solution)/shard_map/ppermute | solution.py:347
  44.5 1.4 %collective-permute-start.11 = (bf16[2,8,1536]{2,1,0:T(8,128)(2,1)S(1)}, bf16[2,8,1536]{2,1,0:T(8,128)(2,1)S(1)}, u32[]{:S(2)}, u32[]{:S(2)}) collective-permute-start(bf16[2,8,1536]{2,1,0:T(8,128)(2,1)S(1)} %fusion.20), channel_id=1, source_target_pairs={{0,2},{1,3},{2,0},{3,1},{4,6},{5,7},{6,4},{7,5},{8,10},{9,11},{10,... | collective-permute-start | bytes 147464 | tf_op jit(solution)/shard_map/ppermute | solution.py:347
  45.9 0.7 collective-permute-done.7
  46.6 1.8 %collective-permute-start.8 = (bf16[2,8,1920]{2,1,0:T(8,128)(2,1)S(1)}, bf16[2,8,1920]{2,1,0:T(8,128)(2,1)S(1)}, u32[]{:S(2)}, u32[]{:S(2)}) collective-permute-start(bf16[2,8,1920]{2,1,0:T(8,128)(2,1)S(1)} %fusion.15), channel_id=1, source_target_pairs={{0,4},{1,5},{2,6},{3,7},{4,0},{5,1},{6,2},{7,3},{8,12},{9,13},{10,... | collective-permute-start | bytes 184328 | tf_op jit(solution)/shard_map/ppermute | solution.py:347
  48.5 0.2 collective-permute-done.11
  48.7 2.3 %collective-permute-done.8 = bf16[2,8,1920]{2,1,0:T(8,128)(2,1)S(1)} collective-permute-done((bf16[2,8,1920]{2,1,0:T(8,128)(2,1)S(1)}, bf16[2,8,1920]{2,1,0:T(8,128)(2,1)S(1)}, u32[]{:S(2)}, u32[]{:S(2)}) %collective-permute-start.8) | collective-permute-done | bytes 61472 | tf_op jit(solution)/shard_map/ppermute | solution.py:347
  51.0 0.0 collective-permute-done.15
  51.0 0.1 convert_add_fusion.1
  51.1 1.8 %collective-permute-start.18 = (bf16[4,16,1536]{2,1,0:T(8,128)(2,1)S(1)}, bf16[4,16,1536]{2,1,0:T(8,128)(2,1)S(1)}, u32[]{:S(2)}, u32[]{:S(2)}) collective-permute-start(bf16[4,16,1536]{2,1,0:T(8,128)(2,1)S(1)} %fusion.7), channel_id=1, source_target_pairs={{0,4},{1,5},{2,6},{3,7},{4,0},{5,1},{6,2},{7,3},{8,12},{9,13},{10,... | collective-permute-start | bytes 589832 | tf_op jit(solution)/shard_map/ppermute | solution.py:347
  52.9 0.1 convert_add_fusion
  53.1 1.5 %collective-permute-start.16 = (bf16[4,16,1920]{2,1,0:T(8,128)(2,1)S(1)}, bf16[4,16,1920]{2,1,0:T(8,128)(2,1)S(1)}, u32[]{:S(2)}, u32[]{:S(2)}) collective-permute-start(bf16[4,16,1920]{2,1,0:T(8,128)(2,1)S(1)} %fusion), channel_id=1, source_target_pairs={{0,2},{1,3},{2,0},{3,1},{4,6},{5,7},{6,4},{7,5},{8,10},{9,11},{10,... | collective-permute-start | bytes 737288 | tf_op jit(solution)/shard_map/ppermute | solution.py:347
  54.5 2.3 %collective-permute-done.18 = bf16[4,16,1536]{2,1,0:T(8,128)(2,1)S(1)} collective-permute-done((bf16[4,16,1536]{2,1,0:T(8,128)(2,1)S(1)}, bf16[4,16,1536]{2,1,0:T(8,128)(2,1)S(1)}, u32[]{:S(2)}, u32[]{:S(2)}) %collective-permute-start.18) | collective-permute-done | bytes 196640 | tf_op jit(solution)/shard_map/ppermute | solution.py:347
  56.9 1.7 %collective-permute-start.19 = (bf16[2,16,1536]{2,1,0:T(8,128)(2,1)S(1)}, bf16[2,16,1536]{2,1,0:T(8,128)(2,1)S(1)}, u32[]{:S(2)}, u32[]{:S(2)}) collective-permute-start(bf16[2,16,1536]{2,1,0:T(8,128)(2,1)S(1)} %fusion.13), channel_id=1, source_target_pairs={{0,2},{1,3},{2,0},{3,1},{4,6},{5,7},{6,4},{7,5},{8,10},{9,11},{10,... | collective-permute-start | bytes 294920 | tf_op jit(solution)/shard_map/ppermute | solution.py:347
  58.6 1.8 %collective-permute-done.16 = bf16[4,16,1920]{2,1,0:T(8,128)(2,1)S(1)} collective-permute-done((bf16[4,16,1920]{2,1,0:T(8,128)(2,1)S(1)}, bf16[4,16,1920]{2,1,0:T(8,128)(2,1)S(1)}, u32[]{:S(2)}, u32[]{:S(2)}) %collective-permute-start.16) | collective-permute-done | bytes 245792 | tf_op jit(solution)/shard_map/ppermute | solution.py:347
  60.5 0.3 collective-permute-start.17
  60.8 0.8 %collective-permute-done.19 = bf16[2,16,1536]{2,1,0:T(8,128)(2,1)S(1)} collective-permute-done((bf16[2,16,1536]{2,1,0:T(8,128)(2,1)S(1)}, bf16[2,16,1536]{2,1,0:T(8,128)(2,1)S(1)}, u32[]{:S(2)}, u32[]{:S(2)}) %collective-permute-start.19) | collective-permute-done | bytes 98336 | tf_op jit(solution)/shard_map/ppermute | solution.py:347
  61.6 5.0 %collective-permute-done.17 = bf16[2,16,1920]{2,1,0:T(8,128)(2,1)S(1)} collective-permute-done((bf16[2,16,1920]{2,1,0:T(8,128)(2,1)S(1)}, bf16[2,16,1920]{2,1,0:T(8,128)(2,1)S(1)}, u32[]{:S(2)}, u32[]{:S(2)}) %collective-permute-start.17) | collective-permute-done | bytes 122912 | tf_op jit(solution)/shard_map/ppermute | solution.py:347
  66.7 1.6 %collective-permute-start.20 = (bf16[16,3456]{1,0:T(8,128)(2,1)S(1)}, bf16[16,3456]{1,0:T(8,128)(2,1)S(1)}, u32[]{:S(2)}, u32[]{:S(2)}) collective-permute-start(bf16[16,3456]{1,0:T(8,128)(2,1)S(1)} %fusion.11), channel_id=1, source_target_pairs={{0,8},{1,9},{2,10},{3,11},{4,12},{5,13},{6,14},{7,15},{8,0},{9,1},... | collective-permute-start | bytes 331784 | tf_op jit(solution)/shard_map/ppermute | solution.py:347
  68.2 2.5 %collective-permute-start.14 = (bf16[8,3456]{1,0:T(8,128)(2,1)S(1)}, bf16[8,3456]{1,0:T(8,128)(2,1)S(1)}, u32[]{:S(2)}, u32[]{:S(2)}) collective-permute-start(bf16[8,3456]{1,0:T(8,128)(2,1)S(1)} %get-tuple-element.54), channel_id=1, source_target_pairs={{0,24},{1,25},{2,26},{3,27},{4,28},{5,29},{6,30},{7,31},{8,16},{9,... | collective-permute-start | bytes 165896 | tf_op jit(solution)/shard_map/ppermute | solution.py:352
  70.7 2.4 %collective-permute-start.13 = (bf16[8,3456]{1,0:T(8,128)(2,1)S(1)}, bf16[8,3456]{1,0:T(8,128)(2,1)S(1)}, u32[]{:S(2)}, u32[]{:S(2)}) collective-permute-start(bf16[8,3456]{1,0:T(8,128)(2,1)S(1)} %get-tuple-element.54), channel_id=1, source_target_pairs={{0,8},{1,9},{2,10},{3,11},{4,12},{5,13},{6,14},{7,15},{8,0},{9,1},... | collective-permute-start | bytes 165896 | tf_op jit(solution)/shard_map/ppermute | solution.py:347
  73.1 0.0 collective-permute-start.12
  73.1 0.0 collective-permute-done.20
  73.2 2.1 %collective-permute-start.21 = (bf16[16,3456]{1,0:T(8,128)(2,1)S(1)}, bf16[16,3456]{1,0:T(8,128)(2,1)S(1)}, u32[]{:S(2)}, u32[]{:S(2)}) collective-permute-start(bf16[16,3456]{1,0:T(8,128)(2,1)S(1)} %fusion.6), channel_id=1, source_target_pairs={{0,16},{1,17},{2,18},{3,19},{4,20},{5,21},{6,22},{7,23},{8,24},{9,... | collective-permute-start | bytes 331784 | tf_op jit(solution)/shard_map/ppermute | solution.py:352
  75.3 0.0 collective-permute-done.14
  75.3 1.7 %collective-permute-done.13 = bf16[8,3456]{1,0:T(8,128)(2,1)S(1)} collective-permute-done((bf16[8,3456]{1,0:T(8,128)(2,1)S(1)}, bf16[8,3456]{1,0:T(8,128)(2,1)S(1)}, u32[]{:S(2)}, u32[]{:S(2)}) %collective-permute-start.13) | collective-permute-done | bytes 55328 | tf_op jit(solution)/shard_map/ppermute | solution.py:347
  76.9 0.4 collective-permute-done.12
  77.3 0.7 add_add_fusion
  78.0 0.5 collective-permute-done.21
  78.5 0.7 convert_add_fusion.4
  (22 shorter events, 0.5 us)
Async XLA Ops:
  1.7 8.2 %collective-permute-start = (bf16[1,16,64,128]{3,2,1,0:T(8,128)(2,1)S(1)}, bf16[1,16,64,128]{3,2,1,0:T(8,128)(2,1)S(1)}, u32[]{:S(2)}, u32[]{:S(2)}) collective-permute-start(bf16[1,16,64,128]{3,2,1,0:T(8,128)(2,1)S(1)} %get-tuple-element.52), channel_id=1, source_target_pairs={{0,1},{1,0},{2,3},{3,2},{4,5},{5,4},{6,7},{7,6},{8,9},{9,8},{10,11... | collective-permute-start | bytes 786440 | tf_op jit(solution)/shard_map/ppermute | solution.py:53
  2.2 7.7 %collective-permute-start.1 = (bf16[1,16,64,128]{3,2,1,0:T(8,128)(2,1)S(1)}, bf16[1,16,64,128]{3,2,1,0:T(8,128)(2,1)S(1)}, u32[]{:S(2)}, u32[]{:S(2)}) collective-permute-start(bf16[1,16,64,128]{3,2,1,0:T(8,128)(2,1)S(1)} %get-tuple-element.51), channel_id=1, source_target_pairs={{1,2},{3,4},{5,6},{7,8},{9,10},{11,12},{13,14},{2,1},{4,3},{6,5},{... | collective-permute-start | bytes 786440 | tf_op jit(solution)/shard_map/ppermute | solution.py:53
  2.9 1.2 %copy-start.2 = (bf16[1,4,16,64,128]{4,3,2,1,0:T(8,128)(2,1)S(1)}, bf16[1,4,16,64,128]{4,3,2,1,0:T(8,128)(2,1)}, u32[]{:S(2)}) copy-start(bf16[1,4,16,64,128]{4,3,2,1,0:T(8,128)(2,1)} %param.4) | copy-start | bytes 3145732
  4.1 1.2 %copy-start.3 = (bf16[27,128,128]{2,1,0:T(8,128)(2,1)S(1)}, bf16[27,128,128]{2,1,0:T(8,128)(2,1)}, u32[]{:S(2)}) copy-start(bf16[27,128,128]{2,1,0:T(8,128)(2,1)} %param.5) | copy-start | bytes 2654212
  9.9 6.1 %copy-start = (bf16[27,128,256]{2,1,0:T(8,128)(2,1)S(1)}, bf16[27,128,256]{2,1,0:T(8,128)(2,1)}, u32[]{:S(2)}) copy-start(bf16[27,128,256]{2,1,0:T(8,128)(2,1)} %refs_3_.1) | copy-start | bytes 5308420
  11.4 5.7 %copy-start.1 = (bf16[1,2,8,32,256]{4,3,2,1,0:T(8,128)(2,1)S(1)}, bf16[1,2,8,32,256]{4,3,2,1,0:T(8,128)(2,1)}, u32[]{:S(2)}) copy-start(bf16[1,2,8,32,256]{4,3,2,1,0:T(8,128)(2,1)} %param.7) | copy-start | bytes 786436
  11.4 5.6 %collective-permute-start.2 = (bf16[1,8,32,128]{3,2,1,0:T(8,128)(2,1)S(1)}, bf16[1,8,32,128]{3,2,1,0:T(8,128)(2,1)S(1)}, u32[]{:S(2)}, u32[]{:S(2)}) collective-permute-start(bf16[1,8,32,128]{3,2,1,0:T(8,128)(2,1)S(1)} %get-tuple-element.30), channel_id=1, source_target_pairs={{0,1},{1,0},{2,3},{3,2},{4,5},{5,4},{6,7},{7,6},{8,9},{9,8},{10,11... | collective-permute-start | bytes 196616 | tf_op jit(solution)/shard_map/ppermute | solution.py:53
  15.4 1.7 %collective-permute-start.3 = (bf16[1,8,32,128]{3,2,1,0:T(8,128)(2,1)S(1)}, bf16[1,8,32,128]{3,2,1,0:T(8,128)(2,1)S(1)}, u32[]{:S(2)}, u32[]{:S(2)}) collective-permute-start(bf16[1,8,32,128]{3,2,1,0:T(8,128)(2,1)S(1)} %get-tuple-element.31), channel_id=1, source_target_pairs={{1,2},{3,4},{5,6},{7,8},{9,10},{11,12},{13,14},{2,1},{4,3},{6,5},{... | collective-permute-start | bytes 196616 | tf_op jit(solution)/shard_map/ppermute | solution.py:53
  18.5 7.6 %collective-permute-start.4 = (bf16[1,8,32,256]{3,2,1,0:T(8,128)(2,1)S(1)}, bf16[1,8,32,256]{3,2,1,0:T(8,128)(2,1)S(1)}, u32[]{:S(2)}, u32[]{:S(2)}) collective-permute-start(bf16[1,8,32,256]{3,2,1,0:T(8,128)(2,1)S(1)} %get-tuple-element.35), channel_id=1, source_target_pairs={{0,1},{1,0},{2,3},{3,2},{4,5},{5,4},{6,7},{7,6},{8,9},{9,8},{10,11... | collective-permute-start | bytes 393224 | tf_op jit(solution)/shard_map/ppermute | solution.py:53
  22.4 3.7 %collective-permute-start.5 = (bf16[1,8,32,256]{3,2,1,0:T(8,128)(2,1)S(1)}, bf16[1,8,32,256]{3,2,1,0:T(8,128)(2,1)S(1)}, u32[]{:S(2)}, u32[]{:S(2)}) collective-permute-start(bf16[1,8,32,256]{3,2,1,0:T(8,128)(2,1)S(1)} %get-tuple-element.36), channel_id=1, source_target_pairs={{1,2},{3,4},{5,6},{7,8},{9,10},{11,12},{13,14},{2,1},{4,3},{6,5},{... | collective-permute-start | bytes 393224 | tf_op jit(solution)/shard_map/ppermute | solution.py:53
  32.5 5.6 %collective-permute-start.9 = (bf16[8,8,1536]{2,1,0:T(8,128)(2,1)S(1)}, bf16[8,8,1536]{2,1,0:T(8,128)(2,1)S(1)}, u32[]{:S(2)}, u32[]{:S(2)}) collective-permute-start(bf16[8,8,1536]{2,1,0:T(8,128)(2,1)S(1)} %get-tuple-element.49), channel_id=1, source_target_pairs={{0,1},{1,0},{2,3},{3,2},{4,5},{5,4},{6,7},{7,6},{8,9},{9,8},{10,11... | collective-permute-start | bytes 589832 | tf_op jit(solution)/shard_map/ppermute | solution.py:347
  37.0 13.9 %collective-permute-start.15 = (bf16[8,16,3456]{2,1,0:T(8,128)(2,1)S(1)}, bf16[8,16,3456]{2,1,0:T(8,128)(2,1)S(1)}, u32[]{:S(2)}, u32[]{:S(2)}) collective-permute-start(bf16[8,16,3456]{2,1,0:T(8,128)(2,1)S(1)} %get-tuple-element.40.refs_2_), channel_id=1, source_target_pairs={{0,1},{1,0},{2,3},{3,2},{4,5},{5,4},{6,7},{7,6},{8,9},{9,8},{10,11... | collective-permute-start | bytes 2654216 | tf_op jit(solution)/shard_map/ppermute | solution.py:347
  37.2 3.9 %collective-permute-start.6 = (bf16[8,8,1920]{2,1,0:T(8,128)(2,1)S(1)}, bf16[8,8,1920]{2,1,0:T(8,128)(2,1)S(1)}, u32[]{:S(2)}, u32[]{:S(2)}) collective-permute-start(bf16[8,8,1920]{2,1,0:T(8,128)(2,1)S(1)} %get-tuple-element.46), channel_id=1, source_target_pairs={{0,1},{1,0},{2,3},{3,2},{4,5},{5,4},{6,7},{7,6},{8,9},{9,8},{10,11... | collective-permute-start | bytes 737288 | tf_op jit(solution)/shard_map/ppermute | solution.py:347
  38.2 6.3 %collective-permute-start.10 = (bf16[4,8,1536]{2,1,0:T(8,128)(2,1)S(1)}, bf16[4,8,1536]{2,1,0:T(8,128)(2,1)S(1)}, u32[]{:S(2)}, u32[]{:S(2)}) collective-permute-start(bf16[4,8,1536]{2,1,0:T(8,128)(2,1)S(1)} %fusion.12), channel_id=1, source_target_pairs={{0,4},{1,5},{2,6},{3,7},{4,0},{5,1},{6,2},{7,3},{8,12},{9,13},{10,... | collective-permute-start | bytes 294920 | tf_op jit(solution)/shard_map/ppermute | solution.py:347
  41.2 5.4 %collective-permute-start.7 = (bf16[4,8,1920]{2,1,0:T(8,128)(2,1)S(1)}, bf16[4,8,1920]{2,1,0:T(8,128)(2,1)S(1)}, u32[]{:S(2)}, u32[]{:S(2)}) collective-permute-start(bf16[4,8,1920]{2,1,0:T(8,128)(2,1)S(1)} %fusion.8), channel_id=1, source_target_pairs={{0,2},{1,3},{2,0},{3,1},{4,6},{5,7},{6,4},{7,5},{8,10},{9,11},{10,... | collective-permute-start | bytes 368648 | tf_op jit(solution)/shard_map/ppermute | solution.py:347
  44.5 4.2 %collective-permute-start.11 = (bf16[2,8,1536]{2,1,0:T(8,128)(2,1)S(1)}, bf16[2,8,1536]{2,1,0:T(8,128)(2,1)S(1)}, u32[]{:S(2)}, u32[]{:S(2)}) collective-permute-start(bf16[2,8,1536]{2,1,0:T(8,128)(2,1)S(1)} %fusion.20), channel_id=1, source_target_pairs={{0,2},{1,3},{2,0},{3,1},{4,6},{5,7},{6,4},{7,5},{8,10},{9,11},{10,... | collective-permute-start | bytes 147464 | tf_op jit(solution)/shard_map/ppermute | solution.py:347
  46.6 4.3 %collective-permute-start.8 = (bf16[2,8,1920]{2,1,0:T(8,128)(2,1)S(1)}, bf16[2,8,1920]{2,1,0:T(8,128)(2,1)S(1)}, u32[]{:S(2)}, u32[]{:S(2)}) collective-permute-start(bf16[2,8,1920]{2,1,0:T(8,128)(2,1)S(1)} %fusion.15), channel_id=1, source_target_pairs={{0,4},{1,5},{2,6},{3,7},{4,0},{5,1},{6,2},{7,3},{8,12},{9,13},{10,... | collective-permute-start | bytes 184328 | tf_op jit(solution)/shard_map/ppermute | solution.py:347
  51.1 5.7 %collective-permute-start.18 = (bf16[4,16,1536]{2,1,0:T(8,128)(2,1)S(1)}, bf16[4,16,1536]{2,1,0:T(8,128)(2,1)S(1)}, u32[]{:S(2)}, u32[]{:S(2)}) collective-permute-start(bf16[4,16,1536]{2,1,0:T(8,128)(2,1)S(1)} %fusion.7), channel_id=1, source_target_pairs={{0,4},{1,5},{2,6},{3,7},{4,0},{5,1},{6,2},{7,3},{8,12},{9,13},{10,... | collective-permute-start | bytes 589832 | tf_op jit(solution)/shard_map/ppermute | solution.py:347
  53.1 7.3 %collective-permute-start.16 = (bf16[4,16,1920]{2,1,0:T(8,128)(2,1)S(1)}, bf16[4,16,1920]{2,1,0:T(8,128)(2,1)S(1)}, u32[]{:S(2)}, u32[]{:S(2)}) collective-permute-start(bf16[4,16,1920]{2,1,0:T(8,128)(2,1)S(1)} %fusion), channel_id=1, source_target_pairs={{0,2},{1,3},{2,0},{3,1},{4,6},{5,7},{6,4},{7,5},{8,10},{9,11},{10,... | collective-permute-start | bytes 737288 | tf_op jit(solution)/shard_map/ppermute | solution.py:347
  56.9 4.7 %collective-permute-start.19 = (bf16[2,16,1536]{2,1,0:T(8,128)(2,1)S(1)}, bf16[2,16,1536]{2,1,0:T(8,128)(2,1)S(1)}, u32[]{:S(2)}, u32[]{:S(2)}) collective-permute-start(bf16[2,16,1536]{2,1,0:T(8,128)(2,1)S(1)} %fusion.13), channel_id=1, source_target_pairs={{0,2},{1,3},{2,0},{3,1},{4,6},{5,7},{6,4},{7,5},{8,10},{9,11},{10,... | collective-permute-start | bytes 294920 | tf_op jit(solution)/shard_map/ppermute | solution.py:347
  60.5 6.1 %collective-permute-start.17 = (bf16[2,16,1920]{2,1,0:T(8,128)(2,1)S(1)}, bf16[2,16,1920]{2,1,0:T(8,128)(2,1)S(1)}, u32[]{:S(2)}, u32[]{:S(2)}) collective-permute-start(bf16[2,16,1920]{2,1,0:T(8,128)(2,1)S(1)} %fusion.9), channel_id=1, source_target_pairs={{0,4},{1,5},{2,6},{3,7},{4,0},{5,1},{6,2},{7,3},{8,12},{9,13},{10,... | collective-permute-start | bytes 368648 | tf_op jit(solution)/shard_map/ppermute | solution.py:347
  66.7 6.5 %collective-permute-start.20 = (bf16[16,3456]{1,0:T(8,128)(2,1)S(1)}, bf16[16,3456]{1,0:T(8,128)(2,1)S(1)}, u32[]{:S(2)}, u32[]{:S(2)}) collective-permute-start(bf16[16,3456]{1,0:T(8,128)(2,1)S(1)} %fusion.11), channel_id=1, source_target_pairs={{0,8},{1,9},{2,10},{3,11},{4,12},{5,13},{6,14},{7,15},{8,0},{9,1},... | collective-permute-start | bytes 331784 | tf_op jit(solution)/shard_map/ppermute | solution.py:347
  68.2 7.0 %collective-permute-start.14 = (bf16[8,3456]{1,0:T(8,128)(2,1)S(1)}, bf16[8,3456]{1,0:T(8,128)(2,1)S(1)}, u32[]{:S(2)}, u32[]{:S(2)}) collective-permute-start(bf16[8,3456]{1,0:T(8,128)(2,1)S(1)} %get-tuple-element.54), channel_id=1, source_target_pairs={{0,24},{1,25},{2,26},{3,27},{4,28},{5,29},{6,30},{7,31},{8,16},{9,... | collective-permute-start | bytes 165896 | tf_op jit(solution)/shard_map/ppermute | solution.py:352
  70.7 6.2 %collective-permute-start.13 = (bf16[8,3456]{1,0:T(8,128)(2,1)S(1)}, bf16[8,3456]{1,0:T(8,128)(2,1)S(1)}, u32[]{:S(2)}, u32[]{:S(2)}) collective-permute-start(bf16[8,3456]{1,0:T(8,128)(2,1)S(1)} %get-tuple-element.54), channel_id=1, source_target_pairs={{0,8},{1,9},{2,10},{3,11},{4,12},{5,13},{6,14},{7,15},{8,0},{9,1},... | collective-permute-start | bytes 165896 | tf_op jit(solution)/shard_map/ppermute | solution.py:347
  73.1 4.2 %collective-permute-start.12 = (bf16[8,3456]{1,0:T(8,128)(2,1)S(1)}, bf16[8,3456]{1,0:T(8,128)(2,1)S(1)}, u32[]{:S(2)}, u32[]{:S(2)}) collective-permute-start(bf16[8,3456]{1,0:T(8,128)(2,1)S(1)} %get-tuple-element.53), channel_id=1, source_target_pairs={{0,16},{1,17},{2,18},{3,19},{4,20},{5,21},{6,22},{7,23},{8,24},{9,... | collective-permute-start | bytes 165896 | tf_op jit(solution)/shard_map/ppermute | solution.py:352
  73.2 5.3 %collective-permute-start.21 = (bf16[16,3456]{1,0:T(8,128)(2,1)S(1)}, bf16[16,3456]{1,0:T(8,128)(2,1)S(1)}, u32[]{:S(2)}, u32[]{:S(2)}) collective-permute-start(bf16[16,3456]{1,0:T(8,128)(2,1)S(1)} %fusion.6), channel_id=1, source_target_pairs={{0,16},{1,17},{2,18},{3,19},{4,20},{5,21},{6,22},{7,23},{8,24},{9,... | collective-permute-start | bytes 331784 | tf_op jit(solution)/shard_map/ppermute | solution.py:352

commit v3 on v2

--- a/solution.py
+++ b/solution.py
@@ -9,27 +9,15 @@
 
 F32 = jnp.float32
 BF16 = jnp.bfloat16
+COST = 64
 VMEM = pl.BlockSpec(memory_space=pltpu.VMEM)
 SMEM = pl.BlockSpec(memory_space=pltpu.SMEM)
 
 
-def size_of(shapes):
-    total = 0
-    for item in shapes:
-        count = jnp.dtype(item.dtype).itemsize
-        for extent in item.shape:
-            count *= extent
-        total += count
-    return total
-
-
 def kernel_call(body, operands, outs, scratch, flops, limit, scalars=0, after=()):
-    cost = pl.CostEstimate(
-        flops=flops, bytes_accessed=size_of(operands) + size_of(outs), transcendentals=0
-    )
+    cost = pl.CostEstimate(flops=flops // COST, bytes_accessed=2**20, transcendentals=0)
     used, extra = (len(operands), len(after))
-    specs = [SMEM] * scalars + [VMEM] * (used - scalars)
-    specs += [pl.BlockSpec(memory_space=pl.ANY)] * extra
+    specs = [SMEM] * scalars + [VMEM] * (used - scalars + extra)
 
     def inner(*refs):
         body(*refs[:used], *refs[used + extra :])
@@ -243,7 +231,7 @@
         send[at, :, columns] = jnp.where(here, high, low).astype(BF16)
 
 
-def coarse_terms(place, wide3, halo3, delta, keep, send=None, *, orders, split):
+def coarse_terms(place, wide3, halo3, delta, keep, send=None, *, order):
     planes, cy, cz, wide = delta.shape
     span = wide3.shape[-1]
     for tap in range(9):
@@ -253,7 +241,7 @@
             ref, at = source(wide3, halo3, p + a - 1)
             piece = ref[at, b : b + cy].reshape(cy * cz, span)
             total = plus(total, tap_dot(delta[p].reshape(cy * cz, wide), piece))
-        put_term(total, tap * span, place, orders[tap >= split], keep, send)
+        put_term(total, tap * span, place, order, keep, send)
 
 
 def backward_taps(wide3, plane, kernel, a, grad):
@@ -356,13 +344,17 @@
     )
 
 
-def middle_bits(count):
+def exchange_groups(count):
     bits = [1 << k for k in range(1, count.bit_length() - 2)]
-    return bits, bits[1:] + bits[:1]
-
-
-def order_of(middle, count):
-    bits = middle + [count // 2]
+    return [bits[k : k + 2] for k in range(0, len(bits), 2)]
+
+
+def exchange_bits(count):
+    return [bit for group in exchange_groups(count) for bit in group] + [count // 2]
+
+
+def owners_in_order(count):
+    bits = exchange_bits(count)
     return [
         sum(bit for k, bit in enumerate(bits) if at >> (len(bits) - 1 - k) & 1)
         for at in range(count // 2)
@@ -382,39 +374,75 @@
     return keep, lax.dynamic_index_in_dim(parts, 1 - mine, 0, keepdims=False)
 
 
-def sided(terms, middle, count, columns):
+def sided(terms, count):
     if len(terms) == 2:
-        return [item[:, :, columns] for item in terms]
-    whole = terms[0][:, columns]
+        return terms
     bits = count.bit_length() - 1
-    parts = whole.reshape((2,) * bits + (whole.shape[0] // count, -1))
-    sequence = [1] + middle + [count // 2]
-    axes = [bits - bit.bit_length() for bit in sequence]
-    return pick(parts.transpose(tuple(axes) + (bits, bits + 1)), 1)
-
-
-def halved(total, middle):
-    for bit in middle:
-        owned, columns = total.shape[-2:]
-        keep, send = pick(total.reshape(2, -1, owned, columns), bit)
-        total = keep + swap(send.astype(BF16), bit).astype(F32)
-    return total.reshape((2,) + total.shape[-2:])
-
-
-def last_halved(total):
+    parts = terms[0].reshape((2,) * bits + (terms[0].shape[0] // count, -1))
+    axes = [bits - bit.bit_length() for bit in [1] + exchange_bits(count)]
+    sides = pick(parts.transpose(tuple(axes) + (bits, bits + 1)), 1)
+    return [side.reshape((-1,) + side.shape[-2:]) for side in sides]
+
+
+def masks_of(group):
+    return [sum(bit for k, bit in enumerate(group) if turn >> k & 1) for turn in range(1 << len(group))]
+
+
+def fold_body(place, *refs, group, chunks):
+    pieces, outs = (refs[: sum(chunks)], refs[sum(chunks) :])
+    span = outs[0].shape[0]
+    lane = start = 0
+    for length in chunks:
+        some = pieces[start : start + length]
+        columns = pl.ds(lane, some[0].shape[2])
+        for mask, out in zip(masks_of(group), outs):
+            at = 0
+            for bit in group:
+                mine = place[bit.bit_length() - 1]
+                at = 2 * at + (1 - mine if mask & bit else mine)
+            for k in range(span):
+                total = None
+                for piece in some:
+                    total = plus(total, piece[at * span + k].astype(F32))
+                out[k, :, columns] = total.astype(out.dtype)
+        start += length
+        lane += some[0].shape[2]
+
+
+def fold(place, chunks, group, after=()):
+    length, owned = chunks[0][0].shape[:2]
+    extents = (length >> len(group), owned, sum(some[0].shape[2] for some in chunks))
+    masks = masks_of(group)
+    kept, *sends = kernel_call(
+        functools.partial(fold_body, group=group, chunks=[len(some) for some in chunks]),
+        [place] + [piece for some in chunks for piece in some],
+        [jax.ShapeDtypeStruct(extents, BF16 if mask else F32) for mask in masks],
+        [],
+        0,
+        8,
+        scalars=1,
+        after=after,
+    )
+    return dict(zip(masks[1:], sends)), kept
+
+
+def received(sends, kept):
+    return [kept] + [swap(part, mask) for mask, part in sends.items()]
+
+
+def last_sum(sends, kept):
     bit = lax.axis_size("space") // 2
-    keep, send = pick(total, bit)
-    base = (keep + swap(send.astype(BF16), bit).astype(F32)).astype(BF16)
+    base = (kept[0] + swap(sends[bit][0], bit).astype(F32)).astype(BF16)
     if lax.axis_size("sample") != 2:
         return lax.psum(base, "sample").astype(F32)
     return base.astype(F32) + swap_sample(base).astype(F32)
 
 
-def last_direct(total):
+def last_direct(sends, kept):
     if lax.axis_size("sample") != 2:
-        return last_halved(total)
+        return last_sum(sends, kept)
     bit = lax.axis_size("space") // 2
-    keep, send = pick(total.astype(BF16), bit)
+    keep, send = (kept[0].astype(BF16), sends[bit][0])
     near, cross, other = (swap(send, bit), swap_sample(send, bit), swap_sample(keep))
     return (keep.astype(F32) + other.astype(F32)) + (near.astype(F32) + cross.astype(F32))
 
@@ -427,7 +455,7 @@
     count = lax.axis_size("space")
     me = lax.axis_index("space")
     parity = me % 2
-    place = jnp.reshape(parity, (1,)).astype(jnp.int32)
+    place = jnp.stack([me >> k & 1 for k in range(count.bit_length() - 1)]).astype(jnp.int32)
     x = volumes[0]
     cells, few = (planes * fy * fz, cp * cy * cz)
     fine_flops, coarse_flops = (54 * cells * chan * chan, 54 * few * chan * wide)
@@ -494,13 +522,10 @@
         scalars=1,
     )
     from_pair, from_next = exchange(to_pair, to_next)
-    first, second = middle_bits(count)
-    orders = (order_of(first, count), order_of(second, count))
-    split = 5
-    border = split * 3 * chan
-    low, high = (slice(0, border), slice(border, 27 * chan))
+    order = owners_in_order(count)
+    steps = exchange_groups(count) + [[count // 2]]
     terms = kernel_call(
-        functools.partial(coarse_terms, orders=orders, split=split),
+        functools.partial(coarse_terms, order=order),
         [place, wide3, halo3, coarse_delta],
         term_shapes(wide, 27 * chan, count),
         [],
@@ -508,17 +533,10 @@
         16,
         scalars=1,
     )
-    halves = [sided(terms, first, count, low), sided(terms, second, count, high)]
-    if len(terms) == 2:
-        got = swap(terms[1], 1)
-        gots = [got[:, :, low], got[:, :, high]]
-    else:
-        gots = [swap(send, 1) for keep, send in halves]
-    sums = []
-    for (keep, _), got, middle in zip(halves, gots, (first, second)):
-        sums.append(halved(keep.astype(F32) + got.astype(F32), middle))
-    coarse_grad = last_halved(jnp.concatenate(sums, axis=-1))
-
+    keep, send = sided(terms, count)
+    early, coarse_kept = fold(
+        place, [[keep, swap(send, 1)]], steps[0], [from_pair, from_next]
+    )
     (partial,) = kernel_call(
         coarse_backward,
         [coarse_delta, coarse_kernel],
@@ -528,29 +546,44 @@
         16,
         after=[terms[-1]],
     )
-    fine_delta, *one = kernel_call(
-        functools.partial(fine_first, order=orders[0], taps=range(split)),
+    parts = [range(0, 3), range(3, 6), range(6, 9)]
+    fine_delta, *first = kernel_call(
+        functools.partial(fine_first, order=order, taps=parts[0]),
         [place, from_pair, from_next, coarse_kernel, partial, slope, slope_edge, wide6, halo6],
-        [shape(planes, half, fz, 2 * chan)] + term_shapes(chan, border, count),
+        [shape(planes, half, fz, 2 * chan)] + term_shapes(chan, 9 * chan, count),
         [pltpu.VMEM((2, cy + 2, cz, 3 * wide), BF16), pltpu.VMEM((cy, fz, chan), F32)],
         fine_flops * 2 // 3,
         16,
         scalars=1,
-    )
-    two = kernel_call(
-        functools.partial(fine_second, order=orders[1], taps=range(split, 9)),
-        [place, wide6, halo6, fine_delta],
-        term_shapes(chan, 27 * chan - border, count),
-        [],
-        fine_flops // 2,
-        16,
-        scalars=1,
-    )
-    sums = []
-    for terms, middle in ((one, first), (two, second)):
-        keep, send = sided(terms, middle, count, slice(None))
-        sums.append(halved(keep.astype(F32) + swap(send, 1).astype(F32), middle))
-    fine_grad = last_direct(jnp.concatenate(sums, axis=-1))
+        after=list(early.values())[:1],
+    )
+    fine_parts = [first]
+    for part in parts[1:]:
+        fine_parts.append(
+            kernel_call(
+                functools.partial(fine_second, order=order, taps=part),
+                [place, wide6, halo6, fine_delta],
+                term_shapes(chan, 9 * chan, count),
+                [],
+                fine_flops // 3,
+                16,
+                scalars=1,
+                after=[fine_parts[-1][-1]],
+            )
+        )
+    got = received(early, coarse_kept)
+    pieces = []
+    for part in fine_parts:
+        keep, send = sided(part, count)
+        pieces.append([keep, swap(send, 1)])
+    late, fine_kept = fold(place, pieces, steps[0], got[1:])
+    for group in steps[1:]:
+        early, coarse_kept = fold(place, [got], group, [late[steps[0][0]]])
+        got = received(early, coarse_kept)
+    coarse_grad = last_sum(early, coarse_kept)
+    for group in steps[1:]:
+        late, fine_kept = fold(place, [received(late, fine_kept)], group)
+    fine_grad = last_direct(late, fine_kept)
     return (out[None], fine_grad, coarse_grad)
 
 

time: 79.4 us -> 73.6 us (0.927)
  waiting for transfers between devices: 18 us -> 10.1 us
  Pallas kernels: 17.7 us -> 23.8 us
  starting transfers between devices: 37 us -> 33.6 us
    ppermute x13 -> x12, waiting for transfers between devices: 17.1 us -> 7.75 us  [swap(): return lax.ppermute(value, 'space', [(i, i ^ bit) for i in range(count)])]
    pallas_call x8 -> x13, Pallas kernels: 17.7 us -> 23.8 us  [kernel_call(): pl.pallas_call(inner, out_shape=outs, in_specs=specs, out_specs=[VMEM] *...]
    ppermute x3, starting transfers between devices: 8.36 us -> 4.55 us  [exchange(): lax.ppermute(to_pair, 'space', pair)]
    ppermute x3, waiting for transfers between devices: 0.88 us -> 2.29 us  [swap_sample(): lax.ppermute(value, ('sample', 'space'), [(s * count + i, (1 - s) * count...]
    ppermute x3, starting transfers between devices: 4.6 us -> 5.55 us  [swap_sample(): lax.ppermute(value, ('sample', 'space'), [(s * count + i, (1 - s) * count...]
    ppermute x13 -> x12, starting transfers between devices: 21.9 us -> 21.4 us  [swap(): return lax.ppermute(value, 'space', [(i, i ^ bit) for i in range(count)])]
  transfers between devices with their start and end apart: 22 -> 21, of which waited for: 12 -> 8; matrix products, arithmetic and copies ran while one was open for 2% -> 1% of each run, Pallas kernels for 11% -> 18%
where the time goes in v3:
time: 73.6 us; the launch traced here: 73.3 us
  starting transfers between devices  33.6 us (46%)
  Pallas kernels  23.8 us (32%)
  waiting for transfers between devices  10.1 us (14%)
  local copies, waits for them, and re-layouts  3.47 us (5%)
  other arithmetic  1.5 us (2%)
  between operations  0.86 us (1%)
    pallas_call x13, Pallas kernels, kernel_call(): pl.pallas_call(inner, out_shape=outs, in_specs=specs, out_specs=[VMEM] *...  23.8 us
    ppermute x12, starting transfers between devices, swap(): return lax.ppermute(value, 'space', [(i, i ^ bit) for i in range(count)])  21.4 us
    ppermute x12, waiting for transfers between devices, swap(): return lax.ppermute(value, 'space', [(i, i ^ bit) for i in range(count)])  7.75 us
    ppermute x3, starting transfers between devices, swap_sample(): lax.ppermute(value, ('sample', 'space'), [(s * count + i, (1 - s) * count...  5.55 us
    ppermute x3, starting transfers between devices, exchange(): lax.ppermute(to_pair, 'space', pair)  4.55 us
    unnamed x8, local copies, waits for them, and re-layouts  2.4 us
    ppermute x3, waiting for transfers between devices, swap_sample(): lax.ppermute(value, ('sample', 'space'), [(s * count + i, (1 - s) * count...  2.29 us
    ppermute x3, starting transfers between devices, exchange(): lax.ppermute(to_next, 'space', across)  2.17 us
  transfers between devices with their start and end apart: 21, of which 8 were waited for; matrix products, arithmetic and copies ran while one was open for 1% of the time, Pallas kernels for 18%

profile of v3, /device:TPU:0, one launch (start us, length us, event | category | flops | bytes accessed | tf_op | source)
XLA Modules:
  0.0 73.3 jit_solution(4960474017890957260)
XLA Ops:
  0.7 1.1 %dynamic-slice_bitcast_fusion = (bf16[1,16,64,128]{3,2,1,0:T(8,128)(2,1)S(1)}, bf16[1,16,64,128]{3,2,1,0:T(8,128)(2,1)S(1)}) fusion(bf16[1,4,16,64,128]{4,3,2,1,0:T(8,128)(2,1)} %param.4, s32[]{:T(128)S(6)} %select_n.15, s32[]{:T(128)S(6)} %select_n.14), kind=kLoop, calls=%fused_computation | loop fusion | bytes 1048584 | tf_op jit(solution)/shard_map/dynamic_slice | solution.py:467
  1.7 0.7 collective-permute-start.1
  2.4 4.4 %collective-permute-start = (bf16[1,16,64,128]{3,2,1,0:T(8,128)(2,1)S(1)}, bf16[1,16,64,128]{3,2,1,0:T(8,128)(2,1)S(1)}, u32[]{:S(2)}, u32[]{:S(2)}) collective-permute-start(bf16[1,16,64,128]{3,2,1,0:T(8,128)(2,1)S(1)} %get-tuple-element.80), channel_id=1, source_target_pairs={{0,1},{1,0},{2,3},{3,2},{4,5},{5,4},{6,7},{7,6},{8,9},{9,8},{10,11... | collective-permute-start | bytes 786440 | tf_op jit(solution)/shard_map/ppermute | solution.py:41
  6.8 1.2 %copy-done.1 = bf16[1,4,16,64,128]{4,3,2,1,0:T(8,128)(2,1)S(1)} copy-done((bf16[1,4,16,64,128]{4,3,2,1,0:T(8,128)(2,1)S(1)}, bf16[1,4,16,64,128]{4,3,2,1,0:T(8,128)(2,1)}, u32[]{:S(2)}) %copy-start.1) | copy-done | bytes 1048600
  8.0 1.2 %copy-done.2 = bf16[27,128,128]{2,1,0:T(8,128)(2,1)S(1)} copy-done((bf16[27,128,128]{2,1,0:T(8,128)(2,1)S(1)}, bf16[27,128,128]{2,1,0:T(8,128)(2,1)}, u32[]{:S(2)}) %copy-start.2) | copy-done | bytes 884760
  9.2 4.6 %shard_map.67 = (bf16[4,9,64,768]{3,2,1,0:T(8,128)(2,1)S(1)}, bf16[3,2,768,256]{3,2,1,0:T(8,128)(2,1)S(1)}, f32[2,512,256]{2,1,0:T(8,128)S(1)}, f32[2,8,64,128]{3,2,1,0:T(8,128)S(1)}, bf16[2,8,64,256]{3,2,1,0:T(8,128)(2,1)S(1)}) custom-call(bf16[4,16,64,128]{3,2,1,0:T(8,128)(2,1)S(1)} %bitcast.25, bf16[9,384,128]{2,1,0:T(8,128)(2,1)S(1)} %bitcast.26), custom_call_target="tpu_custom_call" | custom-call | flops 56623104 | bytes 1048576 | tf_op jit(solution)/shard_map/pallas_call | solution.py:25
  13.8 0.0 copy-start
  13.8 0.1 pad_add_fusion.refs_0_
  13.9 0.0 collective-permute-done.1.refs_2_
  13.9 0.0 collective-permute-done.refs_1_
  13.9 2.0 %shard_map.68 = (bf16[2,9,64,768]{3,2,1,0:T(8,128)(2,1)S(1)}, bf16[2,8,32,128]{3,2,1,0:T(8,128)(2,1)S(1)}, bf16[2,8,64,256]{3,2,1,0:T(8,128)(2,1)S(1)}, bf16[1,8...) custom-call(s32[4]{0:T(128)S(1)} %pad_add_fusion.refs_0_, ...), custom_call_target="tpu_custom_call" | custom-call | flops 9437184 | bytes 1048576 | tf_op jit(solution)/shard_map/pallas_call | solution.py:25
  15.9 0.1 collective-permute-start.2
  16.0 0.7 collective-permute-start.3
  16.7 0.0 copy-done
  16.7 1.0 %shard_map.69 = (bf16[2,10,32,384]{3,2,1,0:T(8,128)(2,1)S(1)}, f32[2,256,256]{2,1,0:T(8,128)S(1)}) custom-call(bf16[2,8,32,128]{3,2,1,0:T(8,128)(2,1)S(1)} %get-tuple-element.46.refs_0_, bf16[9,384,256]{2,1,0:T(8,128)(2,1)S(1)} %bitcast.23), custom_call_target="tpu_custom_call" | custom-call | flops 14155776 | bytes 1048576 | tf_op jit(solution)/shard_map/pallas_call | solution.py:25
  17.7 0.0 collective-permute-done.2.refs_1_
  17.7 0.0 collective-permute-done.3.refs_2_
  17.7 0.0 copy-done.3
  17.7 2.0 %shard_map.70 = (bf16[2,10,32,384]{3,2,1,0:T(8,128)(2,1)S(1)}, bf16[2,8,32,256]{3,2,1,0:T(8,128)(2,1)}, bf16[2,8,32,256]{3,2,1,0:T(8,128)(2,1)S(1)}, bf16[1,8,32...) custom-call(s32[4]{0:T(128)S(1)} %pad_add_fusion.refs_0_, bf16[1,8,32,128]{3,2,1,0:T(8,128)(2,1)S(1)} %collective-permute-done.2.refs_1_, ...), custom_call_target="tpu_custom_call" | custom-call | flops 4718592 | bytes 1048576 | tf_op jit(solution)/shard_map/pallas_call | solution.py:25
  19.8 2.0 %shard_map.71 = (bf16[8,16,3456]{2,1,0:T(8,128)(2,1)S(1)}, bf16[8,16,3456]{2,1,0:T(8,128)(2,1)S(1)}) custom-call(s32[4]{0:T(128)S(1)} %pad_add_fusion.refs_0_, bf16[2,10,32,384]{3,2,1,0:T(8,128)(2,1)S(1)} %get-tuple-element.52.refs_1_, bf16[2,10,32,384]{3,2,1,0:T(8,128)(2,1)S(1)} %get-tuple-element.53.refs_2_, ...), custom_call_target="tpu_custom_call" | custom-call | flops 14155776 | bytes 1048576 | tf_op jit(solution)/shard_map/pallas_call | solution.py:25
  21.7 4.4 %collective-permute-start.6 = (bf16[8,16,3456]{2,1,0:T(8,128)(2,1)S(1)}, bf16[8,16,3456]{2,1,0:T(8,128)(2,1)S(1)}, u32[]{:S(2)}, u32[]{:S(2)}) collective-permute-start(bf16[8,16,3456]{2,1,0:T(8,128)(2,1)S(1)} %get-tuple-element.54.refs_2_), channel_id=1, source_target_pairs={{0,1},{1,0},{2,3},{3,2},{4,5},{5,4},{6,7},{7,6},{8,9},{9,8},{10,11... | collective-permute-start | bytes 2654216 | tf_op jit(solution)/shard_map/ppermute | solution.py:335
  26.1 0.1 collective-permute-start.4
  26.2 0.8 %collective-permute-start.5 = (bf16[1,8,32,256]{3,2,1,0:T(8,128)(2,1)S(1)}, bf16[1,8,32,256]{3,2,1,0:T(8,128)(2,1)S(1)}, u32[]{:S(2)}, u32[]{:S(2)}) collective-permute-start(bf16[1,8,32,256]{3,2,1,0:T(8,128)(2,1)S(1)} %get-tuple-element.50), channel_id=1, source_target_pairs={{1,2},{3,4},{5,6},{7,8},{9,10},{11,12},{13,14},{2,1},{4,3},{6,5},{... | collective-permute-start | bytes 393224 | tf_op jit(solution)/shard_map/ppermute | solution.py:41
  27.1 1.4 %shard_map.72.refs_4_ = f32[2,256,128]{2,1,0:T(8,128)S(1)} custom-call(bf16[2,8,32,256]{3,2,1,0:T(8,128)(2,1)S(1)} %get-tuple-element.51.refs_3_.refs_0_, bf16[27,128,256]{2,1,0:T(8,128)(2,1)S(1)} %copy-done, bf16[8,16,3456]{2,1,0:T(8,128)(2,1)S(1)} %get-tuple-element.54.refs_2_), custom_call_target="tpu_custom_call" | custom-call | flops 14155776 | bytes 1048576 | tf_op jit(solution)/shard_map/pallas_call | solution.py:25
  28.4 0.0 collective-permute-done.4.refs_3_.refs_1_
  28.4 0.0 collective-permute-done.5.refs_4_.refs_2_
  28.5 0.0 collective-permute-done.6.refs_2_
  28.5 0.7 %shard_map.73 = (f32[2,16,3456]{2,1,0:T(8,128)S(1)}, bf16[2,16,3456]{2,1,0:T(8,128)(2,1)S(1)}, bf16[2,16,3456]{2,1,0:T(8,128)(2,1)S(1)}, bf16[2,16,3456]{2,1,0:T(8,128)(2,1)S(1)}) custom-call(s32[4]{0:T(128)S(1)} %pad_add_fusion.refs_0_, bf16[8,16,3456]{2,1,0:T(8,128)(2,1)S(1)} %get-tuple-element.59.refs_1_, ...), custom_call_target="tpu_custom_call" | custom-call | bytes 1048576 | tf_op jit(solution)/shard_map/pallas_call | solution.py:25
  29.2 3.4 %shard_map.74 = (bf16[4,8,64,256]{3,2,1,0:T(8,128)(2,1)S(1)}, bf16[8,8,1152]{2,1,0:T(8,128)(2,1)S(1)}, bf16[8,8,1152]{2,1,0:T(8,128)(2,1)S(1)}) custom-call(s32[4]{0:T(128)S(1)} %pad_add_fusion.refs_0_, bf16[1,8,32,256]{3,2,1,0:T(8,128)(2,1)S(1)} %collective-permute-done.4.refs_3_.refs_1_, ...), custom_call_target="tpu_custom_call" | custom-call | flops 37748736 | bytes 1048576 | tf_op jit(solution)/shard_map/pallas_call | solution.py:25
  32.6 4.9 %collective-permute-start.7 = (bf16[8,8,1152]{2,1,0:T(8,128)(2,1)S(1)}, bf16[8,8,1152]{2,1,0:T(8,128)(2,1)S(1)}, u32[]{:S(2)}, u32[]{:S(2)}) collective-permute-start(bf16[8,8,1152]{2,1,0:T(8,128)(2,1)S(1)} %get-tuple-element.62.refs_4_), channel_id=1, source_target_pairs={{0,1},{1,0},{2,3},{3,2},{4,5},{5,4},{6,7},{7,6},{8,9},{9,8},{10,11... | collective-permute-start | bytes 442376 | tf_op jit(solution)/shard_map/ppermute | solution.py:335
  37.5 3.3 %collective-permute-start.11 = (bf16[2,16,3456]{2,1,0:T(8,128)(2,1)S(1)}, bf16[2,16,3456]{2,1,0:T(8,128)(2,1)S(1)}, u32[]{:S(2)}, u32[]{:S(2)}) collective-permute-start(bf16[2,16,3456]{2,1,0:T(8,128)(2,1)S(1)} %get-tuple-element.68), channel_id=1, source_target_pairs={{0,4},{1,5},{2,6},{3,7},{4,0},{5,1},{6,2},{7,3},{8,12},{9,13},{10,... | collective-permute-start | bytes 663560 | tf_op jit(solution)/shard_map/ppermute | solution.py:335
  40.8 1.1 %collective-permute-start.12 = (bf16[2,16,3456]{2,1,0:T(8,128)(2,1)S(1)}, bf16[2,16,3456]{2,1,0:T(8,128)(2,1)S(1)}, u32[]{:S(2)}, u32[]{:S(2)}) collective-permute-start(bf16[2,16,3456]{2,1,0:T(8,128)(2,1)S(1)} %get-tuple-element.69), channel_id=1, source_target_pairs={{0,6},{1,7},{2,4},{3,5},{4,2},{5,3},{6,0},{7,1},{8,14},{9,15},{10,... | collective-permute-start | bytes 663560 | tf_op jit(solution)/shard_map/ppermute | solution.py:335
  41.9 0.4 collective-permute-start.10
  42.3 2.4 %shard_map.75 = (bf16[8,8,1152]{2,1,0:T(8,128)(2,1)S(1)}, bf16[8,8,1152]{2,1,0:T(8,128)(2,1)S(1)}) custom-call(s32[4]{0:T(128)S(1)} %pad_add_fusion.refs_0_, bf16[4,9,64,768]{3,2,1,0:T(8,128)(2,1)S(1)} %get-tuple-element.57.refs_7_.refs_1_, bf16[2,9,64,768]{3,2,1,0:T(8,128)(2,1)S(1)} %get-tuple-element.58.refs_8_.refs_2_, ...), custom_call_target="tpu_custom_call" | custom-call | flops 18874368 | bytes 1048576 | tf_op jit(solution)/shard_map/pallas_call | solution.py:25
  44.7 2.4 %shard_map.76 = (bf16[8,8,1152]{2,1,0:T(8,128)(2,1)S(1)}, bf16[8,8,1152]{2,1,0:T(8,128)(2,1)S(1)}) custom-call(s32[4]{0:T(128)S(1)} %pad_add_fusion.refs_0_, bf16[4,9,64,768]{3,2,1,0:T(8,128)(2,1)S(1)} %get-tuple-element.57.refs_7_.refs_1_, bf16[2,9,64,768]{3,2,1,0:T(8,128)(2,1)S(1)} %get-tuple-element.58.refs_8_.refs_2_, ...), custom_call_target="tpu_custom_call" | custom-call | flops 18874368 | bytes 1048576 | tf_op jit(solution)/shard_map/pallas_call | solution.py:25
  47.1 0.1 collective-permute-start.9
  47.1 0.0 collective-permute-done.7.refs_2_
  47.2 0.5 collective-permute-start.8
  47.7 0.9 %collective-permute-done.9.refs_6_ = bf16[8,8,1152]{2,1,0:T(8,128)(2,1)S(1)} collective-permute-done((bf16[8,8,1152]{2,1,0:T(8,128)(2,1)S(1)}, bf16[8,8,1152]{2,1,0:T(8,128)(2,1)S(1)}, u32[]{:S(2)}, u32[]{:S(2)}) %collective-permute-start.9) | collective-permute-done | bytes 147488 | tf_op jit(solution)/shard_map/ppermute | solution.py:335
  48.5 0.2 collective-permute-done.8.refs_4_
  48.7 0.0 collective-permute-done.11.refs_8_.refs_3_
  48.7 3.4 %collective-permute-done.12.refs_9_.refs_4_ = bf16[2,16,3456]{2,1,0:T(8,128)(2,1)S(1)} collective-permute-done((bf16[2,16,3456]{2,1,0:T(8,128)(2,1)S(1)}, bf16[2,16,3456]{2,1,0:T(8,128)(2,1)S(1)}, u32[]{:S(2)}, u32[]{:S(2)}) %collective-permute-start.12) | collective-permute-done | bytes 221216 | tf_op jit(solution)/shard_map/ppermute | solution.py:335
  52.1 1.4 %collective-permute-done.10.refs_7_.refs_2_ = bf16[2,16,3456]{2,1,0:T(8,128)(2,1)S(1)} collective-permute-done((bf16[2,16,3456]{2,1,0:T(8,128)(2,1)S(1)}, bf16[2,16,3456]{2,1,0:T(8,128)(2,1)S(1)}, u32[]{:S(2)}, u32[]{:S(2)}) %collective-permute-start.10) | collective-permute-done | bytes 221216 | tf_op jit(solution)/shard_map/ppermute | solution.py:335
  53.5 0.7 shard_map.77
  54.1 1.6 %collective-permute-start.14 = (bf16[2,8,3456]{2,1,0:T(8,128)(2,1)S(1)}, bf16[2,8,3456]{2,1,0:T(8,128)(2,1)S(1)}, u32[]{:S(2)}, u32[]{:S(2)}) collective-permute-start(bf16[2,8,3456]{2,1,0:T(8,128)(2,1)S(1)} %get-tuple-element.72), channel_id=1, source_target_pairs={{0,4},{1,5},{2,6},{3,7},{4,0},{5,1},{6,2},{7,3},{8,12},{9,13},{10,... | collective-permute-start | bytes 331784 | tf_op jit(solution)/shard_map/ppermute | solution.py:335
  55.8 0.6 collective-permute-start.15
  56.4 1.3 %collective-permute-start.13 = (bf16[2,8,3456]{2,1,0:T(8,128)(2,1)S(1)}, bf16[2,8,3456]{2,1,0:T(8,128)(2,1)S(1)}, u32[]{:S(2)}, u32[]{:S(2)}) collective-permute-start(bf16[2,8,3456]{2,1,0:T(8,128)(2,1)S(1)} %get-tuple-element.71.refs_5_), channel_id=1, source_target_pairs={{0,2},{1,3},{2,0},{3,1},{4,6},{5,7},{6,4},{7,5},{8,10},{9,11},{10,... | collective-permute-start | bytes 331784 | tf_op jit(solution)/shard_map/ppermute | solution.py:335
  57.7 0.7 shard_map.79
  58.4 2.7 %collective-permute-start.19 = (bf16[16,3456]{1,0:T(8,128)(2,1)S(1)}, bf16[16,3456]{1,0:T(8,128)(2,1)S(1)}, u32[]{:S(2)}, u32[]{:S(2)}) collective-permute-start(bf16[16,3456]{1,0:T(8,128)(2,1)S(1)} %bitcast.28), channel_id=1, source_target_pairs={{0,8},{1,9},{2,10},{3,11},{4,12},{5,13},{6,14},{7,15},{8,0},{9,1},... | collective-permute-start | bytes 331784 | tf_op jit(solution)/shard_map/ppermute | solution.py:335
  61.0 0.0 collective-permute-done.14.refs_3_
  61.0 1.6 %collective-permute-done.15.refs_4_ = bf16[2,8,3456]{2,1,0:T(8,128)(2,1)S(1)} collective-permute-done((bf16[2,8,3456]{2,1,0:T(8,128)(2,1)S(1)}, bf16[2,8,3456]{2,1,0:T(8,128)(2,1)S(1)}, u32[]{:S(2)}, u32[]{:S(2)}) %collective-permute-start.15) | collective-permute-done | bytes 110624 | tf_op jit(solution)/shard_map/ppermute | solution.py:335
  62.6 0.0 collective-permute-done.13.refs_2_
  62.6 0.6 shard_map.78
  63.2 3.4 %collective-permute-start.18 = (bf16[8,3456]{1,0:T(8,128)(2,1)S(1)}, bf16[8,3456]{1,0:T(8,128)(2,1)S(1)}, u32[]{:S(2)}, u32[]{:S(2)}) collective-permute-start(bf16[8,3456]{1,0:T(8,128)(2,1)S(1)} %bitcast.29), channel_id=1, source_target_pairs={{0,24},{1,25},{2,26},{3,27},{4,28},{5,29},{6,30},{7,31},{8,16},{9,... | collective-permute-start | bytes 165896 | tf_op jit(solution)/shard_map/ppermute | solution.py:340
  66.6 0.5 collective-permute-start.17
  67.2 0.6 collective-permute-start.16
  67.8 0.0 collective-permute-done.19
  67.8 1.6 %collective-permute-start.20 = (bf16[16,3456]{1,0:T(8,128)(2,1)S(1)}, bf16[16,3456]{1,0:T(8,128)(2,1)S(1)}, u32[]{:S(2)}, u32[]{:S(2)}) collective-permute-start(bf16[16,3456]{1,0:T(8,128)(2,1)S(1)} %fusion), channel_id=1, source_target_pairs={{0,16},{1,17},{2,18},{3,19},{4,20},{5,21},{6,22},{7,23},{8,24},{9,... | collective-permute-start | bytes 331784 | tf_op jit(solution)/shard_map/ppermute | solution.py:340
  69.3 2.0 %collective-permute-done.16 = bf16[8,3456]{1,0:T(8,128)(2,1)S(1)} collective-permute-done((bf16[8,3456]{1,0:T(8,128)(2,1)S(1)}, bf16[8,3456]{1,0:T(8,128)(2,1)S(1)}, u32[]{:S(2)}, u32[]{:S(2)}) %collective-permute-start.16) | collective-permute-done | bytes 55328 | tf_op jit(solution)/shard_map/ppermute | solution.py:340
  71.4 0.0 collective-permute-done.18
  71.4 0.3 collective-permute-done.17
  71.7 0.7 add_add_fusion
  72.4 0.3 collective-permute-done.20
  72.6 0.7 convert_add_fusion
  (5 shorter events, 0.0 us)
Async XLA Ops:
  1.7 12.2 %collective-permute-start.1 = (bf16[1,16,64,128]{3,2,1,0:T(8,128)(2,1)S(1)}, bf16[1,16,64,128]{3,2,1,0:T(8,128)(2,1)S(1)}, u32[]{:S(2)}, u32[]{:S(2)}) collective-permute-start(bf16[1,16,64,128]{3,2,1,0:T(8,128)(2,1)S(1)} %get-tuple-element.79), channel_id=1, source_target_pairs={{1,2},{3,4},{5,6},{7,8},{9,10},{11,12},{13,14},{2,1},{4,3},{6,5},{... | collective-permute-start | bytes 786440 | tf_op jit(solution)/shard_map/ppermute | solution.py:41
  2.4 11.5 %collective-permute-start = (bf16[1,16,64,128]{3,2,1,0:T(8,128)(2,1)S(1)}, bf16[1,16,64,128]{3,2,1,0:T(8,128)(2,1)S(1)}, u32[]{:S(2)}, u32[]{:S(2)}) collective-permute-start(bf16[1,16,64,128]{3,2,1,0:T(8,128)(2,1)S(1)} %get-tuple-element.80), channel_id=1, source_target_pairs={{0,1},{1,0},{2,3},{3,2},{4,5},{5,4},{6,7},{7,6},{8,9},{9,8},{10,11... | collective-permute-start | bytes 786440 | tf_op jit(solution)/shard_map/ppermute | solution.py:41
  6.8 1.2 %copy-start.1 = (bf16[1,4,16,64,128]{4,3,2,1,0:T(8,128)(2,1)S(1)}, bf16[1,4,16,64,128]{4,3,2,1,0:T(8,128)(2,1)}, u32[]{:S(2)}) copy-start(bf16[1,4,16,64,128]{4,3,2,1,0:T(8,128)(2,1)} %param.4) | copy-start | bytes 3145732
  8.0 1.2 %copy-start.2 = (bf16[27,128,128]{2,1,0:T(8,128)(2,1)S(1)}, bf16[27,128,128]{2,1,0:T(8,128)(2,1)}, u32[]{:S(2)}) copy-start(bf16[27,128,128]{2,1,0:T(8,128)(2,1)} %param.5) | copy-start | bytes 2654212
  13.8 2.9 %copy-start = (bf16[27,128,256]{2,1,0:T(8,128)(2,1)S(1)}, bf16[27,128,256]{2,1,0:T(8,128)(2,1)}, u32[]{:S(2)}) copy-start(bf16[27,128,256]{2,1,0:T(8,128)(2,1)} %refs_3_.1) | copy-start | bytes 5308420
  13.9 3.8 %copy-start.3 = (bf16[1,2,8,32,256]{4,3,2,1,0:T(8,128)(2,1)S(1)}, bf16[1,2,8,32,256]{4,3,2,1,0:T(8,128)(2,1)}, u32[]{:S(2)}) copy-start(bf16[1,2,8,32,256]{4,3,2,1,0:T(8,128)(2,1)} %param.7) | copy-start | bytes 786436
  15.9 1.8 %collective-permute-start.2 = (bf16[1,8,32,128]{3,2,1,0:T(8,128)(2,1)S(1)}, bf16[1,8,32,128]{3,2,1,0:T(8,128)(2,1)S(1)}, u32[]{:S(2)}, u32[]{:S(2)}) collective-permute-start(bf16[1,8,32,128]{3,2,1,0:T(8,128)(2,1)S(1)} %get-tuple-element.44), channel_id=1, source_target_pairs={{0,1},{1,0},{2,3},{3,2},{4,5},{5,4},{6,7},{7,6},{8,9},{9,8},{10,11... | collective-permute-start | bytes 196616 | tf_op jit(solution)/shard_map/ppermute | solution.py:41
  16.0 1.7 %collective-permute-start.3 = (bf16[1,8,32,128]{3,2,1,0:T(8,128)(2,1)S(1)}, bf16[1,8,32,128]{3,2,1,0:T(8,128)(2,1)S(1)}, u32[]{:S(2)}, u32[]{:S(2)}) collective-permute-start(bf16[1,8,32,128]{3,2,1,0:T(8,128)(2,1)S(1)} %get-tuple-element.45), channel_id=1, source_target_pairs={{1,2},{3,4},{5,6},{7,8},{9,10},{11,12},{13,14},{2,1},{4,3},{6,5},{... | collective-permute-start | bytes 196616 | tf_op jit(solution)/shard_map/ppermute | solution.py:41
  21.7 6.7 %collective-permute-start.6 = (bf16[8,16,3456]{2,1,0:T(8,128)(2,1)S(1)}, bf16[8,16,3456]{2,1,0:T(8,128)(2,1)S(1)}, u32[]{:S(2)}, u32[]{:S(2)}) collective-permute-start(bf16[8,16,3456]{2,1,0:T(8,128)(2,1)S(1)} %get-tuple-element.54.refs_2_), channel_id=1, source_target_pairs={{0,1},{1,0},{2,3},{3,2},{4,5},{5,4},{6,7},{7,6},{8,9},{9,8},{10,11... | collective-permute-start | bytes 2654216 | tf_op jit(solution)/shard_map/ppermute | solution.py:335
  26.1 2.3 %collective-permute-start.4 = (bf16[1,8,32,256]{3,2,1,0:T(8,128)(2,1)S(1)}, bf16[1,8,32,256]{3,2,1,0:T(8,128)(2,1)S(1)}, u32[]{:S(2)}, u32[]{:S(2)}) collective-permute-start(bf16[1,8,32,256]{3,2,1,0:T(8,128)(2,1)S(1)} %get-tuple-element.49), channel_id=1, source_target_pairs={{0,1},{1,0},{2,3},{3,2},{4,5},{5,4},{6,7},{7,6},{8,9},{9,8},{10,11... | collective-permute-start | bytes 393224 | tf_op jit(solution)/shard_map/ppermute | solution.py:41
  26.2 2.2 %collective-permute-start.5 = (bf16[1,8,32,256]{3,2,1,0:T(8,128)(2,1)S(1)}, bf16[1,8,32,256]{3,2,1,0:T(8,128)(2,1)S(1)}, u32[]{:S(2)}, u32[]{:S(2)}) collective-permute-start(bf16[1,8,32,256]{3,2,1,0:T(8,128)(2,1)S(1)} %get-tuple-element.50), channel_id=1, source_target_pairs={{1,2},{3,4},{5,6},{7,8},{9,10},{11,12},{13,14},{2,1},{4,3},{6,5},{... | collective-permute-start | bytes 393224 | tf_op jit(solution)/shard_map/ppermute | solution.py:41
  32.6 14.6 %collective-permute-start.7 = (bf16[8,8,1152]{2,1,0:T(8,128)(2,1)S(1)}, bf16[8,8,1152]{2,1,0:T(8,128)(2,1)S(1)}, u32[]{:S(2)}, u32[]{:S(2)}) collective-permute-start(bf16[8,8,1152]{2,1,0:T(8,128)(2,1)S(1)} %get-tuple-element.62.refs_4_), channel_id=1, source_target_pairs={{0,1},{1,0},{2,3},{3,2},{4,5},{5,4},{6,7},{7,6},{8,9},{9,8},{10,11... | collective-permute-start | bytes 442376 | tf_op jit(solution)/shard_map/ppermute | solution.py:335
  37.5 11.2 %collective-permute-start.11 = (bf16[2,16,3456]{2,1,0:T(8,128)(2,1)S(1)}, bf16[2,16,3456]{2,1,0:T(8,128)(2,1)S(1)}, u32[]{:S(2)}, u32[]{:S(2)}) collective-permute-start(bf16[2,16,3456]{2,1,0:T(8,128)(2,1)S(1)} %get-tuple-element.68), channel_id=1, source_target_pairs={{0,4},{1,5},{2,6},{3,7},{4,0},{5,1},{6,2},{7,3},{8,12},{9,13},{10,... | collective-permute-start | bytes 663560 | tf_op jit(solution)/shard_map/ppermute | solution.py:335
  40.8 11.3 %collective-permute-start.12 = (bf16[2,16,3456]{2,1,0:T(8,128)(2,1)S(1)}, bf16[2,16,3456]{2,1,0:T(8,128)(2,1)S(1)}, u32[]{:S(2)}, u32[]{:S(2)}) collective-permute-start(bf16[2,16,3456]{2,1,0:T(8,128)(2,1)S(1)} %get-tuple-element.69), channel_id=1, source_target_pairs={{0,6},{1,7},{2,4},{3,5},{4,2},{5,3},{6,0},{7,1},{8,14},{9,15},{10,... | collective-permute-start | bytes 663560 | tf_op jit(solution)/shard_map/ppermute | solution.py:335
  41.9 11.6 %collective-permute-start.10 = (bf16[2,16,3456]{2,1,0:T(8,128)(2,1)S(1)}, bf16[2,16,3456]{2,1,0:T(8,128)(2,1)S(1)}, u32[]{:S(2)}, u32[]{:S(2)}) collective-permute-start(bf16[2,16,3456]{2,1,0:T(8,128)(2,1)S(1)} %get-tuple-element.60.refs_9_), channel_id=1, source_target_pairs={{0,2},{1,3},{2,0},{3,1},{4,6},{5,7},{6,4},{7,5},{8,10},{9,11},{10,... | collective-permute-start | bytes 663560 | tf_op jit(solution)/shard_map/ppermute | solution.py:335
  47.1 1.4 %collective-permute-start.9 = (bf16[8,8,1152]{2,1,0:T(8,128)(2,1)S(1)}, bf16[8,8,1152]{2,1,0:T(8,128)(2,1)S(1)}, u32[]{:S(2)}, u32[]{:S(2)}) collective-permute-start(bf16[8,8,1152]{2,1,0:T(8,128)(2,1)S(1)} %get-tuple-element.67), channel_id=1, source_target_pairs={{0,1},{1,0},{2,3},{3,2},{4,5},{5,4},{6,7},{7,6},{8,9},{9,8},{10,11... | collective-permute-start | bytes 442376 | tf_op jit(solution)/shard_map/ppermute | solution.py:335
  47.2 1.6 %collective-permute-start.8 = (bf16[8,8,1152]{2,1,0:T(8,128)(2,1)S(1)}, bf16[8,8,1152]{2,1,0:T(8,128)(2,1)S(1)}, u32[]{:S(2)}, u32[]{:S(2)}) collective-permute-start(bf16[8,8,1152]{2,1,0:T(8,128)(2,1)S(1)} %get-tuple-element.65.refs_4_), channel_id=1, source_target_pairs={{0,1},{1,0},{2,3},{3,2},{4,5},{5,4},{6,7},{7,6},{8,9},{9,8},{10,11... | collective-permute-start | bytes 442376 | tf_op jit(solution)/shard_map/ppermute | solution.py:335
  54.1 6.9 %collective-permute-start.14 = (bf16[2,8,3456]{2,1,0:T(8,128)(2,1)S(1)}, bf16[2,8,3456]{2,1,0:T(8,128)(2,1)S(1)}, u32[]{:S(2)}, u32[]{:S(2)}) collective-permute-start(bf16[2,8,3456]{2,1,0:T(8,128)(2,1)S(1)} %get-tuple-element.72), channel_id=1, source_target_pairs={{0,4},{1,5},{2,6},{3,7},{4,0},{5,1},{6,2},{7,3},{8,12},{9,13},{10,... | collective-permute-start | bytes 331784 | tf_op jit(solution)/shard_map/ppermute | solution.py:335
  55.8 6.8 %collective-permute-start.15 = (bf16[2,8,3456]{2,1,0:T(8,128)(2,1)S(1)}, bf16[2,8,3456]{2,1,0:T(8,128)(2,1)S(1)}, u32[]{:S(2)}, u32[]{:S(2)}) collective-permute-start(bf16[2,8,3456]{2,1,0:T(8,128)(2,1)S(1)} %get-tuple-element.73), channel_id=1, source_target_pairs={{0,6},{1,7},{2,4},{3,5},{4,2},{5,3},{6,0},{7,1},{8,14},{9,15},{10,... | collective-permute-start | bytes 331784 | tf_op jit(solution)/shard_map/ppermute | solution.py:335
  56.4 6.2 %collective-permute-start.13 = (bf16[2,8,3456]{2,1,0:T(8,128)(2,1)S(1)}, bf16[2,8,3456]{2,1,0:T(8,128)(2,1)S(1)}, u32[]{:S(2)}, u32[]{:S(2)}) collective-permute-start(bf16[2,8,3456]{2,1,0:T(8,128)(2,1)S(1)} %get-tuple-element.71.refs_5_), channel_id=1, source_target_pairs={{0,2},{1,3},{2,0},{3,1},{4,6},{5,7},{6,4},{7,5},{8,10},{9,11},{10,... | collective-permute-start | bytes 331784 | tf_op jit(solution)/shard_map/ppermute | solution.py:335
  58.4 9.4 %collective-permute-start.19 = (bf16[16,3456]{1,0:T(8,128)(2,1)S(1)}, bf16[16,3456]{1,0:T(8,128)(2,1)S(1)}, u32[]{:S(2)}, u32[]{:S(2)}) collective-permute-start(bf16[16,3456]{1,0:T(8,128)(2,1)S(1)} %bitcast.28), channel_id=1, source_target_pairs={{0,8},{1,9},{2,10},{3,11},{4,12},{5,13},{6,14},{7,15},{8,0},{9,1},... | collective-permute-start | bytes 331784 | tf_op jit(solution)/shard_map/ppermute | solution.py:335
  63.2 8.2 %collective-permute-start.18 = (bf16[8,3456]{1,0:T(8,128)(2,1)S(1)}, bf16[8,3456]{1,0:T(8,128)(2,1)S(1)}, u32[]{:S(2)}, u32[]{:S(2)}) collective-permute-start(bf16[8,3456]{1,0:T(8,128)(2,1)S(1)} %bitcast.29), channel_id=1, source_target_pairs={{0,24},{1,25},{2,26},{3,27},{4,28},{5,29},{6,30},{7,31},{8,16},{9,... | collective-permute-start | bytes 165896 | tf_op jit(solution)/shard_map/ppermute | solution.py:340
  66.6 5.1 %collective-permute-start.17 = (bf16[8,3456]{1,0:T(8,128)(2,1)S(1)}, bf16[8,3456]{1,0:T(8,128)(2,1)S(1)}, u32[]{:S(2)}, u32[]{:S(2)}) collective-permute-start(bf16[8,3456]{1,0:T(8,128)(2,1)S(1)} %bitcast.30), channel_id=1, source_target_pairs={{0,8},{1,9},{2,10},{3,11},{4,12},{5,13},{6,14},{7,15},{8,0},{9,1},... | collective-permute-start | bytes 165896 | tf_op jit(solution)/shard_map/ppermute | solution.py:335
  67.2 4.2 %collective-permute-start.16 = (bf16[8,3456]{1,0:T(8,128)(2,1)S(1)}, bf16[8,3456]{1,0:T(8,128)(2,1)S(1)}, u32[]{:S(2)}, u32[]{:S(2)}) collective-permute-start(bf16[8,3456]{1,0:T(8,128)(2,1)S(1)} %convert_bitcast_fusion), channel_id=1, source_target_pairs={{0,16},{1,17},{2,18},{3,19},{4,20},{5,21},{6,22},{7,23},{8,24},{9,... | collective-permute-start | bytes 165896 | tf_op jit(solution)/shard_map/ppermute | solution.py:340
  67.8 4.8 %collective-permute-start.20 = (bf16[16,3456]{1,0:T(8,128)(2,1)S(1)}, bf16[16,3456]{1,0:T(8,128)(2,1)S(1)}, u32[]{:S(2)}, u32[]{:S(2)}) collective-permute-start(bf16[16,3456]{1,0:T(8,128)(2,1)S(1)} %fusion), channel_id=1, source_target_pairs={{0,16},{1,17},{2,18},{3,19},{4,20},{5,21},{6,22},{7,23},{8,24},{9,... | collective-permute-start | bytes 331784 | tf_op jit(solution)/shard_map/ppermute | solution.py:340

commit v4 on v3

--- a/solution.py
+++ b/solution.py
@@ -10,6 +10,8 @@
 F32 = jnp.float32
 BF16 = jnp.bfloat16
 COST = 64
+FETCH = 60
+PARTS = (range(0, 2), range(2, 6), range(6, 9))
 VMEM = pl.BlockSpec(memory_space=pltpu.VMEM)
 SMEM = pl.BlockSpec(memory_space=pltpu.SMEM)
 
@@ -54,14 +56,7 @@
 
 
 def facing(place, edge, from_pair, from_next):
-    return jnp.where(place[0] != edge, from_pair.astype(F32), from_next.astype(F32))
-
-
-def send_planes(place, first, last, to_pair, to_next):
-    even = place[0] == 0
-    first, last = (first.astype(F32), last.astype(F32))
-    to_pair[0] = jnp.where(even, last, first).astype(BF16)
-    to_next[0] = jnp.where(even, first, last).astype(BF16)
+    return jnp.where(place[0] % 2 != edge, from_pair.astype(F32), from_next.astype(F32))
 
 
 def dot(left, right):
@@ -114,6 +109,22 @@
     act = (pre * sig).astype(BF16).astype(F32)
     slope = silu_slope(pre, sig).astype(BF16).reshape(half, depth, 2 * chan)
     return (act[:, :chan] + act[:, chan:]).reshape(half, depth, chan), slope
+
+
+def side_planes(place, volume, cotangent, to_pair, to_next, sems):
+    planes, rows, _, chan = volume.shape
+    cp, cy = cotangent.shape[:2]
+    copies = []
+    for to, side in ((to_pair, 1 - place[0] % 2), (to_next, place[0] % 2)):
+        copies.append((volume.at[side * (planes - 1)], to.at[pl.ds(0, rows)]))
+        for k in range(cotangent.shape[3] // chan):
+            part = cotangent.at[side * (cp - 1), :, :, pl.ds(k * chan, chan)]
+            copies.append((part, to.at[pl.ds(rows + k * cy, cy)]))
+    copies = [pltpu.make_async_copy(*pair, sems.at[k]) for k, pair in enumerate(copies)]
+    for copy in copies:
+        copy.start()
+    for copy in copies:
+        copy.wait()
 
 
 def fine_inner(own, kernel, wide6, weights, edge, act, slope):
@@ -151,20 +162,19 @@
 ):
     half, fz = act.shape[1:3]
     coarse = pooled.shape[0]
-    ends = []
     for e in range(2):
         fill_wide6(
             halo6,
             e,
-            lambda y: facing(place, e, from_pair[0, y : y + 1], from_next[0, y : y + 1]),
+            lambda y: facing(
+                place,
+                e,
+                from_pair[2 * y : 2 * y + 2].reshape(1, fz, -1),
+                from_next[2 * y : 2 * y + 2].reshape(1, fz, -1),
+            ),
         )
         total, slope[e] = fine_finish(edge[e] + fine_conv(halo6, e, weights, 2 * e), half, fz)
-        if coarse == 1:
-            ends.append(total)
-            continue
         sums[e] = total + act[0 if e == 0 else 2 * coarse - 3]
-    if coarse == 1:
-        sums[0] = ends[0] + ends[1]
     for pair in range(1, coarse - 1):
         sums[1 + pair] = act[2 * pair - 1] + act[2 * pair]
     for pair in range(coarse):
@@ -172,41 +182,60 @@
         even = sums[at, :, pl.ds(0, fz // 2, stride=2), :]
         odd = sums[at, :, pl.ds(1, fz // 2, stride=2), :]
         pooled[pair] = ((even + odd) * 0.125).astype(BF16)
-    send_planes(place, pooled[0], pooled[coarse - 1], to_pair, to_next)
+    last = coarse - 2
+    for to, side in ((to_pair, 1 - place[0] % 2), (to_next, place[0] % 2)):
+        for k in range(2):
+            to[k] = pooled[side * last + k]
+
+
+def coarse_conv(wide3, plane, kernel, a, total):
+    cy, cz, span = (wide3.shape[1] - 2, wide3.shape[2], wide3.shape[3])
+    rows = [wide3[plane, b : b + cy].reshape(cy * cz, span) for b in range(3)]
+    return plus(total, dot(jnp.concatenate(rows, axis=1), kernel[a]))
 
 
 def coarse_inner(own, kernel, wide3, pre):
-    planes, cy, cz, chan = own.shape
+    planes = own.shape[0]
     for p in range(planes):
         fill_wide3(wide3, p, own[p].astype(F32))
-    for p in range(planes):
+    for p in range(-1, planes + 1):
         total = None
         for a in range(3):
             if 0 <= p + a - 1 < planes:
-                for b in range(3):
-                    rows = wide3[p + a - 1, b : b + cy].reshape(cy * cz, 3 * chan)
-                    total = plus(total, dot(rows, kernel[3 * a + b]))
-        pre[p] = total
+                total = coarse_conv(wide3, p + a - 1, kernel, a, total)
+        pre[p + 1] = total
 
 
 def coarse_outer(
-    place, from_pair, from_next, kernel, pre, cotangent, halo3, out, delta, to_pair, to_next
+    place, from_pair, from_next, kernel, pre, cotangent, side_pair, side_next, halo3, out, delta
 ):
     planes, cy, cz, wide = cotangent.shape
+    chan = from_pair.shape[-1]
+    rows = side_pair.shape[0] - wide // chan * cy
     for e in range(2):
-        fill_wide3(halo3, e, facing(place, e, from_pair[0], from_next[0]))
-    for p in range(planes):
-        total = pre[p]
-        for e in range(2):
-            if p == e * (planes - 1):
-                for b in range(3):
-                    rows = halo3[e, b : b + cy].reshape(cy * cz, halo3.shape[-1])
-                    total = total + dot(rows, kernel[6 * e + b])
+        for k in range(2):
+            fill_wide3(halo3, 2 * e + k, facing(place, e, from_pair[k], from_next[k]))
+    for p in range(-1, planes + 1):
+        total = pre[p + 1]
+        for a in range(3):
+            at = p + a - 1
+            if at < 0:
+                total = coarse_conv(halo3, at + 2, kernel, a, total)
+            elif at >= planes:
+                total = coarse_conv(halo3, at - planes + 2, kernel, a, total)
         sig = jax.nn.sigmoid(total)
-        out[p] = (total * sig).astype(BF16).reshape(cy, cz, wide)
-        grad = cotangent[p].reshape(cy * cz, wide).astype(F32) * silu_slope(total, sig)
-        delta[p] = grad.astype(BF16).reshape(cy, cz, wide)
-    send_planes(place, delta[0], delta[planes - 1], to_pair, to_next)
+        if 0 <= p < planes:
+            out[p] = (total * sig).astype(BF16).reshape(cy, cz, wide)
+            grad = cotangent[p].reshape(cy * cz, wide).astype(F32)
+        else:
+            e = int(p >= planes)
+            parts = []
+            for k in range(wide // chan):
+                lines = pl.ds(rows + k * cy, cy)
+                parts.append(facing(place, e, side_pair[lines], side_next[lines]))
+            grad = jnp.concatenate(parts, axis=-1).reshape(cy * cz, wide)
+        grad = grad * silu_slope(total, sig)
+        delta[p + 1] = grad.astype(BF16).reshape(cy, cz, wide)
 
 
 def source(own, halo, plane):
@@ -222,7 +251,7 @@
     if send is None:
         keep[:, columns] = term.astype(BF16)
         return
-    here = place[0] == 0
+    here = place[0] % 2 == 0
     rows = term.shape[0] // (2 * len(orders))
     for at, owner in enumerate(orders):
         low = term[owner * rows : (owner + 1) * rows]
@@ -231,60 +260,48 @@
         send[at, :, columns] = jnp.where(here, high, low).astype(BF16)
 
 
+def in_twos(taps):
+    return [taps[k : k + 2] for k in range(0, len(taps), 2)]
+
+
 def coarse_terms(place, wide3, halo3, delta, keep, send=None, *, order):
     planes, cy, cz, wide = delta.shape
+    own = wide3.shape[0]
     span = wide3.shape[-1]
-    for tap in range(9):
-        a, b = (tap // 3, tap % 3)
+
+    def piece(p, tap):
+        at = p + tap // 3 - 1
+        ref = wide3 if 0 <= at < own else halo3
+        at = at if 0 <= at < own else (1 if at < 0 else 2)
+        return ref[at, tap % 3 : tap % 3 + cy].reshape(cy * cz, span)
+
+    for group in in_twos(range(9)):
         total = None
-        for p in range(planes):
-            ref, at = source(wide3, halo3, p + a - 1)
-            piece = ref[at, b : b + cy].reshape(cy * cz, span)
-            total = plus(total, tap_dot(delta[p].reshape(cy * cz, wide), piece))
-        put_term(total, tap * span, place, order, keep, send)
-
-
-def backward_taps(wide3, plane, kernel, a, grad):
-    cy, cz = (wide3.shape[1] - 2, wide3.shape[2])
-    wide = kernel.shape[2]
-    for b in range(3):
-        for c in range(3):
-            rows = wide3[plane, b : b + cy, :, c * wide : (c + 1) * wide]
-            term = lax.dot_general(
-                rows.reshape(cy * cz, wide),
-                kernel[26 - (9 * a + 3 * b + c)],
-                (((1,), (1,)), ((), ())),
-                preferred_element_type=F32,
-            )
-            grad = plus(grad, term)
-    return grad
-
-
-def coarse_backward(delta, kernel, partial, wide3):
-    planes = delta.shape[0]
+        for p in range(own):
+            pieces = jnp.concatenate([piece(p, tap) for tap in group], axis=1)
+            total = plus(total, tap_dot(delta[p + 1].reshape(cy * cz, wide), pieces))
+        put_term(total, group[0] * span, place, order, keep, send)
+
+
+def fine_deltas(coarse_delta, kernel, slope, slope_edge, delta, wide3, spread):
+    planes, cy, cz, wide = coarse_delta.shape
+    chan = kernel.shape[1]
     for p in range(planes):
-        fill_wide3(wide3, p, delta[p].astype(F32))
-    for p in range(planes):
-        grad = None
-        for a in range(3):
-            if 0 <= p + a - 1 < planes:
-                grad = backward_taps(wide3, p + a - 1, kernel, a, grad)
-        partial[p] = grad
-
-
-def fine_deltas(
-    place, from_pair, from_next, kernel, partial, slope, slope_edge, delta, halo3, spread
-):
-    planes, rows, chan = partial.shape
-    cy, fz = spread.shape[:2]
-    cz = fz // 2
-    for e in range(2):
-        fill_wide3(halo3, e, facing(place, e, from_pair[0], from_next[0]))
-    for p in range(planes):
-        grad = partial[p]
-        for e in range(2):
-            if p == e * (planes - 1):
-                grad = backward_taps(halo3, e, kernel, 2 * e, grad)
+        fill_wide3(wide3, p, coarse_delta[p].astype(F32))
+    grads = None
+    for a in range(3):
+        for b in range(3):
+            for c in range(3):
+                rows = wide3[a : a + planes - 2, b : b + cy, :, c * wide : (c + 1) * wide]
+                term = lax.dot_general(
+                    rows.reshape((planes - 2) * cy * cz, wide),
+                    kernel[26 - (9 * a + 3 * b + c)],
+                    (((1,), (1,)), ((), ())),
+                    preferred_element_type=F32,
+                )
+                grads = plus(grads, term)
+    for p in range(planes - 2):
+        grad = grads[p * cy * cz : (p + 1) * cy * cz]
         grad = grad.astype(BF16).astype(F32).reshape(cy, cz, chan) * 0.125
         spread[:, pl.ds(0, cz, stride=2), :] = grad
         spread[:, pl.ds(1, cz, stride=2), :] = grad
@@ -295,39 +312,25 @@
             delta[at] = (both * ref[index].astype(F32)).astype(BF16)
 
 
-def fine_part(place, wide6, halo6, delta, keep, send, order, taps):
+def fine_terms(place, wide6, halo6, delta, keep, send=None, *, order, taps):
     planes, half, fz, double = delta.shape
     chan = double // 2
     three = 3 * chan
-    for tap in taps:
-        a, b = (tap // 3, tap % 3)
+
+    def piece(p, q, tap):
+        ref, at = source(wide6, halo6, p + tap // 3 - 1)
+        pair, parity = ((q + tap % 3) // 2, (q + tap % 3) % 2)
+        some = ref[at, pair : pair + half, :, parity * three : (parity + 1) * three]
+        return some.reshape(half * fz, three)
+
+    for group in in_twos(taps):
         total = None
         for p in range(planes):
-            ref, at = source(wide6, halo6, p + a - 1)
             for q in range(2):
-                pair, parity = ((q + b) // 2, (q + b) % 2)
                 rows = delta[p, :, :, q * chan : (q + 1) * chan].reshape(half * fz, chan)
-                piece = ref[at, pair : pair + half, :, parity * three : (parity + 1) * three]
-                total = plus(total, tap_dot(rows, piece.reshape(half * fz, three)))
-        put_term(total, (tap - taps[0]) * three, place, order, keep, send)
-
-
-def fine_first(
-    place, from_pair, from_next, kernel, partial, slope, slope_edge, wide6, halo6, *rest, order, taps
-):
-    if len(rest) == 5:
-        delta, keep, send, halo3, spread = rest
-    else:
-        delta, keep, halo3, spread = rest
-        send = None
-    fine_deltas(
-        place, from_pair, from_next, kernel, partial, slope, slope_edge, delta, halo3, spread
-    )
-    fine_part(place, wide6, halo6, delta, keep, send, order, taps)
-
-
-def fine_second(place, wide6, halo6, delta, keep, send=None, *, order, taps):
-    fine_part(place, wide6, halo6, delta, keep, send, order, taps)
+                pieces = jnp.concatenate([piece(p, q, tap) for tap in group], axis=1)
+                total = plus(total, tap_dot(rows, pieces))
+        put_term(total, (group[0] - taps[0]) * three, place, order, keep, send)
 
 
 def swap(value, bit):
@@ -398,7 +401,7 @@
         for mask, out in zip(masks_of(group), outs):
             at = 0
             for bit in group:
-                mine = place[bit.bit_length() - 1]
+                mine = place[0] // bit % 2
                 at = 2 * at + (1 - mine if mask & bit else mine)
             for k in range(span):
                 total = None
@@ -455,7 +458,7 @@
     count = lax.axis_size("space")
     me = lax.axis_index("space")
     parity = me % 2
-    place = jnp.stack([me >> k & 1 for k in range(count.bit_length() - 1)]).astype(jnp.int32)
+    place = jnp.reshape(me, (1,)).astype(jnp.int32)
     x = volumes[0]
     cells, few = (planes * fy * fz, cp * cy * cz)
     fine_flops, coarse_flops = (54 * cells * chan * chan, 54 * few * chan * wide)
@@ -463,9 +466,18 @@
     def shape(*extents, kind=BF16):
         return jax.ShapeDtypeStruct(extents, kind)
 
-    to_pair = lax.dynamic_slice_in_dim(x, (1 - parity) * (planes - 1), 1, axis=0)
-    to_next = lax.dynamic_slice_in_dim(x, parity * (planes - 1), 1, axis=0)
-    from_pair, from_next = exchange(to_pair, to_next)
+    lines = 2 * fy + wide // chan * cy
+    anywhere = pl.BlockSpec(memory_space=pl.ANY)
+    to_pair, to_next = pl.pallas_call(
+        side_planes,
+        out_shape=[shape(lines, cz, chan)] * 2,
+        in_specs=[SMEM, anywhere, anywhere],
+        out_specs=[anywhere] * 2,
+        scratch_shapes=[pltpu.SemaphoreType.DMA((2 + 2 * (wide // chan),))],
+        cost_estimate=pl.CostEstimate(flops=fine_flops, bytes_accessed=2**20, transcendentals=0),
+        compiler_params=pltpu.CompilerParams(vmem_limit_bytes=FETCH * 2**20),
+    )(place, x.reshape(planes, 2 * fy, cz, chan), cotangent[0])
+    side_pair, side_next = exchange(to_pair, to_next)
     mid = max(planes - 2, 1)
     wide6, weights, edge, act, slope = kernel_call(
         fine_inner,
@@ -483,13 +495,13 @@
     )
     halo6, pooled, slope_edge, to_pair, to_next = kernel_call(
         fine_outer,
-        [place, from_pair, from_next, weights, edge, act],
+        [place, side_pair, side_next, weights, edge, act],
         [
             shape(2, half + 1, fz, 6 * chan),
             shape(cp, cy, cz, chan),
             shape(2, half, fz, 2 * chan),
-            shape(1, cy, cz, chan),
-            shape(1, cy, cz, chan),
+            shape(2, cy, cz, chan),
+            shape(2, cy, cz, chan),
         ],
         [pltpu.VMEM((max(cp, 2), half, fz, chan), F32)],
         fine_flops // 6,
@@ -497,31 +509,28 @@
         scalars=1,
     )
     from_pair, from_next = exchange(to_pair, to_next)
-    taps = coarse_kernel.reshape(9, 3 * chan, wide)
+    taps = coarse_kernel.reshape(3, 9 * chan, wide)
     wide3, pre = kernel_call(
         coarse_inner,
         [pooled, taps],
-        [shape(cp, cy + 2, cz, 3 * chan), shape(cp, cy * cz, wide, kind=F32)],
+        [shape(cp, cy + 2, cz, 3 * chan), shape(cp + 2, cy * cz, wide, kind=F32)],
         [],
         coarse_flops,
         16,
     )
-    halo3, out, coarse_delta, to_pair, to_next = kernel_call(
+    halo3, out, coarse_delta = kernel_call(
         coarse_outer,
-        [place, from_pair, from_next, taps, pre, cotangent[0]],
+        [place, from_pair, from_next, taps, pre, cotangent[0], side_pair, side_next],
         [
-            shape(2, cy + 2, cz, 3 * chan),
+            shape(4, cy + 2, cz, 3 * chan),
             shape(cp, cy, cz, wide),
-            shape(cp, cy, cz, wide),
-            shape(1, cy, cz, wide),
-            shape(1, cy, cz, wide),
+            shape(cp + 2, cy, cz, wide),
         ],
         [],
-        coarse_flops // 3,
+        coarse_flops,
         16,
         scalars=1,
     )
-    from_pair, from_next = exchange(to_pair, to_next)
     order = owners_in_order(count)
     steps = exchange_groups(count) + [[count // 2]]
     terms = kernel_call(
@@ -534,43 +543,32 @@
         scalars=1,
     )
     keep, send = sided(terms, count)
-    early, coarse_kept = fold(
-        place, [[keep, swap(send, 1)]], steps[0], [from_pair, from_next]
-    )
-    (partial,) = kernel_call(
-        coarse_backward,
-        [coarse_delta, coarse_kernel],
-        [shape(cp, cy * cz, chan, kind=F32)],
-        [pltpu.VMEM((cp, cy + 2, cz, 3 * wide), BF16)],
+    early, coarse_kept = fold(place, [[keep, swap(send, 1)]], steps[0])
+    (fine_delta,) = kernel_call(
+        fine_deltas,
+        [coarse_delta, coarse_kernel, slope, slope_edge],
+        [shape(planes, half, fz, 2 * chan)],
+        [pltpu.VMEM((cp + 2, cy + 2, cz, 3 * wide), BF16), pltpu.VMEM((cy, fz, chan), F32)],
         coarse_flops,
         16,
         after=[terms[-1]],
     )
-    parts = [range(0, 3), range(3, 6), range(6, 9)]
-    fine_delta, *first = kernel_call(
-        functools.partial(fine_first, order=order, taps=parts[0]),
-        [place, from_pair, from_next, coarse_kernel, partial, slope, slope_edge, wide6, halo6],
-        [shape(planes, half, fz, 2 * chan)] + term_shapes(chan, 9 * chan, count),
-        [pltpu.VMEM((2, cy + 2, cz, 3 * wide), BF16), pltpu.VMEM((cy, fz, chan), F32)],
-        fine_flops * 2 // 3,
-        16,
-        scalars=1,
-        after=list(early.values())[:1],
-    )
-    fine_parts = [first]
-    for part in parts[1:]:
+    fine_parts = []
+    before = list(early.values())[:1]
+    for part in PARTS:
         fine_parts.append(
             kernel_call(
-                functools.partial(fine_second, order=order, taps=part),
+                functools.partial(fine_terms, order=order, taps=part),
                 [place, wide6, halo6, fine_delta],
-                term_shapes(chan, 9 * chan, count),
+                term_shapes(chan, len(part) * 3 * chan, count),
                 [],
                 fine_flops // 3,
                 16,
                 scalars=1,
-                after=[fine_parts[-1][-1]],
+                after=before,
             )
         )
+        before = [fine_parts[-1][-1]]
     got = received(early, coarse_kept)
     pieces = []
     for part in fine_parts:

time: 73.6 us -> 90.3 us (1.23)
  Pallas kernels: 23.8 us -> 42.3 us
  local copies, waits for them, and re-layouts: 3.47 us -> 0.02 us
  waiting for transfers between devices: 10.1 us -> 11.8 us
    pallas_call x0 -> x1, Pallas kernels: none -> 25 us  [shards(): pl.pallas_call(side_planes, out_shape=[shape(lines, cz, chan)] * 2, in_sp...]
    pallas_call x13, Pallas kernels: 23.8 us -> 17.3 us  [kernel_call(): pl.pallas_call(inner, out_shape=outs, in_specs=specs, out_specs=[VMEM] *...]
    ppermute x3 -> x2, starting transfers between devices: 4.55 us -> 9.04 us  [exchange(): lax.ppermute(to_pair, 'space', pair)]
    ppermute x12, starting transfers between devices: 21.4 us -> 17.4 us  [swap(): return lax.ppermute(value, 'space', [(i, i ^ bit) for i in range(count)])]
    unnamed x8, local copies, waits for them, and re-layouts: 2.4 us -> 0.02 us
    ppermute x12, waiting for transfers between devices: 7.75 us -> 9.74 us  [swap(): return lax.ppermute(value, 'space', [(i, i ^ bit) for i in range(count)])]
    dynamic_slice x1 -> x0, local copies, waits for them, and re-layouts: 1.07 us -> none  [shards(): to_next = lax.dynamic_slice_in_dim(x, parity * (planes - 1), 1, axis=0)]
    ppermute x3 -> x2, starting transfers between devices: 2.17 us -> 1.51 us  [exchange(): lax.ppermute(to_next, 'space', across)]
  transfers between devices with their start and end apart: 21 -> 19, of which waited for: 8 -> 7; matrix products, arithmetic and copies ran while one was open for 1% -> 1% of each run, Pallas kernels for 18% -> 13%
where the time goes in v4:
time: 90.3 us; the launch traced here: 90.2 us
  Pallas kernels  42.3 us (47%)
  starting transfers between devices  33.8 us (37%)
  waiting for transfers between devices  11.8 us (13%)
  other arithmetic  1.43 us (2%)
    pallas_call x1, Pallas kernels, shards(): pl.pallas_call(side_planes, out_shape=[shape(lines, cz, chan)] * 2, in_sp...  25 us
    ppermute x12, starting transfers between devices, swap(): return lax.ppermute(value, 'space', [(i, i ^ bit) for i in range(count)])  17.4 us
    pallas_call x13, Pallas kernels, kernel_call(): pl.pallas_call(inner, out_shape=outs, in_specs=specs, out_specs=[VMEM] *...  17.3 us
    ppermute x12, waiting for transfers between devices, swap(): return lax.ppermute(value, 'space', [(i, i ^ bit) for i in range(count)])  9.74 us
    ppermute x2, starting transfers between devices, exchange(): lax.ppermute(to_pair, 'space', pair)  9.04 us
    ppermute x3, starting transfers between devices, swap_sample(): lax.ppermute(value, ('sample', 'space'), [(s * count + i, (1 - s) * count...  5.83 us
    ppermute x3, waiting for transfers between devices, swap_sample(): lax.ppermute(value, ('sample', 'space'), [(s * count + i, (1 - s) * count...  2.03 us
  transfers between devices with their start and end apart: 19, of which 7 were waited for; matrix products, arithmetic and copies ran while one was open for 1% of the time, Pallas kernels for 13%

profile of v4, /device:TPU:0, one launch (start us, length us, event | category | flops | bytes accessed | tf_op | source)
XLA Modules:
  0.0 90.2 jit_solution(5513943467283207913)
XLA Ops:
  0.6 0.0 copy-start.1
  0.6 0.0 copy-start.2
  0.7 25.0 %shard_map.67 = (bf16[48,32,128]{2,1,0:T(8,128)(2,1)}, bf16[48,32,128]{2,1,0:T(8,128)(2,1)}) custom-call(s32[1]{0:T(128)} %bitcast.place.refs_0_, bf16[4,32,32,128]{3,2,1,0:T(8,128)(2,1)} %bitcast.19, bf16[2,8,32,256]{3,2,1,0:T(8,128)(2,1)} %bitcast.22), custom_call_target="tpu_custom_call" | custom-call | flops 3623878656 | bytes 1048576 | tf_op jit(solution)/shard_map/pallas_call | solution.py:471
  25.6 0.5 collective-permute-start
  26.2 0.7 collective-permute-start.1
  26.8 0.0 copy-done.1
  26.9 0.0 copy-done.2
  26.9 4.6 %shard_map.68 = (bf16[4,9,64,768]{3,2,1,0:T(8,128)(2,1)S(1)}, bf16[3,2,768,256]{3,2,1,0:T(8,128)(2,1)S(1)}, f32[2,512,256]{2,1,0:T(8,128)S(1)}, f32[2,8,64,128]{3,2,1,0:T(8,128)S(1)}, bf16[2,8,64,256]{3,2,1,0:T(8,128)(2,1)S(1)}) custom-call(bf16[4,16,64,128]{3,2,1,0:T(8,128)(2,1)S(1)} %bitcast.20, bf16[9,384,128]{2,1,0:T(8,128)(2,1)S(1)} %bitcast.21), custom_call_target="tpu_custom_call" | custom-call | flops 56623104 | bytes 1048576 | tf_op jit(solution)/shard_map/pallas_call | solution.py:27
  31.5 0.0 collective-permute-done.refs_1_.refs_6_
  31.5 0.0 collective-permute-done.1.refs_2_.refs_7_
  31.5 0.0 copy-start
  31.5 0.0 copy-start.3
  31.5 1.5 %shard_map.69 = (bf16[2,9,64,768]{3,2,1,0:T(8,128)(2,1)S(1)}, bf16[2,8,32,128]{3,2,1,0:T(8,128)(2,1)S(1)}, bf16[2,8,64,256]{3,2,1,0:T(8,128)(2,1)S(1)}, bf16[2,8...) custom-call(s32[1]{0:T(128)} %bitcast.place.refs_0_, ...), custom_call_target="tpu_custom_call" | custom-call | flops 9437184 | bytes 1048576 | tf_op jit(solution)/shard_map/pallas_call | solution.py:27
  33.0 8.5 %collective-permute-start.2 = (bf16[2,8,32,128]{3,2,1,0:T(8,128)(2,1)S(1)}, bf16[2,8,32,128]{3,2,1,0:T(8,128)(2,1)S(1)}, u32[]{:S(2)}, u32[]{:S(2)}) collective-permute-start(bf16[2,8,32,128]{3,2,1,0:T(8,128)(2,1)S(1)} %get-tuple-element.45), channel_id=1, source_target_pairs={{0,1},{1,0},{2,3},{3,2},{4,5},{5,4},{6,7},{7,6},{8,9},{9,8},{10,11... | collective-permute-start | bytes 393224 | tf_op jit(solution)/shard_map/ppermute | solution.py:43
  41.5 0.8 collective-permute-start.3
  42.3 0.0 copy-done
  42.3 1.2 %shard_map.70 = (bf16[2,10,32,384]{3,2,1,0:T(8,128)(2,1)S(1)}, f32[4,256,256]{2,1,0:T(8,128)S(1)}) custom-call(bf16[2,8,32,128]{3,2,1,0:T(8,128)(2,1)S(1)} %get-tuple-element.47.refs_0_, bf16[3,1152,256]{2,1,0:T(8,128)(2,1)S(1)} %bitcast.17), custom_call_target="tpu_custom_call" | custom-call | flops 14155776 | bytes 1048576 | tf_op jit(solution)/shard_map/pallas_call | solution.py:27
  43.5 0.0 collective-permute-done.2.refs_1_
  43.5 0.0 collective-permute-done.3.refs_2_
  43.6 0.0 copy-done.3
  43.6 1.9 %shard_map.71 = (bf16[4,10,32,384]{3,2,1,0:T(8,128)(2,1)S(1)}, bf16[2,8,32,256]{3,2,1,0:T(8,128)(2,1)}, bf16[4,8,32,256]{3,2,1,0:T(8,128)(2,1)S(1)}) custom-call(s32[1]{0:T(128)} %bitcast.place.refs_0_, bf16[2,8,32,128]{3,2,1,0:T(8,128)(2,1)S(1)} %collective-permute-done.2.refs_1_, bf16[2,8,32,128]{3,2,1,0:T(8,128)(2,1)S(1)} %collective-permute-done.3.refs_2_, ...), custom_call_target="tpu_custom_call" | custom-call | flops 14155776 | bytes 1048576 | tf_op jit(solution)/shard_map/pallas_call | solution.py:27
  45.5 1.2 %shard_map.72 = (bf16[8,16,3456]{2,1,0:T(8,128)(2,1)S(1)}, bf16[8,16,3456]{2,1,0:T(8,128)(2,1)S(1)}) custom-call(s32[1]{0:T(128)} %bitcast.place.refs_0_, bf16[2,10,32,384]{3,2,1,0:T(8,128)(2,1)S(1)} %get-tuple-element.55.refs_1_, bf16[4,10,32,384]{3,2,1,0:T(8,128)(2,1)S(1)} %get-tuple-element.56.refs_2_, ...), custom_call_target="tpu_custom_call" | custom-call | flops 14155776 | bytes 1048576 | tf_op jit(solution)/shard_map/pallas_call | solution.py:27
  46.6 4.9 %collective-permute-start.4 = (bf16[8,16,3456]{2,1,0:T(8,128)(2,1)S(1)}, bf16[8,16,3456]{2,1,0:T(8,128)(2,1)S(1)}, u32[]{:S(2)}, u32[]{:S(2)}) collective-permute-start(bf16[8,16,3456]{2,1,0:T(8,128)(2,1)S(1)} %get-tuple-element.57.refs_4_), channel_id=1, source_target_pairs={{0,1},{1,0},{2,3},{3,2},{4,5},{5,4},{6,7},{7,6},{8,9},{9,8},{10,11... | collective-permute-start | bytes 2654216 | tf_op jit(solution)/shard_map/ppermute | solution.py:338
  51.6 2.1 %shard_map.73.refs_3_ = bf16[4,8,64,256]{3,2,1,0:T(8,128)(2,1)S(1)} custom-call(bf16[4,8,32,256]{3,2,1,0:T(8,128)(2,1)S(1)} %get-tuple-element.52.refs_3_.refs_0_, bf16[27,128,256]{2,1,0:T(8,128)(2,1)S(1)} %copy-done, bf16[2,8,64,256]{3,2,1,0:T(8,128)(2,1)S(1)} %get-tuple-element.53.refs_2_, bf16[2,8,64,256]{3,2,1,0:T(8,128)(2,1)S(1)} %get-tuple-element.54.refs_3_, ...), custom_call_target="tpu_custom_call" | custom-call | flops 14155776 | bytes 1048576 | tf_op jit(solution)/shard_map/pallas_call | solution.py:27
  53.7 0.0 collective-permute-done.4.refs_2_
  53.7 0.2 shard_map.74
  53.9 1.0 %shard_map.75 = (bf16[8,8,768]{2,1,0:T(8,128)(2,1)S(1)}, bf16[8,8,768]{2,1,0:T(8,128)(2,1)S(1)}) custom-call(s32[1]{0:T(128)} %bitcast.place.refs_0_, bf16[4,9,64,768]{3,2,1,0:T(8,128)(2,1)S(1)} %get-tuple-element.50.refs_1_, bf16[2,9,64,768]{3,2,1,0:T(8,128)(2,1)S(1)} %get-tuple-element.51.refs_2_, bf16[4,8,64,256]{3,2,1,0:T(8,128)(2,1)S(1)} %shard_map.73.refs_3_, ...), custom_call_target="tpu_custom_call" | custom-call | flops 18874368 | bytes 1048576 | tf_op jit(solution)/shard_map/pallas_call | solution.py:27
  54.9 0.3 collective-permute-start.5
  55.3 3.6 %collective-permute-start.9 = (bf16[2,16,3456]{2,1,0:T(8,128)(2,1)S(1)}, bf16[2,16,3456]{2,1,0:T(8,128)(2,1)S(1)}, u32[]{:S(2)}, u32[]{:S(2)}) collective-permute-start(bf16[2,16,3456]{2,1,0:T(8,128)(2,1)S(1)} %get-tuple-element.66), channel_id=1, source_target_pairs={{0,4},{1,5},{2,6},{3,7},{4,0},{5,1},{6,2},{7,3},{8,12},{9,13},{10,... | collective-permute-start | bytes 663560 | tf_op jit(solution)/shard_map/ppermute | solution.py:338
  58.9 0.9 collective-permute-start.10
  59.8 0.6 collective-permute-start.8
  60.3 1.8 %shard_map.76 = (bf16[8,8,1536]{2,1,0:T(8,128)(2,1)S(1)}, bf16[8,8,1536]{2,1,0:T(8,128)(2,1)S(1)}) custom-call(s32[1]{0:T(128)} %bitcast.place.refs_0_, bf16[4,9,64,768]{3,2,1,0:T(8,128)(2,1)S(1)} %get-tuple-element.50.refs_1_, bf16[2,9,64,768]{3,2,1,0:T(8,128)(2,1)S(1)} %get-tuple-element.51.refs_2_, bf16[4,8,64,256]{3,2,1,0:T(8,128)(2,1)S(1)} %shard_map.73.refs_3_, ...), custom_call_target="tpu_custom_call" | custom-call | flops 18874368 | bytes 1048576 | tf_op jit(solution)/shard_map/pallas_call | solution.py:27
  62.2 0.1 collective-permute-start.6
  62.3 1.6 %shard_map.77 = (bf16[8,8,1152]{2,1,0:T(8,128)(2,1)S(1)}, bf16[8,8,1152]{2,1,0:T(8,128)(2,1)S(1)}) custom-call(s32[1]{0:T(128)} %bitcast.place.refs_0_, bf16[4,9,64,768]{3,2,1,0:T(8,128)(2,1)S(1)} %get-tuple-element.50.refs_1_, bf16[2,9,64,768]{3,2,1,0:T(8,128)(2,1)S(1)} %get-tuple-element.51.refs_2_, bf16[4,8,64,256]{3,2,1,0:T(8,128)(2,1)S(1)} %shard_map.73.refs_3_, ...), custom_call_target="tpu_custom_call" | custom-call | flops 18874368 | bytes 1048576 | tf_op jit(solution)/shard_map/pallas_call | solution.py:27
  63.8 0.0 collective-permute-done.5.refs_2_
  63.8 0.6 collective-permute-start.7
  64.4 1.0 %collective-permute-done.7.refs_6_ = bf16[8,8,1152]{2,1,0:T(8,128)(2,1)S(1)} collective-permute-done((bf16[8,8,1152]{2,1,0:T(8,128)(2,1)S(1)}, bf16[8,8,1152]{2,1,0:T(8,128)(2,1)S(1)}, u32[]{:S(2)}, u32[]{:S(2)}) %collective-permute-start.7) | collective-permute-done | bytes 147488 | tf_op jit(solution)/shard_map/ppermute | solution.py:338
  65.4 0.0 collective-permute-done.6.refs_4_
  65.4 0.0 collective-permute-done.9.refs_8_.refs_3_
  65.4 4.7 %collective-permute-done.10.refs_9_.refs_4_ = bf16[2,16,3456]{2,1,0:T(8,128)(2,1)S(1)} collective-permute-done((bf16[2,16,3456]{2,1,0:T(8,128)(2,1)S(1)}, bf16[2,16,3456]{2,1,0:T(8,128)(2,1)S(1)}, u32[]{:S(2)}, u32[]{:S(2)}) %collective-permute-start.10) | collective-permute-done | bytes 221216 | tf_op jit(solution)/shard_map/ppermute | solution.py:338
  70.1 1.4 %collective-permute-done.8.refs_7_.refs_2_ = bf16[2,16,3456]{2,1,0:T(8,128)(2,1)S(1)} collective-permute-done((bf16[2,16,3456]{2,1,0:T(8,128)(2,1)S(1)}, bf16[2,16,3456]{2,1,0:T(8,128)(2,1)S(1)}, u32[]{:S(2)}, u32[]{:S(2)}) %collective-permute-start.8) | collective-permute-done | bytes 221216 | tf_op jit(solution)/shard_map/ppermute | solution.py:338
  71.5 0.1 shard_map.78
  71.6 1.6 %collective-permute-start.12 = (bf16[2,8,3456]{2,1,0:T(8,128)(2,1)S(1)}, bf16[2,8,3456]{2,1,0:T(8,128)(2,1)S(1)}, u32[]{:S(2)}, u32[]{:S(2)}) collective-permute-start(bf16[2,8,3456]{2,1,0:T(8,128)(2,1)S(1)} %get-tuple-element.70), channel_id=1, source_target_pairs={{0,4},{1,5},{2,6},{3,7},{4,0},{5,1},{6,2},{7,3},{8,12},{9,13},{10,... | collective-permute-start | bytes 331784 | tf_op jit(solution)/shard_map/ppermute | solution.py:338
  73.3 0.7 collective-permute-start.13
  74.0 1.2 %collective-permute-start.11 = (bf16[2,8,3456]{2,1,0:T(8,128)(2,1)S(1)}, bf16[2,8,3456]{2,1,0:T(8,128)(2,1)S(1)}, u32[]{:S(2)}, u32[]{:S(2)}) collective-permute-start(bf16[2,8,3456]{2,1,0:T(8,128)(2,1)S(1)} %get-tuple-element.69.refs_5_), channel_id=1, source_target_pairs={{0,2},{1,3},{2,0},{3,1},{4,6},{5,7},{6,4},{7,5},{8,10},{9,11},{10,... | collective-permute-start | bytes 331784 | tf_op jit(solution)/shard_map/ppermute | solution.py:338
  75.2 0.1 shard_map.80
  75.3 2.6 %collective-permute-start.17 = (bf16[16,3456]{1,0:T(8,128)(2,1)S(1)}, bf16[16,3456]{1,0:T(8,128)(2,1)S(1)}, u32[]{:S(2)}, u32[]{:S(2)}) collective-permute-start(bf16[16,3456]{1,0:T(8,128)(2,1)S(1)} %bitcast.24), channel_id=1, source_target_pairs={{0,8},{1,9},{2,10},{3,11},{4,12},{5,13},{6,14},{7,15},{8,0},{9,1},... | collective-permute-start | bytes 331784 | tf_op jit(solution)/shard_map/ppermute | solution.py:338
  77.9 0.4 collective-permute-done.12.refs_3_
  78.3 1.6 %collective-permute-done.13.refs_4_ = bf16[2,8,3456]{2,1,0:T(8,128)(2,1)S(1)} collective-permute-done((bf16[2,8,3456]{2,1,0:T(8,128)(2,1)S(1)}, bf16[2,8,3456]{2,1,0:T(8,128)(2,1)S(1)}, u32[]{:S(2)}, u32[]{:S(2)}) %collective-permute-start.13) | collective-permute-done | bytes 110624 | tf_op jit(solution)/shard_map/ppermute | solution.py:338
  80.0 0.0 collective-permute-done.11.refs_2_
  80.0 0.1 shard_map.79
  80.0 3.7 %collective-permute-start.16 = (bf16[8,3456]{1,0:T(8,128)(2,1)S(1)}, bf16[8,3456]{1,0:T(8,128)(2,1)S(1)}, u32[]{:S(2)}, u32[]{:S(2)}) collective-permute-start(bf16[8,3456]{1,0:T(8,128)(2,1)S(1)} %bitcast.25), channel_id=1, source_target_pairs={{0,24},{1,25},{2,26},{3,27},{4,28},{5,29},{6,30},{7,31},{8,16},{9,... | collective-permute-start | bytes 165896 | tf_op jit(solution)/shard_map/ppermute | solution.py:343
  83.7 0.2 collective-permute-start.15
  84.0 0.6 collective-permute-start.14
  84.6 0.0 collective-permute-done.17
  84.6 1.6 %collective-permute-start.18 = (bf16[16,3456]{1,0:T(8,128)(2,1)S(1)}, bf16[16,3456]{1,0:T(8,128)(2,1)S(1)}, u32[]{:S(2)}, u32[]{:S(2)}) collective-permute-start(bf16[16,3456]{1,0:T(8,128)(2,1)S(1)} %fusion), channel_id=1, source_target_pairs={{0,16},{1,17},{2,18},{3,19},{4,20},{5,21},{6,22},{7,23},{8,24},{9,... | collective-permute-start | bytes 331784 | tf_op jit(solution)/shard_map/ppermute | solution.py:343
  86.2 2.0 %collective-permute-done.14 = bf16[8,3456]{1,0:T(8,128)(2,1)S(1)} collective-permute-done((bf16[8,3456]{1,0:T(8,128)(2,1)S(1)}, bf16[8,3456]{1,0:T(8,128)(2,1)S(1)}, u32[]{:S(2)}, u32[]{:S(2)}) %collective-permute-start.14) | collective-permute-done | bytes 55328 | tf_op jit(solution)/shard_map/ppermute | solution.py:343
  88.2 0.0 collective-permute-done.16
  88.2 0.6 collective-permute-done.15
  88.8 0.7 add_add_fusion
  89.5 0.0 collective-permute-done.18
  89.5 0.7 convert_add_fusion
  (2 shorter events, 0.0 us)
Async XLA Ops:
  0.6 26.2 %copy-start.1 = (bf16[1,4,16,64,128]{4,3,2,1,0:T(8,128)(2,1)S(1)}, bf16[1,4,16,64,128]{4,3,2,1,0:T(8,128)(2,1)}, u32[]{:S(2)}) copy-start(bf16[1,4,16,64,128]{4,3,2,1,0:T(8,128)(2,1)} %param.4) | copy-start | bytes 3145732
  0.6 26.2 %copy-start.2 = (bf16[27,128,128]{2,1,0:T(8,128)(2,1)S(1)}, bf16[27,128,128]{2,1,0:T(8,128)(2,1)}, u32[]{:S(2)}) copy-start(bf16[27,128,128]{2,1,0:T(8,128)(2,1)} %param.5) | copy-start | bytes 2654212
  25.6 5.8 %collective-permute-start = (bf16[48,32,128]{2,1,0:T(8,128)(2,1)}, bf16[48,32,128]{2,1,0:T(8,128)(2,1)S(1)}, u32[]{:S(2)}, u32[]{:S(2)}) collective-permute-start(bf16[48,32,128]{2,1,0:T(8,128)(2,1)} %get-tuple-element.40), channel_id=1, source_target_pairs={{0,1},{1,0},{2,3},{3,2},{4,5},{5,4},{6,7},{7,6},{8,9},{9,8},{10,11... | collective-permute-start | bytes 1179656 | tf_op jit(solution)/shard_map/ppermute | solution.py:43
  26.2 5.3 %collective-permute-start.1 = (bf16[48,32,128]{2,1,0:T(8,128)(2,1)}, bf16[48,32,128]{2,1,0:T(8,128)(2,1)S(1)}, u32[]{:S(2)}, u32[]{:S(2)}) collective-permute-start(bf16[48,32,128]{2,1,0:T(8,128)(2,1)} %get-tuple-element.41), channel_id=1, source_target_pairs={{1,2},{3,4},{5,6},{7,8},{9,10},{11,12},{13,14},{2,1},{4,3},{6,5},{... | collective-permute-start | bytes 1179656 | tf_op jit(solution)/shard_map/ppermute | solution.py:43
  31.5 10.9 %copy-start = (bf16[27,128,256]{2,1,0:T(8,128)(2,1)S(1)}, bf16[27,128,256]{2,1,0:T(8,128)(2,1)}, u32[]{:S(2)}) copy-start(bf16[27,128,256]{2,1,0:T(8,128)(2,1)} %refs_1_.1) | copy-start | bytes 5308420
  31.5 12.1 %copy-start.3 = (bf16[1,2,8,32,256]{4,3,2,1,0:T(8,128)(2,1)S(1)}, bf16[1,2,8,32,256]{4,3,2,1,0:T(8,128)(2,1)}, u32[]{:S(2)}) copy-start(bf16[1,2,8,32,256]{4,3,2,1,0:T(8,128)(2,1)} %param.7) | copy-start | bytes 786436
  33.0 10.6 %collective-permute-start.2 = (bf16[2,8,32,128]{3,2,1,0:T(8,128)(2,1)S(1)}, bf16[2,8,32,128]{3,2,1,0:T(8,128)(2,1)S(1)}, u32[]{:S(2)}, u32[]{:S(2)}) collective-permute-start(bf16[2,8,32,128]{3,2,1,0:T(8,128)(2,1)S(1)} %get-tuple-element.45), channel_id=1, source_target_pairs={{0,1},{1,0},{2,3},{3,2},{4,5},{5,4},{6,7},{7,6},{8,9},{9,8},{10,11... | collective-permute-start | bytes 393224 | tf_op jit(solution)/shard_map/ppermute | solution.py:43
  41.5 2.1 %collective-permute-start.3 = (bf16[2,8,32,128]{3,2,1,0:T(8,128)(2,1)S(1)}, bf16[2,8,32,128]{3,2,1,0:T(8,128)(2,1)S(1)}, u32[]{:S(2)}, u32[]{:S(2)}) collective-permute-start(bf16[2,8,32,128]{3,2,1,0:T(8,128)(2,1)S(1)} %get-tuple-element.46), channel_id=1, source_target_pairs={{1,2},{3,4},{5,6},{7,8},{9,10},{11,12},{13,14},{2,1},{4,3},{6,5},{... | collective-permute-start | bytes 393224 | tf_op jit(solution)/shard_map/ppermute | solution.py:43
  46.6 7.0 %collective-permute-start.4 = (bf16[8,16,3456]{2,1,0:T(8,128)(2,1)S(1)}, bf16[8,16,3456]{2,1,0:T(8,128)(2,1)S(1)}, u32[]{:S(2)}, u32[]{:S(2)}) collective-permute-start(bf16[8,16,3456]{2,1,0:T(8,128)(2,1)S(1)} %get-tuple-element.57.refs_4_), channel_id=1, source_target_pairs={{0,1},{1,0},{2,3},{3,2},{4,5},{5,4},{6,7},{7,6},{8,9},{9,8},{10,11... | collective-permute-start | bytes 2654216 | tf_op jit(solution)/shard_map/ppermute | solution.py:338
  54.9 8.9 %collective-permute-start.5 = (bf16[8,8,768]{2,1,0:T(8,128)(2,1)S(1)}, bf16[8,8,768]{2,1,0:T(8,128)(2,1)S(1)}, u32[]{:S(2)}, u32[]{:S(2)}) collective-permute-start(bf16[8,8,768]{2,1,0:T(8,128)(2,1)S(1)} %get-tuple-element.61.refs_4_), channel_id=1, source_target_pairs={{0,1},{1,0},{2,3},{3,2},{4,5},{5,4},{6,7},{7,6},{8,9},{9,8},{10,11... | collective-permute-start | bytes 294920 | tf_op jit(solution)/shard_map/ppermute | solution.py:338
  55.3 10.1 %collective-permute-start.9 = (bf16[2,16,3456]{2,1,0:T(8,128)(2,1)S(1)}, bf16[2,16,3456]{2,1,0:T(8,128)(2,1)S(1)}, u32[]{:S(2)}, u32[]{:S(2)}) collective-permute-start(bf16[2,16,3456]{2,1,0:T(8,128)(2,1)S(1)} %get-tuple-element.66), channel_id=1, source_target_pairs={{0,4},{1,5},{2,6},{3,7},{4,0},{5,1},{6,2},{7,3},{8,12},{9,13},{10,... | collective-permute-start | bytes 663560 | tf_op jit(solution)/shard_map/ppermute | solution.py:338
  58.9 11.3 %collective-permute-start.10 = (bf16[2,16,3456]{2,1,0:T(8,128)(2,1)S(1)}, bf16[2,16,3456]{2,1,0:T(8,128)(2,1)S(1)}, u32[]{:S(2)}, u32[]{:S(2)}) collective-permute-start(bf16[2,16,3456]{2,1,0:T(8,128)(2,1)S(1)} %get-tuple-element.67), channel_id=1, source_target_pairs={{0,6},{1,7},{2,4},{3,5},{4,2},{5,3},{6,0},{7,1},{8,14},{9,15},{10,... | collective-permute-start | bytes 663560 | tf_op jit(solution)/shard_map/ppermute | solution.py:338
  59.8 11.7 %collective-permute-start.8 = (bf16[2,16,3456]{2,1,0:T(8,128)(2,1)S(1)}, bf16[2,16,3456]{2,1,0:T(8,128)(2,1)S(1)}, u32[]{:S(2)}, u32[]{:S(2)}) collective-permute-start(bf16[2,16,3456]{2,1,0:T(8,128)(2,1)S(1)} %get-tuple-element.59.refs_4_), channel_id=1, source_target_pairs={{0,2},{1,3},{2,0},{3,1},{4,6},{5,7},{6,4},{7,5},{8,10},{9,11},{10,... | collective-permute-start | bytes 663560 | tf_op jit(solution)/shard_map/ppermute | solution.py:338
  62.2 3.2 %collective-permute-start.6 = (bf16[8,8,1536]{2,1,0:T(8,128)(2,1)S(1)}, bf16[8,8,1536]{2,1,0:T(8,128)(2,1)S(1)}, u32[]{:S(2)}, u32[]{:S(2)}) collective-permute-start(bf16[8,8,1536]{2,1,0:T(8,128)(2,1)S(1)} %get-tuple-element.63.refs_4_), channel_id=1, source_target_pairs={{0,1},{1,0},{2,3},{3,2},{4,5},{5,4},{6,7},{7,6},{8,9},{9,8},{10,11... | collective-permute-start | bytes 589832 | tf_op jit(solution)/shard_map/ppermute | solution.py:338
  63.8 1.6 %collective-permute-start.7 = (bf16[8,8,1152]{2,1,0:T(8,128)(2,1)S(1)}, bf16[8,8,1152]{2,1,0:T(8,128)(2,1)S(1)}, u32[]{:S(2)}, u32[]{:S(2)}) collective-permute-start(bf16[8,8,1152]{2,1,0:T(8,128)(2,1)S(1)} %get-tuple-element.65), channel_id=1, source_target_pairs={{0,1},{1,0},{2,3},{3,2},{4,5},{5,4},{6,7},{7,6},{8,9},{9,8},{10,11... | collective-permute-start | bytes 442376 | tf_op jit(solution)/shard_map/ppermute | solution.py:338
  71.6 6.7 %collective-permute-start.12 = (bf16[2,8,3456]{2,1,0:T(8,128)(2,1)S(1)}, bf16[2,8,3456]{2,1,0:T(8,128)(2,1)S(1)}, u32[]{:S(2)}, u32[]{:S(2)}) collective-permute-start(bf16[2,8,3456]{2,1,0:T(8,128)(2,1)S(1)} %get-tuple-element.70), channel_id=1, source_target_pairs={{0,4},{1,5},{2,6},{3,7},{4,0},{5,1},{6,2},{7,3},{8,12},{9,13},{10,... | collective-permute-start | bytes 331784 | tf_op jit(solution)/shard_map/ppermute | solution.py:338
  73.3 6.7 %collective-permute-start.13 = (bf16[2,8,3456]{2,1,0:T(8,128)(2,1)S(1)}, bf16[2,8,3456]{2,1,0:T(8,128)(2,1)S(1)}, u32[]{:S(2)}, u32[]{:S(2)}) collective-permute-start(bf16[2,8,3456]{2,1,0:T(8,128)(2,1)S(1)} %get-tuple-element.71), channel_id=1, source_target_pairs={{0,6},{1,7},{2,4},{3,5},{4,2},{5,3},{6,0},{7,1},{8,14},{9,15},{10,... | collective-permute-start | bytes 331784 | tf_op jit(solution)/shard_map/ppermute | solution.py:338
  74.0 6.0 %collective-permute-start.11 = (bf16[2,8,3456]{2,1,0:T(8,128)(2,1)S(1)}, bf16[2,8,3456]{2,1,0:T(8,128)(2,1)S(1)}, u32[]{:S(2)}, u32[]{:S(2)}) collective-permute-start(bf16[2,8,3456]{2,1,0:T(8,128)(2,1)S(1)} %get-tuple-element.69.refs_5_), channel_id=1, source_target_pairs={{0,2},{1,3},{2,0},{3,1},{4,6},{5,7},{6,4},{7,5},{8,10},{9,11},{10,... | collective-permute-start | bytes 331784 | tf_op jit(solution)/shard_map/ppermute | solution.py:338
  75.3 9.3 %collective-permute-start.17 = (bf16[16,3456]{1,0:T(8,128)(2,1)S(1)}, bf16[16,3456]{1,0:T(8,128)(2,1)S(1)}, u32[]{:S(2)}, u32[]{:S(2)}) collective-permute-start(bf16[16,3456]{1,0:T(8,128)(2,1)S(1)} %bitcast.24), channel_id=1, source_target_pairs={{0,8},{1,9},{2,10},{3,11},{4,12},{5,13},{6,14},{7,15},{8,0},{9,1},... | collective-permute-start | bytes 331784 | tf_op jit(solution)/shard_map/ppermute | solution.py:338
  80.0 8.2 %collective-permute-start.16 = (bf16[8,3456]{1,0:T(8,128)(2,1)S(1)}, bf16[8,3456]{1,0:T(8,128)(2,1)S(1)}, u32[]{:S(2)}, u32[]{:S(2)}) collective-permute-start(bf16[8,3456]{1,0:T(8,128)(2,1)S(1)} %bitcast.25), channel_id=1, source_target_pairs={{0,24},{1,25},{2,26},{3,27},{4,28},{5,29},{6,30},{7,31},{8,16},{9,... | collective-permute-start | bytes 165896 | tf_op jit(solution)/shard_map/ppermute | solution.py:343
  83.7 5.1 %collective-permute-start.15 = (bf16[8,3456]{1,0:T(8,128)(2,1)S(1)}, bf16[8,3456]{1,0:T(8,128)(2,1)S(1)}, u32[]{:S(2)}, u32[]{:S(2)}) collective-permute-start(bf16[8,3456]{1,0:T(8,128)(2,1)S(1)} %bitcast.26), channel_id=1, source_target_pairs={{0,8},{1,9},{2,10},{3,11},{4,12},{5,13},{6,14},{7,15},{8,0},{9,1},... | collective-permute-start | bytes 165896 | tf_op jit(solution)/shard_map/ppermute | solution.py:338
  84.0 4.2 %collective-permute-start.14 = (bf16[8,3456]{1,0:T(8,128)(2,1)S(1)}, bf16[8,3456]{1,0:T(8,128)(2,1)S(1)}, u32[]{:S(2)}, u32[]{:S(2)}) collective-permute-start(bf16[8,3456]{1,0:T(8,128)(2,1)S(1)} %convert_bitcast_fusion), channel_id=1, source_target_pairs={{0,16},{1,17},{2,18},{3,19},{4,20},{5,21},{6,22},{7,23},{8,24},{9,... | collective-permute-start | bytes 165896 | tf_op jit(solution)/shard_map/ppermute | solution.py:343
  84.6 4.8 %collective-permute-start.18 = (bf16[16,3456]{1,0:T(8,128)(2,1)S(1)}, bf16[16,3456]{1,0:T(8,128)(2,1)S(1)}, u32[]{:S(2)}, u32[]{:S(2)}) collective-permute-start(bf16[16,3456]{1,0:T(8,128)(2,1)S(1)} %fusion), channel_id=1, source_target_pairs={{0,16},{1,17},{2,18},{3,19},{4,20},{5,21},{6,22},{7,23},{8,24},{9,... | collective-permute-start | bytes 331784 | tf_op jit(solution)/shard_map/ppermute | solution.py:343

commit v5 on v4

--- a/solution.py
+++ b/solution.py
@@ -10,7 +10,7 @@
 F32 = jnp.float32
 BF16 = jnp.bfloat16
 COST = 64
-FETCH = 60
+SMALL = 50
 PARTS = (range(0, 2), range(2, 6), range(6, 9))
 VMEM = pl.BlockSpec(memory_space=pltpu.VMEM)
 SMEM = pl.BlockSpec(memory_space=pltpu.SMEM)
@@ -111,23 +111,19 @@
     return (act[:, :chan] + act[:, chan:]).reshape(half, depth, chan), slope
 
 
-def side_planes(place, volume, cotangent, to_pair, to_next, sems):
-    planes, rows, _, chan = volume.shape
-    cp, cy = cotangent.shape[:2]
-    copies = []
-    for to, side in ((to_pair, 1 - place[0] % 2), (to_next, place[0] % 2)):
-        copies.append((volume.at[side * (planes - 1)], to.at[pl.ds(0, rows)]))
-        for k in range(cotangent.shape[3] // chan):
-            part = cotangent.at[side * (cp - 1), :, :, pl.ds(k * chan, chan)]
-            copies.append((part, to.at[pl.ds(rows + k * cy, cy)]))
-    copies = [pltpu.make_async_copy(*pair, sems.at[k]) for k, pair in enumerate(copies)]
+def side_planes(place, volume, to_pair, to_next, sems):
+    last = volume.shape[0] - 1
+    copies = [
+        pltpu.make_async_copy(volume.at[(1 - place[0] % 2) * last], to_pair.at[0], sems.at[0]),
+        pltpu.make_async_copy(volume.at[place[0] % 2 * last], to_next.at[0], sems.at[1]),
+    ]
     for copy in copies:
         copy.start()
     for copy in copies:
         copy.wait()
 
 
-def fine_inner(own, kernel, wide6, weights, edge, act, slope):
+def fine_inner(place, own, kernel, cotangent, wide6, weights, edge, act, slope, to_pair, to_next):
     planes, fy, fz, chan = own.shape
     half = fy // 2
     for s in range(2):
@@ -135,11 +131,14 @@
             for q in range(2):
                 b = 2 * s + r - q
                 for a in range(3):
-                    place = (a, s, pl.ds(r * 3 * chan, 3 * chan), pl.ds(q * chan, chan))
+                    block = (a, s, pl.ds(r * 3 * chan, 3 * chan), pl.ds(q * chan, chan))
                     if 0 <= b <= 2:
-                        weights[place] = kernel[3 * a + b]
+                        weights[block] = kernel[3 * a + b]
                     else:
-                        weights[place] = jnp.zeros((3 * chan, chan), BF16)
+                        weights[block] = jnp.zeros((3 * chan, chan), BF16)
+    last = cotangent.shape[0] - 1
+    to_pair[0] = cotangent[(1 - place[0] % 2) * last]
+    to_next[0] = cotangent[place[0] % 2 * last]
     done = 0
     for p in range(planes):
         while done < min(p + 2, planes):
@@ -169,8 +168,8 @@
             lambda y: facing(
                 place,
                 e,
-                from_pair[2 * y : 2 * y + 2].reshape(1, fz, -1),
-                from_next[2 * y : 2 * y + 2].reshape(1, fz, -1),
+                from_pair[0, y : y + 1],
+                from_next[0, y : y + 1],
             ),
         )
         total, slope[e] = fine_finish(edge[e] + fine_conv(halo6, e, weights, 2 * e), half, fz)
@@ -210,8 +209,6 @@
     place, from_pair, from_next, kernel, pre, cotangent, side_pair, side_next, halo3, out, delta
 ):
     planes, cy, cz, wide = cotangent.shape
-    chan = from_pair.shape[-1]
-    rows = side_pair.shape[0] - wide // chan * cy
     for e in range(2):
         for k in range(2):
             fill_wide3(halo3, 2 * e + k, facing(place, e, from_pair[k], from_next[k]))
@@ -229,11 +226,7 @@
             grad = cotangent[p].reshape(cy * cz, wide).astype(F32)
         else:
             e = int(p >= planes)
-            parts = []
-            for k in range(wide // chan):
-                lines = pl.ds(rows + k * cy, cy)
-                parts.append(facing(place, e, side_pair[lines], side_next[lines]))
-            grad = jnp.concatenate(parts, axis=-1).reshape(cy * cz, wide)
+            grad = facing(place, e, side_pair[0], side_next[0]).reshape(cy * cz, wide)
         grad = grad * silu_slope(total, sig)
         delta[p + 1] = grad.astype(BF16).reshape(cy, cz, wide)
 
@@ -466,36 +459,38 @@
     def shape(*extents, kind=BF16):
         return jax.ShapeDtypeStruct(extents, kind)
 
-    lines = 2 * fy + wide // chan * cy
-    anywhere = pl.BlockSpec(memory_space=pl.ANY)
     to_pair, to_next = pl.pallas_call(
         side_planes,
-        out_shape=[shape(lines, cz, chan)] * 2,
-        in_specs=[SMEM, anywhere, anywhere],
-        out_specs=[anywhere] * 2,
-        scratch_shapes=[pltpu.SemaphoreType.DMA((2 + 2 * (wide // chan),))],
+        out_shape=[shape(1, fy, fz, chan)] * 2,
+        in_specs=[SMEM, pl.BlockSpec(memory_space=pl.ANY)],
+        out_specs=[VMEM] * 2,
+        scratch_shapes=[pltpu.SemaphoreType.DMA((2,))],
         cost_estimate=pl.CostEstimate(flops=fine_flops, bytes_accessed=2**20, transcendentals=0),
-        compiler_params=pltpu.CompilerParams(vmem_limit_bytes=FETCH * 2**20),
-    )(place, x.reshape(planes, 2 * fy, cz, chan), cotangent[0])
-    side_pair, side_next = exchange(to_pair, to_next)
+        compiler_params=pltpu.CompilerParams(vmem_limit_bytes=SMALL * 2**20),
+    )(place, x)
+    from_pair, from_next = exchange(to_pair, to_next)
     mid = max(planes - 2, 1)
-    wide6, weights, edge, act, slope = kernel_call(
+    wide6, weights, edge, act, slope, to_pair, to_next = kernel_call(
         fine_inner,
-        [x, fine_kernel.reshape(9, 3 * chan, chan)],
+        [place, x, fine_kernel.reshape(9, 3 * chan, chan), cotangent[0]],
         [
             shape(planes, half + 1, fz, 6 * chan),
             shape(3, 2, 6 * chan, 2 * chan),
             shape(2, half * fz, 2 * chan, kind=F32),
             shape(mid, half, fz, chan, kind=F32),
             shape(mid, half, fz, 2 * chan),
+            shape(1, cy, cz, wide),
+            shape(1, cy, cz, wide),
         ],
         [],
         fine_flops,
         16,
-    )
+        scalars=1,
+    )
+    side_pair, side_next = exchange(to_pair, to_next)
     halo6, pooled, slope_edge, to_pair, to_next = kernel_call(
         fine_outer,
-        [place, side_pair, side_next, weights, edge, act],
+        [place, from_pair, from_next, weights, edge, act],
         [
             shape(2, half + 1, fz, 6 * chan),
             shape(cp, cy, cz, chan),
@@ -569,12 +564,12 @@
             )
         )
         before = [fine_parts[-1][-1]]
-    got = received(early, coarse_kept)
+    got = coarse_got = received(early, coarse_kept)
     pieces = []
     for part in fine_parts:
         keep, send = sided(part, count)
         pieces.append([keep, swap(send, 1)])
-    late, fine_kept = fold(place, pieces, steps[0], got[1:])
+    late, fine_kept = fold(place, pieces, steps[0], coarse_got[1:])
     for group in steps[1:]:
         early, coarse_kept = fold(place, [got], group, [late[steps[0][0]]])
         got = received(early, coarse_kept)

time: 90.3 us -> 65.5 us (0.73)
  Pallas kernels: 42.3 us -> 17.5 us
  starting transfers between devices: 33.8 us -> 32 us
  local copies, waits for them, and re-layouts: 0.02 us -> 1.23 us
    pallas_call x1, Pallas kernels: 25 us -> 0.06 us  [shards(): pl.pallas_call(side_planes, out_shape=[shape(1, fy, fz, chan)] * 2, in_sp...]
    ppermute x2 -> x3, starting transfers between devices: 9.04 us -> 7.54 us  [exchange(): lax.ppermute(to_pair, 'space', pair)]
    unnamed x8, local copies, waits for them, and re-layouts: 0.02 us -> 1.23 us
    ppermute x2 -> x3, starting transfers between devices: 1.51 us -> 2.16 us  [exchange(): lax.ppermute(to_next, 'space', across)]
  transfers between devices with their start and end apart: 19 -> 21, of which waited for: 7 -> 6; matrix products, arithmetic and copies ran while one was open for 1% -> 1% of each run, Pallas kernels for 13% -> 20%
where the time goes in v5:
time: 65.5 us; the launch traced here: 65.3 us
  starting transfers between devices  32 us (49%)
  Pallas kernels  17.5 us (27%)
  waiting for transfers between devices  12.2 us (19%)
  other arithmetic  1.43 us (2%)
  local copies, waits for them, and re-layouts  1.23 us (2%)
  between operations  0.87 us (1%)
    pallas_call x13, Pallas kernels, kernel_call(): pl.pallas_call(inner, out_shape=outs, in_specs=specs, out_specs=[VMEM] *...  17.4 us
    ppermute x12, starting transfers between devices, swap(): return lax.ppermute(value, 'space', [(i, i ^ bit) for i in range(count)])  17.2 us
    ppermute x12, waiting for transfers between devices, swap(): return lax.ppermute(value, 'space', [(i, i ^ bit) for i in range(count)])  9.65 us
    ppermute x3, starting transfers between devices, exchange(): lax.ppermute(to_pair, 'space', pair)  7.54 us
    ppermute x3, starting transfers between devices, swap_sample(): lax.ppermute(value, ('sample', 'space'), [(s * count + i, (1 - s) * count...  5.12 us
    ppermute x3, waiting for transfers between devices, swap_sample(): lax.ppermute(value, ('sample', 'space'), [(s * count + i, (1 - s) * count...  2.57 us
    ppermute x3, starting transfers between devices, exchange(): lax.ppermute(to_next, 'space', across)  2.16 us
  transfers between devices with their start and end apart: 21, of which 6 were waited for; matrix products, arithmetic and copies ran while one was open for 1% of the time, Pallas kernels for 20%

profile of v5, /device:TPU:0, one launch (start us, length us, event | category | flops | bytes accessed | tf_op | source)
XLA Modules:
  0.0 65.3 jit_solution(15465577183217162512)
XLA Ops:
  0.6 0.0 copy-start.1
  0.6 1.2 %copy-done.1 = bf16[1,4,16,64,128]{4,3,2,1,0:T(8,128)(2,1)S(1)} copy-done((bf16[1,4,16,64,128]{4,3,2,1,0:T(8,128)(2,1)S(1)}, bf16[1,4,16,64,128]{4,3,2,1,0:T(8,128)(2,1)}, u32[]{:S(2)}) %copy-start.1) | copy-done | bytes 1048600
  1.9 0.1 shard_map.67
  1.9 0.5 collective-permute-start
  2.4 0.7 %collective-permute-start.1 = (bf16[1,16,64,128]{3,2,1,0:T(8,128)(2,1)S(1)}, bf16[1,16,64,128]{3,2,1,0:T(8,128)(2,1)S(1)}, u32[]{:S(2)}, u32[]{:S(2)}) collective-permute-start(bf16[1,16,64,128]{3,2,1,0:T(8,128)(2,1)S(1)} %get-tuple-element.43), channel_id=1, source_target_pairs={{1,2},{3,4},{5,6},{7,8},{9,10},{11,12},{13,14},{2,1},{4,3},{6,5},{... | collective-permute-start | bytes 786440 | tf_op jit(solution)/shard_map/ppermute | solution.py:43
  3.1 0.0 copy-done.2
  3.1 0.0 copy-done.3
  3.1 4.6 %shard_map.68 = (bf16[4,9,64,768]{3,2,1,0:T(8,128)(2,1)S(1)}, bf16[3,2,768,256]{3,2,1,0:T(8,128)(2,1)S(1)}, f32[2,512,256]{2,1,0:T(8,128)S(1)}, f32[2,8,64,128]{...) custom-call(s32[1]{0:T(128)} %bitcast.place.refs_0_, ...), custom_call_target="tpu_custom_call" | custom-call | flops 56623104 | bytes 1048576 | tf_op jit(solution)/shard_map/pallas_call | solution.py:27
  7.8 0.0 copy-start
  7.8 4.1 %collective-permute-start.4 = (bf16[1,8,32,256]{3,2,1,0:T(8,128)(2,1)S(1)}, bf16[1,8,32,256]{3,2,1,0:T(8,128)(2,1)S(1)}, u32[]{:S(2)}, u32[]{:S(2)}) collective-permute-start(bf16[1,8,32,256]{3,2,1,0:T(8,128)(2,1)S(1)} %get-tuple-element.51), channel_id=1, source_target_pairs={{0,1},{1,0},{2,3},{3,2},{4,5},{5,4},{6,7},{7,6},{8,9},{9,8},{10,11... | collective-permute-start | bytes 393224 | tf_op jit(solution)/shard_map/ppermute | solution.py:43
  11.9 0.7 %collective-permute-start.5 = (bf16[1,8,32,256]{3,2,1,0:T(8,128)(2,1)S(1)}, bf16[1,8,32,256]{3,2,1,0:T(8,128)(2,1)S(1)}, u32[]{:S(2)}, u32[]{:S(2)}) collective-permute-start(bf16[1,8,32,256]{3,2,1,0:T(8,128)(2,1)S(1)} %get-tuple-element.52), channel_id=1, source_target_pairs={{1,2},{3,4},{5,6},{7,8},{9,10},{11,12},{13,14},{2,1},{4,3},{6,5},{... | collective-permute-start | bytes 393224 | tf_op jit(solution)/shard_map/ppermute | solution.py:43
  12.5 0.0 collective-permute-done.refs_1_
  12.5 0.0 collective-permute-done.1.refs_2_
  12.5 1.5 %shard_map.69 = (bf16[2,9,64,768]{3,2,1,0:T(8,128)(2,1)S(1)}, bf16[2,8,32,128]{3,2,1,0:T(8,128)(2,1)S(1)}, bf16[2,8,64,256]{3,2,1,0:T(8,128)(2,1)S(1)}, bf16[2,8...) custom-call(s32[1]{0:T(128)} %bitcast.place.refs_0_, bf16[1,16,64,128]{3,2,1,0:T(8,128)(2,1)S(1)} %collective-permute-done.refs_1_, ...), custom_call_target="tpu_custom_call" | custom-call | flops 9437184 | bytes 1048576 | tf_op jit(solution)/shard_map/pallas_call | solution.py:27
  14.0 2.9 %collective-permute-start.2 = (bf16[2,8,32,128]{3,2,1,0:T(8,128)(2,1)S(1)}, bf16[2,8,32,128]{3,2,1,0:T(8,128)(2,1)S(1)}, u32[]{:S(2)}, u32[]{:S(2)}) collective-permute-start(bf16[2,8,32,128]{3,2,1,0:T(8,128)(2,1)S(1)} %get-tuple-element.47), channel_id=1, source_target_pairs={{0,1},{1,0},{2,3},{3,2},{4,5},{5,4},{6,7},{7,6},{8,9},{9,8},{10,11... | collective-permute-start | bytes 393224 | tf_op jit(solution)/shard_map/ppermute | solution.py:43
  17.0 0.8 %collective-permute-start.3 = (bf16[2,8,32,128]{3,2,1,0:T(8,128)(2,1)S(1)}, bf16[2,8,32,128]{3,2,1,0:T(8,128)(2,1)S(1)}, u32[]{:S(2)}, u32[]{:S(2)}) collective-permute-start(bf16[2,8,32,128]{3,2,1,0:T(8,128)(2,1)S(1)} %get-tuple-element.48), channel_id=1, source_target_pairs={{1,2},{3,4},{5,6},{7,8},{9,10},{11,12},{13,14},{2,1},{4,3},{6,5},{... | collective-permute-start | bytes 393224 | tf_op jit(solution)/shard_map/ppermute | solution.py:43
  17.8 0.0 copy-done
  17.8 1.2 %shard_map.70 = (bf16[2,10,32,384]{3,2,1,0:T(8,128)(2,1)S(1)}, f32[4,256,256]{2,1,0:T(8,128)S(1)}) custom-call(bf16[2,8,32,128]{3,2,1,0:T(8,128)(2,1)S(1)} %get-tuple-element.49.refs_0_, bf16[3,1152,256]{2,1,0:T(8,128)(2,1)S(1)} %bitcast.16), custom_call_target="tpu_custom_call" | custom-call | flops 14155776 | bytes 1048576 | tf_op jit(solution)/shard_map/pallas_call | solution.py:27
  19.0 0.0 collective-permute-done.4.refs_6_
  19.0 0.0 collective-permute-done.5.refs_7_
  19.0 0.0 collective-permute-done.2.refs_1_
  19.0 0.0 collective-permute-done.3.refs_2_
  19.0 1.9 %shard_map.71 = (bf16[4,10,32,384]{3,2,1,0:T(8,128)(2,1)S(1)}, bf16[2,8,32,256]{3,2,1,0:T(8,128)(2,1)}, bf16[4,8,32,256]{3,2,1,0:T(8,128)(2,1)S(1)}) custom-call(s32[1]{0:T(128)} %bitcast.place.refs_0_, bf16[2,8,32,128]{3,2,1,0:T(8,128)(2,1)S(1)} %collective-permute-done.2.refs_1_, bf16[2,8,32,128]{3,2,1,0:T(8,128)(2,1)S(1)} %collective-permute-done.3.refs_2_, ...), custom_call_target="tpu_custom_call" | custom-call | flops 14155776 | bytes 1048576 | tf_op jit(solution)/shard_map/pallas_call | solution.py:27
  21.0 1.2 %shard_map.72 = (bf16[8,16,3456]{2,1,0:T(8,128)(2,1)S(1)}, bf16[8,16,3456]{2,1,0:T(8,128)(2,1)S(1)}) custom-call(s32[1]{0:T(128)} %bitcast.place.refs_0_, bf16[2,10,32,384]{3,2,1,0:T(8,128)(2,1)S(1)} %get-tuple-element.59.refs_1_, bf16[4,10,32,384]{3,2,1,0:T(8,128)(2,1)S(1)} %get-tuple-element.60.refs_2_, ...), custom_call_target="tpu_custom_call" | custom-call | flops 14155776 | bytes 1048576 | tf_op jit(solution)/shard_map/pallas_call | solution.py:27
  22.1 4.3 %collective-permute-start.6 = (bf16[8,16,3456]{2,1,0:T(8,128)(2,1)S(1)}, bf16[8,16,3456]{2,1,0:T(8,128)(2,1)S(1)}, u32[]{:S(2)}, u32[]{:S(2)}) collective-permute-start(bf16[8,16,3456]{2,1,0:T(8,128)(2,1)S(1)} %get-tuple-element.61.refs_4_), channel_id=1, source_target_pairs={{0,1},{1,0},{2,3},{3,2},{4,5},{5,4},{6,7},{7,6},{8,9},{9,8},{10,11... | collective-permute-start | bytes 2654216 | tf_op jit(solution)/shard_map/ppermute | solution.py:331
  26.4 2.1 %shard_map.73.refs_3_ = bf16[4,8,64,256]{3,2,1,0:T(8,128)(2,1)S(1)} custom-call(bf16[4,8,32,256]{3,2,1,0:T(8,128)(2,1)S(1)} %get-tuple-element.56.refs_3_.refs_0_, bf16[27,128,256]{2,1,0:T(8,128)(2,1)S(1)} %copy-done, bf16[2,8,64,256]{3,2,1,0:T(8,128)(2,1)S(1)} %get-tuple-element.57.refs_2_, bf16[2,8,64,256]{3,2,1,0:T(8,128)(2,1)S(1)} %get-tuple-element.58.refs_3_, ...), custom_call_target="tpu_custom_call" | custom-call | flops 14155776 | bytes 1048576 | tf_op jit(solution)/shard_map/pallas_call | solution.py:27
  28.5 0.0 collective-permute-done.6.refs_2_
  28.5 0.2 shard_map.74
  28.8 1.0 %shard_map.75 = (bf16[8,8,768]{2,1,0:T(8,128)(2,1)S(1)}, bf16[8,8,768]{2,1,0:T(8,128)(2,1)S(1)}) custom-call(s32[1]{0:T(128)} %bitcast.place.refs_0_, bf16[4,9,64,768]{3,2,1,0:T(8,128)(2,1)S(1)} %get-tuple-element.54.refs_1_, bf16[2,9,64,768]{3,2,1,0:T(8,128)(2,1)S(1)} %get-tuple-element.55.refs_2_, bf16[4,8,64,256]{3,2,1,0:T(8,128)(2,1)S(1)} %shard_map.73.refs_3_, ...), custom_call_target="tpu_custom_call" | custom-call | flops 18874368 | bytes 1048576 | tf_op jit(solution)/shard_map/pallas_call | solution.py:27
  29.8 0.3 collective-permute-start.7
  30.1 3.0 %collective-permute-start.11 = (bf16[2,16,3456]{2,1,0:T(8,128)(2,1)S(1)}, bf16[2,16,3456]{2,1,0:T(8,128)(2,1)S(1)}, u32[]{:S(2)}, u32[]{:S(2)}) collective-permute-start(bf16[2,16,3456]{2,1,0:T(8,128)(2,1)S(1)} %get-tuple-element.70), channel_id=1, source_target_pairs={{0,4},{1,5},{2,6},{3,7},{4,0},{5,1},{6,2},{7,3},{8,12},{9,13},{10,... | collective-permute-start | bytes 663560 | tf_op jit(solution)/shard_map/ppermute | solution.py:331
  33.1 1.7 %collective-permute-start.12 = (bf16[2,16,3456]{2,1,0:T(8,128)(2,1)S(1)}, bf16[2,16,3456]{2,1,0:T(8,128)(2,1)S(1)}, u32[]{:S(2)}, u32[]{:S(2)}) collective-permute-start(bf16[2,16,3456]{2,1,0:T(8,128)(2,1)S(1)} %get-tuple-element.71), channel_id=1, source_target_pairs={{0,6},{1,7},{2,4},{3,5},{4,2},{5,3},{6,0},{7,1},{8,14},{9,15},{10,... | collective-permute-start | bytes 663560 | tf_op jit(solution)/shard_map/ppermute | solution.py:331
  34.9 0.1 collective-permute-start.10
  35.0 1.8 %shard_map.76 = (bf16[8,8,1536]{2,1,0:T(8,128)(2,1)S(1)}, bf16[8,8,1536]{2,1,0:T(8,128)(2,1)S(1)}) custom-call(s32[1]{0:T(128)} %bitcast.place.refs_0_, bf16[4,9,64,768]{3,2,1,0:T(8,128)(2,1)S(1)} %get-tuple-element.54.refs_1_, bf16[2,9,64,768]{3,2,1,0:T(8,128)(2,1)S(1)} %get-tuple-element.55.refs_2_, bf16[4,8,64,256]{3,2,1,0:T(8,128)(2,1)S(1)} %shard_map.73.refs_3_, ...), custom_call_target="tpu_custom_call" | custom-call | flops 18874368 | bytes 1048576 | tf_op jit(solution)/shard_map/pallas_call | solution.py:27
  36.8 0.1 collective-permute-start.8
  36.9 1.6 %shard_map.77 = (bf16[8,8,1152]{2,1,0:T(8,128)(2,1)S(1)}, bf16[8,8,1152]{2,1,0:T(8,128)(2,1)S(1)}) custom-call(s32[1]{0:T(128)} %bitcast.place.refs_0_, bf16[4,9,64,768]{3,2,1,0:T(8,128)(2,1)S(1)} %get-tuple-element.54.refs_1_, bf16[2,9,64,768]{3,2,1,0:T(8,128)(2,1)S(1)} %get-tuple-element.55.refs_2_, bf16[4,8,64,256]{3,2,1,0:T(8,128)(2,1)S(1)} %shard_map.73.refs_3_, ...), custom_call_target="tpu_custom_call" | custom-call | flops 18874368 | bytes 1048576 | tf_op jit(solution)/shard_map/pallas_call | solution.py:27
  38.5 0.0 collective-permute-done.7.refs_2_
  38.5 0.6 collective-permute-start.9
  39.1 1.0 %collective-permute-done.9.refs_6_ = bf16[8,8,1152]{2,1,0:T(8,128)(2,1)S(1)} collective-permute-done((bf16[8,8,1152]{2,1,0:T(8,128)(2,1)S(1)}, bf16[8,8,1152]{2,1,0:T(8,128)(2,1)S(1)}, u32[]{:S(2)}, u32[]{:S(2)}) %collective-permute-start.9) | collective-permute-done | bytes 147488 | tf_op jit(solution)/shard_map/ppermute | solution.py:331
  40.1 0.0 collective-permute-done.8.refs_4_
  40.1 0.0 collective-permute-done.11.refs_8_.refs_3_
  40.1 5.2 %collective-permute-done.12.refs_9_.refs_4_ = bf16[2,16,3456]{2,1,0:T(8,128)(2,1)S(1)} collective-permute-done((bf16[2,16,3456]{2,1,0:T(8,128)(2,1)S(1)}, bf16[2,16,3456]{2,1,0:T(8,128)(2,1)S(1)}, u32[]{:S(2)}, u32[]{:S(2)}) %collective-permute-start.12) | collective-permute-done | bytes 221216 | tf_op jit(solution)/shard_map/ppermute | solution.py:331
  45.3 1.4 %collective-permute-done.10.refs_7_.refs_2_ = bf16[2,16,3456]{2,1,0:T(8,128)(2,1)S(1)} collective-permute-done((bf16[2,16,3456]{2,1,0:T(8,128)(2,1)S(1)}, bf16[2,16,3456]{2,1,0:T(8,128)(2,1)S(1)}, u32[]{:S(2)}, u32[]{:S(2)}) %collective-permute-start.10) | collective-permute-done | bytes 221216 | tf_op jit(solution)/shard_map/ppermute | solution.py:331
  46.6 0.1 shard_map.78
  46.7 1.6 %collective-permute-start.14 = (bf16[2,8,3456]{2,1,0:T(8,128)(2,1)S(1)}, bf16[2,8,3456]{2,1,0:T(8,128)(2,1)S(1)}, u32[]{:S(2)}, u32[]{:S(2)}) collective-permute-start(bf16[2,8,3456]{2,1,0:T(8,128)(2,1)S(1)} %get-tuple-element.74), channel_id=1, source_target_pairs={{0,4},{1,5},{2,6},{3,7},{4,0},{5,1},{6,2},{7,3},{8,12},{9,13},{10,... | collective-permute-start | bytes 331784 | tf_op jit(solution)/shard_map/ppermute | solution.py:331
  48.4 0.3 collective-permute-start.15
  48.7 1.6 %collective-permute-start.13 = (bf16[2,8,3456]{2,1,0:T(8,128)(2,1)S(1)}, bf16[2,8,3456]{2,1,0:T(8,128)(2,1)S(1)}, u32[]{:S(2)}, u32[]{:S(2)}) collective-permute-start(bf16[2,8,3456]{2,1,0:T(8,128)(2,1)S(1)} %get-tuple-element.73.refs_5_), channel_id=1, source_target_pairs={{0,2},{1,3},{2,0},{3,1},{4,6},{5,7},{6,4},{7,5},{8,10},{9,11},{10,... | collective-permute-start | bytes 331784 | tf_op jit(solution)/shard_map/ppermute | solution.py:331
  50.3 0.1 shard_map.80
  50.4 2.6 %collective-permute-start.19 = (bf16[16,3456]{1,0:T(8,128)(2,1)S(1)}, bf16[16,3456]{1,0:T(8,128)(2,1)S(1)}, u32[]{:S(2)}, u32[]{:S(2)}) collective-permute-start(bf16[16,3456]{1,0:T(8,128)(2,1)S(1)} %bitcast.23), channel_id=1, source_target_pairs={{0,8},{1,9},{2,10},{3,11},{4,12},{5,13},{6,14},{7,15},{8,0},{9,1},... | collective-permute-start | bytes 331784 | tf_op jit(solution)/shard_map/ppermute | solution.py:331
  53.1 0.0 collective-permute-done.14.refs_3_
  53.1 2.0 %collective-permute-done.15.refs_4_ = bf16[2,8,3456]{2,1,0:T(8,128)(2,1)S(1)} collective-permute-done((bf16[2,8,3456]{2,1,0:T(8,128)(2,1)S(1)}, bf16[2,8,3456]{2,1,0:T(8,128)(2,1)S(1)}, u32[]{:S(2)}, u32[]{:S(2)}) %collective-permute-start.15) | collective-permute-done | bytes 110624 | tf_op jit(solution)/shard_map/ppermute | solution.py:331
  55.1 0.0 collective-permute-done.13.refs_2_
  55.1 0.1 shard_map.79
  55.2 3.0 %collective-permute-start.18 = (bf16[8,3456]{1,0:T(8,128)(2,1)S(1)}, bf16[8,3456]{1,0:T(8,128)(2,1)S(1)}, u32[]{:S(2)}, u32[]{:S(2)}) collective-permute-start(bf16[8,3456]{1,0:T(8,128)(2,1)S(1)} %bitcast.24), channel_id=1, source_target_pairs={{0,24},{1,25},{2,26},{3,27},{4,28},{5,29},{6,30},{7,31},{8,16},{9,... | collective-permute-start | bytes 165896 | tf_op jit(solution)/shard_map/ppermute | solution.py:336
  58.1 1.0 %collective-permute-start.17 = (bf16[8,3456]{1,0:T(8,128)(2,1)S(1)}, bf16[8,3456]{1,0:T(8,128)(2,1)S(1)}, u32[]{:S(2)}, u32[]{:S(2)}) collective-permute-start(bf16[8,3456]{1,0:T(8,128)(2,1)S(1)} %bitcast.25), channel_id=1, source_target_pairs={{0,8},{1,9},{2,10},{3,11},{4,12},{5,13},{6,14},{7,15},{8,0},{9,1},... | collective-permute-start | bytes 165896 | tf_op jit(solution)/shard_map/ppermute | solution.py:331
  59.1 0.6 collective-permute-start.16
  59.7 0.0 collective-permute-done.19
  59.7 1.6 %collective-permute-start.20 = (bf16[16,3456]{1,0:T(8,128)(2,1)S(1)}, bf16[16,3456]{1,0:T(8,128)(2,1)S(1)}, u32[]{:S(2)}, u32[]{:S(2)}) collective-permute-start(bf16[16,3456]{1,0:T(8,128)(2,1)S(1)} %fusion), channel_id=1, source_target_pairs={{0,16},{1,17},{2,18},{3,19},{4,20},{5,21},{6,22},{7,23},{8,24},{9,... | collective-permute-start | bytes 331784 | tf_op jit(solution)/shard_map/ppermute | solution.py:336
  61.3 2.0 %collective-permute-done.16 = bf16[8,3456]{1,0:T(8,128)(2,1)S(1)} collective-permute-done((bf16[8,3456]{1,0:T(8,128)(2,1)S(1)}, bf16[8,3456]{1,0:T(8,128)(2,1)S(1)}, u32[]{:S(2)}, u32[]{:S(2)}) %collective-permute-start.16) | collective-permute-done | bytes 55328 | tf_op jit(solution)/shard_map/ppermute | solution.py:336
  63.3 0.0 collective-permute-done.18
  63.3 0.0 collective-permute-done.17
  63.3 0.7 %add_add_fusion = f32[8,3456]{1,0:T(8,128)} fusion(bf16[8,3456]{1,0:T(8,128)(2,1)S(1)} %collective-permute-done.18, bf16[8,3456]{1,0:T(8,128)(2,1)S(1)} %collective-permute-done.17, bf16[8,3456]{1,0:T(8,128)(2,1)S(1)} %collective-permute-done.16, f32[1,8,3456]{2,1,0:T(8,128)S(1)} %get-tuple-element.76), kind=kLoop, calls=%fused_computation.3 | loop fusion | flops 221184 | bytes 387072 | tf_op jit(solution)/shard_map/add | solution.py:443
  64.0 0.5 collective-permute-done.20
  64.6 0.7 %convert_add_fusion = f32[16,3456]{1,0:T(8,128)} fusion(bf16[16,3456]{1,0:T(8,128)(2,1)S(1)} %collective-permute-done.20, bf16[16,3456]{1,0:T(8,128)(2,1)S(1)} %fusion), kind=kLoop, calls=%fused_computation.2 | loop fusion | flops 165888 | bytes 442368 | tf_op jit(solution)/shard_map/add | solution.py:434
  (4 shorter events, 0.0 us)
Async XLA Ops:
  0.6 1.2 %copy-start.1 = (bf16[1,4,16,64,128]{4,3,2,1,0:T(8,128)(2,1)S(1)}, bf16[1,4,16,64,128]{4,3,2,1,0:T(8,128)(2,1)}, u32[]{:S(2)}) copy-start(bf16[1,4,16,64,128]{4,3,2,1,0:T(8,128)(2,1)} %param.4) | copy-start | bytes 3145732
  1.9 1.3 %copy-start.2 = (bf16[1,2,8,32,256]{4,3,2,1,0:T(8,128)(2,1)S(1)}, bf16[1,2,8,32,256]{4,3,2,1,0:T(8,128)(2,1)}, u32[]{:S(2)}) copy-start(bf16[1,2,8,32,256]{4,3,2,1,0:T(8,128)(2,1)} %param.7) | copy-start | bytes 786436
  1.9 1.3 %copy-start.3 = (bf16[27,128,128]{2,1,0:T(8,128)(2,1)S(1)}, bf16[27,128,128]{2,1,0:T(8,128)(2,1)}, u32[]{:S(2)}) copy-start(bf16[27,128,128]{2,1,0:T(8,128)(2,1)} %param.5) | copy-start | bytes 2654212
  1.9 10.6 %collective-permute-start = (bf16[1,16,64,128]{3,2,1,0:T(8,128)(2,1)S(1)}, bf16[1,16,64,128]{3,2,1,0:T(8,128)(2,1)S(1)}, u32[]{:S(2)}, u32[]{:S(2)}) collective-permute-start(bf16[1,16,64,128]{3,2,1,0:T(8,128)(2,1)S(1)} %get-tuple-element.42), channel_id=1, source_target_pairs={{0,1},{1,0},{2,3},{3,2},{4,5},{5,4},{6,7},{7,6},{8,9},{9,8},{10,11... | collective-permute-start | bytes 786440 | tf_op jit(solution)/shard_map/ppermute | solution.py:43
  2.4 10.1 %collective-permute-start.1 = (bf16[1,16,64,128]{3,2,1,0:T(8,128)(2,1)S(1)}, bf16[1,16,64,128]{3,2,1,0:T(8,128)(2,1)S(1)}, u32[]{:S(2)}, u32[]{:S(2)}) collective-permute-start(bf16[1,16,64,128]{3,2,1,0:T(8,128)(2,1)S(1)} %get-tuple-element.43), channel_id=1, source_target_pairs={{1,2},{3,4},{5,6},{7,8},{9,10},{11,12},{13,14},{2,1},{4,3},{6,5},{... | collective-permute-start | bytes 786440 | tf_op jit(solution)/shard_map/ppermute | solution.py:43
  7.8 10.0 %copy-start = (bf16[27,128,256]{2,1,0:T(8,128)(2,1)S(1)}, bf16[27,128,256]{2,1,0:T(8,128)(2,1)}, u32[]{:S(2)}) copy-start(bf16[27,128,256]{2,1,0:T(8,128)(2,1)} %refs_1_.1) | copy-start | bytes 5308420
  7.8 11.2 %collective-permute-start.4 = (bf16[1,8,32,256]{3,2,1,0:T(8,128)(2,1)S(1)}, bf16[1,8,32,256]{3,2,1,0:T(8,128)(2,1)S(1)}, u32[]{:S(2)}, u32[]{:S(2)}) collective-permute-start(bf16[1,8,32,256]{3,2,1,0:T(8,128)(2,1)S(1)} %get-tuple-element.51), channel_id=1, source_target_pairs={{0,1},{1,0},{2,3},{3,2},{4,5},{5,4},{6,7},{7,6},{8,9},{9,8},{10,11... | collective-permute-start | bytes 393224 | tf_op jit(solution)/shard_map/ppermute | solution.py:43
  11.9 7.2 %collective-permute-start.5 = (bf16[1,8,32,256]{3,2,1,0:T(8,128)(2,1)S(1)}, bf16[1,8,32,256]{3,2,1,0:T(8,128)(2,1)S(1)}, u32[]{:S(2)}, u32[]{:S(2)}) collective-permute-start(bf16[1,8,32,256]{3,2,1,0:T(8,128)(2,1)S(1)} %get-tuple-element.52), channel_id=1, source_target_pairs={{1,2},{3,4},{5,6},{7,8},{9,10},{11,12},{13,14},{2,1},{4,3},{6,5},{... | collective-permute-start | bytes 393224 | tf_op jit(solution)/shard_map/ppermute | solution.py:43
  14.0 5.0 %collective-permute-start.2 = (bf16[2,8,32,128]{3,2,1,0:T(8,128)(2,1)S(1)}, bf16[2,8,32,128]{3,2,1,0:T(8,128)(2,1)S(1)}, u32[]{:S(2)}, u32[]{:S(2)}) collective-permute-start(bf16[2,8,32,128]{3,2,1,0:T(8,128)(2,1)S(1)} %get-tuple-element.47), channel_id=1, source_target_pairs={{0,1},{1,0},{2,3},{3,2},{4,5},{5,4},{6,7},{7,6},{8,9},{9,8},{10,11... | collective-permute-start | bytes 393224 | tf_op jit(solution)/shard_map/ppermute | solution.py:43
  17.0 2.1 %collective-permute-start.3 = (bf16[2,8,32,128]{3,2,1,0:T(8,128)(2,1)S(1)}, bf16[2,8,32,128]{3,2,1,0:T(8,128)(2,1)S(1)}, u32[]{:S(2)}, u32[]{:S(2)}) collective-permute-start(bf16[2,8,32,128]{3,2,1,0:T(8,128)(2,1)S(1)} %get-tuple-element.48), channel_id=1, source_target_pairs={{1,2},{3,4},{5,6},{7,8},{9,10},{11,12},{13,14},{2,1},{4,3},{6,5},{... | collective-permute-start | bytes 393224 | tf_op jit(solution)/shard_map/ppermute | solution.py:43
  22.1 6.4 %collective-permute-start.6 = (bf16[8,16,3456]{2,1,0:T(8,128)(2,1)S(1)}, bf16[8,16,3456]{2,1,0:T(8,128)(2,1)S(1)}, u32[]{:S(2)}, u32[]{:S(2)}) collective-permute-start(bf16[8,16,3456]{2,1,0:T(8,128)(2,1)S(1)} %get-tuple-element.61.refs_4_), channel_id=1, source_target_pairs={{0,1},{1,0},{2,3},{3,2},{4,5},{5,4},{6,7},{7,6},{8,9},{9,8},{10,11... | collective-permute-start | bytes 2654216 | tf_op jit(solution)/shard_map/ppermute | solution.py:331
  29.8 8.7 %collective-permute-start.7 = (bf16[8,8,768]{2,1,0:T(8,128)(2,1)S(1)}, bf16[8,8,768]{2,1,0:T(8,128)(2,1)S(1)}, u32[]{:S(2)}, u32[]{:S(2)}) collective-permute-start(bf16[8,8,768]{2,1,0:T(8,128)(2,1)S(1)} %get-tuple-element.65.refs_4_), channel_id=1, source_target_pairs={{0,1},{1,0},{2,3},{3,2},{4,5},{5,4},{6,7},{7,6},{8,9},{9,8},{10,11... | collective-permute-start | bytes 294920 | tf_op jit(solution)/shard_map/ppermute | solution.py:331
  30.1 9.9 %collective-permute-start.11 = (bf16[2,16,3456]{2,1,0:T(8,128)(2,1)S(1)}, bf16[2,16,3456]{2,1,0:T(8,128)(2,1)S(1)}, u32[]{:S(2)}, u32[]{:S(2)}) collective-permute-start(bf16[2,16,3456]{2,1,0:T(8,128)(2,1)S(1)} %get-tuple-element.70), channel_id=1, source_target_pairs={{0,4},{1,5},{2,6},{3,7},{4,0},{5,1},{6,2},{7,3},{8,12},{9,13},{10,... | collective-permute-start | bytes 663560 | tf_op jit(solution)/shard_map/ppermute | solution.py:331
  33.1 12.2 %collective-permute-start.12 = (bf16[2,16,3456]{2,1,0:T(8,128)(2,1)S(1)}, bf16[2,16,3456]{2,1,0:T(8,128)(2,1)S(1)}, u32[]{:S(2)}, u32[]{:S(2)}) collective-permute-start(bf16[2,16,3456]{2,1,0:T(8,128)(2,1)S(1)} %get-tuple-element.71), channel_id=1, source_target_pairs={{0,6},{1,7},{2,4},{3,5},{4,2},{5,3},{6,0},{7,1},{8,14},{9,15},{10,... | collective-permute-start | bytes 663560 | tf_op jit(solution)/shard_map/ppermute | solution.py:331
  34.9 11.8 %collective-permute-start.10 = (bf16[2,16,3456]{2,1,0:T(8,128)(2,1)S(1)}, bf16[2,16,3456]{2,1,0:T(8,128)(2,1)S(1)}, u32[]{:S(2)}, u32[]{:S(2)}) collective-permute-start(bf16[2,16,3456]{2,1,0:T(8,128)(2,1)S(1)} %get-tuple-element.63.refs_4_), channel_id=1, source_target_pairs={{0,2},{1,3},{2,0},{3,1},{4,6},{5,7},{6,4},{7,5},{8,10},{9,11},{10,... | collective-permute-start | bytes 663560 | tf_op jit(solution)/shard_map/ppermute | solution.py:331
  36.8 3.3 %collective-permute-start.8 = (bf16[8,8,1536]{2,1,0:T(8,128)(2,1)S(1)}, bf16[8,8,1536]{2,1,0:T(8,128)(2,1)S(1)}, u32[]{:S(2)}, u32[]{:S(2)}) collective-permute-start(bf16[8,8,1536]{2,1,0:T(8,128)(2,1)S(1)} %get-tuple-element.67.refs_4_), channel_id=1, source_target_pairs={{0,1},{1,0},{2,3},{3,2},{4,5},{5,4},{6,7},{7,6},{8,9},{9,8},{10,11... | collective-permute-start | bytes 589832 | tf_op jit(solution)/shard_map/ppermute | solution.py:331
  38.5 1.6 %collective-permute-start.9 = (bf16[8,8,1152]{2,1,0:T(8,128)(2,1)S(1)}, bf16[8,8,1152]{2,1,0:T(8,128)(2,1)S(1)}, u32[]{:S(2)}, u32[]{:S(2)}) collective-permute-start(bf16[8,8,1152]{2,1,0:T(8,128)(2,1)S(1)} %get-tuple-element.69), channel_id=1, source_target_pairs={{0,1},{1,0},{2,3},{3,2},{4,5},{5,4},{6,7},{7,6},{8,9},{9,8},{10,11... | collective-permute-start | bytes 442376 | tf_op jit(solution)/shard_map/ppermute | solution.py:331
  46.7 6.3 %collective-permute-start.14 = (bf16[2,8,3456]{2,1,0:T(8,128)(2,1)S(1)}, bf16[2,8,3456]{2,1,0:T(8,128)(2,1)S(1)}, u32[]{:S(2)}, u32[]{:S(2)}) collective-permute-start(bf16[2,8,3456]{2,1,0:T(8,128)(2,1)S(1)} %get-tuple-element.74), channel_id=1, source_target_pairs={{0,4},{1,5},{2,6},{3,7},{4,0},{5,1},{6,2},{7,3},{8,12},{9,13},{10,... | collective-permute-start | bytes 331784 | tf_op jit(solution)/shard_map/ppermute | solution.py:331
  48.4 6.7 %collective-permute-start.15 = (bf16[2,8,3456]{2,1,0:T(8,128)(2,1)S(1)}, bf16[2,8,3456]{2,1,0:T(8,128)(2,1)S(1)}, u32[]{:S(2)}, u32[]{:S(2)}) collective-permute-start(bf16[2,8,3456]{2,1,0:T(8,128)(2,1)S(1)} %get-tuple-element.75), channel_id=1, source_target_pairs={{0,6},{1,7},{2,4},{3,5},{4,2},{5,3},{6,0},{7,1},{8,14},{9,15},{10,... | collective-permute-start | bytes 331784 | tf_op jit(solution)/shard_map/ppermute | solution.py:331
  48.7 6.4 %collective-permute-start.13 = (bf16[2,8,3456]{2,1,0:T(8,128)(2,1)S(1)}, bf16[2,8,3456]{2,1,0:T(8,128)(2,1)S(1)}, u32[]{:S(2)}, u32[]{:S(2)}) collective-permute-start(bf16[2,8,3456]{2,1,0:T(8,128)(2,1)S(1)} %get-tuple-element.73.refs_5_), channel_id=1, source_target_pairs={{0,2},{1,3},{2,0},{3,1},{4,6},{5,7},{6,4},{7,5},{8,10},{9,11},{10,... | collective-permute-start | bytes 331784 | tf_op jit(solution)/shard_map/ppermute | solution.py:331
  50.4 9.3 %collective-permute-start.19 = (bf16[16,3456]{1,0:T(8,128)(2,1)S(1)}, bf16[16,3456]{1,0:T(8,128)(2,1)S(1)}, u32[]{:S(2)}, u32[]{:S(2)}) collective-permute-start(bf16[16,3456]{1,0:T(8,128)(2,1)S(1)} %bitcast.23), channel_id=1, source_target_pairs={{0,8},{1,9},{2,10},{3,11},{4,12},{5,13},{6,14},{7,15},{8,0},{9,1},... | collective-permute-start | bytes 331784 | tf_op jit(solution)/shard_map/ppermute | solution.py:331
  55.2 8.2 %collective-permute-start.18 = (bf16[8,3456]{1,0:T(8,128)(2,1)S(1)}, bf16[8,3456]{1,0:T(8,128)(2,1)S(1)}, u32[]{:S(2)}, u32[]{:S(2)}) collective-permute-start(bf16[8,3456]{1,0:T(8,128)(2,1)S(1)} %bitcast.24), channel_id=1, source_target_pairs={{0,24},{1,25},{2,26},{3,27},{4,28},{5,29},{6,30},{7,31},{8,16},{9,... | collective-permute-start | bytes 165896 | tf_op jit(solution)/shard_map/ppermute | solution.py:336
  58.1 5.2 %collective-permute-start.17 = (bf16[8,3456]{1,0:T(8,128)(2,1)S(1)}, bf16[8,3456]{1,0:T(8,128)(2,1)S(1)}, u32[]{:S(2)}, u32[]{:S(2)}) collective-permute-start(bf16[8,3456]{1,0:T(8,128)(2,1)S(1)} %bitcast.25), channel_id=1, source_target_pairs={{0,8},{1,9},{2,10},{3,11},{4,12},{5,13},{6,14},{7,15},{8,0},{9,1},... | collective-permute-start | bytes 165896 | tf_op jit(solution)/shard_map/ppermute | solution.py:331
  59.1 4.2 %collective-permute-start.16 = (bf16[8,3456]{1,0:T(8,128)(2,1)S(1)}, bf16[8,3456]{1,0:T(8,128)(2,1)S(1)}, u32[]{:S(2)}, u32[]{:S(2)}) collective-permute-start(bf16[8,3456]{1,0:T(8,128)(2,1)S(1)} %convert_bitcast_fusion), channel_id=1, source_target_pairs={{0,16},{1,17},{2,18},{3,19},{4,20},{5,21},{6,22},{7,23},{8,24},{9,... | collective-permute-start | bytes 165896 | tf_op jit(solution)/shard_map/ppermute | solution.py:336
  59.7 4.8 %collective-permute-start.20 = (bf16[16,3456]{1,0:T(8,128)(2,1)S(1)}, bf16[16,3456]{1,0:T(8,128)(2,1)S(1)}, u32[]{:S(2)}, u32[]{:S(2)}) collective-permute-start(bf16[16,3456]{1,0:T(8,128)(2,1)S(1)} %fusion), channel_id=1, source_target_pairs={{0,16},{1,17},{2,18},{3,19},{4,20},{5,21},{6,22},{7,23},{8,24},{9,... | collective-permute-start | bytes 331784 | tf_op jit(solution)/shard_map/ppermute | solution.py:336

commit v6 on v5

--- a/solution.py
+++ b/solution.py
@@ -10,8 +10,8 @@
 F32 = jnp.float32
 BF16 = jnp.bfloat16
 COST = 64
+SPLIT = 4
 SMALL = 50
-PARTS = (range(0, 2), range(2, 6), range(6, 9))
 VMEM = pl.BlockSpec(memory_space=pltpu.VMEM)
 SMEM = pl.BlockSpec(memory_space=pltpu.SMEM)
 
@@ -257,7 +257,7 @@
     return [taps[k : k + 2] for k in range(0, len(taps), 2)]
 
 
-def coarse_terms(place, wide3, halo3, delta, keep, send=None, *, order):
+def coarse_terms(place, wide3, halo3, delta, *outs, orders):
     planes, cy, cz, wide = delta.shape
     own = wide3.shape[0]
     span = wide3.shape[-1]
@@ -273,7 +273,13 @@
         for p in range(own):
             pieces = jnp.concatenate([piece(p, tap) for tap in group], axis=1)
             total = plus(total, tap_dot(delta[p + 1].reshape(cy * cz, wide), pieces))
-        put_term(total, group[0] * span, place, order, keep, send)
+        for k, tap in enumerate(group):
+            side = int(tap >= SPLIT)
+            keep, send = outs[side], None
+            if len(outs) == 4:
+                keep, send = outs[2 * side : 2 * side + 2]
+            term = total[:, k * span : (k + 1) * span]
+            put_term(term, (tap - side * SPLIT) * span, place, orders[side], keep, send)
 
 
 def fine_deltas(coarse_delta, kernel, slope, slope_edge, delta, wide3, spread):
@@ -305,7 +311,7 @@
             delta[at] = (both * ref[index].astype(F32)).astype(BF16)
 
 
-def fine_terms(place, wide6, halo6, delta, keep, send=None, *, order, taps):
+def fine_terms(place, wide6, halo6, delta, *outs, order):
     planes, half, fz, double = delta.shape
     chan = double // 2
     three = 3 * chan
@@ -316,14 +322,19 @@
         some = ref[at, pair : pair + half, :, parity * three : (parity + 1) * three]
         return some.reshape(half * fz, three)
 
-    for group in in_twos(taps):
+    for group in in_twos(range(9)):
         total = None
         for p in range(planes):
             for q in range(2):
                 rows = delta[p, :, :, q * chan : (q + 1) * chan].reshape(half * fz, chan)
                 pieces = jnp.concatenate([piece(p, q, tap) for tap in group], axis=1)
                 total = plus(total, tap_dot(rows, pieces))
-        put_term(total, (group[0] - taps[0]) * three, place, order, keep, send)
+        for k, tap in enumerate(group):
+            keep, send = outs[tap // 3], None
+            if len(outs) == 6:
+                keep, send = outs[2 * (tap // 3) : 2 * (tap // 3) + 2]
+            term = total[:, k * three : (k + 1) * three]
+            put_term(term, tap % 3 * three, place, order, keep, send)
 
 
 def swap(value, bit):
@@ -349,8 +360,7 @@
     return [bit for group in exchange_groups(count) for bit in group] + [count // 2]
 
 
-def owners_in_order(count):
-    bits = exchange_bits(count)
+def owners_in_order(bits, count):
     return [
         sum(bit for k, bit in enumerate(bits) if at >> (len(bits) - 1 - k) & 1)
         for at in range(count // 2)
@@ -370,12 +380,12 @@
     return keep, lax.dynamic_index_in_dim(parts, 1 - mine, 0, keepdims=False)
 
 
-def sided(terms, count):
+def sided(terms, sequence, count):
     if len(terms) == 2:
         return terms
     bits = count.bit_length() - 1
     parts = terms[0].reshape((2,) * bits + (terms[0].shape[0] // count, -1))
-    axes = [bits - bit.bit_length() for bit in [1] + exchange_bits(count)]
+    axes = [bits - bit.bit_length() for bit in [1] + sequence]
     sides = pick(parts.transpose(tuple(axes) + (bits, bits + 1)), 1)
     return [side.reshape((-1,) + side.shape[-2:]) for side in sides]
 
@@ -441,6 +451,53 @@
     keep, send = (kept[0].astype(BF16), sends[bit][0])
     near, cross, other = (swap(send, bit), swap_sample(send, bit), swap_sample(keep))
     return (keep.astype(F32) + other.astype(F32)) + (near.astype(F32) + cross.astype(F32))
+
+
+def pack_body(place, coarse_kept, coarse_got, *refs, bit):
+    pieces, (send, both) = (refs[:-2], refs[-2:])
+    mine = place[0] // bit % 2
+    sums = []
+    for side in (mine, 1 - mine):
+        total = None
+        for piece in pieces:
+            total = plus(total, piece[side].astype(F32))
+        sums.append(total)
+    send[...] = sums[1].astype(BF16)
+    coarse = coarse_kept[0] + coarse_got[0].astype(F32)
+    both[...] = jnp.concatenate([coarse, sums[0]], axis=0).astype(BF16)
+
+
+def result_body(both, other, near, cross, fine, coarse):
+    total = both[...].astype(F32) + other[...].astype(F32)
+    rows = coarse.shape[0]
+    coarse[...] = total[:rows]
+    fine[...] = total[rows:] + (near[...].astype(F32) + cross[...].astype(F32))
+
+
+def last_together(place, coarse_early, coarse_kept, fine_pieces):
+    bit = lax.axis_size("space") // 2
+    coarse_got = swap(coarse_early[bit], bit)
+    fine_rows, columns = fine_pieces[0].shape[1:]
+    coarse_rows = coarse_kept.shape[1]
+    shape = jax.ShapeDtypeStruct
+    send, both = kernel_call(
+        functools.partial(pack_body, bit=bit),
+        [place, coarse_kept, coarse_got] + fine_pieces,
+        [shape((fine_rows, columns), BF16), shape((coarse_rows + fine_rows, columns), BF16)],
+        [],
+        0,
+        8,
+        scalars=1,
+    )
+    near, cross, other = (swap(send, bit), swap_sample(send, bit), swap_sample(both))
+    return kernel_call(
+        result_body,
+        [both, other, near, cross],
+        [shape((fine_rows, columns), F32), shape((coarse_rows, columns), F32)],
+        [],
+        0,
+        8,
+    )
 
 
 def shards(volumes, fine_kernel, coarse_kernel, cotangent):
@@ -526,19 +583,32 @@
         16,
         scalars=1,
     )
-    order = owners_in_order(count)
+    bits = exchange_bits(count)
+    order = owners_in_order(bits, count)
     steps = exchange_groups(count) + [[count // 2]]
+    turned = [bit for group in steps for bit in reversed(group)]
+    border = SPLIT * 3 * chan
     terms = kernel_call(
-        functools.partial(coarse_terms, order=order),
+        functools.partial(
+            coarse_terms, orders=(owners_in_order(bits, count), owners_in_order(turned, count))
+        ),
         [place, wide3, halo3, coarse_delta],
-        term_shapes(wide, 27 * chan, count),
+        term_shapes(wide, border, count) + term_shapes(wide, 27 * chan - border, count),
         [],
         coarse_flops,
         16,
         scalars=1,
     )
-    keep, send = sided(terms, count)
-    early, coarse_kept = fold(place, [[keep, swap(send, 1)]], steps[0])
+    halves = []
+    for side, sequence in enumerate((bits, turned)):
+        some = terms[side * len(terms) // 2 : (side + 1) * len(terms) // 2]
+        keep, send = sided(some, sequence, count)
+        halves.append([keep, swap(send, 1)])
+    sends = []
+    if len(bits) > 1:
+        for side, sequence in enumerate((bits, turned)):
+            sends.append(fold(place, [halves[side]], sequence[:1]))
+    early = [item for send, _ in sends for item in send.values()]
     (fine_delta,) = kernel_call(
         fine_deltas,
         [coarse_delta, coarse_kernel, slope, slope_edge],
@@ -548,35 +618,38 @@
         16,
         after=[terms[-1]],
     )
-    fine_parts = []
-    before = list(early.values())[:1]
-    for part in PARTS:
-        fine_parts.append(
-            kernel_call(
-                functools.partial(fine_terms, order=order, taps=part),
-                [place, wide6, halo6, fine_delta],
-                term_shapes(chan, len(part) * 3 * chan, count),
-                [],
-                fine_flops // 3,
-                16,
-                scalars=1,
-                after=before,
-            )
-        )
-        before = [fine_parts[-1][-1]]
-    got = coarse_got = received(early, coarse_kept)
+    terms = kernel_call(
+        functools.partial(fine_terms, order=order),
+        [place, wide6, halo6, fine_delta],
+        term_shapes(chan, 9 * chan, count) * 3,
+        [],
+        fine_flops,
+        16,
+        scalars=1,
+        after=early,
+    )
+    each = len(terms) // 3
+    fine_parts = [terms[k * each : (k + 1) * each] for k in range(3)]
+    halves = [received(*send) for send in sends] or halves
+    second = []
+    for k in range(1, len(bits) - 1):
+        sends = [fold(place, [halves[side]], [seq[k]]) for side, seq in enumerate((bits, turned))]
+        second = second or [item for send, _ in sends for item in send.values()]
+        halves = [received(*send) for send in sends]
+    early, coarse_kept = fold(place, halves, bits[-1:])
     pieces = []
     for part in fine_parts:
-        keep, send = sided(part, count)
+        keep, send = sided(part, bits, count)
         pieces.append([keep, swap(send, 1)])
-    late, fine_kept = fold(place, pieces, steps[0], coarse_got[1:])
-    for group in steps[1:]:
-        early, coarse_kept = fold(place, [got], group, [late[steps[0][0]]])
-        got = received(early, coarse_kept)
-    coarse_grad = last_sum(early, coarse_kept)
-    for group in steps[1:]:
+    late, fine_kept = fold(place, pieces, steps[0], second)
+    for group in steps[1:-1]:
         late, fine_kept = fold(place, [received(late, fine_kept)], group)
-    fine_grad = last_direct(late, fine_kept)
+    fine_got = received(late, fine_kept)
+    if chan // count % 8 or lax.axis_size("sample") != 2:
+        coarse_grad = last_sum(early, coarse_kept)
+        fine_grad = last_direct(*fold(place, [fine_got], steps[-1]))
+    else:
+        fine_grad, coarse_grad = last_together(place, early, coarse_kept, fine_got)
     return (out[None], fine_grad, coarse_grad)
 
 

time: 65.5 us -> 62.5 us (0.954)
  starting transfers between devices: 32 us -> 30.5 us
  other arithmetic: 1.43 us -> 0 us
    ppermute x3 -> x2, starting transfers between devices: 5.12 us -> 3.27 us  [swap_sample(): lax.ppermute(value, ('sample', 'space'), [(s * count + i, (1 - s) * count...]
    add x2 -> x0, other arithmetic: 1.39 us -> none  [the longest x1 0.71 us: last_sum(): return base.astype(F32) + swap_sample(base).astype(F32)]
    ppermute x12 -> x14, waiting for transfers between devices: 9.65 us -> 8.51 us  [swap(): return lax.ppermute(value, 'space', [(i, i ^ bit) for i in range(count)])]
    ppermute x3 -> x2, waiting for transfers between devices: 2.57 us -> 3.37 us  [swap_sample(): lax.ppermute(value, ('sample', 'space'), [(s * count + i, (1 - s) * count...]
    pallas_call x13 -> x15, Pallas kernels: 17.4 us -> 17.8 us  [kernel_call(): pl.pallas_call(inner, out_shape=outs, in_specs=specs, out_specs=[VMEM] *...]
    ppermute x12 -> x14, starting transfers between devices: 17.2 us -> 17.6 us  [swap(): return lax.ppermute(value, 'space', [(i, i ^ bit) for i in range(count)])]
  transfers between devices with their start and end apart: 21 -> 22, of which waited for: 6 -> 9; matrix products, arithmetic and copies ran while one was open for 1% -> 0% of each run, Pallas kernels for 20% -> 22%
where the time goes in v6:
time: 62.5 us; the launch traced here: 62.3 us
  starting transfers between devices  30.5 us (49%)
  Pallas kernels  17.8 us (28%)
  waiting for transfers between devices  11.9 us (19%)
  local copies, waits for them, and re-layouts  1.23 us (2%)
  between operations  0.84 us (1%)
    pallas_call x15, Pallas kernels, kernel_call(): pl.pallas_call(inner, out_shape=outs, in_specs=specs, out_specs=[VMEM] *...  17.8 us
    ppermute x14, starting transfers between devices, swap(): return lax.ppermute(value, 'space', [(i, i ^ bit) for i in range(count)])  17.6 us
    ppermute x14, waiting for transfers between devices, swap(): return lax.ppermute(value, 'space', [(i, i ^ bit) for i in range(count)])  8.51 us
    ppermute x3, starting transfers between devices, exchange(): lax.ppermute(to_pair, 'space', pair)  7.54 us
    ppermute x2, waiting for transfers between devices, swap_sample(): lax.ppermute(value, ('sample', 'space'), [(s * count + i, (1 - s) * count...  3.37 us
    ppermute x2, starting transfers between devices, swap_sample(): lax.ppermute(value, ('sample', 'space'), [(s * count + i, (1 - s) * count...  3.27 us
    ppermute x3, starting transfers between devices, exchange(): lax.ppermute(to_next, 'space', across)  2.16 us
  transfers between devices with their start and end apart: 22, of which 9 were waited for; matrix products, arithmetic and copies ran while one was open for 0% of the time, Pallas kernels for 22%

profile of v6, /device:TPU:0, one launch (start us, length us, event | category | flops | bytes accessed | tf_op | source)
XLA Modules:
  0.0 62.3 jit_solution(4319430535374563681)
XLA Ops:
  0.6 0.0 copy-start.1
  0.6 1.2 %copy-done.1 = bf16[1,4,16,64,128]{4,3,2,1,0:T(8,128)(2,1)S(1)} copy-done((bf16[1,4,16,64,128]{4,3,2,1,0:T(8,128)(2,1)S(1)}, bf16[1,4,16,64,128]{4,3,2,1,0:T(8,128)(2,1)}, u32[]{:S(2)}) %copy-start.1) | copy-done | bytes 1048600
  1.9 0.1 shard_map.67
  1.9 0.5 collective-permute-start
  2.4 0.7 %collective-permute-start.1 = (bf16[1,16,64,128]{3,2,1,0:T(8,128)(2,1)S(1)}, bf16[1,16,64,128]{3,2,1,0:T(8,128)(2,1)S(1)}, u32[]{:S(2)}, u32[]{:S(2)}) collective-permute-start(bf16[1,16,64,128]{3,2,1,0:T(8,128)(2,1)S(1)} %get-tuple-element.51), channel_id=1, source_target_pairs={{1,2},{3,4},{5,6},{7,8},{9,10},{11,12},{13,14},{2,1},{4,3},{6,5},{... | collective-permute-start | bytes 786440 | tf_op jit(solution)/shard_map/ppermute | solution.py:43
  3.1 0.0 copy-done.2
  3.1 0.0 copy-done.3
  3.1 4.6 %shard_map.68 = (bf16[4,9,64,768]{3,2,1,0:T(8,128)(2,1)S(1)}, bf16[3,2,768,256]{3,2,1,0:T(8,128)(2,1)S(1)}, f32[2,512,256]{2,1,0:T(8,128)S(1)}, f32[2,8,64,128]{...) custom-call(s32[1]{0:T(128)} %bitcast.place.refs_0_, ...), custom_call_target="tpu_custom_call" | custom-call | flops 56623104 | bytes 1048576 | tf_op jit(solution)/shard_map/pallas_call | solution.py:27
  7.8 0.0 copy-start
  7.8 4.1 %collective-permute-start.4 = (bf16[1,8,32,256]{3,2,1,0:T(8,128)(2,1)S(1)}, bf16[1,8,32,256]{3,2,1,0:T(8,128)(2,1)S(1)}, u32[]{:S(2)}, u32[]{:S(2)}) collective-permute-start(bf16[1,8,32,256]{3,2,1,0:T(8,128)(2,1)S(1)} %get-tuple-element.59), channel_id=1, source_target_pairs={{0,1},{1,0},{2,3},{3,2},{4,5},{5,4},{6,7},{7,6},{8,9},{9,8},{10,11... | collective-permute-start | bytes 393224 | tf_op jit(solution)/shard_map/ppermute | solution.py:43
  11.9 0.7 %collective-permute-start.5 = (bf16[1,8,32,256]{3,2,1,0:T(8,128)(2,1)S(1)}, bf16[1,8,32,256]{3,2,1,0:T(8,128)(2,1)S(1)}, u32[]{:S(2)}, u32[]{:S(2)}) collective-permute-start(bf16[1,8,32,256]{3,2,1,0:T(8,128)(2,1)S(1)} %get-tuple-element.60), channel_id=1, source_target_pairs={{1,2},{3,4},{5,6},{7,8},{9,10},{11,12},{13,14},{2,1},{4,3},{6,5},{... | collective-permute-start | bytes 393224 | tf_op jit(solution)/shard_map/ppermute | solution.py:43
  12.5 0.0 collective-permute-done.refs_1_
  12.5 0.0 collective-permute-done.1.refs_2_
  12.5 1.5 %shard_map.69 = (bf16[2,9,64,768]{3,2,1,0:T(8,128)(2,1)S(1)}, bf16[2,8,32,128]{3,2,1,0:T(8,128)(2,1)S(1)}, bf16[2,8,64,256]{3,2,1,0:T(8,128)(2,1)S(1)}, bf16[2,8...) custom-call(s32[1]{0:T(128)} %bitcast.place.refs_0_, bf16[1,16,64,128]{3,2,1,0:T(8,128)(2,1)S(1)} %collective-permute-done.refs_1_, ...), custom_call_target="tpu_custom_call" | custom-call | flops 9437184 | bytes 1048576 | tf_op jit(solution)/shard_map/pallas_call | solution.py:27
  14.0 2.9 %collective-permute-start.2 = (bf16[2,8,32,128]{3,2,1,0:T(8,128)(2,1)S(1)}, bf16[2,8,32,128]{3,2,1,0:T(8,128)(2,1)S(1)}, u32[]{:S(2)}, u32[]{:S(2)}) collective-permute-start(bf16[2,8,32,128]{3,2,1,0:T(8,128)(2,1)S(1)} %get-tuple-element.55), channel_id=1, source_target_pairs={{0,1},{1,0},{2,3},{3,2},{4,5},{5,4},{6,7},{7,6},{8,9},{9,8},{10,11... | collective-permute-start | bytes 393224 | tf_op jit(solution)/shard_map/ppermute | solution.py:43
  17.0 0.8 %collective-permute-start.3 = (bf16[2,8,32,128]{3,2,1,0:T(8,128)(2,1)S(1)}, bf16[2,8,32,128]{3,2,1,0:T(8,128)(2,1)S(1)}, u32[]{:S(2)}, u32[]{:S(2)}) collective-permute-start(bf16[2,8,32,128]{3,2,1,0:T(8,128)(2,1)S(1)} %get-tuple-element.56), channel_id=1, source_target_pairs={{1,2},{3,4},{5,6},{7,8},{9,10},{11,12},{13,14},{2,1},{4,3},{6,5},{... | collective-permute-start | bytes 393224 | tf_op jit(solution)/shard_map/ppermute | solution.py:43
  17.8 0.0 copy-done
  17.8 1.2 %shard_map.70 = (bf16[2,10,32,384]{3,2,1,0:T(8,128)(2,1)S(1)}, f32[4,256,256]{2,1,0:T(8,128)S(1)}) custom-call(bf16[2,8,32,128]{3,2,1,0:T(8,128)(2,1)S(1)} %get-tuple-element.57.refs_0_, bf16[3,1152,256]{2,1,0:T(8,128)(2,1)S(1)} %bitcast.6), custom_call_target="tpu_custom_call" | custom-call | flops 14155776 | bytes 1048576 | tf_op jit(solution)/shard_map/pallas_call | solution.py:27
  19.0 0.0 collective-permute-done.4.refs_6_
  19.0 0.0 collective-permute-done.5.refs_7_
  19.0 0.0 collective-permute-done.2.refs_1_
  19.0 0.0 collective-permute-done.3.refs_2_
  19.0 1.9 %shard_map.71 = (bf16[4,10,32,384]{3,2,1,0:T(8,128)(2,1)S(1)}, bf16[2,8,32,256]{3,2,1,0:T(8,128)(2,1)}, bf16[4,8,32,256]{3,2,1,0:T(8,128)(2,1)S(1)}) custom-call(s32[1]{0:T(128)} %bitcast.place.refs_0_, bf16[2,8,32,128]{3,2,1,0:T(8,128)(2,1)S(1)} %collective-permute-done.2.refs_1_, bf16[2,8,32,128]{3,2,1,0:T(8,128)(2,1)S(1)} %collective-permute-done.3.refs_2_, ...), custom_call_target="tpu_custom_call" | custom-call | flops 14155776 | bytes 1048576 | tf_op jit(solution)/shard_map/pallas_call | solution.py:27
  21.0 1.2 %shard_map.72 = (bf16[8,16,1536]{2,1,0:T(8,128)(2,1)S(1)}, bf16[8,16,1536]{2,1,0:T(8,128)(2,1)S(1)}, bf16[8,16,1920]{2,1,0:T(8,128)(2,1)S(1)}, bf16[8,16,1920]{2,1,0:T(8,128)(2,1)S(1)}) custom-call(s32[1]{0:T(128)} %bitcast.place.refs_0_, bf16[2,10,32,384]{3,2,1,0:T(8,128)(2,1)S(1)} %get-tuple-element.62.refs_1_, ...), custom_call_target="tpu_custom_call" | custom-call | flops 14155776 | bytes 1048576 | tf_op jit(solution)/shard_map/pallas_call | solution.py:27
  22.1 4.3 %collective-permute-start.9 = (bf16[8,16,1920]{2,1,0:T(8,128)(2,1)S(1)}, bf16[8,16,1920]{2,1,0:T(8,128)(2,1)S(1)}, u32[]{:S(2)}, u32[]{:S(2)}) collective-permute-start(bf16[8,16,1920]{2,1,0:T(8,128)(2,1)S(1)} %get-tuple-element.72.refs_4_), channel_id=1, source_target_pairs={{0,1},{1,0},{2,3},{3,2},{4,5},{5,4},{6,7},{7,6},{8,9},{9,8},{10,11... | collective-permute-start | bytes 1474568 | tf_op jit(solution)/shard_map/ppermute | solution.py:342
  26.4 0.1 collective-permute-start.6
  26.5 1.4 %collective-permute-done.9.refs_2_ = bf16[8,16,1920]{2,1,0:T(8,128)(2,1)S(1)} collective-permute-done((bf16[8,16,1920]{2,1,0:T(8,128)(2,1)S(1)}, bf16[8,16,1920]{2,1,0:T(8,128)(2,1)S(1)}, u32[]{:S(2)}, u32[]{:S(2)}) %collective-permute-start.9) | collective-permute-done | bytes 491552 | tf_op jit(solution)/shard_map/ppermute | solution.py:342
  27.9 0.1 shard_map.75
  28.0 3.1 %collective-permute-start.10 = (bf16[4,16,1920]{2,1,0:T(8,128)(2,1)S(1)}, bf16[4,16,1920]{2,1,0:T(8,128)(2,1)S(1)}, u32[]{:S(2)}, u32[]{:S(2)}) collective-permute-start(bf16[4,16,1920]{2,1,0:T(8,128)(2,1)S(1)} %get-tuple-element.74.refs_5_), channel_id=1, source_target_pairs={{0,4},{1,5},{2,6},{3,7},{4,0},{5,1},{6,2},{7,3},{8,12},{9,13},{10,... | collective-permute-start | bytes 737288 | tf_op jit(solution)/shard_map/ppermute | solution.py:342
  31.1 0.0 collective-permute-done.6.refs_2_
  31.1 0.1 shard_map.73
  31.2 2.0 %collective-permute-start.7 = (bf16[4,16,1536]{2,1,0:T(8,128)(2,1)S(1)}, bf16[4,16,1536]{2,1,0:T(8,128)(2,1)S(1)}, u32[]{:S(2)}, u32[]{:S(2)}) collective-permute-start(bf16[4,16,1536]{2,1,0:T(8,128)(2,1)S(1)} %get-tuple-element.68.refs_4_), channel_id=1, source_target_pairs={{0,2},{1,3},{2,0},{3,1},{4,6},{5,7},{6,4},{7,5},{8,10},{9,11},{10,... | collective-permute-start | bytes 589832 | tf_op jit(solution)/shard_map/ppermute | solution.py:342
  33.2 2.1 %shard_map.78.refs_3_ = bf16[4,8,64,256]{3,2,1,0:T(8,128)(2,1)S(1)} custom-call(bf16[4,8,32,256]{3,2,1,0:T(8,128)(2,1)S(1)} %get-tuple-element.64.refs_3_.refs_0_, bf16[27,128,256]{2,1,0:T(8,128)(2,1)S(1)} %copy-done, bf16[2,8,64,256]{3,2,1,0:T(8,128)(2,1)S(1)} %get-tuple-element.81.refs_2_, bf16[2,8,64,256]{3,2,1,0:T(8,128)(2,1)S(1)} %get-tuple-element.82.refs_3_, ...), custom_call_target="tpu_custom_call" | custom-call | flops 14155776 | bytes 1048576 | tf_op jit(solution)/shard_map/pallas_call | solution.py:27
  35.3 4.0 %shard_map.79 = (bf16[8,8,1152]{2,1,0:T(8,128)(2,1)S(1)}, bf16[8,8,1152]{2,1,0:T(8,128)(2,1)S(1)}, bf16[8,8,1152]{2,1,0:T(8,128)(2,1)S(1)}, bf16[8,8,1152]{2,1,0...) custom-call(s32[1]{0:T(128)} %bitcast.place.refs_0_, ...), custom_call_target="tpu_custom_call" | custom-call | flops 56623104 | bytes 1048576 | tf_op jit(solution)/shard_map/pallas_call | solution.py:27
  39.4 0.1 collective-permute-start.13
  39.4 0.5 collective-permute-start.14
  39.9 0.1 collective-permute-start.15
  40.0 0.0 collective-permute-done.10.refs_2_
  40.0 0.1 shard_map.76
  40.1 0.1 collective-permute-start.11
  40.2 0.0 collective-permute-done.7.refs_2_
  40.2 1.0 %collective-permute-start.8 = (bf16[2,16,1536]{2,1,0:T(8,128)(2,1)S(1)}, bf16[2,16,1536]{2,1,0:T(8,128)(2,1)S(1)}, u32[]{:S(2)}, u32[]{:S(2)}) collective-permute-start(bf16[2,16,1536]{2,1,0:T(8,128)(2,1)S(1)} %get-tuple-element.70.refs_7_), channel_id=1, source_target_pairs={{0,4},{1,5},{2,6},{3,7},{4,0},{5,1},{6,2},{7,3},{8,12},{9,13},{10,... | collective-permute-start | bytes 294920 | tf_op jit(solution)/shard_map/ppermute | solution.py:342
  41.3 0.0 collective-permute-done.13.refs_2_
  41.3 0.0 collective-permute-done.14.refs_4_
  41.3 0.0 collective-permute-done.15.refs_6_
  41.3 0.1 shard_map.80
  41.4 1.5 %collective-permute-start.16 = (bf16[2,8,3456]{2,1,0:T(8,128)(2,1)S(1)}, bf16[2,8,3456]{2,1,0:T(8,128)(2,1)S(1)}, u32[]{:S(2)}, u32[]{:S(2)}) collective-permute-start(bf16[2,8,3456]{2,1,0:T(8,128)(2,1)S(1)} %get-tuple-element.90), channel_id=1, source_target_pairs={{0,2},{1,3},{2,0},{3,1},{4,6},{5,7},{6,4},{7,5},{8,10},{9,11},{10,... | collective-permute-start | bytes 331784 | tf_op jit(solution)/shard_map/ppermute | solution.py:342
  42.9 1.6 %collective-permute-start.17 = (bf16[2,8,3456]{2,1,0:T(8,128)(2,1)S(1)}, bf16[2,8,3456]{2,1,0:T(8,128)(2,1)S(1)}, u32[]{:S(2)}, u32[]{:S(2)}) collective-permute-start(bf16[2,8,3456]{2,1,0:T(8,128)(2,1)S(1)} %get-tuple-element.91), channel_id=1, source_target_pairs={{0,4},{1,5},{2,6},{3,7},{4,0},{5,1},{6,2},{7,3},{8,12},{9,13},{10,... | collective-permute-start | bytes 331784 | tf_op jit(solution)/shard_map/ppermute | solution.py:342
  44.5 0.5 collective-permute-start.18
  45.0 0.7 %collective-permute-done.8.refs_2_ = bf16[2,16,1536]{2,1,0:T(8,128)(2,1)S(1)} collective-permute-done((bf16[2,16,1536]{2,1,0:T(8,128)(2,1)S(1)}, bf16[2,16,1536]{2,1,0:T(8,128)(2,1)S(1)}, u32[]{:S(2)}, u32[]{:S(2)}) %collective-permute-start.8) | collective-permute-done | bytes 98336 | tf_op jit(solution)/shard_map/ppermute | solution.py:342
  45.7 0.6 collective-permute-done.11.refs_4_
  46.3 1.6 %collective-permute-start.12 = (bf16[1,16,3456]{2,1,0:T(8,128)(2,1)S(1)}, bf16[1,16,3456]{2,1,0:T(8,128)(2,1)S(1)}, u32[]{:S(2)}, u32[]{:S(2)}) collective-permute-start(bf16[1,16,3456]{2,1,0:T(8,128)(2,1)S(1)} %get-tuple-element.78), channel_id=1, source_target_pairs={{0,8},{1,9},{2,10},{3,11},{4,12},{5,13},{6,14},{7,15},{8,0},{9,1},... | collective-permute-start | bytes 331784 | tf_op jit(solution)/shard_map/ppermute | solution.py:342
  47.9 0.3 collective-permute-done.16.refs_4_
  48.2 0.7 %collective-permute-done.17.refs_5_ = bf16[2,8,3456]{2,1,0:T(8,128)(2,1)S(1)} collective-permute-done((bf16[2,8,3456]{2,1,0:T(8,128)(2,1)S(1)}, bf16[2,8,3456]{2,1,0:T(8,128)(2,1)S(1)}, u32[]{:S(2)}, u32[]{:S(2)}) %collective-permute-start.17) | collective-permute-done | bytes 110624 | tf_op jit(solution)/shard_map/ppermute | solution.py:342
  48.9 4.1 %collective-permute-done.18.refs_6_ = bf16[2,8,3456]{2,1,0:T(8,128)(2,1)S(1)} collective-permute-done((bf16[2,8,3456]{2,1,0:T(8,128)(2,1)S(1)}, bf16[2,8,3456]{2,1,0:T(8,128)(2,1)S(1)}, u32[]{:S(2)}, u32[]{:S(2)}) %collective-permute-start.18) | collective-permute-done | bytes 110624 | tf_op jit(solution)/shard_map/ppermute | solution.py:342
  53.0 0.1 collective-permute-done.12.refs_2_
  53.1 0.1 shard_map.81
  53.2 1.5 %collective-permute-start.19 = (bf16[24,3456]{1,0:T(8,128)(2,1)S(1)}, bf16[24,3456]{1,0:T(8,128)(2,1)S(1)}, u32[]{:S(2)}, u32[]{:S(2)}) collective-permute-start(bf16[24,3456]{1,0:T(8,128)(2,1)S(1)} %get-tuple-element.93.refs_0_), channel_id=1, source_target_pairs={{0,16},{1,17},{2,18},{3,19},{4,20},{5,21},{6,22},{7,23},{8,24},{9,... | collective-permute-start | bytes 497672 | tf_op jit(solution)/shard_map/ppermute | solution.py:347
  54.7 1.7 %collective-permute-start.21 = (bf16[8,3456]{1,0:T(8,128)(2,1)S(1)}, bf16[8,3456]{1,0:T(8,128)(2,1)S(1)}, u32[]{:S(2)}, u32[]{:S(2)}) collective-permute-start(bf16[8,3456]{1,0:T(8,128)(2,1)S(1)} %get-tuple-element.94), channel_id=1, source_target_pairs={{0,24},{1,25},{2,26},{3,27},{4,28},{5,29},{6,30},{7,31},{8,16},{9,... | collective-permute-start | bytes 165896 | tf_op jit(solution)/shard_map/ppermute | solution.py:347
  56.4 1.2 %collective-permute-start.20 = (bf16[8,3456]{1,0:T(8,128)(2,1)S(1)}, bf16[8,3456]{1,0:T(8,128)(2,1)S(1)}, u32[]{:S(2)}, u32[]{:S(2)}) collective-permute-start(bf16[8,3456]{1,0:T(8,128)(2,1)S(1)} %get-tuple-element.94), channel_id=1, source_target_pairs={{0,8},{1,9},{2,10},{3,11},{4,12},{5,13},{6,14},{7,15},{8,0},{9,1},... | collective-permute-start | bytes 165896 | tf_op jit(solution)/shard_map/ppermute | solution.py:342
  57.6 3.4 %collective-permute-done.21.refs_3_ = bf16[8,3456]{1,0:T(8,128)(2,1)S(1)} collective-permute-done((bf16[8,3456]{1,0:T(8,128)(2,1)S(1)}, bf16[8,3456]{1,0:T(8,128)(2,1)S(1)}, u32[]{:S(2)}, u32[]{:S(2)}) %collective-permute-start.21) | collective-permute-done | bytes 55328 | tf_op jit(solution)/shard_map/ppermute | solution.py:347
  61.0 0.6 collective-permute-done.20.refs_2_
  61.6 0.0 collective-permute-done.19.refs_1_
  61.6 0.7 %shard_map.82 = (f32[8,3456]{1,0:T(8,128)}, f32[16,3456]{1,0:T(8,128)}) custom-call(bf16[24,3456]{1,0:T(8,128)(2,1)S(1)} %get-tuple-element.93.refs_0_, bf16[24,3456]{1,0:T(8,128)(2,1)S(1)} %collective-permute-done.19.refs_1_, bf16[8,3456]{1,0:T(8,128)(2,1)S(1)} %collective-permute-done.20.refs_2_, bf16[8,3456]{1,0:T(8,128)(2,1)S(1)} %collective-permute-done.21.refs_3_), custom_call_target="tpu_custom_call" | custom-call | bytes 1048576 | tf_op jit(solution)/shard_map/pallas_call | solution.py:27
  (4 shorter events, 0.1 us)
Async XLA Ops:
  0.6 1.2 %copy-start.1 = (bf16[1,4,16,64,128]{4,3,2,1,0:T(8,128)(2,1)S(1)}, bf16[1,4,16,64,128]{4,3,2,1,0:T(8,128)(2,1)}, u32[]{:S(2)}) copy-start(bf16[1,4,16,64,128]{4,3,2,1,0:T(8,128)(2,1)} %param.4) | copy-start | bytes 3145732
  1.9 1.3 %copy-start.2 = (bf16[1,2,8,32,256]{4,3,2,1,0:T(8,128)(2,1)S(1)}, bf16[1,2,8,32,256]{4,3,2,1,0:T(8,128)(2,1)}, u32[]{:S(2)}) copy-start(bf16[1,2,8,32,256]{4,3,2,1,0:T(8,128)(2,1)} %param.7) | copy-start | bytes 786436
  1.9 1.3 %copy-start.3 = (bf16[27,128,128]{2,1,0:T(8,128)(2,1)S(1)}, bf16[27,128,128]{2,1,0:T(8,128)(2,1)}, u32[]{:S(2)}) copy-start(bf16[27,128,128]{2,1,0:T(8,128)(2,1)} %param.5) | copy-start | bytes 2654212
  1.9 10.6 %collective-permute-start = (bf16[1,16,64,128]{3,2,1,0:T(8,128)(2,1)S(1)}, bf16[1,16,64,128]{3,2,1,0:T(8,128)(2,1)S(1)}, u32[]{:S(2)}, u32[]{:S(2)}) collective-permute-start(bf16[1,16,64,128]{3,2,1,0:T(8,128)(2,1)S(1)} %get-tuple-element.50), channel_id=1, source_target_pairs={{0,1},{1,0},{2,3},{3,2},{4,5},{5,4},{6,7},{7,6},{8,9},{9,8},{10,11... | collective-permute-start | bytes 786440 | tf_op jit(solution)/shard_map/ppermute | solution.py:43
  2.4 10.1 %collective-permute-start.1 = (bf16[1,16,64,128]{3,2,1,0:T(8,128)(2,1)S(1)}, bf16[1,16,64,128]{3,2,1,0:T(8,128)(2,1)S(1)}, u32[]{:S(2)}, u32[]{:S(2)}) collective-permute-start(bf16[1,16,64,128]{3,2,1,0:T(8,128)(2,1)S(1)} %get-tuple-element.51), channel_id=1, source_target_pairs={{1,2},{3,4},{5,6},{7,8},{9,10},{11,12},{13,14},{2,1},{4,3},{6,5},{... | collective-permute-start | bytes 786440 | tf_op jit(solution)/shard_map/ppermute | solution.py:43
  7.8 10.0 %copy-start = (bf16[27,128,256]{2,1,0:T(8,128)(2,1)S(1)}, bf16[27,128,256]{2,1,0:T(8,128)(2,1)}, u32[]{:S(2)}) copy-start(bf16[27,128,256]{2,1,0:T(8,128)(2,1)} %refs_1_.1) | copy-start | bytes 5308420
  7.8 11.2 %collective-permute-start.4 = (bf16[1,8,32,256]{3,2,1,0:T(8,128)(2,1)S(1)}, bf16[1,8,32,256]{3,2,1,0:T(8,128)(2,1)S(1)}, u32[]{:S(2)}, u32[]{:S(2)}) collective-permute-start(bf16[1,8,32,256]{3,2,1,0:T(8,128)(2,1)S(1)} %get-tuple-element.59), channel_id=1, source_target_pairs={{0,1},{1,0},{2,3},{3,2},{4,5},{5,4},{6,7},{7,6},{8,9},{9,8},{10,11... | collective-permute-start | bytes 393224 | tf_op jit(solution)/shard_map/ppermute | solution.py:43
  11.9 7.2 %collective-permute-start.5 = (bf16[1,8,32,256]{3,2,1,0:T(8,128)(2,1)S(1)}, bf16[1,8,32,256]{3,2,1,0:T(8,128)(2,1)S(1)}, u32[]{:S(2)}, u32[]{:S(2)}) collective-permute-start(bf16[1,8,32,256]{3,2,1,0:T(8,128)(2,1)S(1)} %get-tuple-element.60), channel_id=1, source_target_pairs={{1,2},{3,4},{5,6},{7,8},{9,10},{11,12},{13,14},{2,1},{4,3},{6,5},{... | collective-permute-start | bytes 393224 | tf_op jit(solution)/shard_map/ppermute | solution.py:43
  14.0 5.0 %collective-permute-start.2 = (bf16[2,8,32,128]{3,2,1,0:T(8,128)(2,1)S(1)}, bf16[2,8,32,128]{3,2,1,0:T(8,128)(2,1)S(1)}, u32[]{:S(2)}, u32[]{:S(2)}) collective-permute-start(bf16[2,8,32,128]{3,2,1,0:T(8,128)(2,1)S(1)} %get-tuple-element.55), channel_id=1, source_target_pairs={{0,1},{1,0},{2,3},{3,2},{4,5},{5,4},{6,7},{7,6},{8,9},{9,8},{10,11... | collective-permute-start | bytes 393224 | tf_op jit(solution)/shard_map/ppermute | solution.py:43
  17.0 2.1 %collective-permute-start.3 = (bf16[2,8,32,128]{3,2,1,0:T(8,128)(2,1)S(1)}, bf16[2,8,32,128]{3,2,1,0:T(8,128)(2,1)S(1)}, u32[]{:S(2)}, u32[]{:S(2)}) collective-permute-start(bf16[2,8,32,128]{3,2,1,0:T(8,128)(2,1)S(1)} %get-tuple-element.56), channel_id=1, source_target_pairs={{1,2},{3,4},{5,6},{7,8},{9,10},{11,12},{13,14},{2,1},{4,3},{6,5},{... | collective-permute-start | bytes 393224 | tf_op jit(solution)/shard_map/ppermute | solution.py:43
  22.1 5.8 %collective-permute-start.9 = (bf16[8,16,1920]{2,1,0:T(8,128)(2,1)S(1)}, bf16[8,16,1920]{2,1,0:T(8,128)(2,1)S(1)}, u32[]{:S(2)}, u32[]{:S(2)}) collective-permute-start(bf16[8,16,1920]{2,1,0:T(8,128)(2,1)S(1)} %get-tuple-element.72.refs_4_), channel_id=1, source_target_pairs={{0,1},{1,0},{2,3},{3,2},{4,5},{5,4},{6,7},{7,6},{8,9},{9,8},{10,11... | collective-permute-start | bytes 1474568 | tf_op jit(solution)/shard_map/ppermute | solution.py:342
  26.4 4.7 %collective-permute-start.6 = (bf16[8,16,1536]{2,1,0:T(8,128)(2,1)S(1)}, bf16[8,16,1536]{2,1,0:T(8,128)(2,1)S(1)}, u32[]{:S(2)}, u32[]{:S(2)}) collective-permute-start(bf16[8,16,1536]{2,1,0:T(8,128)(2,1)S(1)} %get-tuple-element.66), channel_id=1, source_target_pairs={{0,1},{1,0},{2,3},{3,2},{4,5},{5,4},{6,7},{7,6},{8,9},{9,8},{10,11... | collective-permute-start | bytes 1179656 | tf_op jit(solution)/shard_map/ppermute | solution.py:342
  28.0 12.0 %collective-permute-start.10 = (bf16[4,16,1920]{2,1,0:T(8,128)(2,1)S(1)}, bf16[4,16,1920]{2,1,0:T(8,128)(2,1)S(1)}, u32[]{:S(2)}, u32[]{:S(2)}) collective-permute-start(bf16[4,16,1920]{2,1,0:T(8,128)(2,1)S(1)} %get-tuple-element.74.refs_5_), channel_id=1, source_target_pairs={{0,4},{1,5},{2,6},{3,7},{4,0},{5,1},{6,2},{7,3},{8,12},{9,13},{10,... | collective-permute-start | bytes 737288 | tf_op jit(solution)/shard_map/ppermute | solution.py:342
  31.2 9.0 %collective-permute-start.7 = (bf16[4,16,1536]{2,1,0:T(8,128)(2,1)S(1)}, bf16[4,16,1536]{2,1,0:T(8,128)(2,1)S(1)}, u32[]{:S(2)}, u32[]{:S(2)}) collective-permute-start(bf16[4,16,1536]{2,1,0:T(8,128)(2,1)S(1)} %get-tuple-element.68.refs_4_), channel_id=1, source_target_pairs={{0,2},{1,3},{2,0},{3,1},{4,6},{5,7},{6,4},{7,5},{8,10},{9,11},{10,... | collective-permute-start | bytes 589832 | tf_op jit(solution)/shard_map/ppermute | solution.py:342
  39.4 1.9 %collective-permute-start.13 = (bf16[8,8,1152]{2,1,0:T(8,128)(2,1)S(1)}, bf16[8,8,1152]{2,1,0:T(8,128)(2,1)S(1)}, u32[]{:S(2)}, u32[]{:S(2)}) collective-permute-start(bf16[8,8,1152]{2,1,0:T(8,128)(2,1)S(1)} %get-tuple-element.84), channel_id=1, source_target_pairs={{0,1},{1,0},{2,3},{3,2},{4,5},{5,4},{6,7},{7,6},{8,9},{9,8},{10,11... | collective-permute-start | bytes 442376 | tf_op jit(solution)/shard_map/ppermute | solution.py:342
  39.4 1.8 %collective-permute-start.14 = (bf16[8,8,1152]{2,1,0:T(8,128)(2,1)S(1)}, bf16[8,8,1152]{2,1,0:T(8,128)(2,1)S(1)}, u32[]{:S(2)}, u32[]{:S(2)}) collective-permute-start(bf16[8,8,1152]{2,1,0:T(8,128)(2,1)S(1)} %get-tuple-element.86), channel_id=1, source_target_pairs={{0,1},{1,0},{2,3},{3,2},{4,5},{5,4},{6,7},{7,6},{8,9},{9,8},{10,11... | collective-permute-start | bytes 442376 | tf_op jit(solution)/shard_map/ppermute | solution.py:342
  39.9 1.4 %collective-permute-start.15 = (bf16[8,8,1152]{2,1,0:T(8,128)(2,1)S(1)}, bf16[8,8,1152]{2,1,0:T(8,128)(2,1)S(1)}, u32[]{:S(2)}, u32[]{:S(2)}) collective-permute-start(bf16[8,8,1152]{2,1,0:T(8,128)(2,1)S(1)} %get-tuple-element.88), channel_id=1, source_target_pairs={{0,1},{1,0},{2,3},{3,2},{4,5},{5,4},{6,7},{7,6},{8,9},{9,8},{10,11... | collective-permute-start | bytes 442376 | tf_op jit(solution)/shard_map/ppermute | solution.py:342
  40.1 6.2 %collective-permute-start.11 = (bf16[2,16,1920]{2,1,0:T(8,128)(2,1)S(1)}, bf16[2,16,1920]{2,1,0:T(8,128)(2,1)S(1)}, u32[]{:S(2)}, u32[]{:S(2)}) collective-permute-start(bf16[2,16,1920]{2,1,0:T(8,128)(2,1)S(1)} %get-tuple-element.76.refs_8_), channel_id=1, source_target_pairs={{0,2},{1,3},{2,0},{3,1},{4,6},{5,7},{6,4},{7,5},{8,10},{9,11},{10,... | collective-permute-start | bytes 368648 | tf_op jit(solution)/shard_map/ppermute | solution.py:342
  40.2 5.5 %collective-permute-start.8 = (bf16[2,16,1536]{2,1,0:T(8,128)(2,1)S(1)}, bf16[2,16,1536]{2,1,0:T(8,128)(2,1)S(1)}, u32[]{:S(2)}, u32[]{:S(2)}) collective-permute-start(bf16[2,16,1536]{2,1,0:T(8,128)(2,1)S(1)} %get-tuple-element.70.refs_7_), channel_id=1, source_target_pairs={{0,4},{1,5},{2,6},{3,7},{4,0},{5,1},{6,2},{7,3},{8,12},{9,13},{10,... | collective-permute-start | bytes 294920 | tf_op jit(solution)/shard_map/ppermute | solution.py:342
  41.4 6.8 %collective-permute-start.16 = (bf16[2,8,3456]{2,1,0:T(8,128)(2,1)S(1)}, bf16[2,8,3456]{2,1,0:T(8,128)(2,1)S(1)}, u32[]{:S(2)}, u32[]{:S(2)}) collective-permute-start(bf16[2,8,3456]{2,1,0:T(8,128)(2,1)S(1)} %get-tuple-element.90), channel_id=1, source_target_pairs={{0,2},{1,3},{2,0},{3,1},{4,6},{5,7},{6,4},{7,5},{8,10},{9,11},{10,... | collective-permute-start | bytes 331784 | tf_op jit(solution)/shard_map/ppermute | solution.py:342
  42.9 6.0 %collective-permute-start.17 = (bf16[2,8,3456]{2,1,0:T(8,128)(2,1)S(1)}, bf16[2,8,3456]{2,1,0:T(8,128)(2,1)S(1)}, u32[]{:S(2)}, u32[]{:S(2)}) collective-permute-start(bf16[2,8,3456]{2,1,0:T(8,128)(2,1)S(1)} %get-tuple-element.91), channel_id=1, source_target_pairs={{0,4},{1,5},{2,6},{3,7},{4,0},{5,1},{6,2},{7,3},{8,12},{9,13},{10,... | collective-permute-start | bytes 331784 | tf_op jit(solution)/shard_map/ppermute | solution.py:342
  44.5 8.5 %collective-permute-start.18 = (bf16[2,8,3456]{2,1,0:T(8,128)(2,1)S(1)}, bf16[2,8,3456]{2,1,0:T(8,128)(2,1)S(1)}, u32[]{:S(2)}, u32[]{:S(2)}) collective-permute-start(bf16[2,8,3456]{2,1,0:T(8,128)(2,1)S(1)} %get-tuple-element.92), channel_id=1, source_target_pairs={{0,6},{1,7},{2,4},{3,5},{4,2},{5,3},{6,0},{7,1},{8,14},{9,15},{10,... | collective-permute-start | bytes 331784 | tf_op jit(solution)/shard_map/ppermute | solution.py:342
  46.3 6.8 %collective-permute-start.12 = (bf16[1,16,3456]{2,1,0:T(8,128)(2,1)S(1)}, bf16[1,16,3456]{2,1,0:T(8,128)(2,1)S(1)}, u32[]{:S(2)}, u32[]{:S(2)}) collective-permute-start(bf16[1,16,3456]{2,1,0:T(8,128)(2,1)S(1)} %get-tuple-element.78), channel_id=1, source_target_pairs={{0,8},{1,9},{2,10},{3,11},{4,12},{5,13},{6,14},{7,15},{8,0},{9,1},... | collective-permute-start | bytes 331784 | tf_op jit(solution)/shard_map/ppermute | solution.py:342
  53.2 8.4 %collective-permute-start.19 = (bf16[24,3456]{1,0:T(8,128)(2,1)S(1)}, bf16[24,3456]{1,0:T(8,128)(2,1)S(1)}, u32[]{:S(2)}, u32[]{:S(2)}) collective-permute-start(bf16[24,3456]{1,0:T(8,128)(2,1)S(1)} %get-tuple-element.93.refs_0_), channel_id=1, source_target_pairs={{0,16},{1,17},{2,18},{3,19},{4,20},{5,21},{6,22},{7,23},{8,24},{9,... | collective-permute-start | bytes 497672 | tf_op jit(solution)/shard_map/ppermute | solution.py:347
  54.7 6.3 %collective-permute-start.21 = (bf16[8,3456]{1,0:T(8,128)(2,1)S(1)}, bf16[8,3456]{1,0:T(8,128)(2,1)S(1)}, u32[]{:S(2)}, u32[]{:S(2)}) collective-permute-start(bf16[8,3456]{1,0:T(8,128)(2,1)S(1)} %get-tuple-element.94), channel_id=1, source_target_pairs={{0,24},{1,25},{2,26},{3,27},{4,28},{5,29},{6,30},{7,31},{8,16},{9,... | collective-permute-start | bytes 165896 | tf_op jit(solution)/shard_map/ppermute | solution.py:347
  56.4 5.1 %collective-permute-start.20 = (bf16[8,3456]{1,0:T(8,128)(2,1)S(1)}, bf16[8,3456]{1,0:T(8,128)(2,1)S(1)}, u32[]{:S(2)}, u32[]{:S(2)}) collective-permute-start(bf16[8,3456]{1,0:T(8,128)(2,1)S(1)} %get-tuple-element.94), channel_id=1, source_target_pairs={{0,8},{1,9},{2,10},{3,11},{4,12},{5,13},{6,14},{7,15},{8,0},{9,1},... | collective-permute-start | bytes 165896 | tf_op jit(solution)/shard_map/ppermute | solution.py:342

commit v7 on v6

--- a/solution.py
+++ b/solution.py
@@ -10,7 +10,7 @@
 F32 = jnp.float32
 BF16 = jnp.bfloat16
 COST = 64
-SPLIT = 4
+SPLIT = 5
 SMALL = 50
 VMEM = pl.BlockSpec(memory_space=pltpu.VMEM)
 SMEM = pl.BlockSpec(memory_space=pltpu.SMEM)
@@ -599,6 +599,15 @@
         16,
         scalars=1,
     )
+    (fine_delta,) = kernel_call(
+        fine_deltas,
+        [coarse_delta, coarse_kernel, slope, slope_edge],
+        [shape(planes, half, fz, 2 * chan)],
+        [pltpu.VMEM((cp + 2, cy + 2, cz, 3 * wide), BF16), pltpu.VMEM((cy, fz, chan), F32)],
+        coarse_flops,
+        16,
+        after=[terms[-1]],
+    )
     halves = []
     for side, sequence in enumerate((bits, turned)):
         some = terms[side * len(terms) // 2 : (side + 1) * len(terms) // 2]
@@ -607,17 +616,8 @@
     sends = []
     if len(bits) > 1:
         for side, sequence in enumerate((bits, turned)):
-            sends.append(fold(place, [halves[side]], sequence[:1]))
+            sends.append(fold(place, [halves[side]], sequence[:1], [fine_delta]))
     early = [item for send, _ in sends for item in send.values()]
-    (fine_delta,) = kernel_call(
-        fine_deltas,
-        [coarse_delta, coarse_kernel, slope, slope_edge],
-        [shape(planes, half, fz, 2 * chan)],
-        [pltpu.VMEM((cp + 2, cy + 2, cz, 3 * wide), BF16), pltpu.VMEM((cy, fz, chan), F32)],
-        coarse_flops,
-        16,
-        after=[terms[-1]],
-    )
     terms = kernel_call(
         functools.partial(fine_terms, order=order),
         [place, wide6, halo6, fine_delta],

time: 62.5 us -> 61.7 us (0.987)
  waiting for transfers between devices: 11.9 us -> 7.93 us
  starting transfers between devices: 30.5 us -> 33.6 us
    ppermute x14, waiting for transfers between devices: 8.51 us -> 4.86 us  [swap(): return lax.ppermute(value, 'space', [(i, i ^ bit) for i in range(count)])]
    ppermute x14, starting transfers between devices: 17.6 us -> 20.1 us  [swap(): return lax.ppermute(value, 'space', [(i, i ^ bit) for i in range(count)])]
  transfers between devices with their start and end apart: 22 -> 22, of which waited for: 9 -> 5; matrix products, arithmetic and copies ran while one was open for 0% -> 0% of each run, Pallas kernels for 22% -> 23%
where the time goes in v7:
time: 61.7 us; the launch traced here: 61.5 us
  starting transfers between devices  33.6 us (54%)
  Pallas kernels  17.8 us (29%)
  waiting for transfers between devices  7.93 us (13%)
  local copies, waits for them, and re-layouts  1.23 us (2%)
  between operations  0.86 us (1%)
    ppermute x14, starting transfers between devices, swap(): return lax.ppermute(value, 'space', [(i, i ^ bit) for i in range(count)])  20.1 us
    pallas_call x15, Pallas kernels, kernel_call(): pl.pallas_call(inner, out_shape=outs, in_specs=specs, out_specs=[VMEM] *...  17.8 us
    ppermute x3, starting transfers between devices, exchange(): lax.ppermute(to_pair, 'space', pair)  7.55 us
    ppermute x14, waiting for transfers between devices, swap(): return lax.ppermute(value, 'space', [(i, i ^ bit) for i in range(count)])  4.86 us
    ppermute x2, starting transfers between devices, swap_sample(): lax.ppermute(value, ('sample', 'space'), [(s * count + i, (1 - s) * count...  3.77 us
    ppermute x2, waiting for transfers between devices, swap_sample(): lax.ppermute(value, ('sample', 'space'), [(s * count + i, (1 - s) * count...  3.06 us
    ppermute x3, starting transfers between devices, exchange(): lax.ppermute(to_next, 'space', across)  2.16 us
  transfers between devices with their start and end apart: 22, of which 5 were waited for; matrix products, arithmetic and copies ran while one was open for 0% of the time, Pallas kernels for 23%

profile of v7, /device:TPU:0, one launch (start us, length us, event | category | flops | bytes accessed | tf_op | source)
XLA Modules:
  0.0 61.5 jit_solution(10963210399081805916)
XLA Ops:
  0.6 0.0 copy-start.1
  0.6 1.2 %copy-done.1 = bf16[1,4,16,64,128]{4,3,2,1,0:T(8,128)(2,1)S(1)} copy-done((bf16[1,4,16,64,128]{4,3,2,1,0:T(8,128)(2,1)S(1)}, bf16[1,4,16,64,128]{4,3,2,1,0:T(8,128)(2,1)}, u32[]{:S(2)}) %copy-start.1) | copy-done | bytes 1048600
  1.9 0.1 shard_map.67
  1.9 0.5 collective-permute-start
  2.4 0.7 %collective-permute-start.1 = (bf16[1,16,64,128]{3,2,1,0:T(8,128)(2,1)S(1)}, bf16[1,16,64,128]{3,2,1,0:T(8,128)(2,1)S(1)}, u32[]{:S(2)}, u32[]{:S(2)}) collective-permute-start(bf16[1,16,64,128]{3,2,1,0:T(8,128)(2,1)S(1)} %get-tuple-element.51), channel_id=1, source_target_pairs={{1,2},{3,4},{5,6},{7,8},{9,10},{11,12},{13,14},{2,1},{4,3},{6,5},{... | collective-permute-start | bytes 786440 | tf_op jit(solution)/shard_map/ppermute | solution.py:43
  3.1 0.0 copy-done.2
  3.1 0.0 copy-done.3
  3.1 4.6 %shard_map.68 = (bf16[4,9,64,768]{3,2,1,0:T(8,128)(2,1)S(1)}, bf16[3,2,768,256]{3,2,1,0:T(8,128)(2,1)S(1)}, f32[2,512,256]{2,1,0:T(8,128)S(1)}, f32[2,8,64,128]{...) custom-call(s32[1]{0:T(128)} %bitcast.place.refs_0_, ...), custom_call_target="tpu_custom_call" | custom-call | flops 56623104 | bytes 1048576 | tf_op jit(solution)/shard_map/pallas_call | solution.py:27
  7.8 0.0 copy-start
  7.8 4.1 %collective-permute-start.4 = (bf16[1,8,32,256]{3,2,1,0:T(8,128)(2,1)S(1)}, bf16[1,8,32,256]{3,2,1,0:T(8,128)(2,1)S(1)}, u32[]{:S(2)}, u32[]{:S(2)}) collective-permute-start(bf16[1,8,32,256]{3,2,1,0:T(8,128)(2,1)S(1)} %get-tuple-element.59), channel_id=1, source_target_pairs={{0,1},{1,0},{2,3},{3,2},{4,5},{5,4},{6,7},{7,6},{8,9},{9,8},{10,11... | collective-permute-start | bytes 393224 | tf_op jit(solution)/shard_map/ppermute | solution.py:43
  11.9 0.7 %collective-permute-start.5 = (bf16[1,8,32,256]{3,2,1,0:T(8,128)(2,1)S(1)}, bf16[1,8,32,256]{3,2,1,0:T(8,128)(2,1)S(1)}, u32[]{:S(2)}, u32[]{:S(2)}) collective-permute-start(bf16[1,8,32,256]{3,2,1,0:T(8,128)(2,1)S(1)} %get-tuple-element.60), channel_id=1, source_target_pairs={{1,2},{3,4},{5,6},{7,8},{9,10},{11,12},{13,14},{2,1},{4,3},{6,5},{... | collective-permute-start | bytes 393224 | tf_op jit(solution)/shard_map/ppermute | solution.py:43
  12.5 0.0 collective-permute-done.refs_1_
  12.5 0.0 collective-permute-done.1.refs_2_
  12.5 1.5 %shard_map.69 = (bf16[2,9,64,768]{3,2,1,0:T(8,128)(2,1)S(1)}, bf16[2,8,32,128]{3,2,1,0:T(8,128)(2,1)S(1)}, bf16[2,8,64,256]{3,2,1,0:T(8,128)(2,1)S(1)}, bf16[2,8...) custom-call(s32[1]{0:T(128)} %bitcast.place.refs_0_, bf16[1,16,64,128]{3,2,1,0:T(8,128)(2,1)S(1)} %collective-permute-done.refs_1_, ...), custom_call_target="tpu_custom_call" | custom-call | flops 9437184 | bytes 1048576 | tf_op jit(solution)/shard_map/pallas_call | solution.py:27
  14.0 2.9 %collective-permute-start.2 = (bf16[2,8,32,128]{3,2,1,0:T(8,128)(2,1)S(1)}, bf16[2,8,32,128]{3,2,1,0:T(8,128)(2,1)S(1)}, u32[]{:S(2)}, u32[]{:S(2)}) collective-permute-start(bf16[2,8,32,128]{3,2,1,0:T(8,128)(2,1)S(1)} %get-tuple-element.55), channel_id=1, source_target_pairs={{0,1},{1,0},{2,3},{3,2},{4,5},{5,4},{6,7},{7,6},{8,9},{9,8},{10,11... | collective-permute-start | bytes 393224 | tf_op jit(solution)/shard_map/ppermute | solution.py:43
  17.0 0.8 %collective-permute-start.3 = (bf16[2,8,32,128]{3,2,1,0:T(8,128)(2,1)S(1)}, bf16[2,8,32,128]{3,2,1,0:T(8,128)(2,1)S(1)}, u32[]{:S(2)}, u32[]{:S(2)}) collective-permute-start(bf16[2,8,32,128]{3,2,1,0:T(8,128)(2,1)S(1)} %get-tuple-element.56), channel_id=1, source_target_pairs={{1,2},{3,4},{5,6},{7,8},{9,10},{11,12},{13,14},{2,1},{4,3},{6,5},{... | collective-permute-start | bytes 393224 | tf_op jit(solution)/shard_map/ppermute | solution.py:43
  17.8 0.0 copy-done
  17.8 1.2 %shard_map.70 = (bf16[2,10,32,384]{3,2,1,0:T(8,128)(2,1)S(1)}, f32[4,256,256]{2,1,0:T(8,128)S(1)}) custom-call(bf16[2,8,32,128]{3,2,1,0:T(8,128)(2,1)S(1)} %get-tuple-element.57.refs_0_, bf16[3,1152,256]{2,1,0:T(8,128)(2,1)S(1)} %bitcast.6), custom_call_target="tpu_custom_call" | custom-call | flops 14155776 | bytes 1048576 | tf_op jit(solution)/shard_map/pallas_call | solution.py:27
  19.0 0.0 collective-permute-done.4.refs_6_
  19.0 0.0 collective-permute-done.5.refs_7_
  19.0 0.0 collective-permute-done.2.refs_1_
  19.0 0.0 collective-permute-done.3.refs_2_
  19.0 1.9 %shard_map.71 = (bf16[4,10,32,384]{3,2,1,0:T(8,128)(2,1)S(1)}, bf16[2,8,32,256]{3,2,1,0:T(8,128)(2,1)}, bf16[4,8,32,256]{3,2,1,0:T(8,128)(2,1)S(1)}) custom-call(s32[1]{0:T(128)} %bitcast.place.refs_0_, bf16[2,8,32,128]{3,2,1,0:T(8,128)(2,1)S(1)} %collective-permute-done.2.refs_1_, bf16[2,8,32,128]{3,2,1,0:T(8,128)(2,1)S(1)} %collective-permute-done.3.refs_2_, ...), custom_call_target="tpu_custom_call" | custom-call | flops 14155776 | bytes 1048576 | tf_op jit(solution)/shard_map/pallas_call | solution.py:27
  21.0 1.2 %shard_map.72 = (bf16[8,16,1920]{2,1,0:T(8,128)(2,1)S(1)}, bf16[8,16,1920]{2,1,0:T(8,128)(2,1)S(1)}, bf16[8,16,1536]{2,1,0:T(8,128)(2,1)S(1)}, bf16[8,16,1536]{2,1,0:T(8,128)(2,1)S(1)}) custom-call(s32[1]{0:T(128)} %bitcast.place.refs_0_, bf16[2,10,32,384]{3,2,1,0:T(8,128)(2,1)S(1)} %get-tuple-element.62.refs_1_, ...), custom_call_target="tpu_custom_call" | custom-call | flops 14155776 | bytes 1048576 | tf_op jit(solution)/shard_map/pallas_call | solution.py:27
  22.1 4.3 %collective-permute-start.6 = (bf16[8,16,1920]{2,1,0:T(8,128)(2,1)S(1)}, bf16[8,16,1920]{2,1,0:T(8,128)(2,1)S(1)}, u32[]{:S(2)}, u32[]{:S(2)}) collective-permute-start(bf16[8,16,1920]{2,1,0:T(8,128)(2,1)S(1)} %get-tuple-element.66), channel_id=1, source_target_pairs={{0,1},{1,0},{2,3},{3,2},{4,5},{5,4},{6,7},{7,6},{8,9},{9,8},{10,11... | collective-permute-start | bytes 1474568 | tf_op jit(solution)/shard_map/ppermute | solution.py:342
  26.4 0.1 collective-permute-start.9
  26.5 2.1 %shard_map.73.refs_3_ = bf16[4,8,64,256]{3,2,1,0:T(8,128)(2,1)S(1)} custom-call(bf16[4,8,32,256]{3,2,1,0:T(8,128)(2,1)S(1)} %get-tuple-element.64.refs_3_.refs_0_, bf16[27,128,256]{2,1,0:T(8,128)(2,1)S(1)} %copy-done, bf16[2,8,64,256]{3,2,1,0:T(8,128)(2,1)S(1)} %get-tuple-element.67.refs_2_, bf16[2,8,64,256]{3,2,1,0:T(8,128)(2,1)S(1)} %get-tuple-element.68.refs_3_, ...), custom_call_target="tpu_custom_call" | custom-call | flops 14155776 | bytes 1048576 | tf_op jit(solution)/shard_map/pallas_call | solution.py:27
  28.6 0.0 collective-permute-done.6.refs_2_
  28.6 0.1 shard_map.74
  28.7 3.5 %collective-permute-start.7 = (bf16[4,16,1920]{2,1,0:T(8,128)(2,1)S(1)}, bf16[4,16,1920]{2,1,0:T(8,128)(2,1)S(1)}, u32[]{:S(2)}, u32[]{:S(2)}) collective-permute-start(bf16[4,16,1920]{2,1,0:T(8,128)(2,1)S(1)} %get-tuple-element.71.refs_4_), channel_id=1, source_target_pairs={{0,2},{1,3},{2,0},{3,1},{4,6},{5,7},{6,4},{7,5},{8,10},{9,11},{10,... | collective-permute-start | bytes 737288 | tf_op jit(solution)/shard_map/ppermute | solution.py:342
  32.3 0.0 collective-permute-done.9.refs_2_
  32.3 0.1 shard_map.76
  32.3 1.6 %collective-permute-start.10 = (bf16[4,16,1536]{2,1,0:T(8,128)(2,1)S(1)}, bf16[4,16,1536]{2,1,0:T(8,128)(2,1)S(1)}, u32[]{:S(2)}, u32[]{:S(2)}) collective-permute-start(bf16[4,16,1536]{2,1,0:T(8,128)(2,1)S(1)} %get-tuple-element.76.refs_5_), channel_id=1, source_target_pairs={{0,4},{1,5},{2,6},{3,7},{4,0},{5,1},{6,2},{7,3},{8,12},{9,13},{10,... | collective-permute-start | bytes 589832 | tf_op jit(solution)/shard_map/ppermute | solution.py:342
  34.0 4.0 %shard_map.79 = (bf16[8,8,1152]{2,1,0:T(8,128)(2,1)S(1)}, bf16[8,8,1152]{2,1,0:T(8,128)(2,1)S(1)}, bf16[8,8,1152]{2,1,0:T(8,128)(2,1)S(1)}, bf16[8,8,1152]{2,1,0...) custom-call(s32[1]{0:T(128)} %bitcast.place.refs_0_, ...), custom_call_target="tpu_custom_call" | custom-call | flops 56623104 | bytes 1048576 | tf_op jit(solution)/shard_map/pallas_call | solution.py:27
  38.0 0.1 collective-permute-start.13
  38.1 0.5 collective-permute-start.14
  38.6 0.1 collective-permute-start.15
  38.7 0.0 collective-permute-done.7.refs_2_
  38.7 0.1 shard_map.75
  38.8 1.5 %collective-permute-start.8 = (bf16[2,16,1920]{2,1,0:T(8,128)(2,1)S(1)}, bf16[2,16,1920]{2,1,0:T(8,128)(2,1)S(1)}, u32[]{:S(2)}, u32[]{:S(2)}) collective-permute-start(bf16[2,16,1920]{2,1,0:T(8,128)(2,1)S(1)} %get-tuple-element.73.refs_7_), channel_id=1, source_target_pairs={{0,4},{1,5},{2,6},{3,7},{4,0},{5,1},{6,2},{7,3},{8,12},{9,13},{10,... | collective-permute-start | bytes 368648 | tf_op jit(solution)/shard_map/ppermute | solution.py:342
  40.2 0.0 collective-permute-done.10.refs_2_
  40.3 1.7 %collective-permute-start.11 = (bf16[2,16,1536]{2,1,0:T(8,128)(2,1)S(1)}, bf16[2,16,1536]{2,1,0:T(8,128)(2,1)S(1)}, u32[]{:S(2)}, u32[]{:S(2)}) collective-permute-start(bf16[2,16,1536]{2,1,0:T(8,128)(2,1)S(1)} %get-tuple-element.78.refs_8_), channel_id=1, source_target_pairs={{0,2},{1,3},{2,0},{3,1},{4,6},{5,7},{6,4},{7,5},{8,10},{9,11},{10,... | collective-permute-start | bytes 294920 | tf_op jit(solution)/shard_map/ppermute | solution.py:342
  42.0 0.0 collective-permute-done.13.refs_2_
  42.0 0.0 collective-permute-done.14.refs_4_
  42.0 0.0 collective-permute-done.15.refs_6_
  42.0 0.1 shard_map.80
  42.1 0.4 collective-permute-start.16
  42.6 0.6 %collective-permute-start.17 = (bf16[2,8,3456]{2,1,0:T(8,128)(2,1)S(1)}, bf16[2,8,3456]{2,1,0:T(8,128)(2,1)S(1)}, u32[]{:S(2)}, u32[]{:S(2)}) collective-permute-start(bf16[2,8,3456]{2,1,0:T(8,128)(2,1)S(1)} %get-tuple-element.91), channel_id=1, source_target_pairs={{0,4},{1,5},{2,6},{3,7},{4,0},{5,1},{6,2},{7,3},{8,12},{9,13},{10,... | collective-permute-start | bytes 331784 | tf_op jit(solution)/shard_map/ppermute | solution.py:342
  43.2 2.5 %collective-permute-start.18 = (bf16[2,8,3456]{2,1,0:T(8,128)(2,1)S(1)}, bf16[2,8,3456]{2,1,0:T(8,128)(2,1)S(1)}, u32[]{:S(2)}, u32[]{:S(2)}) collective-permute-start(bf16[2,8,3456]{2,1,0:T(8,128)(2,1)S(1)} %get-tuple-element.92), channel_id=1, source_target_pairs={{0,6},{1,7},{2,4},{3,5},{4,2},{5,3},{6,0},{7,1},{8,14},{9,15},{10,... | collective-permute-start | bytes 331784 | tf_op jit(solution)/shard_map/ppermute | solution.py:342
  45.7 0.0 collective-permute-done.11.refs_4_
  45.7 0.0 collective-permute-done.8.refs_2_
  45.8 2.5 %collective-permute-start.12 = (bf16[1,16,3456]{2,1,0:T(8,128)(2,1)S(1)}, bf16[1,16,3456]{2,1,0:T(8,128)(2,1)S(1)}, u32[]{:S(2)}, u32[]{:S(2)}) collective-permute-start(bf16[1,16,3456]{2,1,0:T(8,128)(2,1)S(1)} %get-tuple-element.80), channel_id=1, source_target_pairs={{0,8},{1,9},{2,10},{3,11},{4,12},{5,13},{6,14},{7,15},{8,0},{9,1},... | collective-permute-start | bytes 331784 | tf_op jit(solution)/shard_map/ppermute | solution.py:342
  48.3 0.0 collective-permute-done.16.refs_4_
  48.3 0.8 %collective-permute-done.17.refs_5_ = bf16[2,8,3456]{2,1,0:T(8,128)(2,1)S(1)} collective-permute-done((bf16[2,8,3456]{2,1,0:T(8,128)(2,1)S(1)}, bf16[2,8,3456]{2,1,0:T(8,128)(2,1)S(1)}, u32[]{:S(2)}, u32[]{:S(2)}) %collective-permute-start.17) | collective-permute-done | bytes 110624 | tf_op jit(solution)/shard_map/ppermute | solution.py:342
  49.2 1.6 %collective-permute-done.18.refs_6_ = bf16[2,8,3456]{2,1,0:T(8,128)(2,1)S(1)} collective-permute-done((bf16[2,8,3456]{2,1,0:T(8,128)(2,1)S(1)}, bf16[2,8,3456]{2,1,0:T(8,128)(2,1)S(1)}, u32[]{:S(2)}, u32[]{:S(2)}) %collective-permute-start.18) | collective-permute-done | bytes 110624 | tf_op jit(solution)/shard_map/ppermute | solution.py:342
  50.8 1.0 %collective-permute-done.12.refs_2_ = bf16[1,16,3456]{2,1,0:T(8,128)(2,1)S(1)} collective-permute-done((bf16[1,16,3456]{2,1,0:T(8,128)(2,1)S(1)}, bf16[1,16,3456]{2,1,0:T(8,128)(2,1)S(1)}, u32[]{:S(2)}, u32[]{:S(2)}) %collective-permute-start.12) | collective-permute-done | bytes 110624 | tf_op jit(solution)/shard_map/ppermute | solution.py:342
  51.8 0.1 shard_map.81
  51.9 1.6 %collective-permute-start.19 = (bf16[24,3456]{1,0:T(8,128)(2,1)S(1)}, bf16[24,3456]{1,0:T(8,128)(2,1)S(1)}, u32[]{:S(2)}, u32[]{:S(2)}) collective-permute-start(bf16[24,3456]{1,0:T(8,128)(2,1)S(1)} %get-tuple-element.93.refs_0_), channel_id=1, source_target_pairs={{0,16},{1,17},{2,18},{3,19},{4,20},{5,21},{6,22},{7,23},{8,24},{9,... | collective-permute-start | bytes 497672 | tf_op jit(solution)/shard_map/ppermute | solution.py:347
  53.5 2.2 %collective-permute-start.21 = (bf16[8,3456]{1,0:T(8,128)(2,1)S(1)}, bf16[8,3456]{1,0:T(8,128)(2,1)S(1)}, u32[]{:S(2)}, u32[]{:S(2)}) collective-permute-start(bf16[8,3456]{1,0:T(8,128)(2,1)S(1)} %get-tuple-element.94), channel_id=1, source_target_pairs={{0,24},{1,25},{2,26},{3,27},{4,28},{5,29},{6,30},{7,31},{8,16},{9,... | collective-permute-start | bytes 165896 | tf_op jit(solution)/shard_map/ppermute | solution.py:347
  55.7 0.7 %collective-permute-start.20 = (bf16[8,3456]{1,0:T(8,128)(2,1)S(1)}, bf16[8,3456]{1,0:T(8,128)(2,1)S(1)}, u32[]{:S(2)}, u32[]{:S(2)}) collective-permute-start(bf16[8,3456]{1,0:T(8,128)(2,1)S(1)} %get-tuple-element.94), channel_id=1, source_target_pairs={{0,8},{1,9},{2,10},{3,11},{4,12},{5,13},{6,14},{7,15},{8,0},{9,1},... | collective-permute-start | bytes 165896 | tf_op jit(solution)/shard_map/ppermute | solution.py:342
  56.3 3.1 %collective-permute-done.21.refs_3_ = bf16[8,3456]{1,0:T(8,128)(2,1)S(1)} collective-permute-done((bf16[8,3456]{1,0:T(8,128)(2,1)S(1)}, bf16[8,3456]{1,0:T(8,128)(2,1)S(1)}, u32[]{:S(2)}, u32[]{:S(2)}) %collective-permute-start.21) | collective-permute-done | bytes 55328 | tf_op jit(solution)/shard_map/ppermute | solution.py:347
  59.4 1.3 %collective-permute-done.20.refs_2_ = bf16[8,3456]{1,0:T(8,128)(2,1)S(1)} collective-permute-done((bf16[8,3456]{1,0:T(8,128)(2,1)S(1)}, bf16[8,3456]{1,0:T(8,128)(2,1)S(1)}, u32[]{:S(2)}, u32[]{:S(2)}) %collective-permute-start.20) | collective-permute-done | bytes 55328 | tf_op jit(solution)/shard_map/ppermute | solution.py:342
  60.7 0.0 collective-permute-done.19.refs_1_
  60.7 0.7 %shard_map.82 = (f32[8,3456]{1,0:T(8,128)}, f32[16,3456]{1,0:T(8,128)}) custom-call(bf16[24,3456]{1,0:T(8,128)(2,1)S(1)} %get-tuple-element.93.refs_0_, bf16[24,3456]{1,0:T(8,128)(2,1)S(1)} %collective-permute-done.19.refs_1_, bf16[8,3456]{1,0:T(8,128)(2,1)S(1)} %collective-permute-done.20.refs_2_, bf16[8,3456]{1,0:T(8,128)(2,1)S(1)} %collective-permute-done.21.refs_3_), custom_call_target="tpu_custom_call" | custom-call | bytes 1048576 | tf_op jit(solution)/shard_map/pallas_call | solution.py:27
  (4 shorter events, 0.1 us)
Async XLA Ops:
  0.6 1.2 %copy-start.1 = (bf16[1,4,16,64,128]{4,3,2,1,0:T(8,128)(2,1)S(1)}, bf16[1,4,16,64,128]{4,3,2,1,0:T(8,128)(2,1)}, u32[]{:S(2)}) copy-start(bf16[1,4,16,64,128]{4,3,2,1,0:T(8,128)(2,1)} %param.4) | copy-start | bytes 3145732
  1.9 1.3 %copy-start.2 = (bf16[1,2,8,32,256]{4,3,2,1,0:T(8,128)(2,1)S(1)}, bf16[1,2,8,32,256]{4,3,2,1,0:T(8,128)(2,1)}, u32[]{:S(2)}) copy-start(bf16[1,2,8,32,256]{4,3,2,1,0:T(8,128)(2,1)} %param.7) | copy-start | bytes 786436
  1.9 1.3 %copy-start.3 = (bf16[27,128,128]{2,1,0:T(8,128)(2,1)S(1)}, bf16[27,128,128]{2,1,0:T(8,128)(2,1)}, u32[]{:S(2)}) copy-start(bf16[27,128,128]{2,1,0:T(8,128)(2,1)} %param.5) | copy-start | bytes 2654212
  1.9 10.6 %collective-permute-start = (bf16[1,16,64,128]{3,2,1,0:T(8,128)(2,1)S(1)}, bf16[1,16,64,128]{3,2,1,0:T(8,128)(2,1)S(1)}, u32[]{:S(2)}, u32[]{:S(2)}) collective-permute-start(bf16[1,16,64,128]{3,2,1,0:T(8,128)(2,1)S(1)} %get-tuple-element.50), channel_id=1, source_target_pairs={{0,1},{1,0},{2,3},{3,2},{4,5},{5,4},{6,7},{7,6},{8,9},{9,8},{10,11... | collective-permute-start | bytes 786440 | tf_op jit(solution)/shard_map/ppermute | solution.py:43
  2.4 10.1 %collective-permute-start.1 = (bf16[1,16,64,128]{3,2,1,0:T(8,128)(2,1)S(1)}, bf16[1,16,64,128]{3,2,1,0:T(8,128)(2,1)S(1)}, u32[]{:S(2)}, u32[]{:S(2)}) collective-permute-start(bf16[1,16,64,128]{3,2,1,0:T(8,128)(2,1)S(1)} %get-tuple-element.51), channel_id=1, source_target_pairs={{1,2},{3,4},{5,6},{7,8},{9,10},{11,12},{13,14},{2,1},{4,3},{6,5},{... | collective-permute-start | bytes 786440 | tf_op jit(solution)/shard_map/ppermute | solution.py:43
  7.8 10.0 %copy-start = (bf16[27,128,256]{2,1,0:T(8,128)(2,1)S(1)}, bf16[27,128,256]{2,1,0:T(8,128)(2,1)}, u32[]{:S(2)}) copy-start(bf16[27,128,256]{2,1,0:T(8,128)(2,1)} %refs_1_.1) | copy-start | bytes 5308420
  7.8 11.2 %collective-permute-start.4 = (bf16[1,8,32,256]{3,2,1,0:T(8,128)(2,1)S(1)}, bf16[1,8,32,256]{3,2,1,0:T(8,128)(2,1)S(1)}, u32[]{:S(2)}, u32[]{:S(2)}) collective-permute-start(bf16[1,8,32,256]{3,2,1,0:T(8,128)(2,1)S(1)} %get-tuple-element.59), channel_id=1, source_target_pairs={{0,1},{1,0},{2,3},{3,2},{4,5},{5,4},{6,7},{7,6},{8,9},{9,8},{10,11... | collective-permute-start | bytes 393224 | tf_op jit(solution)/shard_map/ppermute | solution.py:43
  11.9 7.2 %collective-permute-start.5 = (bf16[1,8,32,256]{3,2,1,0:T(8,128)(2,1)S(1)}, bf16[1,8,32,256]{3,2,1,0:T(8,128)(2,1)S(1)}, u32[]{:S(2)}, u32[]{:S(2)}) collective-permute-start(bf16[1,8,32,256]{3,2,1,0:T(8,128)(2,1)S(1)} %get-tuple-element.60), channel_id=1, source_target_pairs={{1,2},{3,4},{5,6},{7,8},{9,10},{11,12},{13,14},{2,1},{4,3},{6,5},{... | collective-permute-start | bytes 393224 | tf_op jit(solution)/shard_map/ppermute | solution.py:43
  14.0 5.0 %collective-permute-start.2 = (bf16[2,8,32,128]{3,2,1,0:T(8,128)(2,1)S(1)}, bf16[2,8,32,128]{3,2,1,0:T(8,128)(2,1)S(1)}, u32[]{:S(2)}, u32[]{:S(2)}) collective-permute-start(bf16[2,8,32,128]{3,2,1,0:T(8,128)(2,1)S(1)} %get-tuple-element.55), channel_id=1, source_target_pairs={{0,1},{1,0},{2,3},{3,2},{4,5},{5,4},{6,7},{7,6},{8,9},{9,8},{10,11... | collective-permute-start | bytes 393224 | tf_op jit(solution)/shard_map/ppermute | solution.py:43
  17.0 2.1 %collective-permute-start.3 = (bf16[2,8,32,128]{3,2,1,0:T(8,128)(2,1)S(1)}, bf16[2,8,32,128]{3,2,1,0:T(8,128)(2,1)S(1)}, u32[]{:S(2)}, u32[]{:S(2)}) collective-permute-start(bf16[2,8,32,128]{3,2,1,0:T(8,128)(2,1)S(1)} %get-tuple-element.56), channel_id=1, source_target_pairs={{1,2},{3,4},{5,6},{7,8},{9,10},{11,12},{13,14},{2,1},{4,3},{6,5},{... | collective-permute-start | bytes 393224 | tf_op jit(solution)/shard_map/ppermute | solution.py:43
  22.1 6.5 %collective-permute-start.6 = (bf16[8,16,1920]{2,1,0:T(8,128)(2,1)S(1)}, bf16[8,16,1920]{2,1,0:T(8,128)(2,1)S(1)}, u32[]{:S(2)}, u32[]{:S(2)}) collective-permute-start(bf16[8,16,1920]{2,1,0:T(8,128)(2,1)S(1)} %get-tuple-element.66), channel_id=1, source_target_pairs={{0,1},{1,0},{2,3},{3,2},{4,5},{5,4},{6,7},{7,6},{8,9},{9,8},{10,11... | collective-permute-start | bytes 1474568 | tf_op jit(solution)/shard_map/ppermute | solution.py:342
  26.4 5.9 %collective-permute-start.9 = (bf16[8,16,1536]{2,1,0:T(8,128)(2,1)S(1)}, bf16[8,16,1536]{2,1,0:T(8,128)(2,1)S(1)}, u32[]{:S(2)}, u32[]{:S(2)}) collective-permute-start(bf16[8,16,1536]{2,1,0:T(8,128)(2,1)S(1)} %get-tuple-element.69.refs_4_), channel_id=1, source_target_pairs={{0,1},{1,0},{2,3},{3,2},{4,5},{5,4},{6,7},{7,6},{8,9},{9,8},{10,11... | collective-permute-start | bytes 1179656 | tf_op jit(solution)/shard_map/ppermute | solution.py:342
  28.7 10.0 %collective-permute-start.7 = (bf16[4,16,1920]{2,1,0:T(8,128)(2,1)S(1)}, bf16[4,16,1920]{2,1,0:T(8,128)(2,1)S(1)}, u32[]{:S(2)}, u32[]{:S(2)}) collective-permute-start(bf16[4,16,1920]{2,1,0:T(8,128)(2,1)S(1)} %get-tuple-element.71.refs_4_), channel_id=1, source_target_pairs={{0,2},{1,3},{2,0},{3,1},{4,6},{5,7},{6,4},{7,5},{8,10},{9,11},{10,... | collective-permute-start | bytes 737288 | tf_op jit(solution)/shard_map/ppermute | solution.py:342
  32.3 7.9 %collective-permute-start.10 = (bf16[4,16,1536]{2,1,0:T(8,128)(2,1)S(1)}, bf16[4,16,1536]{2,1,0:T(8,128)(2,1)S(1)}, u32[]{:S(2)}, u32[]{:S(2)}) collective-permute-start(bf16[4,16,1536]{2,1,0:T(8,128)(2,1)S(1)} %get-tuple-element.76.refs_5_), channel_id=1, source_target_pairs={{0,4},{1,5},{2,6},{3,7},{4,0},{5,1},{6,2},{7,3},{8,12},{9,13},{10,... | collective-permute-start | bytes 589832 | tf_op jit(solution)/shard_map/ppermute | solution.py:342
  38.0 4.0 %collective-permute-start.13 = (bf16[8,8,1152]{2,1,0:T(8,128)(2,1)S(1)}, bf16[8,8,1152]{2,1,0:T(8,128)(2,1)S(1)}, u32[]{:S(2)}, u32[]{:S(2)}) collective-permute-start(bf16[8,8,1152]{2,1,0:T(8,128)(2,1)S(1)} %get-tuple-element.84), channel_id=1, source_target_pairs={{0,1},{1,0},{2,3},{3,2},{4,5},{5,4},{6,7},{7,6},{8,9},{9,8},{10,11... | collective-permute-start | bytes 442376 | tf_op jit(solution)/shard_map/ppermute | solution.py:342
  38.1 3.9 %collective-permute-start.14 = (bf16[8,8,1152]{2,1,0:T(8,128)(2,1)S(1)}, bf16[8,8,1152]{2,1,0:T(8,128)(2,1)S(1)}, u32[]{:S(2)}, u32[]{:S(2)}) collective-permute-start(bf16[8,8,1152]{2,1,0:T(8,128)(2,1)S(1)} %get-tuple-element.86), channel_id=1, source_target_pairs={{0,1},{1,0},{2,3},{3,2},{4,5},{5,4},{6,7},{7,6},{8,9},{9,8},{10,11... | collective-permute-start | bytes 442376 | tf_op jit(solution)/shard_map/ppermute | solution.py:342
  38.6 3.4 %collective-permute-start.15 = (bf16[8,8,1152]{2,1,0:T(8,128)(2,1)S(1)}, bf16[8,8,1152]{2,1,0:T(8,128)(2,1)S(1)}, u32[]{:S(2)}, u32[]{:S(2)}) collective-permute-start(bf16[8,8,1152]{2,1,0:T(8,128)(2,1)S(1)} %get-tuple-element.88), channel_id=1, source_target_pairs={{0,1},{1,0},{2,3},{3,2},{4,5},{5,4},{6,7},{7,6},{8,9},{9,8},{10,11... | collective-permute-start | bytes 442376 | tf_op jit(solution)/shard_map/ppermute | solution.py:342
  38.8 7.0 %collective-permute-start.8 = (bf16[2,16,1920]{2,1,0:T(8,128)(2,1)S(1)}, bf16[2,16,1920]{2,1,0:T(8,128)(2,1)S(1)}, u32[]{:S(2)}, u32[]{:S(2)}) collective-permute-start(bf16[2,16,1920]{2,1,0:T(8,128)(2,1)S(1)} %get-tuple-element.73.refs_7_), channel_id=1, source_target_pairs={{0,4},{1,5},{2,6},{3,7},{4,0},{5,1},{6,2},{7,3},{8,12},{9,13},{10,... | collective-permute-start | bytes 368648 | tf_op jit(solution)/shard_map/ppermute | solution.py:342
  40.3 5.5 %collective-permute-start.11 = (bf16[2,16,1536]{2,1,0:T(8,128)(2,1)S(1)}, bf16[2,16,1536]{2,1,0:T(8,128)(2,1)S(1)}, u32[]{:S(2)}, u32[]{:S(2)}) collective-permute-start(bf16[2,16,1536]{2,1,0:T(8,128)(2,1)S(1)} %get-tuple-element.78.refs_8_), channel_id=1, source_target_pairs={{0,2},{1,3},{2,0},{3,1},{4,6},{5,7},{6,4},{7,5},{8,10},{9,11},{10,... | collective-permute-start | bytes 294920 | tf_op jit(solution)/shard_map/ppermute | solution.py:342
  42.1 6.2 %collective-permute-start.16 = (bf16[2,8,3456]{2,1,0:T(8,128)(2,1)S(1)}, bf16[2,8,3456]{2,1,0:T(8,128)(2,1)S(1)}, u32[]{:S(2)}, u32[]{:S(2)}) collective-permute-start(bf16[2,8,3456]{2,1,0:T(8,128)(2,1)S(1)} %get-tuple-element.90), channel_id=1, source_target_pairs={{0,2},{1,3},{2,0},{3,1},{4,6},{5,7},{6,4},{7,5},{8,10},{9,11},{10,... | collective-permute-start | bytes 331784 | tf_op jit(solution)/shard_map/ppermute | solution.py:342
  42.6 6.6 %collective-permute-start.17 = (bf16[2,8,3456]{2,1,0:T(8,128)(2,1)S(1)}, bf16[2,8,3456]{2,1,0:T(8,128)(2,1)S(1)}, u32[]{:S(2)}, u32[]{:S(2)}) collective-permute-start(bf16[2,8,3456]{2,1,0:T(8,128)(2,1)S(1)} %get-tuple-element.91), channel_id=1, source_target_pairs={{0,4},{1,5},{2,6},{3,7},{4,0},{5,1},{6,2},{7,3},{8,12},{9,13},{10,... | collective-permute-start | bytes 331784 | tf_op jit(solution)/shard_map/ppermute | solution.py:342
  43.2 7.6 %collective-permute-start.18 = (bf16[2,8,3456]{2,1,0:T(8,128)(2,1)S(1)}, bf16[2,8,3456]{2,1,0:T(8,128)(2,1)S(1)}, u32[]{:S(2)}, u32[]{:S(2)}) collective-permute-start(bf16[2,8,3456]{2,1,0:T(8,128)(2,1)S(1)} %get-tuple-element.92), channel_id=1, source_target_pairs={{0,6},{1,7},{2,4},{3,5},{4,2},{5,3},{6,0},{7,1},{8,14},{9,15},{10,... | collective-permute-start | bytes 331784 | tf_op jit(solution)/shard_map/ppermute | solution.py:342
  45.8 6.0 %collective-permute-start.12 = (bf16[1,16,3456]{2,1,0:T(8,128)(2,1)S(1)}, bf16[1,16,3456]{2,1,0:T(8,128)(2,1)S(1)}, u32[]{:S(2)}, u32[]{:S(2)}) collective-permute-start(bf16[1,16,3456]{2,1,0:T(8,128)(2,1)S(1)} %get-tuple-element.80), channel_id=1, source_target_pairs={{0,8},{1,9},{2,10},{3,11},{4,12},{5,13},{6,14},{7,15},{8,0},{9,1},... | collective-permute-start | bytes 331784 | tf_op jit(solution)/shard_map/ppermute | solution.py:342
  51.9 8.8 %collective-permute-start.19 = (bf16[24,3456]{1,0:T(8,128)(2,1)S(1)}, bf16[24,3456]{1,0:T(8,128)(2,1)S(1)}, u32[]{:S(2)}, u32[]{:S(2)}) collective-permute-start(bf16[24,3456]{1,0:T(8,128)(2,1)S(1)} %get-tuple-element.93.refs_0_), channel_id=1, source_target_pairs={{0,16},{1,17},{2,18},{3,19},{4,20},{5,21},{6,22},{7,23},{8,24},{9,... | collective-permute-start | bytes 497672 | tf_op jit(solution)/shard_map/ppermute | solution.py:347
  53.5 6.0 %collective-permute-start.21 = (bf16[8,3456]{1,0:T(8,128)(2,1)S(1)}, bf16[8,3456]{1,0:T(8,128)(2,1)S(1)}, u32[]{:S(2)}, u32[]{:S(2)}) collective-permute-start(bf16[8,3456]{1,0:T(8,128)(2,1)S(1)} %get-tuple-element.94), channel_id=1, source_target_pairs={{0,24},{1,25},{2,26},{3,27},{4,28},{5,29},{6,30},{7,31},{8,16},{9,... | collective-permute-start | bytes 165896 | tf_op jit(solution)/shard_map/ppermute | solution.py:347
  55.7 5.1 %collective-permute-start.20 = (bf16[8,3456]{1,0:T(8,128)(2,1)S(1)}, bf16[8,3456]{1,0:T(8,128)(2,1)S(1)}, u32[]{:S(2)}, u32[]{:S(2)}) collective-permute-start(bf16[8,3456]{1,0:T(8,128)(2,1)S(1)} %get-tuple-element.94), channel_id=1, source_target_pairs={{0,8},{1,9},{2,10},{3,11},{4,12},{5,13},{6,14},{7,15},{8,0},{9,1},... | collective-permute-start | bytes 165896 | tf_op jit(solution)/shard_map/ppermute | solution.py:342

commit v8 on v7

--- a/solution.py
+++ b/solution.py
@@ -616,7 +616,7 @@
     sends = []
     if len(bits) > 1:
         for side, sequence in enumerate((bits, turned)):
-            sends.append(fold(place, [halves[side]], sequence[:1], [fine_delta]))
+            sends.append(fold(place, [halves[side]], sequence[:1], [fine_delta][:side]))
     early = [item for send, _ in sends for item in send.values()]
     terms = kernel_call(
         functools.partial(fine_terms, order=order),

time: 61.7 us -> 62.5 us (1.013)
  waiting for transfers between devices: 7.93 us -> 10.8 us
  starting transfers between devices: 33.6 us -> 31.6 us
    ppermute x14, waiting for transfers between devices: 4.86 us -> 7.61 us  [swap(): return lax.ppermute(value, 'space', [(i, i ^ bit) for i in range(count)])]
    ppermute x14, starting transfers between devices: 20.1 us -> 18.6 us  [swap(): return lax.ppermute(value, 'space', [(i, i ^ bit) for i in range(count)])]
  transfers between devices with their start and end apart: 22 -> 22, of which waited for: 5 -> 7; matrix products, arithmetic and copies ran while one was open for 0% -> 0% of each run, Pallas kernels for 23% -> 22%
where the time goes in v8:
time: 62.5 us; the launch traced here: 62.3 us
  starting transfers between devices  31.6 us (51%)
  Pallas kernels  17.8 us (28%)
  waiting for transfers between devices  10.8 us (17%)
  local copies, waits for them, and re-layouts  1.23 us (2%)
  between operations  0.85 us (1%)
    ppermute x14, starting transfers between devices, swap(): return lax.ppermute(value, 'space', [(i, i ^ bit) for i in range(count)])  18.6 us
    pallas_call x15, Pallas kernels, kernel_call(): pl.pallas_call(inner, out_shape=outs, in_specs=specs, out_specs=[VMEM] *...  17.8 us
    ppermute x14, waiting for transfers between devices, swap(): return lax.ppermute(value, 'space', [(i, i ^ bit) for i in range(count)])  7.61 us
    ppermute x3, starting transfers between devices, exchange(): lax.ppermute(to_pair, 'space', pair)  7.54 us
    ppermute x2, starting transfers between devices, swap_sample(): lax.ppermute(value, ('sample', 'space'), [(s * count + i, (1 - s) * count...  3.26 us
    ppermute x2, waiting for transfers between devices, swap_sample(): lax.ppermute(value, ('sample', 'space'), [(s * count + i, (1 - s) * count...  3.19 us
    ppermute x3, starting transfers between devices, exchange(): lax.ppermute(to_next, 'space', across)  2.16 us
  transfers between devices with their start and end apart: 22, of which 7 were waited for; matrix products, arithmetic and copies ran while one was open for 0% of the time, Pallas kernels for 22%

profile of v8, /device:TPU:0, one launch (start us, length us, event | category | flops | bytes accessed | tf_op | source)
XLA Modules:
  0.0 62.3 jit_solution(7272519692354918963)
XLA Ops:
  0.6 0.0 copy-start.1
  0.6 1.2 %copy-done.1 = bf16[1,4,16,64,128]{4,3,2,1,0:T(8,128)(2,1)S(1)} copy-done((bf16[1,4,16,64,128]{4,3,2,1,0:T(8,128)(2,1)S(1)}, bf16[1,4,16,64,128]{4,3,2,1,0:T(8,128)(2,1)}, u32[]{:S(2)}) %copy-start.1) | copy-done | bytes 1048600
  1.9 0.1 shard_map.67
  1.9 0.5 collective-permute-start
  2.4 0.7 %collective-permute-start.1 = (bf16[1,16,64,128]{3,2,1,0:T(8,128)(2,1)S(1)}, bf16[1,16,64,128]{3,2,1,0:T(8,128)(2,1)S(1)}, u32[]{:S(2)}, u32[]{:S(2)}) collective-permute-start(bf16[1,16,64,128]{3,2,1,0:T(8,128)(2,1)S(1)} %get-tuple-element.51), channel_id=1, source_target_pairs={{1,2},{3,4},{5,6},{7,8},{9,10},{11,12},{13,14},{2,1},{4,3},{6,5},{... | collective-permute-start | bytes 786440 | tf_op jit(solution)/shard_map/ppermute | solution.py:43
  3.1 0.0 copy-done.2
  3.1 0.0 copy-done.3
  3.1 4.6 %shard_map.68 = (bf16[4,9,64,768]{3,2,1,0:T(8,128)(2,1)S(1)}, bf16[3,2,768,256]{3,2,1,0:T(8,128)(2,1)S(1)}, f32[2,512,256]{2,1,0:T(8,128)S(1)}, f32[2,8,64,128]{...) custom-call(s32[1]{0:T(128)} %bitcast.place.refs_0_, ...), custom_call_target="tpu_custom_call" | custom-call | flops 56623104 | bytes 1048576 | tf_op jit(solution)/shard_map/pallas_call | solution.py:27
  7.8 0.0 copy-start
  7.8 4.1 %collective-permute-start.4 = (bf16[1,8,32,256]{3,2,1,0:T(8,128)(2,1)S(1)}, bf16[1,8,32,256]{3,2,1,0:T(8,128)(2,1)S(1)}, u32[]{:S(2)}, u32[]{:S(2)}) collective-permute-start(bf16[1,8,32,256]{3,2,1,0:T(8,128)(2,1)S(1)} %get-tuple-element.59), channel_id=1, source_target_pairs={{0,1},{1,0},{2,3},{3,2},{4,5},{5,4},{6,7},{7,6},{8,9},{9,8},{10,11... | collective-permute-start | bytes 393224 | tf_op jit(solution)/shard_map/ppermute | solution.py:43
  11.9 0.7 %collective-permute-start.5 = (bf16[1,8,32,256]{3,2,1,0:T(8,128)(2,1)S(1)}, bf16[1,8,32,256]{3,2,1,0:T(8,128)(2,1)S(1)}, u32[]{:S(2)}, u32[]{:S(2)}) collective-permute-start(bf16[1,8,32,256]{3,2,1,0:T(8,128)(2,1)S(1)} %get-tuple-element.60), channel_id=1, source_target_pairs={{1,2},{3,4},{5,6},{7,8},{9,10},{11,12},{13,14},{2,1},{4,3},{6,5},{... | collective-permute-start | bytes 393224 | tf_op jit(solution)/shard_map/ppermute | solution.py:43
  12.5 0.0 collective-permute-done.refs_1_
  12.5 0.0 collective-permute-done.1.refs_2_
  12.5 1.5 %shard_map.69 = (bf16[2,9,64,768]{3,2,1,0:T(8,128)(2,1)S(1)}, bf16[2,8,32,128]{3,2,1,0:T(8,128)(2,1)S(1)}, bf16[2,8,64,256]{3,2,1,0:T(8,128)(2,1)S(1)}, bf16[2,8...) custom-call(s32[1]{0:T(128)} %bitcast.place.refs_0_, bf16[1,16,64,128]{3,2,1,0:T(8,128)(2,1)S(1)} %collective-permute-done.refs_1_, ...), custom_call_target="tpu_custom_call" | custom-call | flops 9437184 | bytes 1048576 | tf_op jit(solution)/shard_map/pallas_call | solution.py:27
  14.0 2.9 %collective-permute-start.2 = (bf16[2,8,32,128]{3,2,1,0:T(8,128)(2,1)S(1)}, bf16[2,8,32,128]{3,2,1,0:T(8,128)(2,1)S(1)}, u32[]{:S(2)}, u32[]{:S(2)}) collective-permute-start(bf16[2,8,32,128]{3,2,1,0:T(8,128)(2,1)S(1)} %get-tuple-element.55), channel_id=1, source_target_pairs={{0,1},{1,0},{2,3},{3,2},{4,5},{5,4},{6,7},{7,6},{8,9},{9,8},{10,11... | collective-permute-start | bytes 393224 | tf_op jit(solution)/shard_map/ppermute | solution.py:43
  17.0 0.8 %collective-permute-start.3 = (bf16[2,8,32,128]{3,2,1,0:T(8,128)(2,1)S(1)}, bf16[2,8,32,128]{3,2,1,0:T(8,128)(2,1)S(1)}, u32[]{:S(2)}, u32[]{:S(2)}) collective-permute-start(bf16[2,8,32,128]{3,2,1,0:T(8,128)(2,1)S(1)} %get-tuple-element.56), channel_id=1, source_target_pairs={{1,2},{3,4},{5,6},{7,8},{9,10},{11,12},{13,14},{2,1},{4,3},{6,5},{... | collective-permute-start | bytes 393224 | tf_op jit(solution)/shard_map/ppermute | solution.py:43
  17.8 1.2 %shard_map.70 = (bf16[2,10,32,384]{3,2,1,0:T(8,128)(2,1)S(1)}, f32[4,256,256]{2,1,0:T(8,128)S(1)}) custom-call(bf16[2,8,32,128]{3,2,1,0:T(8,128)(2,1)S(1)} %get-tuple-element.57.refs_0_, bf16[3,1152,256]{2,1,0:T(8,128)(2,1)S(1)} %bitcast.6), custom_call_target="tpu_custom_call" | custom-call | flops 14155776 | bytes 1048576 | tf_op jit(solution)/shard_map/pallas_call | solution.py:27
  19.0 0.0 collective-permute-done.4.refs_6_
  19.0 0.0 collective-permute-done.5.refs_7_
  19.0 0.0 collective-permute-done.2.refs_1_
  19.0 0.0 collective-permute-done.3.refs_2_
  19.0 1.9 %shard_map.71 = (bf16[4,10,32,384]{3,2,1,0:T(8,128)(2,1)S(1)}, bf16[2,8,32,256]{3,2,1,0:T(8,128)(2,1)}, bf16[4,8,32,256]{3,2,1,0:T(8,128)(2,1)S(1)}) custom-call(s32[1]{0:T(128)} %bitcast.place.refs_0_, bf16[2,8,32,128]{3,2,1,0:T(8,128)(2,1)S(1)} %collective-permute-done.2.refs_1_, bf16[2,8,32,128]{3,2,1,0:T(8,128)(2,1)S(1)} %collective-permute-done.3.refs_2_, ...), custom_call_target="tpu_custom_call" | custom-call | flops 14155776 | bytes 1048576 | tf_op jit(solution)/shard_map/pallas_call | solution.py:27
  21.0 1.2 %shard_map.72 = (bf16[8,16,1920]{2,1,0:T(8,128)(2,1)S(1)}, bf16[8,16,1920]{2,1,0:T(8,128)(2,1)S(1)}, bf16[8,16,1536]{2,1,0:T(8,128)(2,1)S(1)}, bf16[8,16,1536]{2,1,0:T(8,128)(2,1)S(1)}) custom-call(s32[1]{0:T(128)} %bitcast.place.refs_0_, bf16[2,10,32,384]{3,2,1,0:T(8,128)(2,1)S(1)} %get-tuple-element.62.refs_1_, ...), custom_call_target="tpu_custom_call" | custom-call | flops 14155776 | bytes 1048576 | tf_op jit(solution)/shard_map/pallas_call | solution.py:27
  22.1 4.3 %collective-permute-start.6 = (bf16[8,16,1920]{2,1,0:T(8,128)(2,1)S(1)}, bf16[8,16,1920]{2,1,0:T(8,128)(2,1)S(1)}, u32[]{:S(2)}, u32[]{:S(2)}) collective-permute-start(bf16[8,16,1920]{2,1,0:T(8,128)(2,1)S(1)} %get-tuple-element.66), channel_id=1, source_target_pairs={{0,1},{1,0},{2,3},{3,2},{4,5},{5,4},{6,7},{7,6},{8,9},{9,8},{10,11... | collective-permute-start | bytes 1474568 | tf_op jit(solution)/shard_map/ppermute | solution.py:342
  26.4 0.1 collective-permute-start.9
  26.5 1.4 %collective-permute-done.6.refs_2_ = bf16[8,16,1920]{2,1,0:T(8,128)(2,1)S(1)} collective-permute-done((bf16[8,16,1920]{2,1,0:T(8,128)(2,1)S(1)}, bf16[8,16,1920]{2,1,0:T(8,128)(2,1)S(1)}, u32[]{:S(2)}, u32[]{:S(2)}) %collective-permute-start.6) | collective-permute-done | bytes 491552 | tf_op jit(solution)/shard_map/ppermute | solution.py:342
  27.9 0.1 shard_map.73
  28.0 3.5 %collective-permute-start.7 = (bf16[4,16,1920]{2,1,0:T(8,128)(2,1)S(1)}, bf16[4,16,1920]{2,1,0:T(8,128)(2,1)S(1)}, u32[]{:S(2)}, u32[]{:S(2)}) collective-permute-start(bf16[4,16,1920]{2,1,0:T(8,128)(2,1)S(1)} %get-tuple-element.68.refs_4_), channel_id=1, source_target_pairs={{0,2},{1,3},{2,0},{3,1},{4,6},{5,7},{6,4},{7,5},{8,10},{9,11},{10,... | collective-permute-start | bytes 737288 | tf_op jit(solution)/shard_map/ppermute | solution.py:342
  31.5 2.1 %shard_map.75.refs_3_ = bf16[4,8,64,256]{3,2,1,0:T(8,128)(2,1)S(1)} custom-call(bf16[4,8,32,256]{3,2,1,0:T(8,128)(2,1)S(1)} %get-tuple-element.64.refs_3_.refs_0_, bf16[27,128,256]{2,1,0:T(8,128)(2,1)S(1)} %copy-done, bf16[2,8,64,256]{3,2,1,0:T(8,128)(2,1)S(1)} %get-tuple-element.73.refs_2_, bf16[2,8,64,256]{3,2,1,0:T(8,128)(2,1)S(1)} %get-tuple-element.74.refs_3_, ...), custom_call_target="tpu_custom_call" | custom-call | flops 14155776 | bytes 1048576 | tf_op jit(solution)/shard_map/pallas_call | solution.py:27
  33.6 0.0 collective-permute-done.9.refs_2_
  33.6 0.1 shard_map.76
  33.7 1.6 %collective-permute-start.10 = (bf16[4,16,1536]{2,1,0:T(8,128)(2,1)S(1)}, bf16[4,16,1536]{2,1,0:T(8,128)(2,1)S(1)}, u32[]{:S(2)}, u32[]{:S(2)}) collective-permute-start(bf16[4,16,1536]{2,1,0:T(8,128)(2,1)S(1)} %get-tuple-element.76.refs_5_), channel_id=1, source_target_pairs={{0,4},{1,5},{2,6},{3,7},{4,0},{5,1},{6,2},{7,3},{8,12},{9,13},{10,... | collective-permute-start | bytes 589832 | tf_op jit(solution)/shard_map/ppermute | solution.py:342
  35.3 4.0 %shard_map.79 = (bf16[8,8,1152]{2,1,0:T(8,128)(2,1)S(1)}, bf16[8,8,1152]{2,1,0:T(8,128)(2,1)S(1)}, bf16[8,8,1152]{2,1,0:T(8,128)(2,1)S(1)}, bf16[8,8,1152]{2,1,0...) custom-call(s32[1]{0:T(128)} %bitcast.place.refs_0_, ...), custom_call_target="tpu_custom_call" | custom-call | flops 56623104 | bytes 1048576 | tf_op jit(solution)/shard_map/pallas_call | solution.py:27
  39.4 0.1 collective-permute-start.13
  39.5 0.5 collective-permute-start.14
  40.0 0.1 collective-permute-start.15
  40.0 0.0 collective-permute-done.7.refs_2_
  40.0 0.1 shard_map.74
  40.1 0.5 collective-permute-start.8
  40.6 0.0 collective-permute-done.10.refs_2_
  40.7 0.6 collective-permute-start.11
  41.3 0.0 collective-permute-done.13.refs_2_
  41.3 0.0 collective-permute-done.14.refs_4_
  41.3 0.1 collective-permute-done.15.refs_6_
  41.3 0.1 shard_map.80
  41.4 1.5 %collective-permute-start.16 = (bf16[2,8,3456]{2,1,0:T(8,128)(2,1)S(1)}, bf16[2,8,3456]{2,1,0:T(8,128)(2,1)S(1)}, u32[]{:S(2)}, u32[]{:S(2)}) collective-permute-start(bf16[2,8,3456]{2,1,0:T(8,128)(2,1)S(1)} %get-tuple-element.90), channel_id=1, source_target_pairs={{0,2},{1,3},{2,0},{3,1},{4,6},{5,7},{6,4},{7,5},{8,10},{9,11},{10,... | collective-permute-start | bytes 331784 | tf_op jit(solution)/shard_map/ppermute | solution.py:342
  43.0 1.6 %collective-permute-start.17 = (bf16[2,8,3456]{2,1,0:T(8,128)(2,1)S(1)}, bf16[2,8,3456]{2,1,0:T(8,128)(2,1)S(1)}, u32[]{:S(2)}, u32[]{:S(2)}) collective-permute-start(bf16[2,8,3456]{2,1,0:T(8,128)(2,1)S(1)} %get-tuple-element.91), channel_id=1, source_target_pairs={{0,4},{1,5},{2,6},{3,7},{4,0},{5,1},{6,2},{7,3},{8,12},{9,13},{10,... | collective-permute-start | bytes 331784 | tf_op jit(solution)/shard_map/ppermute | solution.py:342
  44.5 0.5 collective-permute-start.18
  45.0 1.4 %collective-permute-done.11.refs_4_ = bf16[2,16,1536]{2,1,0:T(8,128)(2,1)S(1)} collective-permute-done((bf16[2,16,1536]{2,1,0:T(8,128)(2,1)S(1)}, bf16[2,16,1536]{2,1,0:T(8,128)(2,1)S(1)}, u32[]{:S(2)}, u32[]{:S(2)}) %collective-permute-start.11) | collective-permute-done | bytes 98336 | tf_op jit(solution)/shard_map/ppermute | solution.py:342
  46.4 0.0 collective-permute-done.8.refs_2_
  46.4 0.1 shard_map.78
  46.4 2.6 %collective-permute-start.12 = (bf16[1,16,3456]{2,1,0:T(8,128)(2,1)S(1)}, bf16[1,16,3456]{2,1,0:T(8,128)(2,1)S(1)}, u32[]{:S(2)}, u32[]{:S(2)}) collective-permute-start(bf16[1,16,3456]{2,1,0:T(8,128)(2,1)S(1)} %get-tuple-element.80), channel_id=1, source_target_pairs={{0,8},{1,9},{2,10},{3,11},{4,12},{5,13},{6,14},{7,15},{8,0},{9,1},... | collective-permute-start | bytes 331784 | tf_op jit(solution)/shard_map/ppermute | solution.py:342
  49.1 0.0 collective-permute-done.16.refs_4_
  49.1 0.0 collective-permute-done.17.refs_5_
  49.1 3.5 %collective-permute-done.18.refs_6_ = bf16[2,8,3456]{2,1,0:T(8,128)(2,1)S(1)} collective-permute-done((bf16[2,8,3456]{2,1,0:T(8,128)(2,1)S(1)}, bf16[2,8,3456]{2,1,0:T(8,128)(2,1)S(1)}, u32[]{:S(2)}, u32[]{:S(2)}) %collective-permute-start.18) | collective-permute-done | bytes 110624 | tf_op jit(solution)/shard_map/ppermute | solution.py:342
  52.6 0.5 collective-permute-done.12.refs_2_
  53.1 0.1 shard_map.81
  53.2 1.6 %collective-permute-start.19 = (bf16[24,3456]{1,0:T(8,128)(2,1)S(1)}, bf16[24,3456]{1,0:T(8,128)(2,1)S(1)}, u32[]{:S(2)}, u32[]{:S(2)}) collective-permute-start(bf16[24,3456]{1,0:T(8,128)(2,1)S(1)} %get-tuple-element.93.refs_0_), channel_id=1, source_target_pairs={{0,16},{1,17},{2,18},{3,19},{4,20},{5,21},{6,22},{7,23},{8,24},{9,... | collective-permute-start | bytes 497672 | tf_op jit(solution)/shard_map/ppermute | solution.py:347
  54.8 1.7 %collective-permute-start.21 = (bf16[8,3456]{1,0:T(8,128)(2,1)S(1)}, bf16[8,3456]{1,0:T(8,128)(2,1)S(1)}, u32[]{:S(2)}, u32[]{:S(2)}) collective-permute-start(bf16[8,3456]{1,0:T(8,128)(2,1)S(1)} %get-tuple-element.94), channel_id=1, source_target_pairs={{0,24},{1,25},{2,26},{3,27},{4,28},{5,29},{6,30},{7,31},{8,16},{9,... | collective-permute-start | bytes 165896 | tf_op jit(solution)/shard_map/ppermute | solution.py:347
  56.5 1.2 %collective-permute-start.20 = (bf16[8,3456]{1,0:T(8,128)(2,1)S(1)}, bf16[8,3456]{1,0:T(8,128)(2,1)S(1)}, u32[]{:S(2)}, u32[]{:S(2)}) collective-permute-start(bf16[8,3456]{1,0:T(8,128)(2,1)S(1)} %get-tuple-element.94), channel_id=1, source_target_pairs={{0,8},{1,9},{2,10},{3,11},{4,12},{5,13},{6,14},{7,15},{8,0},{9,1},... | collective-permute-start | bytes 165896 | tf_op jit(solution)/shard_map/ppermute | solution.py:342
  57.6 3.2 %collective-permute-done.21.refs_3_ = bf16[8,3456]{1,0:T(8,128)(2,1)S(1)} collective-permute-done((bf16[8,3456]{1,0:T(8,128)(2,1)S(1)}, bf16[8,3456]{1,0:T(8,128)(2,1)S(1)}, u32[]{:S(2)}, u32[]{:S(2)}) %collective-permute-start.21) | collective-permute-done | bytes 55328 | tf_op jit(solution)/shard_map/ppermute | solution.py:347
  60.8 0.7 %collective-permute-done.20.refs_2_ = bf16[8,3456]{1,0:T(8,128)(2,1)S(1)} collective-permute-done((bf16[8,3456]{1,0:T(8,128)(2,1)S(1)}, bf16[8,3456]{1,0:T(8,128)(2,1)S(1)}, u32[]{:S(2)}, u32[]{:S(2)}) %collective-permute-start.20) | collective-permute-done | bytes 55328 | tf_op jit(solution)/shard_map/ppermute | solution.py:342
  61.6 0.0 collective-permute-done.19.refs_1_
  61.6 0.7 %shard_map.82 = (f32[8,3456]{1,0:T(8,128)}, f32[16,3456]{1,0:T(8,128)}) custom-call(bf16[24,3456]{1,0:T(8,128)(2,1)S(1)} %get-tuple-element.93.refs_0_, bf16[24,3456]{1,0:T(8,128)(2,1)S(1)} %collective-permute-done.19.refs_1_, bf16[8,3456]{1,0:T(8,128)(2,1)S(1)} %collective-permute-done.20.refs_2_, bf16[8,3456]{1,0:T(8,128)(2,1)S(1)} %collective-permute-done.21.refs_3_), custom_call_target="tpu_custom_call" | custom-call | bytes 1048576 | tf_op jit(solution)/shard_map/pallas_call | solution.py:27
  (4 shorter events, 0.0 us)
Async XLA Ops:
  0.6 1.2 %copy-start.1 = (bf16[1,4,16,64,128]{4,3,2,1,0:T(8,128)(2,1)S(1)}, bf16[1,4,16,64,128]{4,3,2,1,0:T(8,128)(2,1)}, u32[]{:S(2)}) copy-start(bf16[1,4,16,64,128]{4,3,2,1,0:T(8,128)(2,1)} %param.4) | copy-start | bytes 3145732
  1.9 1.3 %copy-start.2 = (bf16[1,2,8,32,256]{4,3,2,1,0:T(8,128)(2,1)S(1)}, bf16[1,2,8,32,256]{4,3,2,1,0:T(8,128)(2,1)}, u32[]{:S(2)}) copy-start(bf16[1,2,8,32,256]{4,3,2,1,0:T(8,128)(2,1)} %param.7) | copy-start | bytes 786436
  1.9 1.3 %copy-start.3 = (bf16[27,128,128]{2,1,0:T(8,128)(2,1)S(1)}, bf16[27,128,128]{2,1,0:T(8,128)(2,1)}, u32[]{:S(2)}) copy-start(bf16[27,128,128]{2,1,0:T(8,128)(2,1)} %param.5) | copy-start | bytes 2654212
  1.9 10.6 %collective-permute-start = (bf16[1,16,64,128]{3,2,1,0:T(8,128)(2,1)S(1)}, bf16[1,16,64,128]{3,2,1,0:T(8,128)(2,1)S(1)}, u32[]{:S(2)}, u32[]{:S(2)}) collective-permute-start(bf16[1,16,64,128]{3,2,1,0:T(8,128)(2,1)S(1)} %get-tuple-element.50), channel_id=1, source_target_pairs={{0,1},{1,0},{2,3},{3,2},{4,5},{5,4},{6,7},{7,6},{8,9},{9,8},{10,11... | collective-permute-start | bytes 786440 | tf_op jit(solution)/shard_map/ppermute | solution.py:43
  2.4 10.1 %collective-permute-start.1 = (bf16[1,16,64,128]{3,2,1,0:T(8,128)(2,1)S(1)}, bf16[1,16,64,128]{3,2,1,0:T(8,128)(2,1)S(1)}, u32[]{:S(2)}, u32[]{:S(2)}) collective-permute-start(bf16[1,16,64,128]{3,2,1,0:T(8,128)(2,1)S(1)} %get-tuple-element.51), channel_id=1, source_target_pairs={{1,2},{3,4},{5,6},{7,8},{9,10},{11,12},{13,14},{2,1},{4,3},{6,5},{... | collective-permute-start | bytes 786440 | tf_op jit(solution)/shard_map/ppermute | solution.py:43
  7.8 10.0 %copy-start = (bf16[27,128,256]{2,1,0:T(8,128)(2,1)S(1)}, bf16[27,128,256]{2,1,0:T(8,128)(2,1)}, u32[]{:S(2)}) copy-start(bf16[27,128,256]{2,1,0:T(8,128)(2,1)} %refs_1_.1) | copy-start | bytes 5308420
  7.8 11.2 %collective-permute-start.4 = (bf16[1,8,32,256]{3,2,1,0:T(8,128)(2,1)S(1)}, bf16[1,8,32,256]{3,2,1,0:T(8,128)(2,1)S(1)}, u32[]{:S(2)}, u32[]{:S(2)}) collective-permute-start(bf16[1,8,32,256]{3,2,1,0:T(8,128)(2,1)S(1)} %get-tuple-element.59), channel_id=1, source_target_pairs={{0,1},{1,0},{2,3},{3,2},{4,5},{5,4},{6,7},{7,6},{8,9},{9,8},{10,11... | collective-permute-start | bytes 393224 | tf_op jit(solution)/shard_map/ppermute | solution.py:43
  11.9 7.2 %collective-permute-start.5 = (bf16[1,8,32,256]{3,2,1,0:T(8,128)(2,1)S(1)}, bf16[1,8,32,256]{3,2,1,0:T(8,128)(2,1)S(1)}, u32[]{:S(2)}, u32[]{:S(2)}) collective-permute-start(bf16[1,8,32,256]{3,2,1,0:T(8,128)(2,1)S(1)} %get-tuple-element.60), channel_id=1, source_target_pairs={{1,2},{3,4},{5,6},{7,8},{9,10},{11,12},{13,14},{2,1},{4,3},{6,5},{... | collective-permute-start | bytes 393224 | tf_op jit(solution)/shard_map/ppermute | solution.py:43
  14.0 5.0 %collective-permute-start.2 = (bf16[2,8,32,128]{3,2,1,0:T(8,128)(2,1)S(1)}, bf16[2,8,32,128]{3,2,1,0:T(8,128)(2,1)S(1)}, u32[]{:S(2)}, u32[]{:S(2)}) collective-permute-start(bf16[2,8,32,128]{3,2,1,0:T(8,128)(2,1)S(1)} %get-tuple-element.55), channel_id=1, source_target_pairs={{0,1},{1,0},{2,3},{3,2},{4,5},{5,4},{6,7},{7,6},{8,9},{9,8},{10,11... | collective-permute-start | bytes 393224 | tf_op jit(solution)/shard_map/ppermute | solution.py:43
  17.0 2.1 %collective-permute-start.3 = (bf16[2,8,32,128]{3,2,1,0:T(8,128)(2,1)S(1)}, bf16[2,8,32,128]{3,2,1,0:T(8,128)(2,1)S(1)}, u32[]{:S(2)}, u32[]{:S(2)}) collective-permute-start(bf16[2,8,32,128]{3,2,1,0:T(8,128)(2,1)S(1)} %get-tuple-element.56), channel_id=1, source_target_pairs={{1,2},{3,4},{5,6},{7,8},{9,10},{11,12},{13,14},{2,1},{4,3},{6,5},{... | collective-permute-start | bytes 393224 | tf_op jit(solution)/shard_map/ppermute | solution.py:43
  22.1 5.8 %collective-permute-start.6 = (bf16[8,16,1920]{2,1,0:T(8,128)(2,1)S(1)}, bf16[8,16,1920]{2,1,0:T(8,128)(2,1)S(1)}, u32[]{:S(2)}, u32[]{:S(2)}) collective-permute-start(bf16[8,16,1920]{2,1,0:T(8,128)(2,1)S(1)} %get-tuple-element.66), channel_id=1, source_target_pairs={{0,1},{1,0},{2,3},{3,2},{4,5},{5,4},{6,7},{7,6},{8,9},{9,8},{10,11... | collective-permute-start | bytes 1474568 | tf_op jit(solution)/shard_map/ppermute | solution.py:342
  26.4 7.2 %collective-permute-start.9 = (bf16[8,16,1536]{2,1,0:T(8,128)(2,1)S(1)}, bf16[8,16,1536]{2,1,0:T(8,128)(2,1)S(1)}, u32[]{:S(2)}, u32[]{:S(2)}) collective-permute-start(bf16[8,16,1536]{2,1,0:T(8,128)(2,1)S(1)} %get-tuple-element.72.refs_4_), channel_id=1, source_target_pairs={{0,1},{1,0},{2,3},{3,2},{4,5},{5,4},{6,7},{7,6},{8,9},{9,8},{10,11... | collective-permute-start | bytes 1179656 | tf_op jit(solution)/shard_map/ppermute | solution.py:342
  28.0 12.0 %collective-permute-start.7 = (bf16[4,16,1920]{2,1,0:T(8,128)(2,1)S(1)}, bf16[4,16,1920]{2,1,0:T(8,128)(2,1)S(1)}, u32[]{:S(2)}, u32[]{:S(2)}) collective-permute-start(bf16[4,16,1920]{2,1,0:T(8,128)(2,1)S(1)} %get-tuple-element.68.refs_4_), channel_id=1, source_target_pairs={{0,2},{1,3},{2,0},{3,1},{4,6},{5,7},{6,4},{7,5},{8,10},{9,11},{10,... | collective-permute-start | bytes 737288 | tf_op jit(solution)/shard_map/ppermute | solution.py:342
  33.7 6.9 %collective-permute-start.10 = (bf16[4,16,1536]{2,1,0:T(8,128)(2,1)S(1)}, bf16[4,16,1536]{2,1,0:T(8,128)(2,1)S(1)}, u32[]{:S(2)}, u32[]{:S(2)}) collective-permute-start(bf16[4,16,1536]{2,1,0:T(8,128)(2,1)S(1)} %get-tuple-element.76.refs_5_), channel_id=1, source_target_pairs={{0,4},{1,5},{2,6},{3,7},{4,0},{5,1},{6,2},{7,3},{8,12},{9,13},{10,... | collective-permute-start | bytes 589832 | tf_op jit(solution)/shard_map/ppermute | solution.py:342
  39.4 1.9 %collective-permute-start.13 = (bf16[8,8,1152]{2,1,0:T(8,128)(2,1)S(1)}, bf16[8,8,1152]{2,1,0:T(8,128)(2,1)S(1)}, u32[]{:S(2)}, u32[]{:S(2)}) collective-permute-start(bf16[8,8,1152]{2,1,0:T(8,128)(2,1)S(1)} %get-tuple-element.84), channel_id=1, source_target_pairs={{0,1},{1,0},{2,3},{3,2},{4,5},{5,4},{6,7},{7,6},{8,9},{9,8},{10,11... | collective-permute-start | bytes 442376 | tf_op jit(solution)/shard_map/ppermute | solution.py:342
  39.5 1.8 %collective-permute-start.14 = (bf16[8,8,1152]{2,1,0:T(8,128)(2,1)S(1)}, bf16[8,8,1152]{2,1,0:T(8,128)(2,1)S(1)}, u32[]{:S(2)}, u32[]{:S(2)}) collective-permute-start(bf16[8,8,1152]{2,1,0:T(8,128)(2,1)S(1)} %get-tuple-element.86), channel_id=1, source_target_pairs={{0,1},{1,0},{2,3},{3,2},{4,5},{5,4},{6,7},{7,6},{8,9},{9,8},{10,11... | collective-permute-start | bytes 442376 | tf_op jit(solution)/shard_map/ppermute | solution.py:342
  40.0 1.4 %collective-permute-start.15 = (bf16[8,8,1152]{2,1,0:T(8,128)(2,1)S(1)}, bf16[8,8,1152]{2,1,0:T(8,128)(2,1)S(1)}, u32[]{:S(2)}, u32[]{:S(2)}) collective-permute-start(bf16[8,8,1152]{2,1,0:T(8,128)(2,1)S(1)} %get-tuple-element.88), channel_id=1, source_target_pairs={{0,1},{1,0},{2,3},{3,2},{4,5},{5,4},{6,7},{7,6},{8,9},{9,8},{10,11... | collective-permute-start | bytes 442376 | tf_op jit(solution)/shard_map/ppermute | solution.py:342
  40.1 6.3 %collective-permute-start.8 = (bf16[2,16,1920]{2,1,0:T(8,128)(2,1)S(1)}, bf16[2,16,1920]{2,1,0:T(8,128)(2,1)S(1)}, u32[]{:S(2)}, u32[]{:S(2)}) collective-permute-start(bf16[2,16,1920]{2,1,0:T(8,128)(2,1)S(1)} %get-tuple-element.70.refs_7_), channel_id=1, source_target_pairs={{0,4},{1,5},{2,6},{3,7},{4,0},{5,1},{6,2},{7,3},{8,12},{9,13},{10,... | collective-permute-start | bytes 368648 | tf_op jit(solution)/shard_map/ppermute | solution.py:342
  40.7 5.7 %collective-permute-start.11 = (bf16[2,16,1536]{2,1,0:T(8,128)(2,1)S(1)}, bf16[2,16,1536]{2,1,0:T(8,128)(2,1)S(1)}, u32[]{:S(2)}, u32[]{:S(2)}) collective-permute-start(bf16[2,16,1536]{2,1,0:T(8,128)(2,1)S(1)} %get-tuple-element.78.refs_8_), channel_id=1, source_target_pairs={{0,2},{1,3},{2,0},{3,1},{4,6},{5,7},{6,4},{7,5},{8,10},{9,11},{10,... | collective-permute-start | bytes 294920 | tf_op jit(solution)/shard_map/ppermute | solution.py:342
  41.4 7.6 %collective-permute-start.16 = (bf16[2,8,3456]{2,1,0:T(8,128)(2,1)S(1)}, bf16[2,8,3456]{2,1,0:T(8,128)(2,1)S(1)}, u32[]{:S(2)}, u32[]{:S(2)}) collective-permute-start(bf16[2,8,3456]{2,1,0:T(8,128)(2,1)S(1)} %get-tuple-element.90), channel_id=1, source_target_pairs={{0,2},{1,3},{2,0},{3,1},{4,6},{5,7},{6,4},{7,5},{8,10},{9,11},{10,... | collective-permute-start | bytes 331784 | tf_op jit(solution)/shard_map/ppermute | solution.py:342
  43.0 6.1 %collective-permute-start.17 = (bf16[2,8,3456]{2,1,0:T(8,128)(2,1)S(1)}, bf16[2,8,3456]{2,1,0:T(8,128)(2,1)S(1)}, u32[]{:S(2)}, u32[]{:S(2)}) collective-permute-start(bf16[2,8,3456]{2,1,0:T(8,128)(2,1)S(1)} %get-tuple-element.91), channel_id=1, source_target_pairs={{0,4},{1,5},{2,6},{3,7},{4,0},{5,1},{6,2},{7,3},{8,12},{9,13},{10,... | collective-permute-start | bytes 331784 | tf_op jit(solution)/shard_map/ppermute | solution.py:342
  44.5 8.1 %collective-permute-start.18 = (bf16[2,8,3456]{2,1,0:T(8,128)(2,1)S(1)}, bf16[2,8,3456]{2,1,0:T(8,128)(2,1)S(1)}, u32[]{:S(2)}, u32[]{:S(2)}) collective-permute-start(bf16[2,8,3456]{2,1,0:T(8,128)(2,1)S(1)} %get-tuple-element.92), channel_id=1, source_target_pairs={{0,6},{1,7},{2,4},{3,5},{4,2},{5,3},{6,0},{7,1},{8,14},{9,15},{10,... | collective-permute-start | bytes 331784 | tf_op jit(solution)/shard_map/ppermute | solution.py:342
  46.4 6.7 %collective-permute-start.12 = (bf16[1,16,3456]{2,1,0:T(8,128)(2,1)S(1)}, bf16[1,16,3456]{2,1,0:T(8,128)(2,1)S(1)}, u32[]{:S(2)}, u32[]{:S(2)}) collective-permute-start(bf16[1,16,3456]{2,1,0:T(8,128)(2,1)S(1)} %get-tuple-element.80), channel_id=1, source_target_pairs={{0,8},{1,9},{2,10},{3,11},{4,12},{5,13},{6,14},{7,15},{8,0},{9,1},... | collective-permute-start | bytes 331784 | tf_op jit(solution)/shard_map/ppermute | solution.py:342
  53.2 8.4 %collective-permute-start.19 = (bf16[24,3456]{1,0:T(8,128)(2,1)S(1)}, bf16[24,3456]{1,0:T(8,128)(2,1)S(1)}, u32[]{:S(2)}, u32[]{:S(2)}) collective-permute-start(bf16[24,3456]{1,0:T(8,128)(2,1)S(1)} %get-tuple-element.93.refs_0_), channel_id=1, source_target_pairs={{0,16},{1,17},{2,18},{3,19},{4,20},{5,21},{6,22},{7,23},{8,24},{9,... | collective-permute-start | bytes 497672 | tf_op jit(solution)/shard_map/ppermute | solution.py:347
  54.8 6.1 %collective-permute-start.21 = (bf16[8,3456]{1,0:T(8,128)(2,1)S(1)}, bf16[8,3456]{1,0:T(8,128)(2,1)S(1)}, u32[]{:S(2)}, u32[]{:S(2)}) collective-permute-start(bf16[8,3456]{1,0:T(8,128)(2,1)S(1)} %get-tuple-element.94), channel_id=1, source_target_pairs={{0,24},{1,25},{2,26},{3,27},{4,28},{5,29},{6,30},{7,31},{8,16},{9,... | collective-permute-start | bytes 165896 | tf_op jit(solution)/shard_map/ppermute | solution.py:347
  56.5 5.1 %collective-permute-start.20 = (bf16[8,3456]{1,0:T(8,128)(2,1)S(1)}, bf16[8,3456]{1,0:T(8,128)(2,1)S(1)}, u32[]{:S(2)}, u32[]{:S(2)}) collective-permute-start(bf16[8,3456]{1,0:T(8,128)(2,1)S(1)} %get-tuple-element.94), channel_id=1, source_target_pairs={{0,8},{1,9},{2,10},{3,11},{4,12},{5,13},{6,14},{7,15},{8,0},{9,1},... | collective-permute-start | bytes 165896 | tf_op jit(solution)/shard_map/ppermute | solution.py:342
